TPU v7x, 32 devices: a whole 2x2x4 slice. The times are simulated.
32 devices in a mesh: gx: 4 (over y, x), gy: 4 (over z), gz: 2 (over core).
Axes of the slice: x: 2, y: 2, z: 4, core: 2. Of those that a mesh axis runs over, the one named last changes fastest.
Arguments:
- orbitals: float32 [64, 64, 32, 64], P('gx', 'gy', 'gz'), may hold values from -6 to 6
- potential: float32 [64, 64, 32], P('gx', 'gy', 'gz'), may hold values from -1.5 to 1
Outputs:
- basis: float32 [64, 64, 32, 64], P('gx', 'gy', 'gz')
- blocks: float32 [4, 4, 2, 7, 64, 64], P('gx', 'gy', 'gz')
All inputs are finite; a program needn't handle non-finite values.
Results may differ from a plain program's by a relative error of at most 0.0003.
Values sent between devices are 32-bit elements; how exact they have to be, the bound alone decides.
No kernel may reach another device: no remote copies, remote signals or barrier semaphores. Data moves between devices by JAX's collectives and lax.ppermute only.
A program may use at most 128 MiB of HBM per device.

v0:
```python
import jax
import jax.numpy as jnp
import numpy as np
from jax import lax
from jax.sharding import PartitionSpec as P

BUF = 3


PENALTY = 2.0
LOW_BOUND = -1.5
CUTOFF = 8.0
HIGH_BOUND = 16.0


def extended(cells, sides, width):
    for axis, dim in sides:
        count = lax.axis_size(axis)
        head = lax.slice_in_dim(cells, 0, width, axis=dim)
        tail = lax.slice_in_dim(cells, cells.shape[dim] - width, cells.shape[dim], axis=dim)
        cells = jnp.concatenate(
            [
                lax.ppermute(tail, axis, [(i, (i + 1) % count) for i in range(count)]),
                cells,
                lax.ppermute(head, axis, [((i + 1) % count, i) for i in range(count)]),
            ],
            axis=dim,
        )
    return cells


def spectral_tables(points):
    indices = np.arange(points)
    offsets = indices[:, None] - indices[None, :]
    nyquist = points // 2
    deriv_one = np.zeros((points, points))
    deriv_two = np.zeros((points, points))
    for harmonic in range(1, nyquist):
        wavenum = 2.0 * np.pi * harmonic / points
        deriv_one = deriv_one - 2.0 * wavenum * np.sin(wavenum * offsets) / points
        deriv_two = deriv_two - 2.0 * wavenum * wavenum * np.cos(wavenum * offsets) / points
    deriv_two = deriv_two - np.pi * np.pi * np.cos(np.pi * offsets) / points
    return (jnp.asarray(deriv_one, jnp.float32), jnp.asarray(deriv_two, jnp.float32))


def apply_along(matrix, field, axis_pos):
    forms = ("ia,ajko->ijko", "ja,iako->ijko", "ka,ijao->ijko")
    return jnp.einsum(forms[axis_pos], matrix, field, precision=lax.Precision.HIGHEST)


def hamiltonian(field, ext_pot, deriv_two):
    first_len, second_len, third_len, width = field.shape
    flat = field.reshape(first_len, second_len, third_len * width)
    along_x = jnp.einsum("ia,ajk->ijk", deriv_two, flat, precision=lax.Precision.HIGHEST)
    along_y = jnp.einsum("ja,iak->ijk", deriv_two, flat, precision=lax.Precision.HIGHEST)
    laplace = (along_x + along_y).reshape(field.shape) + apply_along(deriv_two, field, 2)
    return -0.5 * laplace + ext_pot[..., None] * field


def chebyshev(start, ext_pot, deriv_two):
    half_width = (HIGH_BOUND - CUTOFF) / 2.0
    center = (HIGH_BOUND + CUTOFF) / 2.0
    scale_now = half_width / (LOW_BOUND - center)
    tau_factor = 2.0 / scale_now
    current = (hamiltonian(start, ext_pot, deriv_two) - center * start) * (scale_now / half_width)
    scale_next = 1.0 / (tau_factor - scale_now)
    applied = hamiltonian(current, ext_pot, deriv_two) - center * current
    following = applied * (2.0 * scale_next / half_width) - scale_now * scale_next * start
    return following


def element_fields(ext_orb, ext_pot, deriv_one, deriv_two, margin, cells):
    filtered = chebyshev(ext_orb, ext_pot, deriv_two)
    stop = margin + cells
    row_block = deriv_one[margin:stop]
    interior = filtered[margin:stop, margin:stop, margin:stop]
    grad_x = apply_along(row_block, filtered[:, margin:stop, margin:stop], 0)
    grad_y = apply_along(row_block, filtered[margin:stop, :, margin:stop], 1)
    grad_z = apply_along(row_block, filtered[margin:stop, margin:stop, :], 2)
    return (interior, grad_x, grad_y, grad_z)


def face_product(left, right):
    return jnp.einsum("...pqi,...pqj->...ij", left, right, precision=lax.Precision.HIGHEST)


def neighbour_block(own_value, own_deriv, other_value, other_deriv, sign):
    skew = face_product(own_deriv, other_value) - face_product(own_value, other_deriv)
    return 0.25 * sign * skew - 0.5 * PENALTY * face_product(own_value, other_value)


def own_face(value, deriv, sign):
    mixed = face_product(value, deriv) + face_product(deriv, value)
    return -0.25 * sign * mixed + 0.5 * PENALTY * face_product(value, value)


def assemble(interior, gradients, pot_el, lowers, uppers):
    volume_form = "...xyzi,...xyzj->...ij"
    diagonal = jnp.einsum(
        volume_form, interior, pot_el[..., None] * interior, precision=lax.Precision.HIGHEST
    )
    for axis_pos in range(3):
        diagonal = diagonal + 0.5 * jnp.einsum(
            volume_form, gradients[axis_pos], gradients[axis_pos], precision=lax.Precision.HIGHEST
        )
    cells = interior.shape[-2]
    coupled = []
    for axis_pos in range(3):
        grid_axis = interior.ndim - 4 + axis_pos
        low_value = jnp.take(interior, 0, axis=grid_axis)
        low_deriv = jnp.take(gradients[axis_pos], 0, axis=grid_axis)
        high_value = jnp.take(interior, cells - 1, axis=grid_axis)
        high_deriv = jnp.take(gradients[axis_pos], cells - 1, axis=grid_axis)
        diagonal = diagonal + own_face(low_value, low_deriv, -1.0)
        diagonal = diagonal + own_face(high_value, high_deriv, 1.0)
        coupled.append(
            neighbour_block(low_value, low_deriv, lowers[axis_pos][0], lowers[axis_pos][1], -1.0)
        )
        coupled.append(
            neighbour_block(high_value, high_deriv, uppers[axis_pos][0], uppers[axis_pos][1], 1.0)
        )
    return jnp.stack([diagonal] + coupled, axis=-3)


def on_device(orbitals, potential):
    ext_orb, ext_pot = (
        extended(orbitals, (("gx", 0), ("gy", 1), ("gz", 2)), BUF),
        extended(potential, (("gx", 0), ("gy", 1), ("gz", 2)), BUF),
    )
    cells = orbitals.shape[0]
    deriv_one, deriv_two = spectral_tables(ext_orb.shape[0])
    interior, grad_x, grad_y, grad_z = element_fields(
        ext_orb, ext_pot, deriv_one, deriv_two, BUF, cells
    )
    gradients = (grad_x, grad_y, grad_z)
    padded_x = (extended(interior, (("gx", 0),), 1), extended(grad_x, (("gx", 0),), 1))
    padded_y = (extended(interior, (("gy", 1),), 1), extended(grad_y, (("gy", 1),), 1))
    padded_z = (extended(interior, (("gz", 2),), 1), extended(grad_z, (("gz", 2),), 1))
    lowers = (
        (padded_x[0][0], padded_x[1][0]),
        (padded_y[0][:, 0], padded_y[1][:, 0]),
        (padded_z[0][:, :, 0], padded_z[1][:, :, 0]),
    )
    uppers = (
        (padded_x[0][-1], padded_x[1][-1]),
        (padded_y[0][:, -1], padded_y[1][:, -1]),
        (padded_z[0][:, :, -1], padded_z[1][:, :, -1]),
    )
    blocks = assemble(interior, gradients, potential, lowers, uppers)
    return (interior, blocks[None, None, None])


def solution(mesh):
    return jax.shard_map(
        on_device,
        mesh=mesh,
        in_specs=(P("gx", "gy", "gz", None), P("gx", "gy", "gz")),
        out_specs=(P("gx", "gy", "gz", None), P("gx", "gy", "gz", None, None, None)),
        check_vma=False,
    )
```

profile of v0, /device:TPU:0, one launch (start us, length us, event | category | flops | bytes accessed | tf_op | source)
XLA Modules:
  0.0 218.8 jit_solution(14471420709127344287)
XLA Ops:
  0.6 0.8 fusion.143
  1.4 3.9 %collective-permute-start.7 = (f32[3,16,16]{2,1,0:T(8,128)S(1)}, f32[3,16,16]{2,1,0:T(8,128)S(1)}, u32[]{:S(2)}, u32[]{:S(2)}) collective-permute-start(f32[3,16,16]{2,1,0:T(8,128)S(1)} %get-tuple-element.98), channel_id=1, source_target_pairs={{8,0},{16,8},{24,16},{0,24},{9,1},{17,9},{25,17},{1,25},{10,2},{18... | collective-permute-start | bytes 9224 | tf_op jit(solution)/shard_map/ppermute | solution.py:25
  5.3 1.2 fusion.140
  6.5 3.0 %collective-permute-start.1 = (f32[3,16,16,64]{3,2,1,0:T(8,128)S(1)}, f32[3,16,16,64]{3,2,1,0:T(8,128)S(1)}, u32[]{:S(2)}, u32[]{:S(2)}) collective-permute-start(f32[3,16,16,64]{3,2,1,0:T(8,128)S(1)} %get-tuple-element.92), channel_id=1, source_target_pairs={{8,0},{16,8},{24,16},{0,24},{9,1},{17,9},{25,17},{1,25},{10,2},{18... | collective-permute-start | bytes 589832 | tf_op jit(solution)/shard_map/ppermute | solution.py:25
  9.4 0.8 collective-permute-done.6
  10.3 0.9 constant_dynamic-update-slice_fusion.4
  11.2 15.5 %collective-permute-done = f32[3,16,16,64]{3,2,1,0:T(8,128)S(1)} collective-permute-done((f32[3,16,16,64]{3,2,1,0:T(8,128)S(1)}, f32[3,16,16,64]{3,2,1,0:T(8,128)S(1)}, u32[]{:S(2)}, u32[]{:S(2)}) %collective-permute-start) | collective-permute-done | bytes 196640 | tf_op jit(solution)/shard_map/ppermute | solution.py:23
  26.7 1.7 constant_dynamic-update-slice_fusion.1
  28.6 1.6 collective-permute-start.2
  30.2 2.2 %collective-permute-start.3 = (f32[22,3,16,64]{3,2,1,0:T(8,128)S(1)}, f32[22,3,16,64]{3,2,1,0:T(8,128)S(1)}, u32[]{:S(2)}, u32[]{:S(2)}) collective-permute-start(f32[22,3,16,64]{3,2,1,0:T(8,128)S(1)} %get-tuple-element.85), channel_id=1, source_target_pairs={{2,0},{4,2},{6,4},{0,6},{3,1},{5,3},{7,5},{1,7},{10,8},{12,10},{14... | collective-permute-start | bytes 811016 | tf_op jit(solution)/shard_map/ppermute | solution.py:25
  32.6 3.8 %collective-permute-start.9 = (f32[22,3,16]{2,1,0:T(4,128)S(1)}, f32[22,3,16]{2,1,0:T(4,128)S(1)}, u32[]{:S(2)}, u32[]{:S(2)}) collective-permute-start(f32[22,3,16]{2,1,0:T(4,128)S(1)} %get-tuple-element.97), channel_id=1, source_target_pairs={{2,0},{4,2},{6,4},{0,6},{3,1},{5,3},{7,5},{1,7},{10,8},{12,10},{14... | collective-permute-start | bytes 12680 | tf_op jit(solution)/shard_map/ppermute | solution.py:25
  36.4 20.4 %collective-permute-done.8 = f32[22,3,16]{2,1,0:T(4,128)S(1)} collective-permute-done((f32[22,3,16]{2,1,0:T(4,128)S(1)}, f32[22,3,16]{2,1,0:T(4,128)S(1)}, u32[]{:S(2)}, u32[]{:S(2)}) %collective-permute-start.8) | collective-permute-done | bytes 4256 | tf_op jit(solution)/shard_map/ppermute | solution.py:23
  56.9 0.4 pad_maximum_fusion.3
  57.6 0.5 collective-permute-start.4
  58.3 0.4 collective-permute-start.11
  58.8 2.6 %collective-permute-done.10 = f32[22,22,3]{2,1,0:T(8,128)S(1)} collective-permute-done((f32[22,22,3]{2,1,0:T(8,128)S(1)}, f32[22,22,3]{2,1,0:T(8,128)S(1)}, u32[]{:S(2)}, u32[]{:S(2)}) %collective-permute-start.10) | collective-permute-done | bytes 5840 | tf_op jit(solution)/shard_map/ppermute | solution.py:23
  61.4 0.4 collective-permute-done.11
  61.8 1.1 broadcast_multiply_fusion.1
  63.4 0.6 copy-done.4
  64.1 1.0 copy-done.5
  65.1 3.5 %pad_maximum_fusion = f32[22,22,22,64]{3,2,1,0:T(8,128)} fusion(f32[22,22,3,64]{3,2,1,0:T(4,128)S(1)} %copy.22, f32[22,3,16,64]{3,2,1,0:T(8,128)S(1)} %collective-permute-done.3, f32[22,16,16,64]{3,2,1,0:T(8,128)S(1)} %constant_dynamic-update-slice_fusion, f32[22,3,16,64]{3,2,1,0:T(8,128)S(1)} %collective-permute-done.2, f32[22,22,3,64]{3,2,1,0:T(4,128)S(1)} %copy.21), kind=kLoop, calls=%fused_computation | loop fusion | flops 2725888 | bytes 5451776 | tf_op jit(solution)/shard_map/concatenate | solution.py:21
  68.6 4.1 %reshape.255 = f32[22,22,1408]{2,1,0:T(8,128)S(1)} reshape(f32[22,22,22,64]{3,2,1,0:T(8,128)} %pad_maximum_fusion) | data formatting | bytes 5451776 | tf_op jit(solution)/shard_map/reshape | solution.py:53
  72.7 2.8 %fusion.144 = f32[22,1408,22]{1,2,0:T(8,128)S(1)} fusion(f32[22,22,1408]{2,1,0:T(8,128)S(1)} %reshape.255, f32[22,22,1]{1,0,2:T(8,128)S(1)} %copy-done.8), kind=kOutput, calls=%fused_computation.198 | convolution fusion | flops 179908608 | bytes 5453712 | tf_op jit(solution)/shard_map/ja,iak->ijk/dot_general | solution.py:55
  75.5 5.0 %convolution_add_fusion.1 = f32[22,22,1408]{2,0,1:T(8,128)} fusion(f32[22,22,1]{1,0,2:T(8,128)S(1)} %copy-done.8, f32[22,22,1408]{2,1,0:T(8,128)S(1)} %reshape.255, f32[22,1408,22]{1,2,0:T(8,128)S(1)} %fusion.144), kind=kOutput, calls=%fused_computation.12 | convolution fusion | flops 180590080 | bytes 8179600 | tf_op jit(solution)/shard_map/ia,ajk->ijk/dot_general | solution.py:54
  80.5 5.6 %reshape.25 = f32[22,22,22,64]{3,2,0,1:T(8,128)} reshape(f32[22,22,1408]{2,0,1:T(8,128)} %convolution_add_fusion.1) | data formatting | bytes 5451776 | tf_op jit(solution)/shard_map/reshape | solution.py:56
  86.1 15.4 %broadcast_multiply_fusion = (f32[22,22,22,64]{3,2,1,0:T(8,128)}, f32[22,22,22,64]{3,2,1,0:T(8,128)}) fusion(f32[22,22,3,64]{3,2,1,0:T(4,128)} %copy-done.4, f32[22,3,16,64]{3,2,1,0:T(8,128)} %copy-done.6, f32[22,16,16,64]{3,2,1,0:T(8,128)S(1)} %copy-done.2, f32[22,3,16,64]{3,2,1,0:T(8,128)S(1)} %collective-permute-done.2, f32[22,22,3,64]{3,2,1,0:T(4,128)} %copy-done.5, ...), kind=kOutput, calls=%fused_computation.21 | convolution fusion | flops 190130688 | bytes 10948080 | tf_op jit(solution)/shard_map/ka,ijao->ijko/dot_general | solution.py:48
  101.5 4.5 %reshape.26 = f32[22,22,1408]{2,1,0:T(8,128)S(1)} reshape(f32[22,22,22,64]{3,2,1,0:T(8,128)} %get-tuple-element.100) | data formatting | bytes 5451776 | tf_op jit(solution)/shard_map/reshape | solution.py:53
  106.0 2.6 %fusion.145 = f32[22,1408,22]{1,2,0:T(8,128)S(1)} fusion(f32[22,22,1408]{2,1,0:T(8,128)S(1)} %reshape.26, f32[22,22,1]{1,0,2:T(8,128)S(1)} %copy-done.8), kind=kOutput, calls=%fused_computation.199 | convolution fusion | flops 179908608 | bytes 5453712 | tf_op jit(solution)/shard_map/ja,iak->ijk/dot_general | solution.py:55
  108.6 3.6 %convolution_add_fusion = f32[22,22,1408]{2,0,1:T(8,128)S(1)} fusion(f32[22,22,1]{1,0,2:T(8,128)S(1)} %copy-done.8, f32[22,1408,22]{1,2,0:T(8,128)S(1)} %fusion.145, f32[22,22,1408]{2,1,0:T(8,128)S(1)} %reshape.26), kind=kOutput, calls=%fused_computation.11 | convolution fusion | flops 180590080 | bytes 8179600 | tf_op jit(solution)/shard_map/ia,ajk->ijk/dot_general | solution.py:54
  112.2 2.1 copy.29
  114.3 5.6 %reshape.27 = f32[22,22,22,64]{3,2,1,0:T(8,128)} reshape(f32[22,22,1408]{2,1,0:T(8,128)} %copy.29) | data formatting | bytes 5451776 | tf_op jit(solution)/shard_map/reshape | solution.py:56
  119.9 15.7 %fusion.4 = f32[22,22,22,64]{3,2,1,0:T(8,128)S(1)} fusion(f32[22,22,22,64]{3,2,1,0:T(8,128)} %reshape.27, f32[22,22,22,64]{3,2,1,0:T(8,128)} %get-tuple-element.101, f32[22,22,22]{2,1,0:T(8,128)} %get-tuple-element.74, f32[22,22,1,1]{1,0,3,2:T(8,128)S(1)} %copy-done.11, f32[22,22,3,64]{3,2,1,0:T(4,128)} %copy-done.4, f32[22,3,16,64]{3,2,1,0:T(8,128)} %copy-done.6, ...), kind=kOutput, calls=%fused_computation.6 | convolution fusion | flops 189449216 | bytes 10948080 | tf_op jit(solution)/shard_map/ka,ijao->ijko/dot_general | solution.py:48
  138.1 0.4 slice.225
  139.1 0.4 collective-permute-start.22
  139.9 2.2 convolution_bitcast_fusion
  142.9 0.4 collective-permute-start.23
  143.7 4.2 %fusion.33 = f32[64,64]{1,0:T(8,128)S(1)} fusion(f32[16,16,16,64]{3,2,1,0:T(8,128)S(1)} %slice.224, f32[16,16,16]{2,1,0:T(8,128)S(1)} %copy-done.7), kind=kOutput, calls=%fused_computation.77 | convolution fusion | flops 201588736 | bytes 1081344 | tf_op jit(solution)/shard_map/...xyzi,...xyzj->...ij/dot_general | solution.py:99
  147.9 3.3 %fusion.16 = f32[16,16,16,64]{3,1,2,0:T(8,128)S(1)} fusion(f32[16,22,1,1]{1,0,3,2:T(8,128)S(1)} %copy-done.9, f32[16,22,16,64]{3,2,1,0:T(8,128)S(1)} %slice.226), kind=kOutput, calls=%fused_computation.23 | convolution fusion | flops 69206016 | bytes 2491776 | tf_op jit(solution)/shard_map/ja,iako->ijko/dot_general | solution.py:48
  151.7 2.1 collective-permute-start.19
  154.2 3.6 %fusion.10 = f32[16,16,16,64]{3,0,2,1:T(8,128)S(1)} fusion(f32[16,22,1,1]{1,0,3,2:T(8,128)S(1)} %copy-done.9, f32[22,16,16,64]{3,2,1,0:T(8,128)S(1)} %slice.225), kind=kOutput, calls=%fused_computation.15 | convolution fusion | flops 69206016 | bytes 2491776 | tf_op jit(solution)/shard_map/ia,ajko->ijko/dot_general | solution.py:48
  158.0 3.6 %fusion.25 = f32[64,64]{1,0:T(8,128)S(1)} fusion(f32[64,64]{1,0:T(8,128)S(1)} %fusion.33, f32[16,16,16,64]{3,0,2,1:T(8,128)S(1)} %fusion.10), kind=kOutput, calls=%fused_computation.69 | convolution fusion | flops 201334784 | bytes 1081344 | tf_op jit(solution)/shard_map/...xyzi,...xyzj->...ij/dot_general | solution.py:103
  161.7 3.6 %fusion.23 = f32[64,64]{1,0:T(8,128)S(1)} fusion(f32[64,64]{1,0:T(8,128)S(1)} %fusion.25, f32[16,16,16,64]{3,1,2,0:T(8,128)S(1)} %fusion.16), kind=kOutput, calls=%fused_computation.66 | convolution fusion | flops 201334784 | bytes 1081344 | tf_op jit(solution)/shard_map/...xyzi,...xyzj->...ij/dot_general | solution.py:103
  165.3 0.4 convolution_bitcast_fusion.32
  165.7 0.4 convolution_bitcast_fusion.35
  166.1 0.4 fusion.53
  166.5 0.4 fusion.50
  166.9 0.6 fusion.47
  167.4 0.4 fusion.44
  167.8 0.4 fusion.41
  168.2 0.4 fusion.38
  168.6 3.7 %fusion.32 = f32[7,64,64]{2,1,0:T(8,128)S(1)} fusion(f32[64,64]{1,0:T(8,128)S(1)} %fusion.53, f32[64,64]{1,0:T(8,128)S(1)} %fusion.50, f32[64,64]{1,0:T(8,128)S(1)} %fusion.47, f32[64,64]{1,0:T(8,128)S(1)} %fusion.44, f32[64,64]{1,0:T(8,128)S(1)} %fusion.41, f32[64,64]{1,0:T(8,128)S(1)} %fusion.38, f32[64,64]{1,0:T(8,128)S(1)} %fusion.23, ...), kind=kOutput, calls=%fused_computation.76 | convolution fusion | flops 201359360 | bytes 4456448 | tf_op jit(solution)/shard_map/...xyzi,...xyzj->...ij/dot_general | solution.py:103
  172.4 0.4 convolution_bitcast_fusion.8
  172.8 6.7 %collective-permute-done.17 = f32[16,1,16,64]{3,1,2,0:T(1,128)S(1)} collective-permute-done((f32[16,1,16,64]{3,1,2,0:T(1,128)S(1)}, f32[16,1,16,64]{3,1,2,0:T(1,128)S(1)}, u32[]{:S(2)}, u32[]{:S(2)}) %collective-permute-start.17) | collective-permute-done | bytes 65568 | tf_op jit(solution)/shard_map/ppermute | solution.py:23
  179.4 0.9 collective-permute-start.15
  180.7 3.7 %collective-permute-done.15 = f32[1,16,16,64]{3,0,2,1:T(1,128)S(1)} collective-permute-done((f32[1,16,16,64]{3,0,2,1:T(1,128)S(1)}, f32[1,16,16,64]{3,0,2,1:T(1,128)S(1)}, u32[]{:S(2)}, u32[]{:S(2)}) %collective-permute-start.15) | collective-permute-done | bytes 65568 | tf_op jit(solution)/shard_map/ppermute | solution.py:25
  184.4 1.8 collective-permute-start.13
  186.6 4.4 %collective-permute-done.13 = f32[1,16,16,64]{3,0,2,1:T(1,128)S(1)} collective-permute-done((f32[1,16,16,64]{3,0,2,1:T(1,128)S(1)}, f32[1,16,16,64]{3,0,2,1:T(1,128)S(1)}, u32[]{:S(2)}, u32[]{:S(2)}) %collective-permute-start.13) | collective-permute-done | bytes 65568 | tf_op jit(solution)/shard_map/ppermute | solution.py:23
  191.5 5.4 %collective-permute-done.14 = f32[1,16,16,64]{3,2,1,0:T(8,128)S(1)} collective-permute-done((f32[1,16,16,64]{3,2,1,0:T(8,128)S(1)}, f32[1,16,16,64]{3,2,1,0:T(8,128)S(1)}, u32[]{:S(2)}, u32[]{:S(2)}) %collective-permute-start.14) | collective-permute-done | bytes 65568 | tf_op jit(solution)/shard_map/ppermute | solution.py:25
  196.9 1.8 collective-permute-start.12
  199.1 3.7 %collective-permute-done.12 = f32[1,16,16,64]{3,2,1,0:T(8,128)S(1)} collective-permute-done((f32[1,16,16,64]{3,2,1,0:T(8,128)S(1)}, f32[1,16,16,64]{3,2,1,0:T(8,128)S(1)}, u32[]{:S(2)}, u32[]{:S(2)}) %collective-permute-start.12) | collective-permute-done | bytes 65568 | tf_op jit(solution)/shard_map/ppermute | solution.py:23
  203.1 5.1 %collective-permute-done.18 = f32[16,1,16,64]{3,2,1,0:T(8,128)S(1)} collective-permute-done((f32[16,1,16,64]{3,2,1,0:T(8,128)S(1)}, f32[16,1,16,64]{3,2,1,0:T(8,128)S(1)}, u32[]{:S(2)}, u32[]{:S(2)}) %collective-permute-start.18) | collective-permute-done | bytes 65568 | tf_op jit(solution)/shard_map/ppermute | solution.py:25
  208.3 0.4 convolution_bitcast_fusion.7
  210.2 4.8 %collective-permute-done.16 = f32[16,1,16,64]{3,2,1,0:T(8,128)S(1)} collective-permute-done((f32[16,1,16,64]{3,2,1,0:T(8,128)S(1)}, f32[16,1,16,64]{3,2,1,0:T(8,128)S(1)}, u32[]{:S(2)}, u32[]{:S(2)}) %collective-permute-start.16) | collective-permute-done | bytes 65568 | tf_op jit(solution)/shard_map/ppermute | solution.py:23
  217.7 0.7 copy-done.10
  (90 shorter events, 13.2 us)
Async XLA Ops:
  1.4 9.8 %collective-permute-start.7 = (f32[3,16,16]{2,1,0:T(8,128)S(1)}, f32[3,16,16]{2,1,0:T(8,128)S(1)}, u32[]{:S(2)}, u32[]{:S(2)}) collective-permute-start(f32[3,16,16]{2,1,0:T(8,128)S(1)} %get-tuple-element.98), channel_id=1, source_target_pairs={{8,0},{16,8},{24,16},{0,24},{9,1},{17,9},{25,17},{1,25},{10,2},{18... | collective-permute-start | bytes 9224 | tf_op jit(solution)/shard_map/ppermute | solution.py:25
  5.3 5.0 %collective-permute-start.6 = (f32[3,16,16]{2,1,0:T(8,128)S(1)}, f32[3,16,16]{2,1,0:T(8,128)S(1)}, u32[]{:S(2)}, u32[]{:S(2)}) collective-permute-start(f32[3,16,16]{2,1,0:T(8,128)S(1)} %get-tuple-element.99), channel_id=1, source_target_pairs={{0,8},{8,16},{16,24},{24,0},{1,9},{9,17},{17,25},{25,1},{2,10},{10... | collective-permute-start | bytes 9224 | tf_op jit(solution)/shard_map/ppermute | solution.py:23
  6.5 22.0 %collective-permute-start.1 = (f32[3,16,16,64]{3,2,1,0:T(8,128)S(1)}, f32[3,16,16,64]{3,2,1,0:T(8,128)S(1)}, u32[]{:S(2)}, u32[]{:S(2)}) collective-permute-start(f32[3,16,16,64]{3,2,1,0:T(8,128)S(1)} %get-tuple-element.92), channel_id=1, source_target_pairs={{8,0},{16,8},{24,16},{0,24},{9,1},{17,9},{25,17},{1,25},{10,2},{18... | collective-permute-start | bytes 589832 | tf_op jit(solution)/shard_map/ppermute | solution.py:25
  9.4 17.2 %collective-permute-start = (f32[3,16,16,64]{3,2,1,0:T(8,128)S(1)}, f32[3,16,16,64]{3,2,1,0:T(8,128)S(1)}, u32[]{:S(2)}, u32[]{:S(2)}) collective-permute-start(f32[3,16,16,64]{3,2,1,0:T(8,128)S(1)} %get-tuple-element.93), channel_id=1, source_target_pairs={{0,8},{8,16},{16,24},{24,0},{1,9},{9,17},{17,25},{25,1},{2,10},{10... | collective-permute-start | bytes 589832 | tf_op jit(solution)/shard_map/ppermute | solution.py:23
  28.5 34.9 %copy-start.1 = (f32[22,16,16,64]{3,2,1,0:T(8,128)}, f32[22,16,16,64]{3,2,1,0:T(8,128)S(1)}, u32[]{:S(2)}) copy-start(f32[22,16,16,64]{3,2,1,0:T(8,128)S(1)} %constant_dynamic-update-slice_fusion) | copy-start | bytes 4325380
  28.6 28.2 %collective-permute-start.2 = (f32[22,3,16,64]{3,2,1,0:T(8,128)S(1)}, f32[22,3,16,64]{3,2,1,0:T(8,128)S(1)}, u32[]{:S(2)}, u32[]{:S(2)}) collective-permute-start(f32[22,3,16,64]{3,2,1,0:T(8,128)S(1)} %get-tuple-element.84), channel_id=1, source_target_pairs={{0,2},{2,4},{4,6},{6,0},{1,3},{3,5},{5,7},{7,1},{8,10},{10,12},{12... | collective-permute-start | bytes 811016 | tf_op jit(solution)/shard_map/ppermute | solution.py:23
  30.2 26.6 %collective-permute-start.3 = (f32[22,3,16,64]{3,2,1,0:T(8,128)S(1)}, f32[22,3,16,64]{3,2,1,0:T(8,128)S(1)}, u32[]{:S(2)}, u32[]{:S(2)}) collective-permute-start(f32[22,3,16,64]{3,2,1,0:T(8,128)S(1)} %get-tuple-element.85), channel_id=1, source_target_pairs={{2,0},{4,2},{6,4},{0,6},{3,1},{5,3},{7,5},{1,7},{10,8},{12,10},{14... | collective-permute-start | bytes 811016 | tf_op jit(solution)/shard_map/ppermute | solution.py:25
  32.5 24.3 %collective-permute-start.8 = (f32[22,3,16]{2,1,0:T(4,128)S(1)}, f32[22,3,16]{2,1,0:T(4,128)S(1)}, u32[]{:S(2)}, u32[]{:S(2)}) collective-permute-start(f32[22,3,16]{2,1,0:T(4,128)S(1)} %get-tuple-element.96), channel_id=1, source_target_pairs={{0,2},{2,4},{4,6},{6,0},{1,3},{3,5},{5,7},{7,1},{8,10},{10,12},{12... | collective-permute-start | bytes 12680 | tf_op jit(solution)/shard_map/ppermute | solution.py:23
  32.6 24.2 %collective-permute-start.9 = (f32[22,3,16]{2,1,0:T(4,128)S(1)}, f32[22,3,16]{2,1,0:T(4,128)S(1)}, u32[]{:S(2)}, u32[]{:S(2)}) collective-permute-start(f32[22,3,16]{2,1,0:T(4,128)S(1)} %get-tuple-element.97), channel_id=1, source_target_pairs={{2,0},{4,2},{6,4},{0,6},{3,1},{5,3},{7,5},{1,7},{10,8},{12,10},{14... | collective-permute-start | bytes 12680 | tf_op jit(solution)/shard_map/ppermute | solution.py:25
  56.9 6.6 %copy-start.6 = (f32[22,3,16,64]{3,2,1,0:T(8,128)}, f32[22,3,16,64]{3,2,1,0:T(8,128)S(1)}, u32[]{:S(2)}) copy-start(f32[22,3,16,64]{3,2,1,0:T(8,128)S(1)} %collective-permute-done.3) | copy-start | bytes 811012
  57.5 5.4 %collective-permute-start.5 = (f32[22,22,3,64]{3,1,2,0:T(8,128)S(1)}, f32[22,22,3,64]{3,1,2,0:T(8,128)S(1)}, u32[]{:S(2)}, u32[]{:S(2)}) collective-permute-start(f32[22,22,3,64]{3,1,2,0:T(8,128)S(1)} %copy.20), channel_id=1, source_target_pairs={{1,0},{0,1},{3,2},{2,3},{5,4},{4,5},{7,6},{6,7},{9,8},{8,9},{11,10... | collective-permute-start | bytes 1115144 | tf_op jit(solution)/shard_map/ppermute | solution.py:25
  57.6 5.6 %collective-permute-start.4 = (f32[22,22,3,64]{3,1,2,0:T(8,128)S(1)}, f32[22,22,3,64]{3,1,2,0:T(8,128)S(1)}, u32[]{:S(2)}, u32[]{:S(2)}) collective-permute-start(f32[22,22,3,64]{3,1,2,0:T(8,128)S(1)} %copy.19), channel_id=1, source_target_pairs={{0,1},{1,0},{2,3},{3,2},{4,5},{5,4},{6,7},{7,6},{8,9},{9,8},{10,11... | collective-permute-start | bytes 1115144 | tf_op jit(solution)/shard_map/ppermute | solution.py:23
  58.2 3.2 %collective-permute-start.10 = (f32[22,22,3]{2,1,0:T(8,128)S(1)}, f32[22,22,3]{2,1,0:T(8,128)S(1)}, u32[]{:S(2)}, u32[]{:S(2)}) collective-permute-start(f32[22,22,3]{2,1,0:T(8,128)S(1)} %get-tuple-element.94), channel_id=1, source_target_pairs={{0,1},{1,0},{2,3},{3,2},{4,5},{5,4},{6,7},{7,6},{8,9},{9,8},{10,11... | collective-permute-start | bytes 17432 | tf_op jit(solution)/shard_map/ppermute | solution.py:23
  58.3 3.5 %collective-permute-start.11 = (f32[22,22,3]{2,1,0:T(8,128)S(1)}, f32[22,22,3]{2,1,0:T(8,128)S(1)}, u32[]{:S(2)}, u32[]{:S(2)}) collective-permute-start(f32[22,22,3]{2,1,0:T(8,128)S(1)} %get-tuple-element.95), channel_id=1, source_target_pairs={{1,0},{0,1},{3,2},{2,3},{5,4},{4,5},{7,6},{6,7},{9,8},{8,9},{11,10... | collective-permute-start | bytes 17432 | tf_op jit(solution)/shard_map/ppermute | solution.py:25
  63.1 0.9 copy-start.4
  64.1 1.0 copy-start.5
  68.6 4.1 %copy-start.8 = (f32[22,22,1]{1,0,2:T(8,128)S(1)}, f32[22,22,1]{1,0,2:T(8,128)}, u32[]{:S(2)}) copy-start(f32[22,22,1]{1,0,2:T(8,128)} %constant.260) | copy-start | bytes 5812
  80.5 5.6 %copy-start.2 = (f32[22,16,16,64]{3,2,1,0:T(8,128)S(1)}, f32[22,16,16,64]{3,2,1,0:T(8,128)}, u32[]{:S(2)}) copy-start(f32[22,16,16,64]{3,2,1,0:T(8,128)} %copy-done.1) | copy-start | bytes 4325380
  80.5 5.6 %copy-start.11 = (f32[22,22,1,1]{1,0,3,2:T(8,128)S(1)}, f32[22,22,1,1]{1,0,3,2:T(8,128)}, u32[]{:S(2)}) copy-start(f32[22,22,1,1]{1,0,3,2:T(8,128)} %constant.261) | copy-start | bytes 5812
  114.3 5.6 %copy-start.3 = (f32[22,16,16,64]{3,2,1,0:T(8,128)S(1)}, f32[22,16,16,64]{3,2,1,0:T(8,128)}, u32[]{:S(2)}) copy-start(f32[22,16,16,64]{3,2,1,0:T(8,128)} %copy-done.1) | copy-start | bytes 4325380
  137.7 6.0 %copy-start = (f32[16,16,16,64]{3,2,1,0:T(8,128)}, f32[16,16,16,64]{3,2,1,0:T(8,128)S(1)}, u32[]{:S(2)}) copy-start(f32[16,16,16,64]{3,2,1,0:T(8,128)S(1)} %slice.224) | copy-start | bytes 3145732
  137.7 2.2 copy-start.9
  138.1 5.6 %copy-start.7 = (f32[16,16,16]{2,1,0:T(8,128)S(1)}, f32[16,16,16]{2,1,0:T(8,128)}, u32[]{:S(2)}) copy-start(f32[16,16,16]{2,1,0:T(8,128)} %param.17) | copy-start | bytes 49156
  138.5 70.5 %collective-permute-start.20 = (f32[16,16,1,64]{3,2,1,0:T(1,128)S(1)}, f32[16,16,1,64]{3,2,1,0:T(1,128)S(1)}, u32[]{:S(2)}, u32[]{:S(2)}) collective-permute-start(f32[16,16,1,64]{3,2,1,0:T(1,128)S(1)} %get-tuple-element.81), channel_id=1, source_target_pairs={{0,1},{1,0},{2,3},{3,2},{4,5},{5,4},{6,7},{7,6},{8,9},{9,8},{10,11... | collective-permute-start | bytes 196616 | tf_op jit(solution)/shard_map/ppermute | solution.py:23
  139.1 69.6 %collective-permute-start.22 = (f32[16,16,1,64]{3,2,1,0:T(1,128)S(1)}, f32[16,16,1,64]{3,2,1,0:T(1,128)S(1)}, u32[]{:S(2)}, u32[]{:S(2)}) collective-permute-start(f32[16,16,1,64]{3,2,1,0:T(1,128)S(1)} %get-tuple-element.80), channel_id=1, source_target_pairs={{1,0},{0,1},{3,2},{2,3},{5,4},{4,5},{7,6},{6,7},{9,8},{8,9},{11,10... | collective-permute-start | bytes 196616 | tf_op jit(solution)/shard_map/ppermute | solution.py:25
  142.3 67.5 %collective-permute-start.21 = (f32[16,16,1,64]{3,2,1,0:T(1,128)S(1)}, f32[16,16,1,64]{3,2,1,0:T(1,128)S(1)}, u32[]{:S(2)}, u32[]{:S(2)}) collective-permute-start(f32[16,16,1,64]{3,2,1,0:T(1,128)S(1)} %get-tuple-element.91), channel_id=1, source_target_pairs={{0,1},{1,0},{2,3},{3,2},{4,5},{5,4},{6,7},{7,6},{8,9},{9,8},{10,11... | collective-permute-start | bytes 196616 | tf_op jit(solution)/shard_map/ppermute | solution.py:23
  142.9 66.6 %collective-permute-start.23 = (f32[16,16,1,64]{3,2,1,0:T(1,128)S(1)}, f32[16,16,1,64]{3,2,1,0:T(1,128)S(1)}, u32[]{:S(2)}, u32[]{:S(2)}) collective-permute-start(f32[16,16,1,64]{3,2,1,0:T(1,128)S(1)} %get-tuple-element.90), channel_id=1, source_target_pairs={{1,0},{0,1},{3,2},{2,3},{5,4},{4,5},{7,6},{6,7},{9,8},{8,9},{11,10... | collective-permute-start | bytes 196616 | tf_op jit(solution)/shard_map/ppermute | solution.py:25
  151.7 20.6 %collective-permute-start.19 = (f32[16,1,16,64]{3,1,2,0:T(1,128)S(1)}, f32[16,1,16,64]{3,1,2,0:T(1,128)S(1)}, u32[]{:S(2)}, u32[]{:S(2)}) collective-permute-start(f32[16,1,16,64]{3,1,2,0:T(1,128)S(1)} %get-tuple-element.88), channel_id=1, source_target_pairs={{2,0},{4,2},{6,4},{0,6},{3,1},{5,3},{7,5},{1,7},{10,8},{12,10},{14... | collective-permute-start | bytes 196616 | tf_op jit(solution)/shard_map/ppermute | solution.py:25
  172.3 7.1 %collective-permute-start.17 = (f32[16,1,16,64]{3,1,2,0:T(1,128)S(1)}, f32[16,1,16,64]{3,1,2,0:T(1,128)S(1)}, u32[]{:S(2)}, u32[]{:S(2)}) collective-permute-start(f32[16,1,16,64]{3,1,2,0:T(1,128)S(1)} %get-tuple-element.89), channel_id=1, source_target_pairs={{0,2},{2,4},{4,6},{6,0},{1,3},{3,5},{5,7},{7,1},{8,10},{10,12},{12... | collective-permute-start | bytes 196616 | tf_op jit(solution)/shard_map/ppermute | solution.py:23
  179.4 5.0 %collective-permute-start.15 = (f32[1,16,16,64]{3,0,2,1:T(1,128)S(1)}, f32[1,16,16,64]{3,0,2,1:T(1,128)S(1)}, u32[]{:S(2)}, u32[]{:S(2)}) collective-permute-start(f32[1,16,16,64]{3,0,2,1:T(1,128)S(1)} %get-tuple-element.86), channel_id=1, source_target_pairs={{8,0},{16,8},{24,16},{0,24},{9,1},{17,9},{25,17},{1,25},{10,2},{18... | collective-permute-start | bytes 196616 | tf_op jit(solution)/shard_map/ppermute | solution.py:25
  184.4 6.6 %collective-permute-start.13 = (f32[1,16,16,64]{3,0,2,1:T(1,128)S(1)}, f32[1,16,16,64]{3,0,2,1:T(1,128)S(1)}, u32[]{:S(2)}, u32[]{:S(2)}) collective-permute-start(f32[1,16,16,64]{3,0,2,1:T(1,128)S(1)} %get-tuple-element.87), channel_id=1, source_target_pairs={{0,8},{8,16},{16,24},{24,0},{1,9},{9,17},{17,25},{25,1},{2,10},{10... | collective-permute-start | bytes 196616 | tf_op jit(solution)/shard_map/ppermute | solution.py:23
  190.9 5.9 %collective-permute-start.14 = (f32[1,16,16,64]{3,2,1,0:T(8,128)S(1)}, f32[1,16,16,64]{3,2,1,0:T(8,128)S(1)}, u32[]{:S(2)}, u32[]{:S(2)}) collective-permute-start(f32[1,16,16,64]{3,2,1,0:T(8,128)S(1)} %get-tuple-element.78), channel_id=1, source_target_pairs={{8,0},{16,8},{24,16},{0,24},{9,1},{17,9},{25,17},{1,25},{10,2},{18... | collective-permute-start | bytes 196616 | tf_op jit(solution)/shard_map/ppermute | solution.py:25
  196.9 5.9 %collective-permute-start.12 = (f32[1,16,16,64]{3,2,1,0:T(8,128)S(1)}, f32[1,16,16,64]{3,2,1,0:T(8,128)S(1)}, u32[]{:S(2)}, u32[]{:S(2)}) collective-permute-start(f32[1,16,16,64]{3,2,1,0:T(8,128)S(1)} %get-tuple-element.79), channel_id=1, source_target_pairs={{0,8},{8,16},{16,24},{24,0},{1,9},{9,17},{17,25},{25,1},{2,10},{10... | collective-permute-start | bytes 196616 | tf_op jit(solution)/shard_map/ppermute | solution.py:23
  202.7 5.5 %collective-permute-start.18 = (f32[16,1,16,64]{3,2,1,0:T(8,128)S(1)}, f32[16,1,16,64]{3,2,1,0:T(8,128)S(1)}, u32[]{:S(2)}, u32[]{:S(2)}) collective-permute-start(f32[16,1,16,64]{3,2,1,0:T(8,128)S(1)} %get-tuple-element.76), channel_id=1, source_target_pairs={{2,0},{4,2},{6,4},{0,6},{3,1},{5,3},{7,5},{1,7},{10,8},{12,10},{14... | collective-permute-start | bytes 196616 | tf_op jit(solution)/shard_map/ppermute | solution.py:25
  208.3 6.8 %collective-permute-start.16 = (f32[16,1,16,64]{3,2,1,0:T(8,128)S(1)}, f32[16,1,16,64]{3,2,1,0:T(8,128)S(1)}, u32[]{:S(2)}, u32[]{:S(2)}) collective-permute-start(f32[16,1,16,64]{3,2,1,0:T(8,128)S(1)} %get-tuple-element.77), channel_id=1, source_target_pairs={{0,2},{2,4},{4,6},{6,0},{1,3},{3,5},{5,7},{7,1},{8,10},{10,12},{12... | collective-permute-start | bytes 196616 | tf_op jit(solution)/shard_map/ppermute | solution.py:23
  217.7 0.7 copy-start.10
where the time goes:
time: 222 us; the launch traced here: 219 us
  matrix products  82.9 us (37%)
  waiting for transfers between devices  73.5 us (33%)
  local copies, waits for them, and re-layouts  31.7 us (14%)
  starting transfers between devices  23.9 us (11%)
  other arithmetic  5.04 us (2%)
    ppermute x12, waiting for transfers between devices, extended(): lax.ppermute(tail, axis, [(i, (i + 1) % count) for i in range(count)])  58.9 us
    dot_general x5, matrix products, apply_along(): jnp.einsum(forms[axis_pos], matrix, field, precision=lax.Precision.HIGHEST)  40.2 us
    ppermute x12, starting transfers between devices, extended(): lax.ppermute(head, axis, [((i + 1) % count, i) for i in range(count)])  17.5 us
    ppermute x12, waiting for transfers between devices, extended(): lax.ppermute(head, axis, [((i + 1) % count, i) for i in range(count)])  14.6 us
    dot_general x36, matrix products, face_product(): jnp.einsum('...pqi,...pqj->...ij', left, right, precision=lax.Precision.H...  13.7 us
    reshape x2, local copies, waits for them, and re-layouts, hamiltonian(): (along_x + along_y).reshape(field.shape) + apply_along(deriv_two, field, 2)  11.2 us
    dot_general x3, matrix products, assemble(): jnp.einsum(volume_form, gradients[axis_pos], gradients[axis_pos], precisi...  10.9 us
    reshape x2, local copies, waits for them, and re-layouts, hamiltonian(): flat = field.reshape(first_len, second_len, third_len * width)  8.63 us
  transfers between devices with their start and end apart: 24, of which 12 were waited for; matrix products, arithmetic and copies ran while one was open for 18% of the time, Pallas kernels for 0%

commit v1 on v0

v1 whole, which is shorter than its diff:
```python
import functools

import jax
import jax.numpy as jnp
import ml_dtypes
import numpy as np
from jax import lax
from jax.experimental import pallas as pl
from jax.experimental.pallas import tpu as pltpu
from jax.sharding import PartitionSpec as P

BUF = 3
PENALTY = 2.0
LOW_BOUND = -1.5
CUTOFF = 8.0
HIGH_BOUND = 16.0
LIMIT = 56 * 1024 * 1024
BF = jnp.bfloat16
F32 = jnp.float32


class Plan:
    def __init__(self, cells, width):
        self.cells, self.width = cells, width
        self.ext = cells + 2 * BUF
        self.groups = self.ext // 2
        self.inner = cells // 2
        self.lanes = 2 * width
        self.face = cells * cells
        self.yext = self.ext * cells
        self.plane = -(-self.ext // 8) * 8
        self.strip = BUF * cells
        self.rows = self.yext + 2 * BUF * self.plane
        self.trows = -(-self.ext // 8) * 8
        order = list(range(BUF, BUF + cells)) + list(range(BUF)) + list(range(BUF + cells, self.ext))
        points = []
        for y in order:
            points += [(y, BUF + z) for z in range(cells)]
        for z in list(range(BUF)) + list(range(BUF + cells, self.ext)):
            points += [(y, z) for y in order] + [None] * (self.plane - self.ext)
        self.points = points
        self.first, self.second = spectral(self.ext)
        inside = np.zeros(self.ext)
        inside[BUF : BUF + cells] = 1.0
        self.inside = inside


def spectral(points):
    indices = np.arange(points)
    offsets = indices[:, None] - indices[None, :]
    first = np.zeros((points, points))
    second = np.zeros((points, points))
    for harmonic in range(1, points // 2):
        wavenum = 2.0 * np.pi * harmonic / points
        first = first - 2.0 * wavenum * np.sin(wavenum * offsets) / points
        second = second - 2.0 * wavenum * wavenum * np.cos(wavenum * offsets) / points
    second = second - np.pi * np.pi * np.cos(np.pi * offsets) / points
    return first, second


def row_matrix(plan, along, masked):
    out = np.zeros((plan.rows, plan.rows))
    for r, p in enumerate(plan.points):
        if p is None:
            continue
        for q, s in enumerate(plan.points):
            if s is None:
                continue
            if p[1] == s[1] and (not masked or plan.inside[p[1]]):
                out[r, q] += along[p[0], s[0]]
            if p[0] == s[0] and (not masked or plan.inside[p[0]]):
                out[r, q] += along[p[1], s[1]]
    return out


def mirrored(plan, along):
    n, g = plan.ext, plan.groups
    plus = along[:g, :g] + along[:g, ::-1][:, :g]
    minus = along[:g, :g] - along[:g, ::-1][:, :g]
    return np.concatenate([np.repeat(plus[:, :, None], plan.width, 2), np.repeat(minus[:, :, None], plan.width, 2)], 2)


def face_rows(plan):
    c = plan.cells
    index = {p: r for r, p in enumerate(plan.points) if p is not None}
    out = np.zeros((4 * c, plan.rows))
    for side, layer in enumerate((BUF, BUF + c - 1)):
        for z in range(c):
            for y in range(plan.ext):
                out[side * c + z, index[(y, BUF + z)]] = plan.first[layer, y]
        for y in range(c):
            for z in range(plan.ext):
                out[(2 + side) * c + y, index[(BUF + y, z)]] = plan.first[layer, z]
    return out


def energy(plan):
    c = plan.cells
    block = plan.first[BUF : BUF + c]
    out = 0.5 * block.T @ block
    for sign, layer in ((-1.0, BUF), (1.0, BUF + c - 1)):
        unit = np.zeros(plan.ext)
        unit[layer] = 1.0
        cross = np.outer(unit, plan.first[layer])
        out = out + 0.5 * PENALTY * np.outer(unit, unit) - 0.25 * sign * (cross + cross.T)
    return out


def halves(matrix):
    high = matrix.astype(np.float32).astype(ml_dtypes.bfloat16)
    low = (matrix - high.astype(np.float64)).astype(np.float32).astype(ml_dtypes.bfloat16)
    return high, low


def split(x):
    high = x.astype(BF)
    return high, (x - high.astype(F32)).astype(BF)


def swap(x):
    return pltpu.roll(x, x.shape[-1] // 2, x.ndim - 1)


def dot(a, b):
    return jnp.dot(a, b, preferred_element_type=F32)


def dot_t(a, b):
    return lax.dot_general(a, b, (((0,), (0,)), ((), ())), preferred_element_type=F32)


def exact(a, b):
    return jnp.dot(a, b, preferred_element_type=F32, precision=lax.Precision.HIGHEST)


def low_lanes(shape):
    return lax.broadcasted_iota(jnp.int32, shape, len(shape) - 1) < shape[-1] // 2


def pack_kernel(plan, orb, pot, spread, pick, xlo, xhi, ylo, yhi, inner, vt):
    c, w = plan.cells, plan.width
    half = plan.face // 2
    for s in range(BUF):
        for out, x in ((xlo, s), (xhi, c - BUF + s)):
            out[s * half : (s + 1) * half, :] = jnp.concatenate([orb[x, :half], orb[x, half:]], axis=1)
    for j in range(plan.inner):
        a, b = orb[j], orb[c - 1 - j]
        e = jnp.concatenate([a + b, a - b], axis=1)
        inner[j] = e
        ylo[j * plan.strip : (j + 1) * plan.strip, :] = e[: plan.strip]
        yhi[j * plan.strip : (j + 1) * plan.strip, :] = e[plan.face - plan.strip :]
    wide = exact(pot[...], spread[...]) * pick[...]
    v = wide.reshape(c, c, plan.face).sum(axis=1)
    vt[...] = v
    lanes = plan.lanes
    base = BUF * half
    xlo[base:, :] = jnp.zeros((8, lanes), F32)
    xhi[base:, :] = jnp.zeros((8, lanes), F32)
    for part in range(2):
        cols = slice(part * lanes, (part + 1) * lanes)
        xlo[base + part * BUF : base + (part + 1) * BUF, :] = v[:BUF, cols]
        xhi[base + part * BUF : base + (part + 1) * BUF, :] = v[c - BUF :, cols]
    ybase = plan.inner * plan.strip
    ylo[ybase:, :] = v[:, :lanes]
    yhi[ybase:, :] = v[:, plan.face - lanes :]


def xhalo_kernel(plan, lo, hi, outer, elo, ehi):
    half = plan.face // 2
    lanes = plan.lanes
    mask = low_lanes((half, lanes))
    for g in range(BUF):
        a = lo[g * half : (g + 1) * half, :]
        b = hi[(BUF - 1 - g) * half : (BUF - g) * half, :]
        s, d = a + b, a - b
        top = jnp.where(mask, s, swap(d))
        bottom = jnp.where(mask, swap(s), d)
        outer[g, :half] = top
        outer[g, half:] = bottom
        elo[g * plan.strip : (g + 1) * plan.strip, :] = top[: plan.strip]
        ehi[g * plan.strip : (g + 1) * plan.strip, :] = bottom[half - plan.strip :]
    base, ebase = BUF * half, BUF * plan.strip
    elo[ebase:, :] = jnp.zeros((8, lanes), F32)
    ehi[ebase:, :] = jnp.zeros((8, lanes), F32)
    for k, src in enumerate((lo, hi)):
        elo[ebase + k * BUF : ebase + (k + 1) * BUF, :] = src[base : base + BUF, :]
        ehi[ebase + k * BUF : ebase + (k + 1) * BUF, :] = src[base + BUF : base + 2 * BUF, :]


def zpack_kernel(plan, inner, outer, vt, xlo, xhi, ylo, yhi, elo, ehi, zpick, field, vfull, z):
    c, lanes, strip, face = plan.cells, plan.lanes, plan.strip, plan.face
    for g in range(BUF):
        field[g, :face] = outer[g]
        field[g, face : face + strip] = elo[g * strip : (g + 1) * strip, :]
        field[g, face + strip : face + 2 * strip] = ehi[g * strip : (g + 1) * strip, :]
    for j in range(plan.inner):
        g = BUF + j
        field[g, :face] = inner[j]
        field[g, face : face + strip] = ylo[j * strip : (j + 1) * strip, :]
        field[g, face + strip : face + 2 * strip] = yhi[j * strip : (j + 1) * strip, :]
    pad = field.shape[1] - plan.yext
    field[:, plan.yext :] = jnp.zeros((plan.groups, pad, lanes), F32)
    plane = plan.plane
    span = BUF * plane
    for side, start in ((0, 0), (1, c - BUF)):
        for g in range(plan.groups):
            for k in range(BUF):
                at = g * span + k * plane
                z[side, at : at + plane, :] = field[g, pl.ds(start + k, plane, stride=c), :]
    base, ebase, ybase = BUF * (face // 2), BUF * strip, plan.inner * strip
    vfull[...] = jnp.zeros(vfull.shape, F32)
    for part in range(2):
        cols = slice(part * lanes, (part + 1) * lanes)
        vfull[:BUF, cols] = xlo[base + part * BUF : base + (part + 1) * BUF, :]
        vfull[BUF + c : plan.ext, cols] = xhi[base + part * BUF : base + (part + 1) * BUF, :]
    vfull[BUF : BUF + c, :face] = vt[...]
    shift = lanes - strip
    vfull[:BUF, face : face + strip] = elo[ebase : ebase + BUF, :][:, shift:]
    vfull[BUF + c : plan.ext, face : face + strip] = elo[ebase + BUF : ebase + 2 * BUF, :][:, shift:]
    vfull[BUF : BUF + c, face : face + strip] = ylo[ybase:, :][:, shift:]
    vfull[:BUF, face + strip : face + 2 * strip] = ehi[ebase : ebase + BUF, :][:, :strip]
    vfull[BUF + c : plan.ext, face + strip : face + 2 * strip] = ehi[ebase + BUF : ebase + 2 * BUF, :][:, :strip]
    vfull[BUF : BUF + c, face + strip : face + 2 * strip] = yhi[ybase:, :][:, :strip]
    for side in range(2):
        z[side, plan.groups * span :, :] = exact(vfull[...], zpick[side])


def mix(plan, coef, table, g, src, r0, r1):
    total = None
    for s in range(plan.groups):
        term = coef[table + s : table + s + 1, :] * src[s, r0:r1, :]
        total = term if total is None else total + term
    return total


def chunks(stop, size=16):
    return [(r, min(r + size, stop)) for r in range(0, stop, size)]


def filter_kernel(plan, field, zlo, zhi, vfull, wh, wl, coef, dcoef, vspread, fh, fl,
                  basis, out, mxlo, mxhi, mylo, myhi, mzlo, mzhi, va_out, vd_out,
                  x, xh, xl, y, yh, yl, va, vd, acc, dacc):
    g_all, lanes, rows, face = plan.groups, plan.lanes, plan.rows, plan.face
    span = BUF * plan.plane
    c = plan.cells
    half_width = (HIGH_BOUND - CUTOFF) / 2.0
    center = (HIGH_BOUND + CUTOFF) / 2.0
    s0 = half_width / (LOW_BOUND - center)
    s1 = 1.0 / (2.0 / s0 - s0)

    def put(dst, dh, dl, g, r0, r1, value):
        dst[g, r0:r1, :] = value
        h, l = split(value)
        dh[r0:r1, g * lanes : (g + 1) * lanes] = h
        dl[r0:r1, g * lanes : (g + 1) * lanes] = l

    for g in range(g_all):
        put(x, xh, xl, g, 0, plan.yext, field[g, : plan.yext, :])
        put(x, xh, xl, g, plan.yext, plan.yext + span, zlo[g * span : (g + 1) * span, :])
        put(x, xh, xl, g, plan.yext + span, rows, zhi[g * span : (g + 1) * span, :])
    pieces = ((0, vfull[...], plan.yext), (plan.yext, zlo[g_all * span :, :], span), (plan.yext + span, zhi[g_all * span :, :], span))
    for at, piece, count in pieces:
        turned = jnp.transpose(piece)[:count, :]
        both = exact(turned, vspread[...])
        for g in range(g_all):
            va[g, at : at + count, :] = both[:, g * lanes : (g + 1) * lanes]
            vd[g, at : at + count, :] = both[:, (g_all + g) * lanes : (g_all + g + 1) * lanes]

    def apply(src, sh, sl, finish):
        for g0 in range(0, g_all, 2):
            g1 = min(g0 + 2, g_all)
            cols = slice(g0 * lanes, g1 * lanes)
            acc[:, : (g1 - g0) * lanes] = (
                dot(wh[...], sh[:, cols]) + dot(wl[...], sh[:, cols]) + dot(wh[...], sl[:, cols])
            )
            for g in range(g0, g1):
                for r0, r1 in chunks(rows):
                    own = src[g, r0:r1, :]
                    value = acc[r0:r1, (g - g0) * lanes : (g - g0 + 1) * lanes]
                    value = value + mix(plan, coef, g * g_all, g, src, r0, r1)
                    value = value + (va[g, r0:r1, :] - center) * own + vd[g, r0:r1, :] * swap(own)
                    finish(g, r0, r1, value)

    def first(g, r0, r1, value):
        put(y, yh, yl, g, r0, r1, value * (s0 / half_width))

    apply(x, xh, xl, first)

    def second(g, r0, r1, value):
        put(out, xh, xl, g, r0, r1, value * (2.0 * s1 / half_width) - (s0 * s1) * x[g, r0:r1, :])

    apply(y, yh, yl, second)

    for j in range(plan.inner):
        g = BUF + j
        for r0, r1 in chunks(face, 64):
            e = out[g, r0:r1, :]
            t = swap(e)
            basis[j, r0:r1, :] = (0.5 * (e + t))[:, : plan.width]
            basis[c - 1 - j, r0:r1, :] = (0.5 * (e - t))[:, : plan.width]
    for r0, r1 in chunks(face, 16):
        mask = low_lanes((r1 - r0, lanes))
        e = out[BUF, r0:r1, :]
        d = mix(plan, dcoef, 0, 0, out, r0, r1)
        te, td = swap(e), swap(d)
        mxlo[r0:r1, :] = 0.5 * jnp.where(mask, e + te, d + td)
        mxhi[r0:r1, :] = 0.5 * jnp.where(mask, e - te, d - td)
    cols = slice(BUF * lanes, g_all * lanes)
    dacc[...] = dot(fh[...], xh[:, cols]) + dot(fl[...], xh[:, cols]) + dot(fh[...], xl[:, cols])
    for j in range(plan.inner):
        g = BUF + j
        own = slice(j * lanes, (j + 1) * lanes)
        to = slice(j * c, (j + 1) * c)
        mylo[0, to, :] = out[g, :c, :]
        myhi[0, to, :] = out[g, face - c : face, :]
        mzlo[0, to, :] = out[g, pl.ds(0, c, stride=c), :]
        mzhi[0, to, :] = out[g, pl.ds(c - 1, c, stride=c), :]
        for k, dst in enumerate((mylo, myhi, mzlo, mzhi)):
            dst[1, to, :] = dacc[k * c : (k + 1) * c, own]
    va_out[...] = va[BUF:, :face, :]
    vd_out[...] = vd[BUF:, :face, :]


def own_kernel(plan, f, va, vd, bh, bl, coef, diag, f2, f2h, f2l, fhi, acc):
    g_all, lanes, rows, face = plan.groups, plan.lanes, plan.rows, plan.face
    for g in range(g_all):
        top = face if g < BUF else rows
        for r0, r1 in chunks(top, 16):
            value = f[g, r0:r1, :]
            high = value.astype(BF)
            fhi[g, r0:r1, :] = high
            twice = 2.0 * value - high.astype(F32)
            f2[g, r0:r1, :] = twice
            if g >= BUF:
                h, l = split(twice)
                f2h[r0:r1, (g - BUF) * lanes : (g - BUF + 1) * lanes] = h
                f2l[r0:r1, (g - BUF) * lanes : (g - BUF + 1) * lanes] = l
    total = jnp.zeros((lanes, 2 * lanes), F32)

    def fold(total, g, top, value):
        h, l = split(value)
        return total + dot_t(fhi[g, :top, :], jnp.concatenate([h, l], axis=1))

    for g in range(BUF):
        parts = [mix(plan, coef, g * g_all, g, f2, r0, r1) for r0, r1 in chunks(face)]
        total = fold(total, g, face, jnp.concatenate(parts, axis=0))
    for j0 in range(0, plan.inner, 2):
        cols = slice(j0 * lanes, (j0 + 2) * lanes)
        acc[...] = dot(bh[...], f2h[:, cols]) + dot(bl[...], f2h[:, cols]) + dot(bh[...], f2l[:, cols])
        for j in (j0, j0 + 1):
            g = BUF + j
            mine = slice((j - j0) * lanes, (j - j0 + 1) * lanes)
            parts = []
            for r0, r1 in chunks(face):
                own = f2[g, r0:r1, :]
                value = acc[r0:r1, mine] + mix(plan, coef, g * g_all, g, f2, r0, r1)
                parts.append(value + va[j, r0:r1, :] * own + vd[j, r0:r1, :] * swap(own))
            parts.append(acc[face:, mine])
            total = fold(total, g, rows, jnp.concatenate(parts, axis=0))
    both = total[:, :lanes] + total[:, lanes:]
    w = plan.width
    block = both[:w, :w] + both[w:, w:]
    diag[...] = 0.25 * (block + jnp.transpose(block))


def face_kernel(plan, diag, oxl, oxh, oyl, oyh, ozl, ozh, nxl, nxh, nyl, nyh, nzl, nzh, blocks):
    w, lanes = plan.width, plan.lanes
    blocks[0] = diag[...]

    def product(a, b):
        ah, al = split(a)
        bh, bl = split(b)
        return dot_t(ah, bh) + dot_t(ah, bl) + dot_t(al, bh)

    for k, (own, other) in enumerate(((oxl, nxl), (oxh, nxh))):
        sign = -1.0 if k % 2 == 0 else 1.0
        m = product(own[...], other[...])
        blocks[1 + k] = 0.25 * sign * (m[w:, :w] - m[:w, w:]) - 0.5 * PENALTY * m[:w, :w]
    for k, (own, other) in enumerate(((oyl, nyl), (oyh, nyh), (ozl, nzl), (ozh, nzh))):
        sign = -1.0 if k % 2 == 0 else 1.0
        a = jnp.concatenate([own[0], own[1]], axis=1)
        b = jnp.concatenate([other[0], other[1]], axis=1)
        m = product(a, b)
        uv = m[:w, :w] + m[w:lanes, w:lanes]
        udv = m[:w, lanes : lanes + w] + m[w:lanes, lanes + w :]
        duv = m[lanes : lanes + w, :w] + m[lanes + w :, w:lanes]
        blocks[3 + k] = 0.5 * (0.25 * sign * (duv - udv) - 0.5 * PENALTY * uv)


def call(kernel, plan, outs, args, scratch=(), flops=0):
    bytes_all = sum(int(np.prod(a.shape)) * a.dtype.itemsize for a in args)
    return pl.pallas_call(
        functools.partial(kernel, plan),
        out_shape=outs,
        in_specs=[pl.BlockSpec(memory_space=pltpu.VMEM)] * len(args),
        out_specs=[pl.BlockSpec(memory_space=pltpu.VMEM)] * len(outs),
        scratch_shapes=list(scratch),
        compiler_params=pltpu.CompilerParams(vmem_limit_bytes=LIMIT),
        cost_estimate=pl.CostEstimate(flops=flops, bytes_accessed=bytes_all, transcendentals=0),
    )(*args)


def f32(*shape):
    return jax.ShapeDtypeStruct(shape, F32)


def shift(array, axis, step):
    count = lax.axis_size(axis)
    return lax.ppermute(array, axis, [(i, (i + step) % count) for i in range(count)])


def on_device(orbitals, potential):
    cells, width = orbitals.shape[0], orbitals.shape[-1]
    plan = Plan(cells, width)
    lanes, face, strip = plan.lanes, plan.face, plan.strip
    g_all = plan.groups

    spread = np.zeros((cells, face), np.float32)
    for y in range(cells):
        spread[np.arange(cells), y * cells + np.arange(cells)] = 1.0
    pick = np.zeros((cells, cells, face), np.float32)
    for y in range(cells):
        pick[:, y, y * cells : (y + 1) * cells] = 1.0
    xrows, yrows, erows = BUF * face // 2 + 8, plan.inner * strip + cells, BUF * strip + 8
    xlo, xhi, ylo, yhi, inner, vt = call(
        pack_kernel, plan,
        [f32(xrows, lanes), f32(xrows, lanes), f32(yrows, lanes), f32(yrows, lanes), f32(plan.inner, face, lanes), f32(cells, face)],
        [orbitals.reshape(cells, face, width), potential.reshape(face, cells), jnp.asarray(spread), jnp.asarray(pick.reshape(face, face))],
    )
    from_xlo, from_xhi = shift(xhi, "gx", 1), shift(xlo, "gx", -1)
    from_ylo, from_yhi = shift(yhi, "gy", 1), shift(ylo, "gy", -1)
    outer, elo, ehi = call(
        xhalo_kernel, plan, [f32(BUF, face, lanes), f32(erows, lanes), f32(erows, lanes)], [from_xlo, from_xhi],
    )
    from_elo, from_ehi = shift(ehi, "gy", 1), shift(elo, "gy", -1)

    frows = plan.plane * cells
    zpick = np.zeros((2, frows, lanes), np.float32)
    for side, start in ((0, 0), (1, cells - BUF)):
        for k in range(BUF):
            for y in range(plan.ext):
                zpick[side, y * cells + start + k, k * plan.plane + y] = 1.0
    zrows = g_all * BUF * plan.plane + plan.trows
    field, vfull, z = call(
        zpack_kernel, plan,
        [f32(g_all, frows, lanes), f32(plan.trows, frows), f32(2, zrows, lanes)],
        [inner, outer, vt, from_xlo, from_xhi, from_ylo, from_yhi, from_elo, from_ehi, jnp.asarray(zpick)],
    )
    if lax.axis_size("gz") == 2:
        other = shift(z, "gz", 1)
        zlo, zhi = other[1], other[0]
    else:
        zlo, zhi = shift(z[1], "gz", 1), shift(z[0], "gz", -1)

    wh, wl = halves(-0.5 * row_matrix(plan, plan.second, False))
    coef = (-0.5 * mirrored(plan, plan.second)).reshape(-1, lanes).astype(np.float32)
    p = plan.first[BUF, :g_all] + plan.first[BUF, ::-1][:g_all]
    q = plan.first[BUF, :g_all] - plan.first[BUF, ::-1][:g_all]
    dcoef = np.concatenate([np.repeat(p[:, None], width, 1), np.repeat(q[:, None], width, 1)], 1).astype(np.float32)
    vspread = np.zeros((plan.trows, 2, g_all, lanes), np.float32)
    for g in range(g_all):
        vspread[g, :, g, :] = 0.5
        vspread[plan.ext - 1 - g, 0, g, :] = 0.5
        vspread[plan.ext - 1 - g, 1, g, :] = -0.5
    fh, fl = halves(face_rows(plan))
    rows = plan.rows
    outs = [f32(cells, face, width), f32(g_all, rows, lanes), f32(face, lanes), f32(face, lanes)]
    outs += [f32(2, plan.inner * cells, lanes)] * 4 + [f32(plan.inner, face, lanes)] * 2
    basis, filtered, mxlo, mxhi, mylo, myhi, mzlo, mzhi, va, vd = call(
        filter_kernel, plan, outs,
        [field, zlo, zhi, vfull, jnp.asarray(wh), jnp.asarray(wl), jnp.asarray(coef), jnp.asarray(dcoef),
         jnp.asarray(vspread.reshape(plan.trows, -1)), jnp.asarray(fh), jnp.asarray(fl)],
        [pltpu.VMEM((g_all, rows, lanes), F32), pltpu.VMEM((rows, g_all * lanes), BF), pltpu.VMEM((rows, g_all * lanes), BF),
         pltpu.VMEM((g_all, rows, lanes), F32), pltpu.VMEM((rows, g_all * lanes), BF), pltpu.VMEM((rows, g_all * lanes), BF),
         pltpu.VMEM((g_all, rows, lanes), F32), pltpu.VMEM((g_all, rows, lanes), F32),
         pltpu.VMEM((rows, 2 * lanes), F32), pltpu.VMEM((4 * cells, plan.inner * lanes), F32)],
    )
    nxl, nxh = shift(mxhi, "gx", 1), shift(mxlo, "gx", -1)
    nyl, nyh = shift(myhi, "gy", 1), shift(mylo, "gy", -1)
    if lax.axis_size("gz") == 2:
        nz = shift(jnp.stack([mzlo, mzhi]), "gz", 1)
        nzl, nzh = nz[1], nz[0]
    else:
        nzl, nzh = shift(mzhi, "gz", 1), shift(mzlo, "gz", -1)

    along = energy(plan)
    bh, bl = halves(row_matrix(plan, along, True))
    bcoef = mirrored(plan, along).reshape(-1, lanes).astype(np.float32)
    (diag,) = call(
        own_kernel, plan, [f32(width, width)],
        [filtered, va, vd, jnp.asarray(bh), jnp.asarray(bl), jnp.asarray(bcoef)],
        [pltpu.VMEM((g_all, rows, lanes), F32), pltpu.VMEM((rows, plan.inner * lanes), BF), pltpu.VMEM((rows, plan.inner * lanes), BF),
         pltpu.VMEM((g_all, rows, lanes), BF), pltpu.VMEM((rows, 2 * lanes), F32)],
        flops=2 * 10**9,
    )
    (blocks,) = call(
        face_kernel, plan, [f32(7, width, width)],
        [diag, mxlo, mxhi, mylo, myhi, mzlo, mzhi, nxl, nxh, nyl, nyh, nzl, nzh],
    )
    return basis.reshape(orbitals.shape), blocks[None, None, None]


def solution(mesh):
    return jax.shard_map(
        on_device,
        mesh=mesh,
        in_specs=(P("gx", "gy", "gz", None), P("gx", "gy", "gz")),
        out_specs=(P("gx", "gy", "gz", None), P("gx", "gy", "gz", None, None, None)),
        check_vma=False,
    )
```

time: 222 us -> 75.1 us (0.34); the launches traced: 219 us -> 74.9 us
  matrix products: 82.9 us -> 0 us
  waiting for transfers between devices: 73.5 us -> 11.4 us
  Pallas kernels: 0 us -> 40.7 us
  local copies, waits for them, and re-layouts: 31.7 us -> 3.78 us
  starting transfers between devices: 23.9 us -> 17.3 us
  other arithmetic: 5.04 us -> 0.99 us
    dot_general x49 -> x0, matrix products: 82.9 us -> none  [the longest x5 40.2 us: apply_along(): jnp.einsum(forms[axis_pos], matrix, field, precision=lax.Precision.HIGHEST)]
    ppermute x24 -> x12, waiting for transfers between devices: 73.5 us -> 11.4 us  [shift(): lax.ppermute(array, axis, [(i, (i + step) % count) for i in range(count)])]
    pallas_call x0 -> x6, Pallas kernels: none -> 40.7 us  [call(): pl.pallas_call(functools.partial(kernel, plan), out_shape=outs, in_specs=...]
    reshape x4 -> x0, local copies, waits for them, and re-layouts: 19.8 us -> none  [the longest x2 11.2 us: hamiltonian(): (along_x + along_y).reshape(field.shape) + apply_along(deriv_two, field, 2)]
    ppermute x24 -> x12, starting transfers between devices: 23.9 us -> 17.3 us  [shift(): lax.ppermute(array, axis, [(i, (i + step) % count) for i in range(count)])]
    concatenate x2 -> x0, other arithmetic: 3.55 us -> none  [extended(): jnp.concatenate([lax.ppermute(tail, axis, [(i, (i + 1) % count) for i in...]
    slice x10 -> x0, local copies, waits for them, and re-layouts: 3.31 us -> none  [the longest x3 2 us: extended(): head = lax.slice_in_dim(cells, 0, width, axis=dim)]
    unnamed x28 -> x20, local copies, waits for them, and re-layouts: 5.06 us -> 2.1 us
  transfers between devices with their start and end apart: 24 -> 12, of which waited for: 12 -> 5; matrix products, arithmetic and copies ran while one was open for 18% -> 1% of each run, Pallas kernels for 0% -> 13%
where the time goes in v1:
time: 75.1 us; the launch traced here: 74.9 us
  Pallas kernels  40.7 us (54%)
  starting transfers between devices  17.3 us (23%)
  waiting for transfers between devices  11.4 us (15%)
  local copies, waits for them, and re-layouts  3.78 us (5%)
  other arithmetic  0.99 us (1%)
    pallas_call x6, Pallas kernels, call(): pl.pallas_call(functools.partial(kernel, plan), out_shape=outs, in_specs=...  40.7 us
    ppermute x12, starting transfers between devices, shift(): lax.ppermute(array, axis, [(i, (i + step) % count) for i in range(count)])  17.3 us
    ppermute x12, waiting for transfers between devices, shift(): lax.ppermute(array, axis, [(i, (i + step) % count) for i in range(count)])  11.4 us
    unnamed x20, local copies, waits for them, and re-layouts  2.1 us
  transfers between devices with their start and end apart: 12, of which 5 were waited for; matrix products, arithmetic and copies ran while one was open for 1% of the time, Pallas kernels for 13%

profile of v1, /device:TPU:0, one launch (start us, length us, event | category | flops | bytes accessed | tf_op | source)
XLA Modules:
  0.0 74.9 jit_solution(6700225382732784159)
XLA Ops:
  0.6 3.3 %shard_map.158 = (f32[392,128]{1,0:T(8,128)}, f32[392,128]{1,0:T(8,128)}, f32[400,128]{1,0:T(8,128)}, f32[400,128]{1,0:T(8,128)}, f32[8,256,128]{2,1,0:T(8,128)}, /*index=5*/f32[16,256]{1,0:T(8,128)}) custom-call(f32[16,256,64]{2,1,0:T(8,128)} %bitcast.14, f32[256,16]{1,0:T(8,128)} %bitcast.18, f32[16,256]{1,0:T(8,128)} %constant.26.clone.spread, ...), custom_call_target="tpu_custom_call" | custom-call | bytes 1343488 | tf_op jit(solution)/shard_map/pallas_call | solution.py:392
  3.9 2.9 %collective-permute-start = (f32[392,128]{1,0:T(8,128)}, f32[392,128]{1,0:T(8,128)S(1)}, u32[]{:S(2)}, u32[]{:S(2)}) collective-permute-start(f32[392,128]{1,0:T(8,128)} %get-tuple-element.25), channel_id=1, source_target_pairs={{0,8},{8,16},{16,24},{24,0},{1,9},{9,17},{17,25},{25,1},{2,10},{10... | collective-permute-start | bytes 602120 | tf_op jit(solution)/shard_map/ppermute | solution.py:409
  6.8 1.0 %collective-permute-start.1 = (f32[392,128]{1,0:T(8,128)}, f32[392,128]{1,0:T(8,128)S(1)}, u32[]{:S(2)}, u32[]{:S(2)}) collective-permute-start(f32[392,128]{1,0:T(8,128)} %get-tuple-element.26), channel_id=1, source_target_pairs={{0,24},{8,0},{16,8},{24,16},{1,25},{9,1},{17,9},{25,17},{2,26},{10... | collective-permute-start | bytes 602120 | tf_op jit(solution)/shard_map/ppermute | solution.py:409
  7.8 2.1 %collective-permute-start.2 = (f32[400,128]{1,0:T(8,128)}, f32[400,128]{1,0:T(8,128)S(1)}, u32[]{:S(2)}, u32[]{:S(2)}) collective-permute-start(f32[400,128]{1,0:T(8,128)} %get-tuple-element.29), channel_id=1, source_target_pairs={{0,2},{2,4},{4,6},{6,0},{1,3},{3,5},{5,7},{7,1},{8,10},{10,12},{12... | collective-permute-start | bytes 614408 | tf_op jit(solution)/shard_map/ppermute | solution.py:409
  9.8 2.0 %collective-permute-start.3 = (f32[400,128]{1,0:T(8,128)}, f32[400,128]{1,0:T(8,128)S(1)}, u32[]{:S(2)}, u32[]{:S(2)}) collective-permute-start(f32[400,128]{1,0:T(8,128)} %get-tuple-element.30), channel_id=1, source_target_pairs={{0,6},{2,0},{4,2},{6,4},{1,7},{3,1},{5,3},{7,5},{8,14},{10,8},{12,... | collective-permute-start | bytes 614408 | tf_op jit(solution)/shard_map/ppermute | solution.py:409
  11.9 1.9 %collective-permute-done.lo.xlo = f32[392,128]{1,0:T(8,128)S(1)} collective-permute-done((f32[392,128]{1,0:T(8,128)}, f32[392,128]{1,0:T(8,128)S(1)}, u32[]{:S(2)}, u32[]{:S(2)}) %collective-permute-start) | collective-permute-done | bytes 200736 | tf_op jit(solution)/shard_map/ppermute | solution.py:409
  13.8 0.0 copy-start
  13.8 3.7 %collective-permute-done.1.hi.xhi = f32[392,128]{1,0:T(8,128)S(1)} collective-permute-done((f32[392,128]{1,0:T(8,128)}, f32[392,128]{1,0:T(8,128)S(1)}, u32[]{:S(2)}, u32[]{:S(2)}) %collective-permute-start.1) | collective-permute-done | bytes 200736 | tf_op jit(solution)/shard_map/ppermute | solution.py:409
  17.5 0.0 copy-done
  17.5 0.0 copy-start.1
  17.5 0.7 copy-done.1
  18.2 2.0 %shard_map.159 = (f32[3,256,128]{2,1,0:T(8,128)}, f32[152,128]{1,0:T(8,128)}, f32[152,128]{1,0:T(8,128)}) custom-call(f32[392,128]{1,0:T(8,128)} %copy-done, f32[392,128]{1,0:T(8,128)} %copy-done.1), custom_call_target="tpu_custom_call" | custom-call | bytes 401408 | tf_op jit(solution)/shard_map/pallas_call | solution.py:392
  20.2 1.6 %collective-permute-start.4 = (f32[152,128]{1,0:T(8,128)}, f32[152,128]{1,0:T(8,128)S(1)}, u32[]{:S(2)}, u32[]{:S(2)}) collective-permute-start(f32[152,128]{1,0:T(8,128)} %get-tuple-element.31), channel_id=1, source_target_pairs={{0,2},{2,4},{4,6},{6,0},{1,3},{3,5},{5,7},{7,1},{8,10},{10,12},{12... | collective-permute-start | bytes 233480 | tf_op jit(solution)/shard_map/ppermute | solution.py:409
  21.8 2.2 %collective-permute-start.5 = (f32[152,128]{1,0:T(8,128)}, f32[152,128]{1,0:T(8,128)S(1)}, u32[]{:S(2)}, u32[]{:S(2)}) collective-permute-start(f32[152,128]{1,0:T(8,128)} %get-tuple-element.32), channel_id=1, source_target_pairs={{0,6},{2,0},{4,2},{6,4},{1,7},{3,1},{5,3},{7,5},{8,14},{10,8},{12,... | collective-permute-start | bytes 233480 | tf_op jit(solution)/shard_map/ppermute | solution.py:409
  24.0 0.0 collective-permute-done.2.ylo
  24.0 0.0 copy-start.2
  24.1 0.0 collective-permute-done.3.yhi
  24.1 0.0 copy-start.3
  24.1 3.0 %collective-permute-done.4.elo = f32[152,128]{1,0:T(8,128)S(1)} collective-permute-done((f32[152,128]{1,0:T(8,128)}, f32[152,128]{1,0:T(8,128)S(1)}, u32[]{:S(2)}, u32[]{:S(2)}) %collective-permute-start.4) | collective-permute-done | bytes 77856 | tf_op jit(solution)/shard_map/ppermute | solution.py:409
  27.0 0.0 copy-start.8
  27.0 0.2 collective-permute-done.5.ehi
  27.2 0.0 copy-start.9
  27.2 0.0 copy-done.2
  27.2 0.0 copy-done.3
  27.2 0.4 copy-done.8
  27.7 0.2 copy-done.9
  27.9 3.7 %shard_map.160 = (f32[11,384,128]{2,1,0:T(8,128)}, f32[24,384]{1,0:T(8,128)}, f32[2,816,128]{2,1,0:T(8,128)}) custom-call(f32[8,256,128]{2,1,0:T(8,128)} %get-tuple-element.24.inner, f32[3,256,128]{2,1,0:T(8,128)} %get-tuple-element.27.outer, f32[16,256]{1,0:T(8,128)} %get-tuple-element.28.vt, f32[392,128]{1,0:T(8,128)} %copy-done, f32[392,128]{1,0:T(8,128)} %copy-done.1, ...), custom_call_target="tpu_custom_call" | custom-call | bytes 2818048 | tf_op jit(solution)/shard_map/pallas_call | solution.py:392
  31.6 0.0 collective-permute-start.6
  31.6 2.6 %collective-permute-done.6 = f32[2,816,128]{2,1,0:T(8,128)S(1)} collective-permute-done((f32[2,816,128]{2,1,0:T(8,128)}, f32[2,816,128]{2,1,0:T(8,128)S(1)}, u32[]{:S(2)}, u32[]{:S(2)}) %collective-permute-start.6) | collective-permute-done | bytes 835616 | tf_op jit(solution)/shard_map/ppermute | solution.py:409
  34.2 1.0 %slice_bitcast_fusion = (f32[816,128]{1,0:T(8,128)}, f32[816,128]{1,0:T(8,128)}) fusion(f32[2,816,128]{2,1,0:T(8,128)S(1)} %collective-permute-done.6), kind=kLoop, calls=%fused_computation | loop fusion | bytes 1671168 | tf_op jit(solution)/shard_map/squeeze | solution.py:451
  35.1 21.1 %shard_map.161 = (f32[16,256,64]{2,1,0:T(8,128)}, f32[11,496,128]{2,1,0:T(8,128)}, f32[256,128]{1,0:T(8,128)}, f32[256,128]{1,0:T(8,128)}, f32[2,128,128]{2,1,0:...) custom-call(f32[11,384,128]{2,1,0:T(8,128)} %get-tuple-element.33.fi, ...), custom_call_target="tpu_custom_call" | custom-call | bytes 4484096 | tf_op jit(solution)/shard_map/pallas_call | solution.py:392
  56.3 1.0 %pad_maximum_fusion = f32[2,2,128,128]{3,2,1,0:T(8,128)S(1)} fusion(f32[1,2,128,128]{3,2,1,0:T(8,128)} %bitcast.16, f32[1,2,128,128]{3,2,1,0:T(8,128)} %bitcast.15), kind=kLoop, calls=%fused_computation.2 | loop fusion | flops 65536 | bytes 524288 | tf_op jit(solution)/shard_map/stack | solution.py:481
  57.3 0.2 collective-permute-start.11
  57.5 1.4 %collective-permute-start.8 = (f32[256,128]{1,0:T(8,128)}, f32[256,128]{1,0:T(8,128)S(1)}, u32[]{:S(2)}, u32[]{:S(2)}) collective-permute-start(f32[256,128]{1,0:T(8,128)} %get-tuple-element.40.oxl), channel_id=1, source_target_pairs={{0,24},{8,0},{16,8},{24,16},{1,25},{9,1},{17,9},{25,17},{2,26},{10... | collective-permute-start | bytes 393224 | tf_op jit(solution)/shard_map/ppermute | solution.py:409
  58.9 0.6 collective-permute-start.7
  59.5 3.2 %collective-permute-start.10 = (f32[2,128,128]{2,1,0:T(8,128)}, f32[2,128,128]{2,1,0:T(8,128)S(1)}, u32[]{:S(2)}, u32[]{:S(2)}) collective-permute-start(f32[2,128,128]{2,1,0:T(8,128)} %get-tuple-element.42.oyl), channel_id=1, source_target_pairs={{0,6},{2,0},{4,2},{6,4},{1,7},{3,1},{5,3},{7,5},{8,14},{10,8},{12,... | collective-permute-start | bytes 393224 | tf_op jit(solution)/shard_map/ppermute | solution.py:409
  62.7 0.0 collective-permute-start.9
  62.7 7.7 %shard_map.162.diag = f32[64,64]{1,0:T(8,128)} custom-call(f32[11,496,128]{2,1,0:T(8,128)} %get-tuple-element.37.f, f32[8,256,128]{2,1,0:T(8,128)} %get-tuple-element.38.va, f32[8,256,128]{2,1,0:T(8,128)} %get-tuple-element.39.vd, bf16[496,496]{1,0:T(8,128)(2,1)} %constant.36.clone.bh, bf16[496,496]{1,0:T(8,128)(2,1)} %constant.37.clone.bl, ...), custom_call_target="tpu_custom_call" | custom-call | flops 2000000000 | bytes 5936640 | tf_op jit(solution)/shard_map/pallas_call | solution.py:392
  70.4 0.0 collective-permute-done.11
  70.4 0.7 slice_bitcast_fusion.2
  71.1 0.0 collective-permute-done.8.nxh
  71.1 0.0 copy-start.4
  71.1 0.0 collective-permute-done.7.nxl
  71.2 0.0 copy-start.5
  71.2 0.0 collective-permute-done.10.nyh
  71.2 0.0 copy-start.6
  71.2 0.0 collective-permute-done.9.nyl
  71.2 0.0 copy-start.7
  71.2 0.6 copy-done.4
  71.8 0.1 copy-done.5
  71.8 0.1 copy-done.6
  71.9 0.1 copy-done.7
  72.0 2.9 %shard_map.163 = f32[7,64,64]{2,1,0:T(8,128)} custom-call(f32[64,64]{1,0:T(8,128)} %shard_map.162.diag, f32[256,128]{1,0:T(8,128)} %get-tuple-element.40.oxl, f32[256,128]{1,0:T(8,128)} %get-tuple-element.41.oxh, f32[2,128,128]{2,1,0:T(8,128)} %get-tuple-element.42.oyl, f32[2,128,128]{2,1,0:T(8,128)} %get-tuple-element.43.oyh, ...), custom_call_target="tpu_custom_call" | custom-call | bytes 1589248 | tf_op jit(solution)/shard_map/pallas_call | solution.py:392
Async XLA Ops:
  3.9 9.9 %collective-permute-start = (f32[392,128]{1,0:T(8,128)}, f32[392,128]{1,0:T(8,128)S(1)}, u32[]{:S(2)}, u32[]{:S(2)}) collective-permute-start(f32[392,128]{1,0:T(8,128)} %get-tuple-element.25), channel_id=1, source_target_pairs={{0,8},{8,16},{16,24},{24,0},{1,9},{9,17},{17,25},{25,1},{2,10},{10... | collective-permute-start | bytes 602120 | tf_op jit(solution)/shard_map/ppermute | solution.py:409
  6.8 10.7 %collective-permute-start.1 = (f32[392,128]{1,0:T(8,128)}, f32[392,128]{1,0:T(8,128)S(1)}, u32[]{:S(2)}, u32[]{:S(2)}) collective-permute-start(f32[392,128]{1,0:T(8,128)} %get-tuple-element.26), channel_id=1, source_target_pairs={{0,24},{8,0},{16,8},{24,16},{1,25},{9,1},{17,9},{25,17},{2,26},{10... | collective-permute-start | bytes 602120 | tf_op jit(solution)/shard_map/ppermute | solution.py:409
  7.8 16.3 %collective-permute-start.2 = (f32[400,128]{1,0:T(8,128)}, f32[400,128]{1,0:T(8,128)S(1)}, u32[]{:S(2)}, u32[]{:S(2)}) collective-permute-start(f32[400,128]{1,0:T(8,128)} %get-tuple-element.29), channel_id=1, source_target_pairs={{0,2},{2,4},{4,6},{6,0},{1,3},{3,5},{5,7},{7,1},{8,10},{10,12},{12... | collective-permute-start | bytes 614408 | tf_op jit(solution)/shard_map/ppermute | solution.py:409
  9.8 14.2 %collective-permute-start.3 = (f32[400,128]{1,0:T(8,128)}, f32[400,128]{1,0:T(8,128)S(1)}, u32[]{:S(2)}, u32[]{:S(2)}) collective-permute-start(f32[400,128]{1,0:T(8,128)} %get-tuple-element.30), channel_id=1, source_target_pairs={{0,6},{2,0},{4,2},{6,4},{1,7},{3,1},{5,3},{7,5},{8,14},{10,8},{12,... | collective-permute-start | bytes 614408 | tf_op jit(solution)/shard_map/ppermute | solution.py:409
  13.8 3.7 %copy-start = (f32[392,128]{1,0:T(8,128)}, f32[392,128]{1,0:T(8,128)S(1)}, u32[]{:S(2)}) copy-start(f32[392,128]{1,0:T(8,128)S(1)} %collective-permute-done.lo.xlo) | copy-start | bytes 602116
  17.5 0.7 copy-start.1
  20.2 6.8 %collective-permute-start.4 = (f32[152,128]{1,0:T(8,128)}, f32[152,128]{1,0:T(8,128)S(1)}, u32[]{:S(2)}, u32[]{:S(2)}) collective-permute-start(f32[152,128]{1,0:T(8,128)} %get-tuple-element.31), channel_id=1, source_target_pairs={{0,2},{2,4},{4,6},{6,0},{1,3},{3,5},{5,7},{7,1},{8,10},{10,12},{12... | collective-permute-start | bytes 233480 | tf_op jit(solution)/shard_map/ppermute | solution.py:409
  21.8 5.4 %collective-permute-start.5 = (f32[152,128]{1,0:T(8,128)}, f32[152,128]{1,0:T(8,128)S(1)}, u32[]{:S(2)}, u32[]{:S(2)}) collective-permute-start(f32[152,128]{1,0:T(8,128)} %get-tuple-element.32), channel_id=1, source_target_pairs={{0,6},{2,0},{4,2},{6,4},{1,7},{3,1},{5,3},{7,5},{8,14},{10,8},{12,... | collective-permute-start | bytes 233480 | tf_op jit(solution)/shard_map/ppermute | solution.py:409
  24.0 3.2 %copy-start.2 = (f32[400,128]{1,0:T(8,128)}, f32[400,128]{1,0:T(8,128)S(1)}, u32[]{:S(2)}) copy-start(f32[400,128]{1,0:T(8,128)S(1)} %collective-permute-done.2.ylo) | copy-start | bytes 614404
  24.1 3.2 %copy-start.3 = (f32[400,128]{1,0:T(8,128)}, f32[400,128]{1,0:T(8,128)S(1)}, u32[]{:S(2)}) copy-start(f32[400,128]{1,0:T(8,128)S(1)} %collective-permute-done.3.yhi) | copy-start | bytes 614404
  27.0 0.6 copy-start.8
  27.2 0.6 copy-start.9
  31.6 2.6 %collective-permute-start.6 = (f32[2,816,128]{2,1,0:T(8,128)}, f32[2,816,128]{2,1,0:T(8,128)S(1)}, u32[]{:S(2)}, u32[]{:S(2)}) collective-permute-start(f32[2,816,128]{2,1,0:T(8,128)} %get-tuple-element.34), channel_id=1, source_target_pairs={{0,1},{1,0},{2,3},{3,2},{4,5},{5,4},{6,7},{7,6},{8,9},{9,8},{10,11... | collective-permute-start | bytes 2506760 | tf_op jit(solution)/shard_map/ppermute | solution.py:409
  57.3 13.1 %collective-permute-start.11 = (f32[2,2,128,128]{3,2,1,0:T(8,128)S(1)}, f32[2,2,128,128]{3,2,1,0:T(8,128)S(1)}, u32[]{:S(2)}, u32[]{:S(2)}) collective-permute-start(f32[2,2,128,128]{3,2,1,0:T(8,128)S(1)} %pad_maximum_fusion), channel_id=1, source_target_pairs={{0,1},{1,0},{2,3},{3,2},{4,5},{5,4},{6,7},{7,6},{8,9},{9,8},{10,11... | collective-permute-start | bytes 786440 | tf_op jit(solution)/shard_map/ppermute | solution.py:409
  57.5 13.7 %collective-permute-start.8 = (f32[256,128]{1,0:T(8,128)}, f32[256,128]{1,0:T(8,128)S(1)}, u32[]{:S(2)}, u32[]{:S(2)}) collective-permute-start(f32[256,128]{1,0:T(8,128)} %get-tuple-element.40.oxl), channel_id=1, source_target_pairs={{0,24},{8,0},{16,8},{24,16},{1,25},{9,1},{17,9},{25,17},{2,26},{10... | collective-permute-start | bytes 393224 | tf_op jit(solution)/shard_map/ppermute | solution.py:409
  58.9 12.2 %collective-permute-start.7 = (f32[256,128]{1,0:T(8,128)}, f32[256,128]{1,0:T(8,128)S(1)}, u32[]{:S(2)}, u32[]{:S(2)}) collective-permute-start(f32[256,128]{1,0:T(8,128)} %get-tuple-element.41.oxh), channel_id=1, source_target_pairs={{0,8},{8,16},{16,24},{24,0},{1,9},{9,17},{17,25},{25,1},{2,10},{10... | collective-permute-start | bytes 393224 | tf_op jit(solution)/shard_map/ppermute | solution.py:409
  59.5 11.6 %collective-permute-start.10 = (f32[2,128,128]{2,1,0:T(8,128)}, f32[2,128,128]{2,1,0:T(8,128)S(1)}, u32[]{:S(2)}, u32[]{:S(2)}) collective-permute-start(f32[2,128,128]{2,1,0:T(8,128)} %get-tuple-element.42.oyl), channel_id=1, source_target_pairs={{0,6},{2,0},{4,2},{6,4},{1,7},{3,1},{5,3},{7,5},{8,14},{10,8},{12,... | collective-permute-start | bytes 393224 | tf_op jit(solution)/shard_map/ppermute | solution.py:409
  62.7 8.4 %collective-permute-start.9 = (f32[2,128,128]{2,1,0:T(8,128)}, f32[2,128,128]{2,1,0:T(8,128)S(1)}, u32[]{:S(2)}, u32[]{:S(2)}) collective-permute-start(f32[2,128,128]{2,1,0:T(8,128)} %get-tuple-element.43.oyh), channel_id=1, source_target_pairs={{0,2},{2,4},{4,6},{6,0},{1,3},{3,5},{5,7},{7,1},{8,10},{10,12},{12... | collective-permute-start | bytes 393224 | tf_op jit(solution)/shard_map/ppermute | solution.py:409
  71.1 0.6 copy-start.4
  71.2 0.7 copy-start.5
  71.2 0.7 copy-start.6
  71.2 0.8 %copy-start.7 = (f32[2,128,128]{2,1,0:T(8,128)}, f32[2,128,128]{2,1,0:T(8,128)S(1)}, u32[]{:S(2)}) copy-start(f32[2,128,128]{2,1,0:T(8,128)S(1)} %collective-permute-done.9.nyl) | copy-start | bytes 393220

commit v2 on v1

v2 whole, which is shorter than its diff:
```python
import functools

import jax
import jax.numpy as jnp
import ml_dtypes
import numpy as np
from jax import lax
from jax.experimental import pallas as pl
from jax.experimental.pallas import tpu as pltpu
from jax.sharding import PartitionSpec as P

BUF = 3
PENALTY = 2.0
LOW_BOUND = -1.5
CUTOFF = 8.0
HIGH_BOUND = 16.0
BF = jnp.bfloat16
F32 = jnp.float32


class Plan:
    def __init__(self, cells, width):
        self.cells, self.width = cells, width
        self.ext = cells + 2 * BUF
        self.groups = self.ext // 2
        self.inner = cells // 2
        self.lanes = 2 * width
        self.face = cells * cells
        self.yext = self.ext * cells
        self.plane = -(-self.ext // 8) * 8
        self.strip = BUF * cells
        self.rows = self.yext + 2 * BUF * self.plane
        self.trows = -(-self.ext // 8) * 8
        order = list(range(BUF, BUF + cells)) + list(range(BUF)) + list(range(BUF + cells, self.ext))
        points = []
        for y in order:
            points += [(y, BUF + z) for z in range(cells)]
        for z in list(range(BUF)) + list(range(BUF + cells, self.ext)):
            points += [(y, z) for y in order] + [None] * (self.plane - self.ext)
        self.points = points
        self.first, self.second = spectral(self.ext)
        inside = np.zeros(self.ext)
        inside[BUF : BUF + cells] = 1.0
        self.inside = inside


def spectral(points):
    indices = np.arange(points)
    offsets = indices[:, None] - indices[None, :]
    first = np.zeros((points, points))
    second = np.zeros((points, points))
    for harmonic in range(1, points // 2):
        wavenum = 2.0 * np.pi * harmonic / points
        first = first - 2.0 * wavenum * np.sin(wavenum * offsets) / points
        second = second - 2.0 * wavenum * wavenum * np.cos(wavenum * offsets) / points
    second = second - np.pi * np.pi * np.cos(np.pi * offsets) / points
    return first, second


def row_matrix(plan, along, masked):
    out = np.zeros((plan.rows, plan.rows))
    for r, p in enumerate(plan.points):
        if p is None:
            continue
        for q, s in enumerate(plan.points):
            if s is None:
                continue
            if p[1] == s[1] and (not masked or plan.inside[p[1]]):
                out[r, q] += along[p[0], s[0]]
            if p[0] == s[0] and (not masked or plan.inside[p[0]]):
                out[r, q] += along[p[1], s[1]]
    return out


def mirrored(plan, along):
    n, g = plan.ext, plan.groups
    plus = along[:g, :g] + along[:g, ::-1][:, :g]
    minus = along[:g, :g] - along[:g, ::-1][:, :g]
    return np.concatenate([np.repeat(plus[:, :, None], plan.width, 2), np.repeat(minus[:, :, None], plan.width, 2)], 2)


def face_rows(plan):
    c = plan.cells
    index = {p: r for r, p in enumerate(plan.points) if p is not None}
    out = np.zeros((4 * c, plan.rows))
    for side, layer in enumerate((BUF, BUF + c - 1)):
        for z in range(c):
            for y in range(plan.ext):
                out[side * c + z, index[(y, BUF + z)]] = plan.first[layer, y]
        for y in range(c):
            for z in range(plan.ext):
                out[(2 + side) * c + y, index[(BUF + y, z)]] = plan.first[layer, z]
    return out


def energy(plan):
    c = plan.cells
    block = plan.first[BUF : BUF + c]
    out = 0.5 * block.T @ block
    for sign, layer in ((-1.0, BUF), (1.0, BUF + c - 1)):
        unit = np.zeros(plan.ext)
        unit[layer] = 1.0
        cross = np.outer(unit, plan.first[layer])
        out = out + 0.5 * PENALTY * np.outer(unit, unit) - 0.25 * sign * (cross + cross.T)
    return out


def halves(matrix):
    high = matrix.astype(np.float32).astype(ml_dtypes.bfloat16)
    low = (matrix - high.astype(np.float64)).astype(np.float32).astype(ml_dtypes.bfloat16)
    return high, low


def split(x):
    high = x.astype(BF)
    return high, (x - high.astype(F32)).astype(BF)


def swap(x):
    return pltpu.roll(x, x.shape[-1] // 2, x.ndim - 1)


def dot(a, b):
    return jnp.dot(a, b, preferred_element_type=F32)


def dot_t(a, b):
    return lax.dot_general(a, b, (((0,), (0,)), ((), ())), preferred_element_type=F32)


def exact(a, b):
    return jnp.dot(a, b, preferred_element_type=F32, precision=lax.Precision.HIGHEST)


def low_lanes(shape):
    return lax.broadcasted_iota(jnp.int32, shape, len(shape) - 1) < shape[-1] // 2


def sides(ref, paired):
    return [ref.at[0], ref.at[1]] if paired else ref


def pack_kernel(plan, orb, pot, spread, pick, xlo, xhi, ylo, yhi, inner, vt):
    c, w = plan.cells, plan.width
    half = plan.face // 2
    for s in range(BUF):
        for out, x in ((xlo, s), (xhi, c - BUF + s)):
            out[s * half : (s + 1) * half, :] = jnp.concatenate([orb[x, :half], orb[x, half:]], axis=1)
    for j in range(plan.inner):
        a, b = orb[j], orb[c - 1 - j]
        e = jnp.concatenate([a + b, a - b], axis=1)
        inner[j] = e
        ylo[j * plan.strip : (j + 1) * plan.strip, :] = e[: plan.strip]
        yhi[j * plan.strip : (j + 1) * plan.strip, :] = e[plan.face - plan.strip :]
    wide = exact(pot[...], spread[...]) * pick[...]
    v = wide.reshape(c, c, plan.face).sum(axis=1)
    vt[...] = v
    lanes = plan.lanes
    base = BUF * half
    xlo[base:, :] = jnp.zeros((8, lanes), F32)
    xhi[base:, :] = jnp.zeros((8, lanes), F32)
    for part in range(2):
        cols = slice(part * lanes, (part + 1) * lanes)
        xlo[base + part * BUF : base + (part + 1) * BUF, :] = v[:BUF, cols]
        xhi[base + part * BUF : base + (part + 1) * BUF, :] = v[c - BUF :, cols]
    ybase = plan.inner * plan.strip
    ylo[ybase:, :] = v[:, :lanes]
    yhi[ybase:, :] = v[:, plan.face - lanes :]


def xhalo_kernel(plan, lo, hi, outer, elo, ehi):
    half = plan.face // 2
    lanes = plan.lanes
    mask = low_lanes((half, lanes))
    for g in range(BUF):
        a = lo[g * half : (g + 1) * half, :]
        b = hi[(BUF - 1 - g) * half : (BUF - g) * half, :]
        s, d = a + b, a - b
        top = jnp.where(mask, s, swap(d))
        bottom = jnp.where(mask, swap(s), d)
        outer[g, :half] = top
        outer[g, half:] = bottom
        elo[g * plan.strip : (g + 1) * plan.strip, :] = top[: plan.strip]
        ehi[g * plan.strip : (g + 1) * plan.strip, :] = bottom[half - plan.strip :]
    base, ebase = BUF * half, BUF * plan.strip
    elo[ebase:, :] = jnp.zeros((8, lanes), F32)
    ehi[ebase:, :] = jnp.zeros((8, lanes), F32)
    for k, src in enumerate((lo, hi)):
        elo[ebase + k * BUF : ebase + (k + 1) * BUF, :] = src[base : base + BUF, :]
        ehi[ebase + k * BUF : ebase + (k + 1) * BUF, :] = src[base + BUF : base + 2 * BUF, :]


def zpack_kernel(plan, inner, outer, vx, vt, ylo, yhi, elo, ehi, zpick, field, vfull, z):
    c, lanes, strip, face = plan.cells, plan.lanes, plan.strip, plan.face
    for g in range(BUF):
        field[g, :face] = outer[g]
        field[g, face : face + strip] = elo[g * strip : (g + 1) * strip, :]
        field[g, face + strip : face + 2 * strip] = ehi[g * strip : (g + 1) * strip, :]
    for j in range(plan.inner):
        g = BUF + j
        field[g, :face] = inner[j]
        field[g, face : face + strip] = ylo[j * strip : (j + 1) * strip, :]
        field[g, face + strip : face + 2 * strip] = yhi[j * strip : (j + 1) * strip, :]
    pad = field.shape[1] - plan.yext
    field[:, plan.yext :] = jnp.zeros((plan.groups, pad, lanes), F32)
    plane = plan.plane
    span = BUF * plane
    for side, start in ((0, 0), (1, c - BUF)):
        for g in range(plan.groups):
            for k in range(BUF):
                at = g * span + k * plane
                z[side, at : at + plane, :] = field[g, pl.ds(start + k, plane, stride=c), :]
    ebase, ybase = BUF * strip, plan.inner * strip
    vfull[...] = jnp.zeros(vfull.shape, F32)
    vfull[: plan.ext, :face] = vx[: plan.ext, :]
    shift = lanes - strip
    vfull[:BUF, face : face + strip] = elo[ebase : ebase + BUF, :][:, shift:]
    vfull[BUF + c : plan.ext, face : face + strip] = elo[ebase + BUF : ebase + 2 * BUF, :][:, shift:]
    vfull[BUF : BUF + c, face : face + strip] = ylo[ybase:, :][:, shift:]
    vfull[:BUF, face + strip : face + 2 * strip] = ehi[ebase : ebase + BUF, :][:, :strip]
    vfull[BUF + c : plan.ext, face + strip : face + 2 * strip] = ehi[ebase + BUF : ebase + 2 * BUF, :][:, :strip]
    vfull[BUF : BUF + c, face + strip : face + 2 * strip] = yhi[ybase:, :][:, :strip]
    for side in range(2):
        z[side, plan.groups * span :, :] = exact(vfull[...], zpick[side])


CENTER = (HIGH_BOUND + CUTOFF) / 2.0
HALF_WIDTH = (HIGH_BOUND - CUTOFF) / 2.0
S0 = HALF_WIDTH / (LOW_BOUND - CENTER)
S1 = 1.0 / (2.0 / S0 - S0)


def mix(plan, coef, table, src, r0, r1):
    total = None
    for s in range(plan.groups):
        term = coef[table + s : table + s + 1, :] * src[s, r0:r1, :]
        total = term if total is None else total + term
    return total


def chunks(stop, size=16, start=0):
    return [(r, min(r + size, stop)) for r in range(start, stop, size)]


def pairs(stop, start=0):
    return [(g, min(g + 2, stop)) for g in range(start, stop, 2)]


def spread_potential(plan, piece, count, vspread, va, vd, at):
    high = piece.astype(BF).astype(F32)
    rest = piece - high
    mid = rest.astype(BF).astype(F32)
    three = jnp.concatenate([high, mid, rest - mid], axis=0)
    turned = jnp.transpose(three)[:count, :].astype(BF)
    g_all, lanes = plan.groups, plan.lanes
    for g0, g1 in pairs(g_all):
        for k, dst, less in ((0, va, CENTER), (1, vd, 0.0)):
            cols = slice((k * g_all + g0) * lanes, (k * g_all + g1) * lanes)
            both = dot(turned, vspread[:, cols]) - less
            for g in range(g0, g1):
                dst[g, at : at + count, :] = both[:, (g - g0) * lanes : (g - g0 + 1) * lanes]


def three(wh, wl, sh, sl):
    return dot(wh, sh) + dot(wl, sh) + dot(wh, sl)


def local_terms(plan, coef, g, src, r0, r1, va, vd, v0):
    own = src[g, r0:r1, :]
    value = mix(plan, coef, g * plan.groups, src, r0, r1)
    return value + va[g, v0 : v0 + r1 - r0, :] * own + vd[g, v0 : v0 + r1 - r0, :] * swap(own)


def inside_kernel(plan, inner, outer, vt, xlo, xhi, wh, wl, coef, vspread, acc, va, vd, vx, x, xh, xl):
    g_all, lanes, face, c = plan.groups, plan.lanes, plan.face, plan.cells
    base = BUF * (face // 2)
    vx[...] = jnp.zeros(vx.shape, F32)
    for part in range(2):
        cols = slice(part * lanes, (part + 1) * lanes)
        vx[:BUF, cols] = xlo[base + part * BUF : base + (part + 1) * BUF, :]
        vx[BUF + c : plan.ext, cols] = xhi[base + part * BUF : base + (part + 1) * BUF, :]
    vx[BUF : BUF + c, :] = vt[...]
    spread_potential(plan, vx[...], face, vspread, va, vd, 0)
    for g in range(g_all):
        value = outer[g] if g < BUF else inner[g - BUF]
        x[g] = value
        h, l = split(value)
        xh[:, g * lanes : (g + 1) * lanes] = h
        xl[:, g * lanes : (g + 1) * lanes] = l
    for g0, g1 in pairs(g_all):
        cols = slice(g0 * lanes, g1 * lanes)
        total = three(wh[...], wl[...], xh[:, cols], xl[:, cols])
        for g in range(g0, g1):
            acc[g] = total[:, (g - g0) * lanes : (g - g0 + 1) * lanes]
            for r0, r1 in chunks(face):
                acc[g, r0:r1, :] = acc[g, r0:r1, :] + local_terms(plan, coef, g, x, r0, r1, va, vd, r0)


def yhalo_kernel(plan, field, vfull, wh, wl, coef, vspread, given, acc, va, vd, xh, xl):
    g_all, lanes, face, yext = plan.groups, plan.lanes, plan.face, plan.yext
    count = yext - face
    spread_potential(plan, vfull[:, face:], count, vspread, va, vd, 0)
    for g in range(g_all):
        h, l = split(field[g, face:yext, :])
        xh[:, g * lanes : (g + 1) * lanes] = h
        xl[:, g * lanes : (g + 1) * lanes] = l
    for g0, g1 in pairs(g_all):
        cols = slice(g0 * lanes, g1 * lanes)
        total = three(wh[...], wl[...], xh[:, cols], xl[:, cols])
        for g in range(g0, g1):
            acc[g] = given[g] + total[:, (g - g0) * lanes : (g - g0 + 1) * lanes]
            for r0, r1 in chunks(yext, 16, face):
                acc[g, r0:r1, :] = acc[g, r0:r1, :] + local_terms(plan, coef, g, field, r0, r1, va, vd, r0 - face)


def filter_kernel(plan, paired, *refs):
    zin, refs = refs[: 1 if paired else 2], refs[1 if paired else 2 :]
    (field, vai, vdi, vay, vdy, given, zwh, zwl, wh, wl, coef, dcoef, vspread, fh, fl,
     out, mx, my, mz,
     x, xh, xl, y, yh, yl, va, vd, acc, dacc) = refs
    g_all, lanes, rows, face, yext, c = plan.groups, plan.lanes, plan.rows, plan.face, plan.yext, plan.cells
    span = BUF * plan.plane
    mz = sides(mz, paired)
    zlo, zhi = (zin[0].at[1], zin[0].at[0]) if paired else zin
    for k, piece in enumerate((zlo, zhi)):
        spread_potential(plan, piece[g_all * span :, :], span, vspread, va, vd, k * span)
        for g in range(g_all):
            value = piece[g * span : (g + 1) * span, :]
            x[g, k * span : (k + 1) * span, :] = value
            h, l = split(value)
            xh[k * span : (k + 1) * span, g * lanes : (g + 1) * lanes] = h
            xl[k * span : (k + 1) * span, g * lanes : (g + 1) * lanes] = l

    def put(dst, dh, dl, g, r0, r1, value):
        dst[g, r0:r1, :] = value
        h, l = split(value)
        dh[r0:r1, g * lanes : (g + 1) * lanes] = h
        dl[r0:r1, g * lanes : (g + 1) * lanes] = l

    for n, (g0, g1) in enumerate(pairs(g_all)):
        slot = n % 2
        cols = slice(g0 * lanes, g1 * lanes)
        acc[slot, :, : (g1 - g0) * lanes] = three(zwh[...], zwl[...], xh[:, cols], xl[:, cols])
        for g in range(g0, g1):
            mine = slice((g - g0) * lanes, (g - g0 + 1) * lanes)
            for r0, r1 in chunks(rows):
                value = given[g, r0:r1, :] + acc[slot, r0:r1, mine]
                if r0 >= yext:
                    value = value + local_terms(plan, coef, g, x, r0 - yext, r1 - yext, va, vd, r0 - yext)
                put(y, yh, yl, g, r0, r1, value * (S0 / HALF_WIDTH))

    for n, (g0, g1) in enumerate(pairs(g_all)):
        slot = n % 2
        top = face if g1 <= BUF else rows
        cols = slice(g0 * lanes, g1 * lanes)
        acc[slot, :top, : (g1 - g0) * lanes] = three(wh[:top], wl[:top], yh[:, cols], yl[:, cols])
        for g in range(g0, g1):
            mine = slice((g - g0) * lanes, (g - g0 + 1) * lanes)
            for r0, r1 in chunks(face if g < BUF else rows):
                v, d, at, start, s0 = (vai, vdi, r0, field, r0)
                if r0 >= yext:
                    v, d, at, start, s0 = (va, vd, r0 - yext, x, r0 - yext)
                elif r0 >= face:
                    v, d, at, start, s0 = (vay, vdy, r0 - face, field, r0)
                value = acc[slot, r0:r1, mine] + local_terms(plan, coef, g, y, r0, r1, v, d, at)
                value = value * (2.0 * S1 / HALF_WIDTH) - (S0 * S1) * start[g, s0 : s0 + r1 - r0, :]
                out[g, r0:r1, :] = value
                if g >= BUF:
                    h, l = split(value)
                    yh[r0:r1, g * lanes : (g + 1) * lanes] = h
                    yl[r0:r1, g * lanes : (g + 1) * lanes] = l

    for r0, r1 in chunks(face, 16):
        mask = low_lanes((r1 - r0, lanes))
        e = out[BUF, r0:r1, :]
        d = mix(plan, dcoef, 0, out, r0, r1)
        te, td = swap(e), swap(d)
        mx[0][r0:r1, :] = 0.5 * jnp.where(mask, e + te, d + td)
        mx[1][r0:r1, :] = 0.5 * jnp.where(mask, e - te, d - td)
    cols = slice(BUF * lanes, g_all * lanes)
    dacc[...] = three(fh[...], fl[...], yh[:, cols], yl[:, cols])
    part = plan.inner * c
    for j in range(plan.inner):
        g = BUF + j
        own = slice(j * lanes, (j + 1) * lanes)
        to = slice(j * c, (j + 1) * c)
        my[0][to, :] = out[g, :c, :]
        my[1][to, :] = out[g, face - c : face, :]
        mz[0][to, :] = out[g, pl.ds(0, c, stride=c), :]
        mz[1][to, :] = out[g, pl.ds(c - 1, c, stride=c), :]
        for k, dst in enumerate((my[0], my[1], mz[0], mz[1])):
            dst[part + j * c : part + (j + 1) * c, :] = dacc[k * c : (k + 1) * c, own]


def own_kernel(plan, f, va, vd, bh, bl, coef, diag, basis, f2, f2h, f2l, fhi, acc):
    g_all, lanes, rows, face, c = plan.groups, plan.lanes, plan.rows, plan.face, plan.cells
    for j in range(plan.inner):
        for r0, r1 in chunks(face, 64):
            e = f[BUF + j, r0:r1, :]
            t = swap(e)
            basis[j, r0:r1, :] = (0.5 * (e + t))[:, : plan.width]
            basis[c - 1 - j, r0:r1, :] = (0.5 * (e - t))[:, : plan.width]
    for g in range(g_all):
        top = face if g < BUF else rows
        for r0, r1 in chunks(top, 16):
            value = f[g, r0:r1, :]
            high = value.astype(BF)
            fhi[g, r0:r1, :] = high
            twice = 2.0 * value - high.astype(F32)
            f2[g, r0:r1, :] = twice
            if g >= BUF:
                h, l = split(twice)
                f2h[r0:r1, (g - BUF) * lanes : (g - BUF + 1) * lanes] = h
                f2l[r0:r1, (g - BUF) * lanes : (g - BUF + 1) * lanes] = l
    total = jnp.zeros((lanes, 2 * lanes), F32)

    def fold(total, g, top, value):
        h, l = split(value)
        return total + dot_t(fhi[g, :top, :], jnp.concatenate([h, l], axis=1))

    for g in range(BUF):
        parts = [mix(plan, coef, g * g_all, f2, r0, r1) for r0, r1 in chunks(face)]
        total = fold(total, g, face, jnp.concatenate(parts, axis=0))
    for n, (j0, j1) in enumerate(pairs(plan.inner)):
        slot = n % 2
        cols = slice(j0 * lanes, j1 * lanes)
        acc[slot] = three(bh[...], bl[...], f2h[:, cols], f2l[:, cols])
        for j in range(j0, j1):
            g = BUF + j
            mine = slice((j - j0) * lanes, (j - j0 + 1) * lanes)
            parts = []
            for r0, r1 in chunks(face):
                own = f2[g, r0:r1, :]
                value = acc[slot, r0:r1, mine] + mix(plan, coef, g * g_all, f2, r0, r1)
                parts.append(value + (va[g, r0:r1, :] + CENTER) * own + vd[g, r0:r1, :] * swap(own))
            parts.append(acc[slot, face:, mine])
            total = fold(total, g, rows, jnp.concatenate(parts, axis=0))
    both = total[:, :lanes] + total[:, lanes:]
    w = plan.width
    block = both[:w, :w] + both[w:, w:]
    diag[...] = 0.25 * (block + jnp.transpose(block))


def face_kernel(plan, paired, diag, ox, oy, oz, nx, ny, nz, blocks):
    w, lanes = plan.width, plan.lanes
    part = plan.inner * plan.cells
    oz, nz = sides(oz, paired), sides(nz, paired)[::-1] if paired else nz
    blocks[0] = diag[...]

    def product(a, b):
        ah, al = split(a)
        bh, bl = split(b)
        return dot_t(ah, bh) + dot_t(ah, bl) + dot_t(al, bh)

    for k in range(2):
        sign = -1.0 if k == 0 else 1.0
        m = product(ox[k][...], nx[k][...])
        blocks[1 + k] = 0.25 * sign * (m[w:, :w] - m[:w, w:]) - 0.5 * PENALTY * m[:w, :w]
        for at, own, other in ((3, oy, ny), (5, oz, nz)):
            a = jnp.concatenate([own[k][:part, :], own[k][part:, :]], axis=1)
            b = jnp.concatenate([other[k][:part, :], other[k][part:, :]], axis=1)
            m = product(a, b)
            uv = m[:w, :w] + m[w:lanes, w:lanes]
            udv = m[:w, lanes : lanes + w] + m[w:lanes, lanes + w :]
            duv = m[lanes : lanes + w, :w] + m[lanes + w :, w:lanes]
            blocks[at + k] = 0.5 * (0.25 * sign * (duv - udv) - 0.5 * PENALTY * uv)


def near(*shape):
    return pltpu.VMEM(shape, F32)


def far(*shape):
    return jax.ShapeDtypeStruct(shape, F32)


def call(kernel, outs, args, scratch=(), flops=0, limit=24, aliases=None, direct=()):
    def place(a):
        return pltpu.with_memory_space_constraint(jnp.asarray(a), pltpu.VMEM)

    placed = [a if i in direct else jax.tree.map(place, a) for i, a in enumerate(args)]
    space = pl.BlockSpec(memory_space=pltpu.VMEM)
    bytes_all = sum(int(np.prod(a.shape)) * a.dtype.itemsize for a in jax.tree.leaves(placed))
    return pl.pallas_call(
        kernel,
        out_shape=outs,
        in_specs=jax.tree.map(lambda a: space, placed),
        out_specs=jax.tree.map(lambda a: space, outs),
        scratch_shapes=list(scratch),
        input_output_aliases=aliases or {},
        compiler_params=pltpu.CompilerParams(vmem_limit_bytes=limit * 1024 * 1024),
        cost_estimate=pl.CostEstimate(flops=flops, bytes_accessed=bytes_all, transcendentals=0),
    )(*placed)


def shift(array, axis, step):
    count = lax.axis_size(axis)
    return lax.ppermute(array, axis, [(i, (i + step) % count) for i in range(count)])


def on_device(orbitals, potential):
    cells, width = orbitals.shape[0], orbitals.shape[-1]
    plan = Plan(cells, width)
    lanes, face, strip, rows, yext = plan.lanes, plan.face, plan.strip, plan.rows, plan.yext
    g_all, inner_all = plan.groups, plan.inner
    paired = lax.axis_size("gz") == 2
    part = functools.partial

    spread = np.zeros((cells, face), np.float32)
    pick = np.zeros((cells, cells, face), np.float32)
    for y in range(cells):
        spread[np.arange(cells), y * cells + np.arange(cells)] = 1.0
        pick[:, y, y * cells : (y + 1) * cells] = 1.0
    xrows, yrows, erows = BUF * face // 2 + 8, inner_all * strip + cells, BUF * strip + 8
    xlo, xhi, ylo, yhi, inner, vt = call(
        part(pack_kernel, plan),
        [near(xrows, lanes), near(xrows, lanes), near(yrows, lanes), near(yrows, lanes), near(inner_all, face, lanes), near(cells, face)],
        [orbitals.reshape(cells, face, width), potential.reshape(face, cells), spread, pick.reshape(face, face)],
        direct=(0, 1),
    )
    from_xlo, from_xhi = shift(xhi, "gx", 1), shift(xlo, "gx", -1)
    from_ylo, from_yhi = shift(yhi, "gy", 1), shift(ylo, "gy", -1)
    outer, elo, ehi = call(
        part(xhalo_kernel, plan), [near(BUF, face, lanes), near(erows, lanes), near(erows, lanes)], [from_xlo, from_xhi],
    )
    from_elo, from_ehi = shift(ehi, "gy", 1), shift(elo, "gy", -1)

    matrix = -0.5 * row_matrix(plan, plan.second, False)
    coef = (-0.5 * mirrored(plan, plan.second)).reshape(-1, lanes).astype(np.float32)
    vspread = np.zeros((plan.trows, 2, g_all, lanes), np.float32)
    for g in range(g_all):
        vspread[g, :, g, :] = 0.5
        vspread[plan.ext - 1 - g, 0, g, :] = 0.5
        vspread[plan.ext - 1 - g, 1, g, :] = -0.5
    vspread = np.tile(vspread.reshape(plan.trows, -1), (3, 1)).astype(ml_dtypes.bfloat16)
    bf = lambda *shape: pltpu.VMEM(shape, BF)
    acc, vai, vdi, vx = call(
        part(inside_kernel, plan),
        [near(g_all, rows, lanes), near(g_all, face, lanes), near(g_all, face, lanes), near(plan.trows, face)],
        [inner, outer, vt, from_xlo, from_xhi, *halves(matrix[:, :face]), coef, vspread],
        [near(g_all, face, lanes), bf(face, g_all * lanes), bf(face, g_all * lanes)],
        flops=10**9,
    )

    frows = plan.plane * cells
    zpick = np.zeros((2, frows, lanes), np.float32)
    for side, start in ((0, 0), (1, cells - BUF)):
        for k in range(BUF):
            for y in range(plan.ext):
                zpick[side, y * cells + start + k, k * plan.plane + y] = 1.0
    span = BUF * plan.plane
    zrows = g_all * span + plan.trows
    field, vfull, z = call(
        part(zpack_kernel, plan),
        [near(g_all, frows, lanes), near(plan.trows, frows), near(2, zrows, lanes)],
        [inner, outer, vx, vt, from_ylo, from_yhi, from_elo, from_ehi, zpick],
    )
    if paired:
        zin = [shift(z, "gz", 1)]
    else:
        zin = [shift(z[1], "gz", 1), shift(z[0], "gz", -1)]
    ycount = yext - face
    acc, vay, vdy = call(
        part(yhalo_kernel, plan),
        [near(g_all, rows, lanes), near(g_all, ycount, lanes), near(g_all, ycount, lanes)],
        [field, vfull, *halves(matrix[:, face:yext]), coef, vspread, acc],
        [bf(ycount, g_all * lanes), bf(ycount, g_all * lanes)],
        flops=10**9,
        aliases={6: 0},
    )

    p = plan.first[BUF, :g_all] + plan.first[BUF, ::-1][:g_all]
    q = plan.first[BUF, :g_all] - plan.first[BUF, ::-1][:g_all]
    dcoef = np.concatenate([np.repeat(p[:, None], width, 1), np.repeat(q[:, None], width, 1)], 1).astype(np.float32)
    msg = near(face, lanes)
    filtered, mx, my, mz = call(
        part(filter_kernel, plan, paired),
        [near(g_all, rows, lanes), [msg, msg], [msg, msg], near(2, face, lanes) if paired else [msg, msg]],
        [*zin, field, vai, vdi, vay, vdy, acc, *halves(matrix[:, yext:]), *halves(matrix), coef, dcoef, vspread, *halves(face_rows(plan))],
        [near(g_all, 2 * span, lanes), bf(2 * span, g_all * lanes), bf(2 * span, g_all * lanes),
         near(g_all, rows, lanes), bf(rows, g_all * lanes), bf(rows, g_all * lanes),
         near(g_all, 2 * span, lanes), near(g_all, 2 * span, lanes),
         near(2, rows, 2 * lanes), near(4 * cells, inner_all * lanes)],
    )
    ny = [shift(my[1], "gy", 1), shift(my[0], "gy", -1)]
    nx = [shift(mx[1], "gx", 1), shift(mx[0], "gx", -1)]
    if paired:
        nz = shift(mz, "gz", 1)
    else:
        nz = [shift(mz[1], "gz", 1), shift(mz[0], "gz", -1)]

    along = energy(plan)
    bcoef = mirrored(plan, along).reshape(-1, lanes).astype(np.float32)
    diag, basis = call(
        part(own_kernel, plan), [near(width, width), far(cells, face, width)],
        [filtered, vai, vdi, *halves(row_matrix(plan, along, True)), bcoef],
        [near(g_all, rows, lanes), bf(rows, inner_all * lanes), bf(rows, inner_all * lanes), bf(g_all, rows, lanes), near(2, rows, 2 * lanes)],
        flops=2 * 10**9,
    )
    blocks = call(
        part(face_kernel, plan, paired), far(7, width, width), [diag, mx, my, mz, nx, ny, nz],
    )
    return basis.reshape(orbitals.shape), blocks[None, None, None]


def solution(mesh):
    return jax.shard_map(
        on_device,
        mesh=mesh,
        in_specs=(P("gx", "gy", "gz", None), P("gx", "gy", "gz")),
        out_specs=(P("gx", "gy", "gz", None), P("gx", "gy", "gz", None, None, None)),
        check_vma=False,
    )
```

time: 75.1 us -> 52.5 us (0.70)
  Pallas kernels: 40.7 us -> 22.8 us
  waiting for transfers between devices: 11.4 us -> 6.67 us
  other arithmetic: 0.99 us -> 0 us
    pallas_call x6 -> x8, Pallas kernels: 40.7 us -> 22.8 us  [call(): pl.pallas_call(kernel, out_shape=outs, in_specs=jax.tree.map(lambda a: sp...]
    ppermute x12, waiting for transfers between devices: 11.4 us -> 6.67 us  [shift(): lax.ppermute(array, axis, [(i, (i + step) % count) for i in range(count)])]
    unnamed x20 -> x42, local copies, waits for them, and re-layouts: 2.1 us -> 4.26 us
    squeeze x2 -> x0, local copies, waits for them, and re-layouts: 1.68 us -> none  [the longest x1 0.96 us: on_device(): zlo, zhi = (other[1], other[0])]
    another operation x1 -> x0, other arithmetic: 0.99 us -> none  [on_device(): nz = shift(jnp.stack([mzlo, mzhi]), 'gz', 1)]
  transfers between devices with their start and end apart: 12 -> 12, of which waited for: 5 -> 5; matrix products, arithmetic and copies ran while one was open for 1% -> 0% of each run, Pallas kernels for 13% -> 21%
where the time goes in v2:
time: 52.5 us; the launch traced here: 52.3 us
  Pallas kernels  22.8 us (43%)
  starting transfers between devices  17.6 us (34%)
  waiting for transfers between devices  6.67 us (13%)
  local copies, waits for them, and re-layouts  4.26 us (8%)
  between operations  0.89 us (2%)
    pallas_call x8, Pallas kernels, call(): pl.pallas_call(kernel, out_shape=outs, in_specs=jax.tree.map(lambda a: sp...  22.8 us
    ppermute x12, starting transfers between devices, shift(): lax.ppermute(array, axis, [(i, (i + step) % count) for i in range(count)])  17.6 us
    ppermute x12, waiting for transfers between devices, shift(): lax.ppermute(array, axis, [(i, (i + step) % count) for i in range(count)])  6.67 us
    unnamed x42, local copies, waits for them, and re-layouts  4.26 us
  transfers between devices with their start and end apart: 12, of which 5 were waited for; matrix products, arithmetic and copies ran while one was open for 0% of the time, Pallas kernels for 21%

profile of v2, /device:TPU:0, one launch (start us, length us, event | category | flops | bytes accessed | tf_op | source)
XLA Modules:
  0.0 52.3 jit_solution(11266425001060682595)
XLA Ops:
  0.6 0.0 copy-start
  0.6 1.6 %copy-done = f32[16,16,16,64]{3,2,1,0:T(8,128)S(1)} copy-done((f32[16,16,16,64]{3,2,1,0:T(8,128)S(1)}, f32[16,16,16,64]{3,2,1,0:T(8,128)}, u32[]{:S(2)}) %copy-start) | copy-done | bytes 1048600
  2.2 0.9 %copy-done.6 = f32[256,256]{1,0:T(8,128)S(1)} copy-done((f32[256,256]{1,0:T(8,128)S(1)}, f32[256,256]{1,0:T(8,128)}, u32[]{:S(2)}) %copy-start.6) | copy-done | bytes 262168
  3.2 0.9 %copy-done.9 = f32[16,16,16]{2,1,0:T(8,128)S(1)} copy-done((f32[16,16,16]{2,1,0:T(8,128)S(1)}, f32[16,16,16]{2,1,0:T(8,128)}, u32[]{:S(2)}) %copy-start.9) | copy-done | bytes 16408
  4.1 0.7 %copy-done.14 = f32[16,256]{1,0:T(8,128)S(1)} copy-done((f32[16,256]{1,0:T(8,128)S(1)}, f32[16,256]{1,0:T(8,128)}, u32[]{:S(2)}) %copy-start.14) | copy-done | bytes 16408
  4.8 0.5 shard_map.212
  5.3 0.0 copy-start.4
  5.3 3.0 %collective-permute-start = (f32[392,128]{1,0:T(8,128)S(1)}, f32[392,128]{1,0:T(8,128)S(1)}, u32[]{:S(2)}, u32[]{:S(2)}) collective-permute-start(f32[392,128]{1,0:T(8,128)S(1)} %get-tuple-element.30), channel_id=1, source_target_pairs={{0,8},{8,16},{16,24},{24,0},{1,9},{9,17},{17,25},{25,1},{2,10},{10... | collective-permute-start | bytes 602120 | tf_op jit(solution)/shard_map/ppermute | solution.py:498
  8.3 1.0 %collective-permute-start.1 = (f32[392,128]{1,0:T(8,128)S(1)}, f32[392,128]{1,0:T(8,128)S(1)}, u32[]{:S(2)}, u32[]{:S(2)}) collective-permute-start(f32[392,128]{1,0:T(8,128)S(1)} %get-tuple-element.31), channel_id=1, source_target_pairs={{0,24},{8,0},{16,8},{24,16},{1,25},{9,1},{17,9},{25,17},{2,26},{10... | collective-permute-start | bytes 602120 | tf_op jit(solution)/shard_map/ppermute | solution.py:498
  9.3 2.0 %collective-permute-start.2 = (f32[400,128]{1,0:T(8,128)S(1)}, f32[400,128]{1,0:T(8,128)S(1)}, u32[]{:S(2)}, u32[]{:S(2)}) collective-permute-start(f32[400,128]{1,0:T(8,128)S(1)} %get-tuple-element.35), channel_id=1, source_target_pairs={{0,2},{2,4},{4,6},{6,0},{1,3},{3,5},{5,7},{7,1},{8,10},{10,12},{12... | collective-permute-start | bytes 614408 | tf_op jit(solution)/shard_map/ppermute | solution.py:498
  11.3 2.0 %collective-permute-start.3 = (f32[400,128]{1,0:T(8,128)S(1)}, f32[400,128]{1,0:T(8,128)S(1)}, u32[]{:S(2)}, u32[]{:S(2)}) collective-permute-start(f32[400,128]{1,0:T(8,128)S(1)} %get-tuple-element.36), channel_id=1, source_target_pairs={{0,6},{2,0},{4,2},{6,4},{1,7},{3,1},{5,3},{7,5},{8,14},{10,8},{12,... | collective-permute-start | bytes 614408 | tf_op jit(solution)/shard_map/ppermute | solution.py:498
  13.4 1.7 %collective-permute-done.lo.xlo = f32[392,128]{1,0:T(8,128)S(1)} collective-permute-done((f32[392,128]{1,0:T(8,128)S(1)}, f32[392,128]{1,0:T(8,128)S(1)}, u32[]{:S(2)}, u32[]{:S(2)}) %collective-permute-start) | collective-permute-done | bytes 200736 | tf_op jit(solution)/shard_map/ppermute | solution.py:498
  15.1 3.7 %collective-permute-done.1.hi.xhi = f32[392,128]{1,0:T(8,128)S(1)} collective-permute-done((f32[392,128]{1,0:T(8,128)S(1)}, f32[392,128]{1,0:T(8,128)S(1)}, u32[]{:S(2)}, u32[]{:S(2)}) %collective-permute-start.1) | collective-permute-done | bytes 200736 | tf_op jit(solution)/shard_map/ppermute | solution.py:498
  18.8 0.2 shard_map.213
  19.0 1.6 %collective-permute-start.4 = (f32[152,128]{1,0:T(8,128)S(1)}, f32[152,128]{1,0:T(8,128)S(1)}, u32[]{:S(2)}, u32[]{:S(2)}) collective-permute-start(f32[152,128]{1,0:T(8,128)S(1)} %get-tuple-element.37), channel_id=1, source_target_pairs={{0,2},{2,4},{4,6},{6,0},{1,3},{3,5},{5,7},{7,1},{8,10},{10,12},{12... | collective-permute-start | bytes 233480 | tf_op jit(solution)/shard_map/ppermute | solution.py:498
  20.6 2.2 %collective-permute-start.5 = (f32[152,128]{1,0:T(8,128)S(1)}, f32[152,128]{1,0:T(8,128)S(1)}, u32[]{:S(2)}, u32[]{:S(2)}) collective-permute-start(f32[152,128]{1,0:T(8,128)S(1)} %get-tuple-element.38), channel_id=1, source_target_pairs={{0,6},{2,0},{4,2},{6,4},{1,7},{3,1},{5,3},{7,5},{8,14},{10,8},{12,... | collective-permute-start | bytes 233480 | tf_op jit(solution)/shard_map/ppermute | solution.py:498
  22.9 0.0 copy-done.1
  22.9 0.0 copy-done.5
  22.9 0.0 copy-done.18
  22.9 0.0 copy-done.19
  22.9 0.0 copy-start.10
  22.9 0.0 copy-start.11
  22.9 2.7 %shard_map.214 = (f32[11,496,128]{2,1,0:T(8,128)S(1)}, f32[11,256,128]{2,1,0:T(8,128)S(1)}, f32[11,256,128]{2,1,0:T(8,128)S(1)}, f32[24,256]{1,0:T(8,128)S(1)}) custom-call(f32[8,256,128]{2,1,0:T(8,128)S(1)} %get-tuple-element.29.inner, f32[3,256,128]{2,1,0:T(8,128)S(1)} %get-tuple-element.32.outer, f32[16,256]{1,0:T(8,128)S(1)} %get-tuple-element.33.vt, ...), custom_call_target="tpu_custom_call" | custom-call | flops 1000000000 | bytes 2834944 | tf_op jit(solution)/shard_map/pallas_call | solution.py:484
  25.6 0.0 collective-permute-done.2.ylo
  25.6 0.0 collective-permute-done.3.yhi
  25.6 0.0 collective-permute-done.4.elo
  25.6 0.2 collective-permute-done.5.ehi
  25.9 0.0 copy-done.4
  25.9 0.8 %shard_map.215 = (f32[11,384,128]{2,1,0:T(8,128)S(1)}, f32[24,384]{1,0:T(8,128)S(1)}, f32[2,816,128]{2,1,0:T(8,128)S(1)}) custom-call(f32[8,256,128]{2,1,0:T(8,128)S(1)} %get-tuple-element.29.inner, f32[3,256,128]{2,1,0:T(8,128)S(1)} %get-tuple-element.32.outer, f32[24,256]{1,0:T(8,128)S(1)} %get-tuple-element.34.vx, f32[16,256]{1,0:T(8,128)S(1)} %get-tuple-element.33.vt, ...), custom_call_target="tpu_custom_call" | custom-call | bytes 2441216 | tf_op jit(solution)/shard_map/pallas_call | solution.py:484
  26.6 0.0 collective-permute-start.6
  26.7 0.0 copy-done.10
  26.7 0.0 copy-done.11
  26.7 0.0 copy-start.2
  26.7 0.0 copy-start.3
  26.7 0.0 copy-start.7
  26.7 0.0 copy-start.8
  26.7 0.0 copy-start.12
  26.7 0.0 copy-start.13
  26.8 0.0 copy-start.15
  26.8 2.1 %shard_map.216 = (f32[11,496,128]{2,1,0:T(8,128)S(1)}, f32[11,96,128]{2,1,0:T(8,128)S(1)}, f32[11,96,128]{2,1,0:T(8,128)S(1)}) custom-call(f32[11,384,128]{2,1,0:T(8,128)S(1)} %get-tuple-element.40.field.refs_1_, f32[24,384]{1,0:T(8,128)S(1)} %get-tuple-element.43.vfull, bf16[496,96]{1,0:T(8,128)(2,1)S(1)} %copy-done.11, ...), custom_call_target="tpu_custom_call", output_to_operand_aliasing={{0}: (6, {})} | custom-call | flops 1000000000 | bytes 5650944 | tf_op jit(solution)/shard_map/pallas_call | solution.py:484
  28.9 0.1 collective-permute-done.6.refs_0_
  29.0 0.0 copy-done.2
  29.0 0.0 copy-done.3
  29.0 0.0 copy-done.7
  29.0 0.0 copy-done.8
  29.0 0.0 copy-done.12
  29.0 0.0 copy-done.13
  29.1 0.0 copy-start.16
  29.1 0.0 copy-start.17
  29.1 0.0 copy-start.20
  29.1 9.3 %shard_map.217 = (f32[11,496,128]{2,1,0:T(8,128)S(1)}, f32[256,128]{1,0:T(8,128)S(1)}, f32[256,128]{1,0:T(8,128)S(1)}, f32[256,128]{1,0:T(8,128)S(1)}, f32[256,1...) custom-call(f32[2,816,128]{2,1,0:T(8,128)S(1)} %collective-permute-done.6.refs_0_, ...), custom_call_target="tpu_custom_call" | custom-call | bytes 11626496 | tf_op jit(solution)/shard_map/pallas_call | solution.py:484
  38.4 0.4 collective-permute-start.11
  38.8 1.4 %collective-permute-start.8 = (f32[256,128]{1,0:T(8,128)S(1)}, f32[256,128]{1,0:T(8,128)S(1)}, u32[]{:S(2)}, u32[]{:S(2)}) collective-permute-start(f32[256,128]{1,0:T(8,128)S(1)} %get-tuple-element.51.ox_0_), channel_id=1, source_target_pairs={{0,24},{8,0},{16,8},{24,16},{1,25},{9,1},{17,9},{25,17},{2,26},{10... | collective-permute-start | bytes 393224 | tf_op jit(solution)/shard_map/ppermute | solution.py:498
  40.2 0.6 %collective-permute-start.7 = (f32[256,128]{1,0:T(8,128)S(1)}, f32[256,128]{1,0:T(8,128)S(1)}, u32[]{:S(2)}, u32[]{:S(2)}) collective-permute-start(f32[256,128]{1,0:T(8,128)S(1)} %get-tuple-element.52.ox_1_), channel_id=1, source_target_pairs={{0,8},{8,16},{16,24},{24,0},{1,9},{9,17},{17,25},{25,1},{2,10},{10... | collective-permute-start | bytes 393224 | tf_op jit(solution)/shard_map/ppermute | solution.py:498
  40.8 3.2 %collective-permute-start.10 = (f32[256,128]{1,0:T(8,128)S(1)}, f32[256,128]{1,0:T(8,128)S(1)}, u32[]{:S(2)}, u32[]{:S(2)}) collective-permute-start(f32[256,128]{1,0:T(8,128)S(1)} %get-tuple-element.53.oy_0_), channel_id=1, source_target_pairs={{0,6},{2,0},{4,2},{6,4},{1,7},{3,1},{5,3},{7,5},{8,14},{10,8},{12,... | collective-permute-start | bytes 393224 | tf_op jit(solution)/shard_map/ppermute | solution.py:498
  44.0 0.0 collective-permute-start.9
  44.0 0.0 copy-done.20
  44.1 5.9 %shard_map.218 = (f32[64,64]{1,0:T(8,128)S(1)}, f32[16,256,64]{2,1,0:T(8,128)}) custom-call(f32[11,496,128]{2,1,0:T(8,128)S(1)} %get-tuple-element.48.f, f32[11,256,128]{2,1,0:T(8,128)S(1)} %get-tuple-element.41.refs_2_.va, f32[11,256,128]{2,1,0:T(8,128)S(1)} %get-tuple-element.42.refs_3_.vd, bf16[496,496]{1,0:T(8,128)(2,1)S(1)} %copy-done.17, ...), custom_call_target="tpu_custom_call" | custom-call | flops 2000000000 | bytes 6723072 | tf_op jit(solution)/shard_map/pallas_call | solution.py:484
  49.9 0.0 collective-permute-done.8.nx_1_
  49.9 0.0 collective-permute-done.7.nx_0_
  49.9 0.0 collective-permute-done.10.ny_1_
  49.9 0.9 %collective-permute-done.9.ny_0_ = f32[256,128]{1,0:T(8,128)S(1)} collective-permute-done((f32[256,128]{1,0:T(8,128)S(1)}, f32[256,128]{1,0:T(8,128)S(1)}, u32[]{:S(2)}, u32[]{:S(2)}) %collective-permute-start.9) | collective-permute-done | bytes 131104 | tf_op jit(solution)/shard_map/ppermute | solution.py:498
  50.8 0.0 collective-permute-done.11.nz
  50.8 1.5 %shard_map.219 = f32[7,64,64]{2,1,0:T(8,128)} custom-call(f32[64,64]{1,0:T(8,128)S(1)} %get-tuple-element.50.diag, f32[256,128]{1,0:T(8,128)S(1)} %get-tuple-element.51.ox_0_, f32[256,128]{1,0:T(8,128)S(1)} %get-tuple-element.52.ox_1_, f32[256,128]{1,0:T(8,128)S(1)} %get-tuple-element.53.oy_0_, f32[256,128]{1,0:T(8,128)S(1)} %get-tuple-element.54.oy_1_, ...), custom_call_target="tpu_custom_call" | custom-call | bytes 1589248 | tf_op jit(solution)/shard_map/pallas_call | solution.py:484
  (10 shorter events, 0.0 us)
Async XLA Ops:
  0.6 1.6 %copy-start = (f32[16,16,16,64]{3,2,1,0:T(8,128)S(1)}, f32[16,16,16,64]{3,2,1,0:T(8,128)}, u32[]{:S(2)}) copy-start(f32[16,16,16,64]{3,2,1,0:T(8,128)} %param.21) | copy-start | bytes 3145732
  2.2 0.9 %copy-start.6 = (f32[256,256]{1,0:T(8,128)S(1)}, f32[256,256]{1,0:T(8,128)}, u32[]{:S(2)}) copy-start(f32[256,256]{1,0:T(8,128)} %constant.39.clone.pick) | copy-start | bytes 786436
  3.2 0.9 %copy-start.9 = (f32[16,16,16]{2,1,0:T(8,128)S(1)}, f32[16,16,16]{2,1,0:T(8,128)}, u32[]{:S(2)}) copy-start(f32[16,16,16]{2,1,0:T(8,128)} %param.22) | copy-start | bytes 49156
  4.1 0.7 %copy-start.14 = (f32[16,256]{1,0:T(8,128)S(1)}, f32[16,256]{1,0:T(8,128)}, u32[]{:S(2)}) copy-start(f32[16,256]{1,0:T(8,128)} %constant.38.clone.spread) | copy-start | bytes 49156
  4.8 18.1 %copy-start.1 = (bf16[72,2816]{1,0:T(8,128)(2,1)S(1)}, bf16[72,2816]{1,0:T(8,128)(2,1)}, u32[]{:S(2)}) copy-start(bf16[72,2816]{1,0:T(8,128)(2,1)} %constant.43.clone.vspread.refs_13_) | copy-start | bytes 1216516
  4.8 18.1 %copy-start.5 = (f32[121,128]{1,0:T(8,128)S(1)}, f32[121,128]{1,0:T(8,128)}, u32[]{:S(2)}) copy-start(f32[121,128]{1,0:T(8,128)} %constant.42.clone.coef.refs_11_) | copy-start | bytes 185860
  4.8 18.1 %copy-start.18 = (bf16[496,256]{1,0:T(8,128)(2,1)S(1)}, bf16[496,256]{1,0:T(8,128)(2,1)}, u32[]{:S(2)}) copy-start(bf16[496,256]{1,0:T(8,128)(2,1)} %constant.41.clone.wl) | copy-start | bytes 761860
  4.8 18.1 %copy-start.19 = (bf16[496,256]{1,0:T(8,128)(2,1)S(1)}, bf16[496,256]{1,0:T(8,128)(2,1)}, u32[]{:S(2)}) copy-start(bf16[496,256]{1,0:T(8,128)(2,1)} %constant.40.clone.wh) | copy-start | bytes 761860
  5.3 20.6 %copy-start.4 = (f32[2,384,128]{2,1,0:T(8,128)S(1)}, f32[2,384,128]{2,1,0:T(8,128)}, u32[]{:S(2)}) copy-start(f32[2,384,128]{2,1,0:T(8,128)} %constant.44.clone.zpick) | copy-start | bytes 1179652
  5.3 9.8 %collective-permute-start = (f32[392,128]{1,0:T(8,128)S(1)}, f32[392,128]{1,0:T(8,128)S(1)}, u32[]{:S(2)}, u32[]{:S(2)}) collective-permute-start(f32[392,128]{1,0:T(8,128)S(1)} %get-tuple-element.30), channel_id=1, source_target_pairs={{0,8},{8,16},{16,24},{24,0},{1,9},{9,17},{17,25},{25,1},{2,10},{10... | collective-permute-start | bytes 602120 | tf_op jit(solution)/shard_map/ppermute | solution.py:498
  8.3 10.5 %collective-permute-start.1 = (f32[392,128]{1,0:T(8,128)S(1)}, f32[392,128]{1,0:T(8,128)S(1)}, u32[]{:S(2)}, u32[]{:S(2)}) collective-permute-start(f32[392,128]{1,0:T(8,128)S(1)} %get-tuple-element.31), channel_id=1, source_target_pairs={{0,24},{8,0},{16,8},{24,16},{1,25},{9,1},{17,9},{25,17},{2,26},{10... | collective-permute-start | bytes 602120 | tf_op jit(solution)/shard_map/ppermute | solution.py:498
  9.3 16.3 %collective-permute-start.2 = (f32[400,128]{1,0:T(8,128)S(1)}, f32[400,128]{1,0:T(8,128)S(1)}, u32[]{:S(2)}, u32[]{:S(2)}) collective-permute-start(f32[400,128]{1,0:T(8,128)S(1)} %get-tuple-element.35), channel_id=1, source_target_pairs={{0,2},{2,4},{4,6},{6,0},{1,3},{3,5},{5,7},{7,1},{8,10},{10,12},{12... | collective-permute-start | bytes 614408 | tf_op jit(solution)/shard_map/ppermute | solution.py:498
  11.3 14.3 %collective-permute-start.3 = (f32[400,128]{1,0:T(8,128)S(1)}, f32[400,128]{1,0:T(8,128)S(1)}, u32[]{:S(2)}, u32[]{:S(2)}) collective-permute-start(f32[400,128]{1,0:T(8,128)S(1)} %get-tuple-element.36), channel_id=1, source_target_pairs={{0,6},{2,0},{4,2},{6,4},{1,7},{3,1},{5,3},{7,5},{8,14},{10,8},{12,... | collective-permute-start | bytes 614408 | tf_op jit(solution)/shard_map/ppermute | solution.py:498
  19.0 6.6 %collective-permute-start.4 = (f32[152,128]{1,0:T(8,128)S(1)}, f32[152,128]{1,0:T(8,128)S(1)}, u32[]{:S(2)}, u32[]{:S(2)}) collective-permute-start(f32[152,128]{1,0:T(8,128)S(1)} %get-tuple-element.37), channel_id=1, source_target_pairs={{0,2},{2,4},{4,6},{6,0},{1,3},{3,5},{5,7},{7,1},{8,10},{10,12},{12... | collective-permute-start | bytes 233480 | tf_op jit(solution)/shard_map/ppermute | solution.py:498
  20.6 5.2 %collective-permute-start.5 = (f32[152,128]{1,0:T(8,128)S(1)}, f32[152,128]{1,0:T(8,128)S(1)}, u32[]{:S(2)}, u32[]{:S(2)}) collective-permute-start(f32[152,128]{1,0:T(8,128)S(1)} %get-tuple-element.38), channel_id=1, source_target_pairs={{0,6},{2,0},{4,2},{6,4},{1,7},{3,1},{5,3},{7,5},{8,14},{10,8},{12,... | collective-permute-start | bytes 233480 | tf_op jit(solution)/shard_map/ppermute | solution.py:498
  22.9 3.8 %copy-start.10 = (bf16[496,96]{1,0:T(8,128)(2,1)S(1)}, bf16[496,96]{1,0:T(8,128)(2,1)}, u32[]{:S(2)}) copy-start(bf16[496,96]{1,0:T(8,128)(2,1)} %constant.46.clone.wl) | copy-start | bytes 285700
  22.9 3.8 %copy-start.11 = (bf16[496,96]{1,0:T(8,128)(2,1)S(1)}, bf16[496,96]{1,0:T(8,128)(2,1)}, u32[]{:S(2)}) copy-start(bf16[496,96]{1,0:T(8,128)(2,1)} %constant.45.clone.wh) | copy-start | bytes 285700
  26.6 2.4 %collective-permute-start.6 = (f32[2,816,128]{2,1,0:T(8,128)S(1)}, f32[2,816,128]{2,1,0:T(8,128)S(1)}, u32[]{:S(2)}, u32[]{:S(2)}) collective-permute-start(f32[2,816,128]{2,1,0:T(8,128)S(1)} %get-tuple-element.39), channel_id=1, source_target_pairs={{0,1},{1,0},{2,3},{3,2},{4,5},{5,4},{6,7},{7,6},{8,9},{9,8},{10,11... | collective-permute-start | bytes 2506760 | tf_op jit(solution)/shard_map/ppermute | solution.py:498
  26.7 2.3 %copy-start.2 = (bf16[496,496]{1,0:T(8,128)(2,1)S(1)}, bf16[496,496]{1,0:T(8,128)(2,1)}, u32[]{:S(2)}) copy-start(bf16[496,496]{1,0:T(8,128)(2,1)} %constant.50.clone.refs_10_) | copy-start | bytes 1476100
  26.7 2.3 %copy-start.3 = (bf16[496,496]{1,0:T(8,128)(2,1)S(1)}, bf16[496,496]{1,0:T(8,128)(2,1)}, u32[]{:S(2)}) copy-start(bf16[496,496]{1,0:T(8,128)(2,1)} %constant.49.clone.refs_9_) | copy-start | bytes 1476100
  26.7 2.3 %copy-start.7 = (bf16[496,144]{1,0:T(8,128)(2,1)S(1)}, bf16[496,144]{1,0:T(8,128)(2,1)}, u32[]{:S(2)}) copy-start(bf16[496,144]{1,0:T(8,128)(2,1)} %constant.48.clone.refs_8_) | copy-start | bytes 428548
  26.7 2.3 %copy-start.8 = (bf16[496,144]{1,0:T(8,128)(2,1)S(1)}, bf16[496,144]{1,0:T(8,128)(2,1)}, u32[]{:S(2)}) copy-start(bf16[496,144]{1,0:T(8,128)(2,1)} %constant.47.clone.refs_7_) | copy-start | bytes 428548
  26.7 2.3 %copy-start.12 = (bf16[64,496]{1,0:T(8,128)(2,1)S(1)}, bf16[64,496]{1,0:T(8,128)(2,1)}, u32[]{:S(2)}) copy-start(bf16[64,496]{1,0:T(8,128)(2,1)} %constant.53.clone.refs_15_) | copy-start | bytes 190468
  26.7 2.3 %copy-start.13 = (bf16[64,496]{1,0:T(8,128)(2,1)S(1)}, bf16[64,496]{1,0:T(8,128)(2,1)}, u32[]{:S(2)}) copy-start(bf16[64,496]{1,0:T(8,128)(2,1)} %constant.52.clone.refs_14_) | copy-start | bytes 190468
  26.8 2.3 %copy-start.15 = (f32[11,128]{1,0:T(8,128)S(1)}, f32[11,128]{1,0:T(8,128)}, u32[]{:S(2)}) copy-start(f32[11,128]{1,0:T(8,128)} %constant.51.clone.refs_12_) | copy-start | bytes 16900
  29.1 15.0 %copy-start.16 = (bf16[496,496]{1,0:T(8,128)(2,1)S(1)}, bf16[496,496]{1,0:T(8,128)(2,1)}, u32[]{:S(2)}) copy-start(bf16[496,496]{1,0:T(8,128)(2,1)} %constant.55.clone.bl) | copy-start | bytes 1476100
  29.1 15.0 %copy-start.17 = (bf16[496,496]{1,0:T(8,128)(2,1)S(1)}, bf16[496,496]{1,0:T(8,128)(2,1)}, u32[]{:S(2)}) copy-start(bf16[496,496]{1,0:T(8,128)(2,1)} %constant.54.clone.bh) | copy-start | bytes 1476100
  29.1 15.0 %copy-start.20 = (f32[121,128]{1,0:T(8,128)S(1)}, f32[121,128]{1,0:T(8,128)}, u32[]{:S(2)}) copy-start(f32[121,128]{1,0:T(8,128)} %constant.56.clone.coef) | copy-start | bytes 185860
  38.4 12.4 %collective-permute-start.11 = (f32[2,256,128]{2,1,0:T(8,128)S(1)}, f32[2,256,128]{2,1,0:T(8,128)S(1)}, u32[]{:S(2)}, u32[]{:S(2)}) collective-permute-start(f32[2,256,128]{2,1,0:T(8,128)S(1)} %get-tuple-element.55.oz), channel_id=1, source_target_pairs={{0,1},{1,0},{2,3},{3,2},{4,5},{5,4},{6,7},{7,6},{8,9},{9,8},{10,11... | collective-permute-start | bytes 786440 | tf_op jit(solution)/shard_map/ppermute | solution.py:498
  38.8 11.1 %collective-permute-start.8 = (f32[256,128]{1,0:T(8,128)S(1)}, f32[256,128]{1,0:T(8,128)S(1)}, u32[]{:S(2)}, u32[]{:S(2)}) collective-permute-start(f32[256,128]{1,0:T(8,128)S(1)} %get-tuple-element.51.ox_0_), channel_id=1, source_target_pairs={{0,24},{8,0},{16,8},{24,16},{1,25},{9,1},{17,9},{25,17},{2,26},{10... | collective-permute-start | bytes 393224 | tf_op jit(solution)/shard_map/ppermute | solution.py:498
  40.2 9.7 %collective-permute-start.7 = (f32[256,128]{1,0:T(8,128)S(1)}, f32[256,128]{1,0:T(8,128)S(1)}, u32[]{:S(2)}, u32[]{:S(2)}) collective-permute-start(f32[256,128]{1,0:T(8,128)S(1)} %get-tuple-element.52.ox_1_), channel_id=1, source_target_pairs={{0,8},{8,16},{16,24},{24,0},{1,9},{9,17},{17,25},{25,1},{2,10},{10... | collective-permute-start | bytes 393224 | tf_op jit(solution)/shard_map/ppermute | solution.py:498
  40.8 9.1 %collective-permute-start.10 = (f32[256,128]{1,0:T(8,128)S(1)}, f32[256,128]{1,0:T(8,128)S(1)}, u32[]{:S(2)}, u32[]{:S(2)}) collective-permute-start(f32[256,128]{1,0:T(8,128)S(1)} %get-tuple-element.53.oy_0_), channel_id=1, source_target_pairs={{0,6},{2,0},{4,2},{6,4},{1,7},{3,1},{5,3},{7,5},{8,14},{10,8},{12,... | collective-permute-start | bytes 393224 | tf_op jit(solution)/shard_map/ppermute | solution.py:498
  44.0 6.8 %collective-permute-start.9 = (f32[256,128]{1,0:T(8,128)S(1)}, f32[256,128]{1,0:T(8,128)S(1)}, u32[]{:S(2)}, u32[]{:S(2)}) collective-permute-start(f32[256,128]{1,0:T(8,128)S(1)} %get-tuple-element.54.oy_1_), channel_id=1, source_target_pairs={{0,2},{2,4},{4,6},{6,0},{1,3},{3,5},{5,7},{7,1},{8,10},{10,12},{12... | collective-permute-start | bytes 393224 | tf_op jit(solution)/shard_map/ppermute | solution.py:498

commit v3 on v2

v3 whole, which is shorter than its diff:
```python
import functools

import jax
import jax.numpy as jnp
import ml_dtypes
import numpy as np
from jax import lax
from jax.experimental import pallas as pl
from jax.experimental.pallas import tpu as pltpu
from jax.sharding import PartitionSpec as P

BUF = 3
PENALTY = 2.0
LOW_BOUND = -1.5
CUTOFF = 8.0
HIGH_BOUND = 16.0
BF = jnp.bfloat16
F32 = jnp.float32


class Plan:
    def __init__(self, cells, width):
        self.cells, self.width = cells, width
        self.ext = cells + 2 * BUF
        self.groups = self.ext // 2
        self.inner = cells // 2
        self.lanes = 2 * width
        self.face = cells * cells
        self.strip = BUF * cells
        self.corner = -(-2 * BUF // 8) * 8
        self.yext = self.face + 2 * self.strip
        self.cross = self.yext + 2 * self.strip
        self.rows = self.cross + 2 * BUF * self.corner
        self.trows = -(-self.ext // 8) * 8
        inside = list(range(BUF, BUF + cells))
        outside = list(range(BUF)) + list(range(BUF + cells, self.ext))
        points = [(y, z) for y in inside for z in inside] + [(y, z) for y in outside for z in inside]
        points += [(y, z) for z in outside for y in inside]
        for z in outside:
            points += [(y, z) for y in outside] + [None] * (self.corner - 2 * BUF)
        self.points = points
        self.first, self.second = spectral(self.ext)
        self.inside = np.isin(np.arange(self.ext), inside)


def spectral(points):
    indices = np.arange(points)
    offsets = indices[:, None] - indices[None, :]
    first = np.zeros((points, points))
    second = np.zeros((points, points))
    for harmonic in range(1, points // 2):
        wavenum = 2.0 * np.pi * harmonic / points
        first = first - 2.0 * wavenum * np.sin(wavenum * offsets) / points
        second = second - 2.0 * wavenum * wavenum * np.cos(wavenum * offsets) / points
    second = second - np.pi * np.pi * np.cos(np.pi * offsets) / points
    return first, second


def row_matrix(plan, along, masked):
    real = np.array([p is not None for p in plan.points])
    y, z = np.array([(0, 0) if p is None else p for p in plan.points]).T
    by_y = along[y[:, None], y[None, :]] * (z[:, None] == z[None, :])
    by_z = along[z[:, None], z[None, :]] * (y[:, None] == y[None, :])
    if masked:
        by_y, by_z = by_y * plan.inside[z][:, None], by_z * plan.inside[y][:, None]
    return (by_y + by_z) * real[:, None] * real[None, :]


def mirrored(plan, along):
    g = plan.groups
    plus = along[:g, :g] + along[:g, ::-1][:, :g]
    minus = along[:g, :g] - along[:g, ::-1][:, :g]
    return np.concatenate([np.repeat(plus[:, :, None], plan.width, 2), np.repeat(minus[:, :, None], plan.width, 2)], 2)


def folded(table):
    g = table.shape[0]
    half, odd = g // 2, g % 2
    out = []
    for t in range(half + odd):
        out += [0.5 * (table[t, s] + table[t, g - 1 - s]) for s in range(half)] + [table[t, half]] * odd
        if t < half:
            out += [0.5 * (table[t, s] - table[t, g - 1 - s]) for s in range(half)]
    return np.stack(out).astype(np.float32)


def energy(plan):
    c = plan.cells
    block = plan.first[BUF : BUF + c]
    out = 0.5 * block.T @ block
    for sign, layer in ((-1.0, BUF), (1.0, BUF + c - 1)):
        unit = np.zeros(plan.ext)
        unit[layer] = 1.0
        cross = np.outer(unit, plan.first[layer])
        out = out + 0.5 * PENALTY * np.outer(unit, unit) - 0.25 * sign * (cross + cross.T)
    return out


def halves(matrix):
    high = matrix.astype(np.float32).astype(ml_dtypes.bfloat16)
    low = (matrix - high.astype(np.float64)).astype(np.float32).astype(ml_dtypes.bfloat16)
    return high, low


def split(x):
    high = x.astype(BF)
    return high, (x - high.astype(F32)).astype(BF)


def swap(x):
    return pltpu.roll(x, x.shape[-1] // 2, x.ndim - 1)


def dot(a, b):
    return jnp.dot(a, b, preferred_element_type=F32)


def dot_t(a, b):
    return lax.dot_general(a, b, (((0,), (0,)), ((), ())), preferred_element_type=F32)


def exact(a, b):
    return jnp.dot(a, b, preferred_element_type=F32, precision=lax.Precision.HIGHEST)


def three(wh, wl, sh, sl):
    return dot(wh, sh) + dot(wl, sh) + dot(wh, sl)


def low_lanes(shape):
    return lax.broadcasted_iota(jnp.int32, shape, len(shape) - 1) < shape[-1] // 2


def sides(ref, paired):
    return [ref.at[0], ref.at[1]] if paired else ref


def chunks(stop, size=16, start=0):
    return [(r, min(r + size, stop)) for r in range(start, stop, size)]


def pairs(stop, start=0):
    return [(g, min(g + 2, stop)) for g in range(start, stop, 2)]


CENTER = (HIGH_BOUND + CUTOFF) / 2.0
HALF_WIDTH = (HIGH_BOUND - CUTOFF) / 2.0
S0 = HALF_WIDTH / (LOW_BOUND - CENTER)
S1 = 1.0 / (2.0 / S0 - S0)


def mix(coef, table, items):
    total = None
    for s, item in enumerate(items):
        term = coef[table + s : table + s + 1, :] * item
        total = term if total is None else total + term
    return total


def fold_mix(coef, items):
    g = len(items)
    half, odd = g // 2, g % 2
    plus = [items[s] + items[g - 1 - s] for s in range(half)] + [items[half]] * odd
    minus = [items[s] - items[g - 1 - s] for s in range(half)]
    out, k = [None] * g, 0
    for t in range(half + odd):
        p = mix(coef, k, plus)
        k += len(plus)
        if t < half:
            q = mix(coef, k, minus)
            k += half
            out[t], out[g - 1 - t] = p + q, p - q
        else:
            out[t] = p
    return out


def spread_potential(plan, piece, count, vspread, va, vd, at):
    high = piece.astype(BF).astype(F32)
    rest = piece - high
    mid = rest.astype(BF).astype(F32)
    stacked = jnp.concatenate([high, mid, rest - mid], axis=0)
    turned = jnp.transpose(stacked)[:count, :].astype(BF)
    g_all, lanes = plan.groups, plan.lanes
    for g0, g1 in pairs(g_all):
        for k, dst, less in ((0, va, CENTER), (1, vd, 0.0)):
            cols = slice((k * g_all + g0) * lanes, (k * g_all + g1) * lanes)
            both = dot(turned, vspread[:, cols]) - less
            for g in range(g0, g1):
                dst[g, at : at + count, :] = both[:, (g - g0) * lanes : (g - g0 + 1) * lanes]


def local_terms(coef, get, count, va, vd, v0):
    items = [get(g) for g in range(va.shape[0])]
    out = fold_mix(coef, items)
    for g, own in enumerate(items):
        out[g] = out[g] + va[g, v0 : v0 + count, :] * own + vd[g, v0 : v0 + count, :] * swap(own)
    return out


def pack_kernel(plan, orb_far, pot_far, xlo, xhi, ylo, yhi, inner, vt, orb, pot, sem):
    c, lanes = plan.cells, plan.lanes
    half = plan.face // 2
    copies = [pltpu.make_async_copy(pot_far, pot, sem.at[c])]
    copies += [pltpu.make_async_copy(orb_far.at[x], orb.at[x], sem.at[x]) for x in range(c)]
    for copy in copies:
        copy.start()
    copies[0].wait()
    lane = lax.broadcasted_iota(jnp.int32, (c, plan.face), 1)
    spread = (lax.rem(lane, c) == lax.broadcasted_iota(jnp.int32, (c, plan.face), 0)).astype(F32)
    shape = (plan.face, plan.face)
    own = lax.div(lax.broadcasted_iota(jnp.int32, shape, 1), c) == lax.rem(lax.broadcasted_iota(jnp.int32, shape, 0), c)
    wide = jnp.where(own, exact(pot[...], spread), 0.0)
    v = wide.reshape(c, c, plan.face).sum(axis=1)
    vt[...] = v
    base = BUF * half
    xlo[base:, :] = jnp.zeros((8, lanes), F32)
    xhi[base:, :] = jnp.zeros((8, lanes), F32)
    for part in range(2):
        cols = slice(part * lanes, (part + 1) * lanes)
        xlo[base + part * BUF : base + (part + 1) * BUF, :] = v[:BUF, cols]
        xhi[base + part * BUF : base + (part + 1) * BUF, :] = v[c - BUF :, cols]
    ybase = plan.inner * plan.strip
    ylo[ybase:, :] = v[:, :lanes]
    yhi[ybase:, :] = v[:, plan.face - lanes :]
    for copy in copies[1:]:
        copy.wait()
    for s in range(BUF):
        for out, x in ((xlo, s), (xhi, c - BUF + s)):
            out[s * half : (s + 1) * half, :] = jnp.concatenate([orb[x, :half], orb[x, half:]], axis=1)
    for j in range(plan.inner):
        a, b = orb[j], orb[c - 1 - j]
        e = jnp.concatenate([a + b, a - b], axis=1)
        inner[j] = e
        ylo[j * plan.strip : (j + 1) * plan.strip, :] = e[: plan.strip]
        yhi[j * plan.strip : (j + 1) * plan.strip, :] = e[plan.face - plan.strip :]


def xhalo_kernel(plan, paired, inner, vt, lo, hi, zpick, outer, elo, ehi, vx, zi):
    half, c, face, strip = plan.face // 2, plan.cells, plan.face, plan.strip
    lanes = plan.lanes
    mask = low_lanes((half, lanes))
    for g in range(BUF):
        a = lo[g * half : (g + 1) * half, :]
        b = hi[(BUF - 1 - g) * half : (BUF - g) * half, :]
        s, d = a + b, a - b
        top = jnp.where(mask, s, swap(d))
        bottom = jnp.where(mask, swap(s), d)
        outer[g, :half] = top
        outer[g, half:] = bottom
        elo[g * strip : (g + 1) * strip, :] = top[:strip]
        ehi[g * strip : (g + 1) * strip, :] = bottom[half - strip :]
    base, ebase = BUF * half, BUF * strip
    vx[...] = jnp.zeros(vx.shape, F32)
    vx[BUF : BUF + c, :] = vt[...]
    elo[ebase:, :] = jnp.zeros((8, lanes), F32)
    ehi[ebase:, :] = jnp.zeros((8, lanes), F32)
    for k, src in enumerate((lo, hi)):
        elo[ebase + k * BUF : ebase + (k + 1) * BUF, :] = src[base : base + BUF, :]
        ehi[ebase + k * BUF : ebase + (k + 1) * BUF, :] = src[base + BUF : base + 2 * BUF, :]
        at = 0 if k == 0 else BUF + c
        vx[at : at + BUF, :lanes] = src[base : base + BUF, :]
        vx[at : at + BUF, lanes:] = src[base + BUF : base + 2 * BUF, :]
    for side, dst in enumerate(sides(zi, paired)):
        start = side * (c - BUF)
        for g in range(plan.groups):
            src = outer.at[g] if g < BUF else inner.at[g - BUF]
            for k in range(BUF):
                at = g * strip + k * c
                dst[at : at + c, :] = src[pl.ds(start + k, c, stride=c), :]
        dst[plan.groups * strip :, :] = exact(vx[...], zpick[side])


def inside_kernel(plan, inner, outer, vx, wh, wl, coef, vspread, acc, va, vd, order, xh, xl):
    g_all, lanes, face = plan.groups, plan.lanes, plan.face
    spread_potential(plan, vx[...], face, vspread, va, vd, 0)
    order[...] = jnp.zeros(order.shape, F32)

    def get(g, r0, r1):
        return outer[g, r0:r1, :] if g < BUF else inner[g - BUF, r0:r1, :]

    for g in range(g_all):
        h, l = split(get(g, 0, face))
        xh[:, g * lanes : (g + 1) * lanes] = h
        xl[:, g * lanes : (g + 1) * lanes] = l
    for g0, g1 in pairs(g_all):
        cols = slice(g0 * lanes, g1 * lanes)
        total = three(wh[...], wl[...], xh[:, cols], xl[:, cols])
        for g in range(g0, g1):
            acc[g] = total[:, (g - g0) * lanes : (g - g0 + 1) * lanes]
    for r0, r1 in chunks(face):
        local = local_terms(coef, lambda g: get(g, r0, r1), r1 - r0, va, vd, r0)
        for g in range(g_all):
            acc[g, r0:r1, :] = acc[g, r0:r1, :] + local[g]


def ypack_kernel(plan, paired, ylo, yhi, elo, ehi, zpick, order, yh, vy, zc):
    c, lanes, strip, corner = plan.cells, plan.lanes, plan.strip, plan.corner
    for g in range(plan.groups):
        lo, hi, at = (elo, ehi, g * strip) if g < BUF else (ylo, yhi, (g - BUF) * strip)
        yh[g, :strip] = lo[at : at + strip, :]
        yh[g, strip : 2 * strip] = hi[at : at + strip, :]
    yh[:, 2 * strip :] = jnp.zeros((plan.groups, yh.shape[1] - 2 * strip, lanes), F32)
    ebase, ybase = BUF * strip, plan.inner * strip
    shift_in = lanes - strip
    vy[...] = jnp.zeros(vy.shape, F32)
    for e, y, cut, at in ((elo, ylo, shift_in, 0), (ehi, yhi, 0, strip)):
        cols = slice(at, at + strip)
        vy[:BUF, cols] = e[ebase : ebase + BUF, :][:, cut : cut + strip]
        vy[BUF + c : plan.ext, cols] = e[ebase + BUF : ebase + 2 * BUF, :][:, cut : cut + strip]
        vy[BUF : BUF + c, cols] = y[ybase:, :][:, cut : cut + strip]
    for side, dst in enumerate(sides(zc, paired)):
        start = side * (c - BUF)
        for g in range(plan.groups):
            for k in range(BUF):
                at = (g * BUF + k) * corner
                dst[at : at + corner, :] = yh[g, pl.ds(start + k, corner, stride=c), :]
        dst[plan.groups * BUF * corner :, :] = exact(vy[...], zpick[side])


def halo_kernel(plan, paired, yh, vy, zi, coef, vspread, given, acc, xr, va, vd, xh, xl):
    g_all, lanes, strip, face = plan.groups, plan.lanes, plan.strip, plan.face
    zlo, zhi = sides(zi, paired)[::-1] if paired else zi
    spread_potential(plan, vy[...], 2 * strip, vspread, va, vd, 0)
    for k, piece in enumerate((zlo, zhi)):
        at = (2 + k) * strip
        spread_potential(plan, piece[g_all * strip :, :], strip, vspread, va, vd, at)
        for g in range(g_all):
            xr[g, at : at + strip, :] = piece[g * strip : (g + 1) * strip, :]
    for g in range(g_all):
        xr[g, : 2 * strip, :] = yh[g, : 2 * strip, :]
        h, l = split(xr[g])
        xh[:, g * lanes : (g + 1) * lanes] = h
        xl[:, g * lanes : (g + 1) * lanes] = l
    for r0, r1 in chunks(4 * strip):
        local = local_terms(coef, lambda g: xr[g, r0:r1, :], r1 - r0, va, vd, r0)
        for g in range(g_all):
            acc[g, face + r0 : face + r1, :] = given[g, face + r0 : face + r1, :] + local[g]


def filter_kernel(plan, paired, zc, inner, outer, xr, xrh, xrl, vai, vdi, vah, vdh, given, wrh, wrl, wh, wl, coef, dcoef,
                  vspread, out, mx, my, mz, xh, xl, xc, y, yh, yl, va, vd, acc):
    g_all, lanes, rows, face, cross, c = plan.groups, plan.lanes, plan.rows, plan.face, plan.cross, plan.cells
    strip = plan.strip
    span = BUF * plan.corner
    mz = sides(mz, paired)
    zlo, zhi = sides(zc, paired)[::-1] if paired else zc
    rest = 4 * strip
    xh[:rest, :] = xrh[...]
    xl[:rest, :] = xrl[...]
    for k, piece in enumerate((zlo, zhi)):
        spread_potential(plan, piece[g_all * span :, :], span, vspread, va, vd, k * span)
        for g in range(g_all):
            xc[g, k * span : (k + 1) * span, :] = piece[g * span : (g + 1) * span, :]
    for g in range(g_all):
        h, l = split(xc[g])
        xh[rest:, g * lanes : (g + 1) * lanes] = h
        xl[rest:, g * lanes : (g + 1) * lanes] = l

    def put(g, r0, r1, value):
        y[g, r0:r1, :] = value
        h, l = split(value)
        yh[r0:r1, g * lanes : (g + 1) * lanes] = h
        yl[r0:r1, g * lanes : (g + 1) * lanes] = l

    corners = {}
    for r0, r1 in chunks(2 * span):
        corners[r0] = local_terms(coef, lambda g: xc[g, r0:r1, :], r1 - r0, va, vd, r0)
        for g in range(g_all):
            y[g, cross + r0 : cross + r1, :] = corners[r0][g]
    for n, (g0, g1) in enumerate(pairs(g_all)):
        slot = n % 2
        cols = slice(g0 * lanes, g1 * lanes)
        acc[slot, :, : (g1 - g0) * lanes] = three(wrh[...], wrl[...], xh[:, cols], xl[:, cols])
        for g in range(g0, g1):
            mine = slice((g - g0) * lanes, (g - g0 + 1) * lanes)
            for r0, r1 in chunks(rows):
                value = given[g, r0:r1, :] + acc[slot, r0:r1, mine]
                if r0 >= cross:
                    value = value + y[g, r0:r1, :]
                put(g, r0, r1, value * (S0 / HALF_WIDTH))

    for r0, r1 in chunks(cross):
        v, d, at = (vai, vdi, r0) if r0 < face else (vah, vdh, r0 - face)
        local = local_terms(coef, lambda g: y[g, r0:r1, :], r1 - r0, v, d, at)
        for g in range(g_all):
            if g >= BUF or r0 < face:
                if r0 >= face:
                    x = xr[g, r0 - face : r1 - face, :]
                else:
                    x = outer[g, r0:r1, :] if g < BUF else inner[g - BUF, r0:r1, :]
                out[g, r0:r1, :] = local[g] * (2.0 * S1 / HALF_WIDTH) - (S0 * S1) * x
    for n, (g0, g1) in enumerate(pairs(g_all)):
        slot = n % 2
        top = face if g1 <= BUF else cross
        cols = slice(g0 * lanes, g1 * lanes)
        acc[slot, :top, : (g1 - g0) * lanes] = three(wh[:top], wl[:top], yh[:, cols], yl[:, cols])
        for g in range(g0, g1):
            mine = slice((g - g0) * lanes, (g - g0 + 1) * lanes)
            for r0, r1 in chunks(face if g < BUF else cross):
                out[g, r0:r1, :] = out[g, r0:r1, :] + acc[slot, r0:r1, mine] * (2.0 * S1 / HALF_WIDTH)

    for r0, r1 in chunks(face):
        mask = low_lanes((r1 - r0, lanes))
        e = out[BUF, r0:r1, :]
        d = mix(dcoef, 0, [out[g, r0:r1, :] for g in range(g_all)])
        te, td = swap(e), swap(d)
        mx[0][r0:r1, :] = 0.5 * jnp.where(mask, e + te, d + td)
        mx[1][r0:r1, :] = 0.5 * jnp.where(mask, e - te, d - td)
    part = plan.inner * c
    order = list(range(BUF, BUF + c)) + list(range(BUF)) + list(range(BUF + c, plan.ext))
    for j in range(plan.inner):
        g = BUF + j
        to = slice(j * c, (j + 1) * c)
        down = slice(part + j * c, part + (j + 1) * c)
        ylayers = [out[g, k * c : (k + 1) * c, :] for k in range(plan.ext)]
        zlayers = [out[g, pl.ds(k, c, stride=c), :] for k in range(c)]
        zlayers += [out[g, plan.yext + k * c : plan.yext + (k + 1) * c, :] for k in range(2 * BUF)]
        for layers, message in ((ylayers, my), (zlayers, mz)):
            for side, layer in enumerate((0, c - 1)):
                message[side][to, :] = layers[layer]
                total = None
                for k, t in enumerate(order):
                    weight = float(plan.first[BUF + layer, t])
                    if t != BUF + layer:
                        term = weight * layers[k]
                        total = term if total is None else total + term
                message[side][down, :] = total


def own_kernel(plan, f, va, vd, bh, bl, coef, diag, basis, local, f2, f2h, f2l, fhi, acc, sem):
    g_all, lanes, face, cross, c = plan.groups, plan.lanes, plan.face, plan.cross, plan.cells
    copies = []
    for j in range(plan.inner):
        for r0, r1 in chunks(face, 64):
            e = f[BUF + j, r0:r1, :]
            t = swap(e)
            local[j, r0:r1, :] = (0.5 * (e + t))[:, : plan.width]
            local[c - 1 - j, r0:r1, :] = (0.5 * (e - t))[:, : plan.width]
        for x in (j, c - 1 - j):
            copies.append(pltpu.make_async_copy(local.at[x], basis.at[x], sem.at[x]))
            copies[-1].start()
    for g in range(g_all):
        top = face if g < BUF else cross
        for r0, r1 in chunks(top):
            value = f[g, r0:r1, :]
            high = value.astype(BF)
            fhi[g, r0:r1, :] = high
            twice = 2.0 * value - high.astype(F32)
            f2[g, r0:r1, :] = twice
            if g >= BUF:
                h, l = split(twice)
                f2h[r0:r1, (g - BUF) * lanes : (g - BUF + 1) * lanes] = h
                f2l[r0:r1, (g - BUF) * lanes : (g - BUF + 1) * lanes] = l
    total = jnp.zeros((lanes, 2 * lanes), F32)

    def fold(total, g, top, value):
        h, l = split(value)
        return total + dot_t(fhi[g, :top, :], jnp.concatenate([h, l], axis=1))

    def mixed(g, r0, r1):
        return mix(coef, g * g_all, [f2[s, r0:r1, :] for s in range(g_all)])

    for g in range(BUF):
        total = fold(total, g, face, jnp.concatenate([mixed(g, r0, r1) for r0, r1 in chunks(face)], axis=0))
    for n, (j0, j1) in enumerate(pairs(plan.inner)):
        slot = n % 2
        cols = slice(j0 * lanes, j1 * lanes)
        acc[slot] = three(bh[...], bl[...], f2h[:, cols], f2l[:, cols])
        for j in range(j0, j1):
            g = BUF + j
            mine = slice((j - j0) * lanes, (j - j0 + 1) * lanes)
            parts = []
            for r0, r1 in chunks(face):
                own = f2[g, r0:r1, :]
                value = acc[slot, r0:r1, mine] + mixed(g, r0, r1)
                parts.append(value + (va[g, r0:r1, :] + CENTER) * own + vd[g, r0:r1, :] * swap(own))
            parts.append(acc[slot, face:, mine])
            total = fold(total, g, cross, jnp.concatenate(parts, axis=0))
    both = total[:, :lanes] + total[:, lanes:]
    w = plan.width
    block = both[:w, :w] + both[w:, w:]
    diag[...] = 0.25 * (block + jnp.transpose(block))
    for copy in copies:
        copy.wait()


def face_kernel(plan, paired, diag, ox, oy, oz, nx, ny, nz, blocks):
    w, lanes = plan.width, plan.lanes
    part = plan.inner * plan.cells
    oz, nz = sides(oz, paired), sides(nz, paired)[::-1] if paired else nz
    blocks[0] = diag[...]

    def product(a, b):
        ah, al = split(a)
        bh, bl = split(b)
        return dot_t(ah, bh) + dot_t(ah, bl) + dot_t(al, bh)

    for k in range(2):
        sign = -1.0 if k == 0 else 1.0
        m = product(ox[k][...], nx[k][...])
        blocks[1 + k] = 0.25 * sign * (m[w:, :w] - m[:w, w:]) - 0.5 * PENALTY * m[:w, :w]
        for at, own, other in ((3, oy, ny), (5, oz, nz)):
            a = jnp.concatenate([own[k][:part, :], own[k][part:, :]], axis=1)
            b = jnp.concatenate([other[k][:part, :], other[k][part:, :]], axis=1)
            m = product(a, b)
            uv = m[:w, :w] + m[w:lanes, w:lanes]
            udv = m[:w, lanes : lanes + w] + m[w:lanes, lanes + w :]
            duv = m[lanes : lanes + w, :w] + m[lanes + w :, w:lanes]
            blocks[at + k] = 0.5 * (0.25 * sign * (duv - udv) - 0.5 * PENALTY * uv)


def near(*shape):
    return pltpu.VMEM(shape, F32)


def far(*shape):
    return jax.ShapeDtypeStruct(shape, F32)


def call(kernel, outs, args, scratch=(), flops=0, limit=24, aliases=None, far_in=(), far_out=()):
    def place(a, where):
        return pltpu.with_memory_space_constraint(jnp.asarray(a), where)

    placed = [jax.tree.map(lambda b: place(b, pltpu.HBM if i in far_in else pltpu.VMEM), a) for i, a in enumerate(args)]
    space, apart = pl.BlockSpec(memory_space=pltpu.VMEM), pl.BlockSpec(memory_space=pl.ANY)
    return pl.pallas_call(
        kernel,
        out_shape=outs,
        in_specs=[apart if i in far_in else jax.tree.map(lambda b: space, a) for i, a in enumerate(placed)],
        out_specs=[apart if i in far_out else jax.tree.map(lambda b: space, a) for i, a in enumerate(outs)],
        scratch_shapes=list(scratch),
        input_output_aliases=aliases or {},
        compiler_params=pltpu.CompilerParams(vmem_limit_bytes=limit * 1024 * 1024),
        cost_estimate=pl.CostEstimate(flops=flops, bytes_accessed=0, transcendentals=0),
    )(*placed)


def shift(array, axis, step):
    count = lax.axis_size(axis)
    return lax.ppermute(array, axis, [(i, (i + step) % count) for i in range(count)])


def shift_z(both, paired):
    if paired:
        return shift(both, "gz", 1)
    return [shift(both[1], "gz", 1), shift(both[0], "gz", -1)]


def on_device(orbitals, potential):
    cells, width = orbitals.shape[0], orbitals.shape[-1]
    plan = Plan(cells, width)
    lanes, face, strip, rows, cross = plan.lanes, plan.face, plan.strip, plan.rows, plan.cross
    g_all, inner_all, corner = plan.groups, plan.inner, plan.corner
    paired = lax.axis_size("gz") == 2
    part = functools.partial
    bf = lambda *shape: pltpu.VMEM(shape, BF)
    wide = g_all * lanes

    def two(*shape):
        return near(2, *shape) if paired else [near(*shape), near(*shape)]

    xrows, yrows, erows = BUF * face // 2 + 8, inner_all * strip + cells, BUF * strip + 8
    xlo, xhi, ylo, yhi, inner, vt = call(
        part(pack_kernel, plan),
        [near(xrows, lanes), near(xrows, lanes), near(yrows, lanes), near(yrows, lanes), near(inner_all, face, lanes), near(cells, face)],
        [orbitals.reshape(cells, face, width), potential.reshape(face, cells)],
        [pltpu.VMEM((cells, face, width), F32), pltpu.VMEM((face, cells), F32), pltpu.SemaphoreType.DMA((cells + 1,))],
        far_in=(0, 1),
    )
    from_ylo, from_yhi = shift(yhi, "gy", 1), shift(ylo, "gy", -1)
    from_xlo, from_xhi = shift(xhi, "gx", 1), shift(xlo, "gx", -1)

    ipick = np.zeros((2, face, lanes), np.float32)
    cpick = np.zeros((2, lanes, lanes), np.float32)
    for side in range(2):
        for k in range(BUF):
            z = side * (cells - BUF) + k
            for y in range(cells):
                ipick[side, y * cells + z, k * cells + y] = 1.0
            for y in range(2 * BUF):
                cpick[side, y * cells + z, k * corner + y] = 1.0
    outer, elo, ehi, vx, zi = call(
        part(xhalo_kernel, plan, paired),
        [near(BUF, face, lanes), near(erows, lanes), near(erows, lanes), near(plan.trows, face), two(g_all * strip + plan.trows, lanes)],
        [inner, vt, from_xlo, from_xhi, ipick],
    )
    from_elo, from_ehi = shift(ehi, "gy", 1), shift(elo, "gy", -1)
    zi = shift_z(zi, paired)

    matrix = -0.5 * row_matrix(plan, plan.second, False)
    coef = folded(-0.5 * mirrored(plan, plan.second))
    vspread = np.zeros((plan.trows, 2, g_all, lanes), np.float32)
    for g in range(g_all):
        vspread[g, :, g, :] = 0.5
        vspread[plan.ext - 1 - g, 0, g, :] = 0.5
        vspread[plan.ext - 1 - g, 1, g, :] = -0.5
    vspread = np.tile(vspread.reshape(plan.trows, -1), (3, 1)).astype(ml_dtypes.bfloat16)
    acc, vai, vdi, order = call(
        part(inside_kernel, plan),
        [near(g_all, rows, lanes), near(g_all, face, lanes), near(g_all, face, lanes), near(8, lanes)],
        [inner, outer, vx, *halves(matrix[:, :face]), coef, vspread],
        [bf(face, wide), bf(face, wide)],
    )

    room = 2 * strip + (corner - 2 * BUF) * cells
    yh, vy, zc = call(
        part(ypack_kernel, plan, paired),
        [near(g_all, room, lanes), near(plan.trows, lanes), two(g_all * BUF * corner + plan.trows, lanes)],
        [from_ylo, from_yhi, from_elo, from_ehi, cpick, order],
        flops=10**10,
    )
    zc = shift_z(zc, paired)
    rest = 4 * strip
    acc, xr, vah, vdh, xrh, xrl = call(
        part(halo_kernel, plan, paired),
        [near(g_all, rows, lanes), near(g_all, rest, lanes), near(g_all, rest, lanes), near(g_all, rest, lanes), bf(rest, wide), bf(rest, wide)],
        [yh, vy, zi, coef, vspread, acc],
        aliases={5 if paired else 6: 0},
    )

    p = plan.first[BUF, :g_all] + plan.first[BUF, ::-1][:g_all]
    q = plan.first[BUF, :g_all] - plan.first[BUF, ::-1][:g_all]
    dcoef = np.concatenate([np.repeat(p[:, None], width, 1), np.repeat(q[:, None], width, 1)], 1).astype(np.float32)
    msg = near(face, lanes)
    corners = 2 * BUF * corner
    filtered, mx, my, mz = call(
        part(filter_kernel, plan, paired),
        [near(g_all, cross, lanes), [msg, msg], [msg, msg], two(face, lanes)],
        [zc, inner, outer, xr, xrh, xrl, vai, vdi, vah, vdh, acc, *halves(matrix[:, face:]), *halves(matrix[:cross]), coef, dcoef, vspread],
        [bf(rest + corners, wide), bf(rest + corners, wide), near(g_all, corners, lanes),
         near(g_all, rows, lanes), bf(rows, wide), bf(rows, wide),
         near(g_all, corners, lanes), near(g_all, corners, lanes), near(2, rows, 2 * lanes)],
    )
    ny = [shift(my[1], "gy", 1), shift(my[0], "gy", -1)]
    nx = [shift(mx[1], "gx", 1), shift(mx[0], "gx", -1)]
    nz = shift_z(mz, paired)

    along = energy(plan)
    bcoef = mirrored(plan, along).reshape(-1, lanes).astype(np.float32)
    diag, basis = call(
        part(own_kernel, plan), [near(width, width), far(cells, face, width)],
        [filtered, vai, vdi, *halves(row_matrix(plan, along, True)[:cross, :cross]), bcoef],
        [near(cells, face, width), near(g_all, cross, lanes), bf(cross, inner_all * lanes), bf(cross, inner_all * lanes), bf(g_all, cross, lanes),
         near(2, cross, 2 * lanes), pltpu.SemaphoreType.DMA((cells,))],
        flops=2 * 10**9,
        far_out=(1,),
    )
    (blocks,) = call(
        part(face_kernel, plan, paired), [far(7, width, width)], [diag, mx, my, mz, nx, ny, nz],
    )
    return basis.reshape(orbitals.shape), blocks[None, None, None]


def solution(mesh):
    return jax.shard_map(
        on_device,
        mesh=mesh,
        in_specs=(P("gx", "gy", "gz", None), P("gx", "gy", "gz")),
        out_specs=(P("gx", "gy", "gz", None), P("gx", "gy", "gz", None, None, None)),
        check_vma=False,
    )
```

time: 52.5 us -> 47.2 us (0.90)
  local copies, waits for them, and re-layouts: 4.26 us -> 0.09 us
  Pallas kernels: 22.8 us -> 21 us
  waiting for transfers between devices: 6.67 us -> 7.29 us
    unnamed x42 -> x28, local copies, waits for them, and re-layouts: 4.26 us -> 0.09 us
    pallas_call x8, Pallas kernels: 22.8 us -> 21 us  [call(): pl.pallas_call(kernel, out_shape=outs, in_specs=[apart if i in far_in els...]
    ppermute x12 -> x13, waiting for transfers between devices: 6.67 us -> 7.29 us  [shift(): lax.ppermute(array, axis, [(i, (i + step) % count) for i in range(count)])]
    ppermute x12 -> x13, starting transfers between devices: 17.6 us -> 17.7 us  [shift(): lax.ppermute(array, axis, [(i, (i + step) % count) for i in range(count)])]
  transfers between devices with their start and end apart: 12 -> 13, of which waited for: 5 -> 5; matrix products, arithmetic and copies ran while one was open for 0% -> 0% of each run, Pallas kernels for 21% -> 22%
where the time goes in v3:
time: 47.2 us; the launch traced here: 47 us
  Pallas kernels  21 us (44%)
  starting transfers between devices  17.7 us (38%)
  waiting for transfers between devices  7.29 us (15%)
  between operations  0.89 us (2%)
    pallas_call x8, Pallas kernels, call(): pl.pallas_call(kernel, out_shape=outs, in_specs=[apart if i in far_in els...  21 us
    ppermute x13, starting transfers between devices, shift(): lax.ppermute(array, axis, [(i, (i + step) % count) for i in range(count)])  17.7 us
    ppermute x13, waiting for transfers between devices, shift(): lax.ppermute(array, axis, [(i, (i + step) % count) for i in range(count)])  7.29 us
  transfers between devices with their start and end apart: 13, of which 5 were waited for; matrix products, arithmetic and copies ran while one was open for 0% of the time, Pallas kernels for 22%

profile of v3, /device:TPU:0, one launch (start us, length us, event | category | flops | bytes accessed | tf_op | source)
XLA Modules:
  0.0 47.0 jit_solution(8720758282315839717)
XLA Ops:
  0.6 0.0 copy-start.4
  0.6 0.0 copy-start
  0.7 0.0 copy-start.3
  0.7 0.0 copy-start.7
  0.7 0.0 copy-start.8
  0.7 2.3 %shard_map.167 = (f32[392,128]{1,0:T(8,128)S(1)}, f32[392,128]{1,0:T(8,128)S(1)}, f32[400,128]{1,0:T(8,128)S(1)}, f32[400,128]{1,0:T(8,128)S(1)}, f32[8,256,128]{2,1,0:T(8,128)S(1)}, /*index=5*/f32[16,256]{1,0:T(8,128)S(1)}) custom-call(f32[16,256,64]{2,1,0:T(8,128)} %bitcast.4, f32[256,16]{1,0:T(8,128)} %bitcast.6), custom_call_target="tpu_custom_call" | custom-call | tf_op jit(solution)/shard_map/pallas_call | solution.py:527
  3.0 0.0 copy-start.12
  3.0 3.0 %collective-permute-start.2 = (f32[392,128]{1,0:T(8,128)S(1)}, f32[392,128]{1,0:T(8,128)S(1)}, u32[]{:S(2)}, u32[]{:S(2)}) collective-permute-start(f32[392,128]{1,0:T(8,128)S(1)} %get-tuple-element.38), channel_id=1, source_target_pairs={{0,8},{8,16},{16,24},{24,0},{1,9},{9,17},{17,25},{25,1},{2,10},{10... | collective-permute-start | bytes 602120 | tf_op jit(solution)/shard_map/ppermute | solution.py:541
  6.0 1.0 %collective-permute-start.3 = (f32[392,128]{1,0:T(8,128)S(1)}, f32[392,128]{1,0:T(8,128)S(1)}, u32[]{:S(2)}, u32[]{:S(2)}) collective-permute-start(f32[392,128]{1,0:T(8,128)S(1)} %get-tuple-element.39), channel_id=1, source_target_pairs={{0,24},{8,0},{16,8},{24,16},{1,25},{9,1},{17,9},{25,17},{2,26},{10... | collective-permute-start | bytes 602120 | tf_op jit(solution)/shard_map/ppermute | solution.py:541
  7.0 2.0 %collective-permute-start = (f32[400,128]{1,0:T(8,128)S(1)}, f32[400,128]{1,0:T(8,128)S(1)}, u32[]{:S(2)}, u32[]{:S(2)}) collective-permute-start(f32[400,128]{1,0:T(8,128)S(1)} %get-tuple-element.34), channel_id=1, source_target_pairs={{0,2},{2,4},{4,6},{6,0},{1,3},{3,5},{5,7},{7,1},{8,10},{10,12},{12... | collective-permute-start | bytes 614408 | tf_op jit(solution)/shard_map/ppermute | solution.py:541
  9.0 2.0 %collective-permute-start.1 = (f32[400,128]{1,0:T(8,128)S(1)}, f32[400,128]{1,0:T(8,128)S(1)}, u32[]{:S(2)}, u32[]{:S(2)}) collective-permute-start(f32[400,128]{1,0:T(8,128)S(1)} %get-tuple-element.35), channel_id=1, source_target_pairs={{0,6},{2,0},{4,2},{6,4},{1,7},{3,1},{5,3},{7,5},{8,14},{10,8},{12,... | collective-permute-start | bytes 614408 | tf_op jit(solution)/shard_map/ppermute | solution.py:541
  11.0 1.7 %collective-permute-done.2.lo = f32[392,128]{1,0:T(8,128)S(1)} collective-permute-done((f32[392,128]{1,0:T(8,128)S(1)}, f32[392,128]{1,0:T(8,128)S(1)}, u32[]{:S(2)}, u32[]{:S(2)}) %collective-permute-start.2) | collective-permute-done | bytes 200736 | tf_op jit(solution)/shard_map/ppermute | solution.py:541
  12.8 3.7 %collective-permute-done.3.hi = f32[392,128]{1,0:T(8,128)S(1)} collective-permute-done((f32[392,128]{1,0:T(8,128)S(1)}, f32[392,128]{1,0:T(8,128)S(1)}, u32[]{:S(2)}, u32[]{:S(2)}) %collective-permute-start.3) | collective-permute-done | bytes 200736 | tf_op jit(solution)/shard_map/ppermute | solution.py:541
  16.5 0.0 copy-done.4
  16.5 0.4 shard_map.168
  16.9 1.6 %collective-permute-start.4 = (f32[152,128]{1,0:T(8,128)S(1)}, f32[152,128]{1,0:T(8,128)S(1)}, u32[]{:S(2)}, u32[]{:S(2)}) collective-permute-start(f32[152,128]{1,0:T(8,128)S(1)} %get-tuple-element.40), channel_id=1, source_target_pairs={{0,2},{2,4},{4,6},{6,0},{1,3},{3,5},{5,7},{7,1},{8,10},{10,12},{12... | collective-permute-start | bytes 233480 | tf_op jit(solution)/shard_map/ppermute | solution.py:541
  18.6 2.2 %collective-permute-start.5 = (f32[152,128]{1,0:T(8,128)S(1)}, f32[152,128]{1,0:T(8,128)S(1)}, u32[]{:S(2)}, u32[]{:S(2)}) collective-permute-start(f32[152,128]{1,0:T(8,128)S(1)} %get-tuple-element.41), channel_id=1, source_target_pairs={{0,6},{2,0},{4,2},{6,4},{1,7},{3,1},{5,3},{7,5},{8,14},{10,8},{12,... | collective-permute-start | bytes 233480 | tf_op jit(solution)/shard_map/ppermute | solution.py:541
  20.8 0.0 collective-permute-start.7
  20.8 0.0 copy-done
  20.8 0.0 copy-done.3
  20.8 0.0 copy-done.7
  20.8 0.0 copy-done.8
  20.8 2.5 %shard_map.169 = (f32[11,496,128]{2,1,0:T(8,128)S(1)}, f32[11,256,128]{2,1,0:T(8,128)S(1)}, f32[11,256,128]{2,1,0:T(8,128)S(1)}, f32[8,128]{1,0:T(8,128)S(1)}) custom-call(f32[8,256,128]{2,1,0:T(8,128)S(1)} %get-tuple-element.36.inner, f32[3,256,128]{2,1,0:T(8,128)S(1)} %get-tuple-element.42.outer, f32[24,256]{1,0:T(8,128)S(1)} %get-tuple-element.43.vx, ...), custom_call_target="tpu_custom_call" | custom-call | tf_op jit(solution)/shard_map/pallas_call | solution.py:527
  23.3 0.0 collective-permute-done.ylo
  23.3 0.0 collective-permute-done.1.yhi
  23.3 0.3 collective-permute-done.4.elo
  23.6 0.2 collective-permute-done.5.ehi
  23.8 0.0 copy-done.12
  23.8 0.4 shard_map.170
  24.2 0.1 collective-permute-start.6
  24.3 0.0 collective-permute-done.7.zi
  24.3 0.0 copy-start.1
  24.3 0.0 copy-start.2
  24.3 0.0 copy-start.5
  24.3 0.0 copy-start.6
  24.3 0.0 copy-start.9
  24.3 1.6 %shard_map.171 = (f32[11,496,128]{2,1,0:T(8,128)S(1)}, f32[11,192,128]{2,1,0:T(8,128)S(1)}, f32[11,192,128]{2,1,0:T(8,128)S(1)}, f32[11,192,128]{2,1,0:T(8,128)S...) custom-call(f32[11,128,128]{2,1,0:T(8,128)S(1)} %get-tuple-element.46.yh, ...), custom_call_target="tpu_custom_call", output_to_operand_aliasing={{0}: (5, {})} | custom-call | tf_op jit(solution)/shard_map/pallas_call | solution.py:527
  25.9 0.0 collective-permute-done.6.zc
  25.9 0.0 copy-done.1
  25.9 0.0 copy-done.2
  25.9 0.0 copy-done.5
  25.9 0.0 copy-done.6
  25.9 0.0 copy-done.9
  26.0 0.0 copy-start.10
  26.0 0.0 copy-start.11
  26.0 0.0 copy-start.13
  26.0 7.0 %shard_map.172 = (f32[11,448,128]{2,1,0:T(8,128)S(1)}, f32[256,128]{1,0:T(8,128)S(1)}, f32[256,128]{1,0:T(8,128)S(1)}, f32[256,128]{1,0:T(8,128)S(1)}, f32[256,1...) custom-call(f32[2,288,128]{2,1,0:T(8,128)S(1)} %collective-permute-done.6.zc, f32[8,256,128]{2,1,0:T(8,128)S(1)} %get-tuple-element.36.inner, ...), custom_call_target="tpu_custom_call" | custom-call | tf_op jit(solution)/shard_map/pallas_call | solution.py:527
  33.0 0.5 %collective-permute-start.12 = (f32[2,256,128]{2,1,0:T(8,128)S(1)}, f32[2,256,128]{2,1,0:T(8,128)S(1)}, u32[]{:S(2)}, u32[]{:S(2)}) collective-permute-start(f32[2,256,128]{2,1,0:T(8,128)S(1)} %get-tuple-element.65.oz), channel_id=1, source_target_pairs={{0,1},{1,0},{2,3},{3,2},{4,5},{5,4},{6,7},{7,6},{8,9},{9,8},{10,11... | collective-permute-start | bytes 786440 | tf_op jit(solution)/shard_map/ppermute | solution.py:541
  33.6 1.4 %collective-permute-start.9 = (f32[256,128]{1,0:T(8,128)S(1)}, f32[256,128]{1,0:T(8,128)S(1)}, u32[]{:S(2)}, u32[]{:S(2)}) collective-permute-start(f32[256,128]{1,0:T(8,128)S(1)} %get-tuple-element.61.ox_0_), channel_id=1, source_target_pairs={{0,24},{8,0},{16,8},{24,16},{1,25},{9,1},{17,9},{25,17},{2,26},{10... | collective-permute-start | bytes 393224 | tf_op jit(solution)/shard_map/ppermute | solution.py:541
  35.0 0.6 %collective-permute-start.8 = (f32[256,128]{1,0:T(8,128)S(1)}, f32[256,128]{1,0:T(8,128)S(1)}, u32[]{:S(2)}, u32[]{:S(2)}) collective-permute-start(f32[256,128]{1,0:T(8,128)S(1)} %get-tuple-element.62.ox_1_), channel_id=1, source_target_pairs={{0,8},{8,16},{16,24},{24,0},{1,9},{9,17},{17,25},{25,1},{2,10},{10... | collective-permute-start | bytes 393224 | tf_op jit(solution)/shard_map/ppermute | solution.py:541
  35.6 3.2 %collective-permute-start.11 = (f32[256,128]{1,0:T(8,128)S(1)}, f32[256,128]{1,0:T(8,128)S(1)}, u32[]{:S(2)}, u32[]{:S(2)}) collective-permute-start(f32[256,128]{1,0:T(8,128)S(1)} %get-tuple-element.63.oy_0_), channel_id=1, source_target_pairs={{0,6},{2,0},{4,2},{6,4},{1,7},{3,1},{5,3},{7,5},{8,14},{10,8},{12,... | collective-permute-start | bytes 393224 | tf_op jit(solution)/shard_map/ppermute | solution.py:541
  38.8 0.0 collective-permute-start.10
  38.8 0.0 copy-done.10
  38.8 0.0 copy-done.11
  38.8 0.0 copy-done.13
  38.8 5.4 %shard_map.173 = (f32[64,64]{1,0:T(8,128)S(1)}, f32[16,256,64]{2,1,0:T(8,128)}) custom-call(f32[11,448,128]{2,1,0:T(8,128)S(1)} %get-tuple-element.58.f, f32[11,256,128]{2,1,0:T(8,128)S(1)} %get-tuple-element.53.vai.va, f32[11,256,128]{2,1,0:T(8,128)S(1)} %get-tuple-element.54.vdi.vd, bf16[448,448]{1,0:T(8,128)(2,1)S(1)} %copy-done.11, ...), custom_call_target="tpu_custom_call" | custom-call | flops 2000000000 | tf_op jit(solution)/shard_map/pallas_call | solution.py:527
  44.2 0.0 collective-permute-done.9.nx_1_
  44.2 0.0 collective-permute-done.8.nx_0_
  44.2 0.0 collective-permute-done.11.ny_1_
  44.2 1.3 %collective-permute-done.10.ny_0_ = f32[256,128]{1,0:T(8,128)S(1)} collective-permute-done((f32[256,128]{1,0:T(8,128)S(1)}, f32[256,128]{1,0:T(8,128)S(1)}, u32[]{:S(2)}, u32[]{:S(2)}) %collective-permute-start.10) | collective-permute-done | bytes 131104 | tf_op jit(solution)/shard_map/ppermute | solution.py:541
  45.6 0.0 collective-permute-done.12.nz
  45.6 1.5 %shard_map.174 = f32[7,64,64]{2,1,0:T(8,128)} custom-call(f32[64,64]{1,0:T(8,128)S(1)} %get-tuple-element.60.diag, f32[256,128]{1,0:T(8,128)S(1)} %get-tuple-element.61.ox_0_, f32[256,128]{1,0:T(8,128)S(1)} %get-tuple-element.62.ox_1_, f32[256,128]{1,0:T(8,128)S(1)} %get-tuple-element.63.oy_0_, f32[256,128]{1,0:T(8,128)S(1)} %get-tuple-element.64.oy_1_, ...), custom_call_target="tpu_custom_call" | custom-call | tf_op jit(solution)/shard_map/pallas_call | solution.py:527
Async XLA Ops:
  0.6 15.9 %copy-start.4 = (f32[2,256,128]{2,1,0:T(8,128)S(1)}, f32[2,256,128]{2,1,0:T(8,128)}, u32[]{:S(2)}) copy-start(f32[2,256,128]{2,1,0:T(8,128)} %constant.28.clone.zpick) | copy-start | bytes 786436
  0.6 20.2 %copy-start = (bf16[72,2816]{1,0:T(8,128)(2,1)S(1)}, bf16[72,2816]{1,0:T(8,128)(2,1)}, u32[]{:S(2)}) copy-start(bf16[72,2816]{1,0:T(8,128)(2,1)} %constant.32.clone.vspread) | copy-start | bytes 1216516
  0.7 20.2 %copy-start.3 = (f32[61,128]{1,0:T(8,128)S(1)}, f32[61,128]{1,0:T(8,128)}, u32[]{:S(2)}) copy-start(f32[61,128]{1,0:T(8,128)} %constant.31.clone.coef) | copy-start | bytes 93700
  0.7 20.2 %copy-start.7 = (bf16[496,256]{1,0:T(8,128)(2,1)S(1)}, bf16[496,256]{1,0:T(8,128)(2,1)}, u32[]{:S(2)}) copy-start(bf16[496,256]{1,0:T(8,128)(2,1)} %constant.30.clone.wl) | copy-start | bytes 761860
  0.7 20.2 %copy-start.8 = (bf16[496,256]{1,0:T(8,128)(2,1)S(1)}, bf16[496,256]{1,0:T(8,128)(2,1)}, u32[]{:S(2)}) copy-start(bf16[496,256]{1,0:T(8,128)(2,1)} %constant.29.clone.wh) | copy-start | bytes 761860
  3.0 20.8 %copy-start.12 = (f32[2,128,128]{2,1,0:T(8,128)S(1)}, f32[2,128,128]{2,1,0:T(8,128)}, u32[]{:S(2)}) copy-start(f32[2,128,128]{2,1,0:T(8,128)} %constant.33.clone.zpick) | copy-start | bytes 393220
  3.0 9.8 %collective-permute-start.2 = (f32[392,128]{1,0:T(8,128)S(1)}, f32[392,128]{1,0:T(8,128)S(1)}, u32[]{:S(2)}, u32[]{:S(2)}) collective-permute-start(f32[392,128]{1,0:T(8,128)S(1)} %get-tuple-element.38), channel_id=1, source_target_pairs={{0,8},{8,16},{16,24},{24,0},{1,9},{9,17},{17,25},{25,1},{2,10},{10... | collective-permute-start | bytes 602120 | tf_op jit(solution)/shard_map/ppermute | solution.py:541
  6.0 10.5 %collective-permute-start.3 = (f32[392,128]{1,0:T(8,128)S(1)}, f32[392,128]{1,0:T(8,128)S(1)}, u32[]{:S(2)}, u32[]{:S(2)}) collective-permute-start(f32[392,128]{1,0:T(8,128)S(1)} %get-tuple-element.39), channel_id=1, source_target_pairs={{0,24},{8,0},{16,8},{24,16},{1,25},{9,1},{17,9},{25,17},{2,26},{10... | collective-permute-start | bytes 602120 | tf_op jit(solution)/shard_map/ppermute | solution.py:541
  7.0 16.3 %collective-permute-start = (f32[400,128]{1,0:T(8,128)S(1)}, f32[400,128]{1,0:T(8,128)S(1)}, u32[]{:S(2)}, u32[]{:S(2)}) collective-permute-start(f32[400,128]{1,0:T(8,128)S(1)} %get-tuple-element.34), channel_id=1, source_target_pairs={{0,2},{2,4},{4,6},{6,0},{1,3},{3,5},{5,7},{7,1},{8,10},{10,12},{12... | collective-permute-start | bytes 614408 | tf_op jit(solution)/shard_map/ppermute | solution.py:541
  9.0 14.3 %collective-permute-start.1 = (f32[400,128]{1,0:T(8,128)S(1)}, f32[400,128]{1,0:T(8,128)S(1)}, u32[]{:S(2)}, u32[]{:S(2)}) collective-permute-start(f32[400,128]{1,0:T(8,128)S(1)} %get-tuple-element.35), channel_id=1, source_target_pairs={{0,6},{2,0},{4,2},{6,4},{1,7},{3,1},{5,3},{7,5},{8,14},{10,8},{12,... | collective-permute-start | bytes 614408 | tf_op jit(solution)/shard_map/ppermute | solution.py:541
  16.9 6.6 %collective-permute-start.4 = (f32[152,128]{1,0:T(8,128)S(1)}, f32[152,128]{1,0:T(8,128)S(1)}, u32[]{:S(2)}, u32[]{:S(2)}) collective-permute-start(f32[152,128]{1,0:T(8,128)S(1)} %get-tuple-element.40), channel_id=1, source_target_pairs={{0,2},{2,4},{4,6},{6,0},{1,3},{3,5},{5,7},{7,1},{8,10},{10,12},{12... | collective-permute-start | bytes 233480 | tf_op jit(solution)/shard_map/ppermute | solution.py:541
  18.6 5.2 %collective-permute-start.5 = (f32[152,128]{1,0:T(8,128)S(1)}, f32[152,128]{1,0:T(8,128)S(1)}, u32[]{:S(2)}, u32[]{:S(2)}) collective-permute-start(f32[152,128]{1,0:T(8,128)S(1)} %get-tuple-element.41), channel_id=1, source_target_pairs={{0,6},{2,0},{4,2},{6,4},{1,7},{3,1},{5,3},{7,5},{8,14},{10,8},{12,... | collective-permute-start | bytes 233480 | tf_op jit(solution)/shard_map/ppermute | solution.py:541
  20.8 3.5 %collective-permute-start.7 = (f32[2,552,128]{2,1,0:T(8,128)S(1)}, f32[2,552,128]{2,1,0:T(8,128)S(1)}, u32[]{:S(2)}, u32[]{:S(2)}) collective-permute-start(f32[2,552,128]{2,1,0:T(8,128)S(1)} %get-tuple-element.48), channel_id=1, source_target_pairs={{0,1},{1,0},{2,3},{3,2},{4,5},{5,4},{6,7},{7,6},{8,9},{9,8},{10,11... | collective-permute-start | bytes 1695752 | tf_op jit(solution)/shard_map/ppermute | solution.py:541
  24.2 1.7 %collective-permute-start.6 = (f32[2,288,128]{2,1,0:T(8,128)S(1)}, f32[2,288,128]{2,1,0:T(8,128)S(1)}, u32[]{:S(2)}, u32[]{:S(2)}) collective-permute-start(f32[2,288,128]{2,1,0:T(8,128)S(1)} %get-tuple-element.45), channel_id=1, source_target_pairs={{0,1},{1,0},{2,3},{3,2},{4,5},{5,4},{6,7},{7,6},{8,9},{9,8},{10,11... | collective-permute-start | bytes 884744 | tf_op jit(solution)/shard_map/ppermute | solution.py:541
  24.3 1.6 %copy-start.1 = (bf16[448,496]{1,0:T(8,128)(2,1)S(1)}, bf16[448,496]{1,0:T(8,128)(2,1)}, u32[]{:S(2)}) copy-start(bf16[448,496]{1,0:T(8,128)(2,1)} %constant.37.clone.wl) | copy-start | bytes 1333252
  24.3 1.6 %copy-start.2 = (bf16[448,496]{1,0:T(8,128)(2,1)S(1)}, bf16[448,496]{1,0:T(8,128)(2,1)}, u32[]{:S(2)}) copy-start(bf16[448,496]{1,0:T(8,128)(2,1)} %constant.36.clone.wh) | copy-start | bytes 1333252
  24.3 1.7 %copy-start.5 = (bf16[496,240]{1,0:T(8,128)(2,1)S(1)}, bf16[496,240]{1,0:T(8,128)(2,1)}, u32[]{:S(2)}) copy-start(bf16[496,240]{1,0:T(8,128)(2,1)} %constant.35.clone.wrl) | copy-start | bytes 714244
  24.3 1.7 %copy-start.6 = (bf16[496,240]{1,0:T(8,128)(2,1)S(1)}, bf16[496,240]{1,0:T(8,128)(2,1)}, u32[]{:S(2)}) copy-start(bf16[496,240]{1,0:T(8,128)(2,1)} %constant.34.clone.wrh) | copy-start | bytes 714244
  24.3 1.7 %copy-start.9 = (f32[11,128]{1,0:T(8,128)S(1)}, f32[11,128]{1,0:T(8,128)}, u32[]{:S(2)}) copy-start(f32[11,128]{1,0:T(8,128)} %constant.38.clone.dcoef) | copy-start | bytes 16900
  26.0 12.8 %copy-start.10 = (bf16[448,448]{1,0:T(8,128)(2,1)S(1)}, bf16[448,448]{1,0:T(8,128)(2,1)}, u32[]{:S(2)}) copy-start(bf16[448,448]{1,0:T(8,128)(2,1)} %constant.40.clone.bl) | copy-start | bytes 1204228
  26.0 12.8 %copy-start.11 = (bf16[448,448]{1,0:T(8,128)(2,1)S(1)}, bf16[448,448]{1,0:T(8,128)(2,1)}, u32[]{:S(2)}) copy-start(bf16[448,448]{1,0:T(8,128)(2,1)} %constant.39.clone.bh) | copy-start | bytes 1204228
  26.0 12.8 %copy-start.13 = (f32[121,128]{1,0:T(8,128)S(1)}, f32[121,128]{1,0:T(8,128)}, u32[]{:S(2)}) copy-start(f32[121,128]{1,0:T(8,128)} %constant.41.clone.coef) | copy-start | bytes 185860
  33.0 12.5 %collective-permute-start.12 = (f32[2,256,128]{2,1,0:T(8,128)S(1)}, f32[2,256,128]{2,1,0:T(8,128)S(1)}, u32[]{:S(2)}, u32[]{:S(2)}) collective-permute-start(f32[2,256,128]{2,1,0:T(8,128)S(1)} %get-tuple-element.65.oz), channel_id=1, source_target_pairs={{0,1},{1,0},{2,3},{3,2},{4,5},{5,4},{6,7},{7,6},{8,9},{9,8},{10,11... | collective-permute-start | bytes 786440 | tf_op jit(solution)/shard_map/ppermute | solution.py:541
  33.6 10.6 %collective-permute-start.9 = (f32[256,128]{1,0:T(8,128)S(1)}, f32[256,128]{1,0:T(8,128)S(1)}, u32[]{:S(2)}, u32[]{:S(2)}) collective-permute-start(f32[256,128]{1,0:T(8,128)S(1)} %get-tuple-element.61.ox_0_), channel_id=1, source_target_pairs={{0,24},{8,0},{16,8},{24,16},{1,25},{9,1},{17,9},{25,17},{2,26},{10... | collective-permute-start | bytes 393224 | tf_op jit(solution)/shard_map/ppermute | solution.py:541
  35.0 9.2 %collective-permute-start.8 = (f32[256,128]{1,0:T(8,128)S(1)}, f32[256,128]{1,0:T(8,128)S(1)}, u32[]{:S(2)}, u32[]{:S(2)}) collective-permute-start(f32[256,128]{1,0:T(8,128)S(1)} %get-tuple-element.62.ox_1_), channel_id=1, source_target_pairs={{0,8},{8,16},{16,24},{24,0},{1,9},{9,17},{17,25},{25,1},{2,10},{10... | collective-permute-start | bytes 393224 | tf_op jit(solution)/shard_map/ppermute | solution.py:541
  35.6 8.6 %collective-permute-start.11 = (f32[256,128]{1,0:T(8,128)S(1)}, f32[256,128]{1,0:T(8,128)S(1)}, u32[]{:S(2)}, u32[]{:S(2)}) collective-permute-start(f32[256,128]{1,0:T(8,128)S(1)} %get-tuple-element.63.oy_0_), channel_id=1, source_target_pairs={{0,6},{2,0},{4,2},{6,4},{1,7},{3,1},{5,3},{7,5},{8,14},{10,8},{12,... | collective-permute-start | bytes 393224 | tf_op jit(solution)/shard_map/ppermute | solution.py:541
  38.8 6.8 %collective-permute-start.10 = (f32[256,128]{1,0:T(8,128)S(1)}, f32[256,128]{1,0:T(8,128)S(1)}, u32[]{:S(2)}, u32[]{:S(2)}) collective-permute-start(f32[256,128]{1,0:T(8,128)S(1)} %get-tuple-element.64.oy_1_), channel_id=1, source_target_pairs={{0,2},{2,4},{4,6},{6,0},{1,3},{3,5},{5,7},{7,1},{8,10},{10,12},{12... | collective-permute-start | bytes 393224 | tf_op jit(solution)/shard_map/ppermute | solution.py:541

commit v4 on v3

--- a/solution.py
+++ b/solution.py
@@ -198,69 +198,79 @@
     return out
 
 
-def pack_kernel(plan, orb_far, pot_far, xlo, xhi, ylo, yhi, inner, vt, orb, pot, sem):
-    c, lanes = plan.cells, plan.lanes
-    half = plan.face // 2
-    copies = [pltpu.make_async_copy(pot_far, pot, sem.at[c])]
-    copies += [pltpu.make_async_copy(orb_far.at[x], orb.at[x], sem.at[x]) for x in range(c)]
+def packx_kernel(plan, orb_far, pot_far, slo, shi, rlo, rhi, vt, orb, pot, sem):
+    c, lanes, face, strip = plan.cells, plan.lanes, plan.face, plan.strip
+    half, rest = face // 2, face // 2 - plan.strip
+    slabs = list(range(BUF)) + list(range(c - BUF, c))
+    copies = [pltpu.make_async_copy(pot_far, pot, sem.at[2 * BUF])]
+    copies += [pltpu.make_async_copy(orb_far.at[x], orb.at[k], sem.at[k]) for k, x in enumerate(slabs)]
     for copy in copies:
         copy.start()
     copies[0].wait()
-    lane = lax.broadcasted_iota(jnp.int32, (c, plan.face), 1)
-    spread = (lax.rem(lane, c) == lax.broadcasted_iota(jnp.int32, (c, plan.face), 0)).astype(F32)
-    shape = (plan.face, plan.face)
-    own = lax.div(lax.broadcasted_iota(jnp.int32, shape, 1), c) == lax.rem(lax.broadcasted_iota(jnp.int32, shape, 0), c)
-    wide = jnp.where(own, exact(pot[...], spread), 0.0)
-    v = wide.reshape(c, c, plan.face).sum(axis=1)
+    v = jnp.concatenate([pot[pl.ds(y, c, stride=c), :] for y in range(c)], axis=1)
     vt[...] = v
-    base = BUF * half
-    xlo[base:, :] = jnp.zeros((8, lanes), F32)
-    xhi[base:, :] = jnp.zeros((8, lanes), F32)
-    for part in range(2):
-        cols = slice(part * lanes, (part + 1) * lanes)
-        xlo[base + part * BUF : base + (part + 1) * BUF, :] = v[:BUF, cols]
-        xhi[base + part * BUF : base + (part + 1) * BUF, :] = v[c - BUF :, cols]
-    ybase = plan.inner * plan.strip
-    ylo[ybase:, :] = v[:, :lanes]
-    yhi[ybase:, :] = v[:, plan.face - lanes :]
-    for copy in copies[1:]:
-        copy.wait()
-    for s in range(BUF):
-        for out, x in ((xlo, s), (xhi, c - BUF + s)):
-            out[s * half : (s + 1) * half, :] = jnp.concatenate([orb[x, :half], orb[x, half:]], axis=1)
+    base = BUF * strip
+    for out, first in ((slo, 0), (shi, c - BUF)):
+        out[base:, :] = jnp.zeros((8, lanes), F32)
+        for part in range(2):
+            out[base + part * BUF : base + (part + 1) * BUF, :] = v[first : first + BUF, part * lanes : (part + 1) * lanes]
+    for k in range(2 * BUF):
+        copies[1 + k].wait()
+        at = k % BUF
+        near_out, rest_out = (slo, rlo) if k < BUF else (shi, rhi)
+        near_out[at * strip : (at + 1) * strip, :] = jnp.concatenate([orb[k, :strip], orb[k, face - strip :]], axis=1)
+        rest_out[at * rest : (at + 1) * rest, :] = jnp.concatenate([orb[k, strip:half], orb[k, half : face - strip]], axis=1)
+
+
+def packy_kernel(plan, orb, vt, ylo, yhi, inner):
+    c, strip, face = plan.cells, plan.strip, plan.face
+    ybase = plan.inner * strip
+    ylo[ybase:, :] = vt[:, : plan.lanes]
+    yhi[ybase:, :] = vt[:, face - plan.lanes :]
     for j in range(plan.inner):
         a, b = orb[j], orb[c - 1 - j]
         e = jnp.concatenate([a + b, a - b], axis=1)
         inner[j] = e
-        ylo[j * plan.strip : (j + 1) * plan.strip, :] = e[: plan.strip]
-        yhi[j * plan.strip : (j + 1) * plan.strip, :] = e[plan.face - plan.strip :]
-
-
-def xhalo_kernel(plan, paired, inner, vt, lo, hi, zpick, outer, elo, ehi, vx, zi):
-    half, c, face, strip = plan.face // 2, plan.cells, plan.face, plan.strip
-    lanes = plan.lanes
-    mask = low_lanes((half, lanes))
+        ylo[j * strip : (j + 1) * strip, :] = e[:strip]
+        yhi[j * strip : (j + 1) * strip, :] = e[face - strip :]
+
+
+def mirror(a, b):
+    mask = low_lanes(a.shape)
+    s, d = a + b, a - b
+    return jnp.where(mask, s, swap(d)), jnp.where(mask, swap(s), d)
+
+
+def edge_kernel(plan, vt, lo, hi, ahead, elo, ehi, vx):
+    c, strip, lanes = plan.cells, plan.strip, plan.lanes
     for g in range(BUF):
-        a = lo[g * half : (g + 1) * half, :]
-        b = hi[(BUF - 1 - g) * half : (BUF - g) * half, :]
-        s, d = a + b, a - b
-        top = jnp.where(mask, s, swap(d))
-        bottom = jnp.where(mask, swap(s), d)
-        outer[g, :half] = top
-        outer[g, half:] = bottom
-        elo[g * strip : (g + 1) * strip, :] = top[:strip]
-        ehi[g * strip : (g + 1) * strip, :] = bottom[half - strip :]
-    base, ebase = BUF * half, BUF * strip
+        back = BUF - 1 - g
+        top, bottom = mirror(lo[g * strip : (g + 1) * strip, :], hi[back * strip : (back + 1) * strip, :])
+        elo[g * strip : (g + 1) * strip, :] = top
+        ehi[g * strip : (g + 1) * strip, :] = bottom
+    base = BUF * strip
     vx[...] = jnp.zeros(vx.shape, F32)
     vx[BUF : BUF + c, :] = vt[...]
-    elo[ebase:, :] = jnp.zeros((8, lanes), F32)
-    ehi[ebase:, :] = jnp.zeros((8, lanes), F32)
+    elo[base:, :] = jnp.zeros((8, lanes), F32)
+    ehi[base:, :] = jnp.zeros((8, lanes), F32)
     for k, src in enumerate((lo, hi)):
-        elo[ebase + k * BUF : ebase + (k + 1) * BUF, :] = src[base : base + BUF, :]
-        ehi[ebase + k * BUF : ebase + (k + 1) * BUF, :] = src[base + BUF : base + 2 * BUF, :]
+        elo[base + k * BUF : base + (k + 1) * BUF, :] = src[base : base + BUF, :]
+        ehi[base + k * BUF : base + (k + 1) * BUF, :] = src[base + BUF : base + 2 * BUF, :]
         at = 0 if k == 0 else BUF + c
         vx[at : at + BUF, :lanes] = src[base : base + BUF, :]
         vx[at : at + BUF, lanes:] = src[base + BUF : base + 2 * BUF, :]
+
+
+def xhalo_kernel(plan, paired, inner, vx, elo, ehi, lo, hi, zpick, ahead, outer, zi):
+    c, face, strip = plan.cells, plan.face, plan.strip
+    half, rest = face // 2, face // 2 - strip
+    for g in range(BUF):
+        back = BUF - 1 - g
+        top, bottom = mirror(lo[g * rest : (g + 1) * rest, :], hi[back * rest : (back + 1) * rest, :])
+        outer[g, :strip] = elo[g * strip : (g + 1) * strip, :]
+        outer[g, strip:half] = top
+        outer[g, half : face - strip] = bottom
+        outer[g, face - strip :] = ehi[g * strip : (g + 1) * strip, :]
     for side, dst in enumerate(sides(zi, paired)):
         start = side * (c - BUF)
         for g in range(plan.groups):
@@ -271,27 +281,37 @@
         dst[plan.groups * strip :, :] = exact(vx[...], zpick[side])
 
 
-def inside_kernel(plan, inner, outer, vx, wh, wl, coef, vspread, acc, va, vd, order, xh, xl):
-    g_all, lanes, face = plan.groups, plan.lanes, plan.face
-    spread_potential(plan, vx[...], face, vspread, va, vd, 0)
-    order[...] = jnp.zeros(order.shape, F32)
-
-    def get(g, r0, r1):
-        return outer[g, r0:r1, :] if g < BUF else inner[g - BUF, r0:r1, :]
-
-    for g in range(g_all):
-        h, l = split(get(g, 0, face))
-        xh[:, g * lanes : (g + 1) * lanes] = h
-        xl[:, g * lanes : (g + 1) * lanes] = l
-    for g0, g1 in pairs(g_all):
-        cols = slice(g0 * lanes, g1 * lanes)
+def row_products(plan, get, first, stop, wh, wl, xh, xl, acc):
+    lanes = plan.lanes
+    for g in range(first, stop):
+        h, l = split(get(g))
+        xh[:, (g - first) * lanes : (g - first + 1) * lanes] = h
+        xl[:, (g - first) * lanes : (g - first + 1) * lanes] = l
+    for g0, g1 in pairs(stop, first):
+        cols = slice((g0 - first) * lanes, (g1 - first) * lanes)
         total = three(wh[...], wl[...], xh[:, cols], xl[:, cols])
         for g in range(g0, g1):
             acc[g] = total[:, (g - g0) * lanes : (g - g0 + 1) * lanes]
-    for r0, r1 in chunks(face):
+
+
+def inside_kernel(plan, inner, vx, wh, wl, vspread, acc, va, vd, order, xh, xl):
+    order[...] = jnp.zeros(order.shape, F32)
+    spread_potential(plan, vx[...], plan.face, vspread, va, vd, 0)
+    row_products(plan, lambda g: inner[g - BUF], BUF, plan.groups, wh, wl, xh, xl, acc)
+
+
+def outside_kernel(plan, inner, outer, wh, wl, coef, va, vd, given, acc, order, xh, xl):
+    order[...] = jnp.zeros(order.shape, F32)
+    row_products(plan, lambda g: outer[g], 0, BUF, wh, wl, xh, xl, acc)
+
+    def get(g, r0, r1):
+        return outer[g, r0:r1, :] if g < BUF else inner[g - BUF, r0:r1, :]
+
+    for r0, r1 in chunks(plan.face):
         local = local_terms(coef, lambda g: get(g, r0, r1), r1 - r0, va, vd, r0)
-        for g in range(g_all):
-            acc[g, r0:r1, :] = acc[g, r0:r1, :] + local[g]
+        for g in range(plan.groups):
+            before = acc if g < BUF else given
+            acc[g, r0:r1, :] = before[g, r0:r1, :] + local[g]
 
 
 def ypack_kernel(plan, paired, ylo, yhi, elo, ehi, zpick, order, yh, vy, zc):
@@ -409,23 +429,23 @@
         mx[1][r0:r1, :] = 0.5 * jnp.where(mask, e - te, d - td)
     part = plan.inner * c
     order = list(range(BUF, BUF + c)) + list(range(BUF)) + list(range(BUF + c, plan.ext))
+    mask = low_lanes((c, lanes))
     for j in range(plan.inner):
         g = BUF + j
-        to = slice(j * c, (j + 1) * c)
-        down = slice(part + j * c, part + (j + 1) * c)
         ylayers = [out[g, k * c : (k + 1) * c, :] for k in range(plan.ext)]
         zlayers = [out[g, pl.ds(k, c, stride=c), :] for k in range(c)]
         zlayers += [out[g, plan.yext + k * c : plan.yext + (k + 1) * c, :] for k in range(2 * BUF)]
         for layers, message in ((ylayers, my), (zlayers, mz)):
             for side, layer in enumerate((0, c - 1)):
-                message[side][to, :] = layers[layer]
                 total = None
                 for k, t in enumerate(order):
                     weight = float(plan.first[BUF + layer, t])
                     if t != BUF + layer:
                         term = weight * layers[k]
                         total = term if total is None else total + term
-                message[side][down, :] = total
+                value = layers[layer]
+                message[side][j * c : (j + 1) * c, :] = jnp.where(mask, value, swap(total))
+                message[side][part + j * c : part + (j + 1) * c, :] = jnp.where(mask, swap(value), total)
 
 
 def own_kernel(plan, f, va, vd, bh, bl, coef, diag, basis, local, f2, f2h, f2l, fhi, acc, sem):
@@ -485,29 +505,26 @@
         copy.wait()
 
 
-def face_kernel(plan, paired, diag, ox, oy, oz, nx, ny, nz, blocks):
+def face_block(plan, own, other, sign, scale):
     w, lanes = plan.width, plan.lanes
-    part = plan.inner * plan.cells
+    ah, al = split(own[...])
+    bh, bl = split(other[...])
+    first = dot_t(ah, jnp.concatenate([bh, bl], axis=1))
+    m = first[:, :lanes] + first[:, lanes:] + dot_t(al, bh)
+    return scale * (0.25 * sign * (m[w:, :w] - m[:w, w:]) - 0.5 * PENALTY * m[:w, :w])
+
+
+def yzface_kernel(plan, paired, oy, oz, ny, nz, blocks):
     oz, nz = sides(oz, paired), sides(nz, paired)[::-1] if paired else nz
+    for k, (own, other) in enumerate(((oy[0], ny[0]), (oy[1], ny[1]), (oz[0], nz[0]), (oz[1], nz[1]))):
+        blocks[k] = face_block(plan, own, other, -1.0 if k % 2 == 0 else 1.0, 0.5)
+
+
+def xface_kernel(plan, diag, yz, ox, nx, blocks):
     blocks[0] = diag[...]
-
-    def product(a, b):
-        ah, al = split(a)
-        bh, bl = split(b)
-        return dot_t(ah, bh) + dot_t(ah, bl) + dot_t(al, bh)
-
     for k in range(2):
-        sign = -1.0 if k == 0 else 1.0
-        m = product(ox[k][...], nx[k][...])
-        blocks[1 + k] = 0.25 * sign * (m[w:, :w] - m[:w, w:]) - 0.5 * PENALTY * m[:w, :w]
-        for at, own, other in ((3, oy, ny), (5, oz, nz)):
-            a = jnp.concatenate([own[k][:part, :], own[k][part:, :]], axis=1)
-            b = jnp.concatenate([other[k][:part, :], other[k][part:, :]], axis=1)
-            m = product(a, b)
-            uv = m[:w, :w] + m[w:lanes, w:lanes]
-            udv = m[:w, lanes : lanes + w] + m[w:lanes, lanes + w :]
-            duv = m[lanes : lanes + w, :w] + m[lanes + w :, w:lanes]
-            blocks[at + k] = 0.5 * (0.25 * sign * (duv - udv) - 0.5 * PENALTY * uv)
+        blocks[1 + k] = face_block(plan, ox[k], nx[k], -1.0 if k == 0 else 1.0, 1.0)
+    blocks[3:] = yz[...]
 
 
 def near(*shape):
@@ -560,16 +577,21 @@
     def two(*shape):
         return near(2, *shape) if paired else [near(*shape), near(*shape)]
 
-    xrows, yrows, erows = BUF * face // 2 + 8, inner_all * strip + cells, BUF * strip + 8
-    xlo, xhi, ylo, yhi, inner, vt = call(
-        part(pack_kernel, plan),
-        [near(xrows, lanes), near(xrows, lanes), near(yrows, lanes), near(yrows, lanes), near(inner_all, face, lanes), near(cells, face)],
-        [orbitals.reshape(cells, face, width), potential.reshape(face, cells)],
-        [pltpu.VMEM((cells, face, width), F32), pltpu.VMEM((face, cells), F32), pltpu.SemaphoreType.DMA((cells + 1,))],
+    srows, rrows, yrows = BUF * strip + 8, BUF * (face // 2 - strip), inner_all * strip + cells
+    orb = orbitals.reshape(cells, face, width)
+    slo, shi, rlo, rhi, vt = call(
+        part(packx_kernel, plan),
+        [near(srows, lanes), near(srows, lanes), near(rrows, lanes), near(rrows, lanes), near(cells, face)],
+        [orb, potential.reshape(face, cells)],
+        [pltpu.VMEM((2 * BUF, face, width), F32), pltpu.VMEM((face, cells), F32), pltpu.SemaphoreType.DMA((2 * BUF + 1,))],
         far_in=(0, 1),
     )
+    from_slo, from_shi = shift(shi, "gx", 1), shift(slo, "gx", -1)
+    ylo, yhi, inner = call(
+        part(packy_kernel, plan), [near(yrows, lanes), near(yrows, lanes), near(inner_all, face, lanes)], [orb, vt],
+    )
     from_ylo, from_yhi = shift(yhi, "gy", 1), shift(ylo, "gy", -1)
-    from_xlo, from_xhi = shift(xhi, "gx", 1), shift(xlo, "gx", -1)
+    from_rlo, from_rhi = shift(rhi, "gx", 1), shift(rlo, "gx", -1)
 
     ipick = np.zeros((2, face, lanes), np.float32)
     cpick = np.zeros((2, lanes, lanes), np.float32)
@@ -580,13 +602,11 @@
                 ipick[side, y * cells + z, k * cells + y] = 1.0
             for y in range(2 * BUF):
                 cpick[side, y * cells + z, k * corner + y] = 1.0
-    outer, elo, ehi, vx, zi = call(
-        part(xhalo_kernel, plan, paired),
-        [near(BUF, face, lanes), near(erows, lanes), near(erows, lanes), near(plan.trows, face), two(g_all * strip + plan.trows, lanes)],
-        [inner, vt, from_xlo, from_xhi, ipick],
+    elo, ehi, vx = call(
+        part(edge_kernel, plan), [near(srows, lanes), near(srows, lanes), near(plan.trows, face)], [vt, from_slo, from_shi, from_ylo],
+        flops=10**9,
     )
     from_elo, from_ehi = shift(ehi, "gy", 1), shift(elo, "gy", -1)
-    zi = shift_z(zi, paired)
 
     matrix = -0.5 * row_matrix(plan, plan.second, False)
     coef = folded(-0.5 * mirrored(plan, plan.second))
@@ -596,11 +616,26 @@
         vspread[plan.ext - 1 - g, 0, g, :] = 0.5
         vspread[plan.ext - 1 - g, 1, g, :] = -0.5
     vspread = np.tile(vspread.reshape(plan.trows, -1), (3, 1)).astype(ml_dtypes.bfloat16)
-    acc, vai, vdi, order = call(
+    inside = halves(matrix[:, :face])
+    acc, vai, vdi, early = call(
         part(inside_kernel, plan),
         [near(g_all, rows, lanes), near(g_all, face, lanes), near(g_all, face, lanes), near(8, lanes)],
-        [inner, outer, vx, *halves(matrix[:, :face]), coef, vspread],
-        [bf(face, wide), bf(face, wide)],
+        [inner, vx, *inside, vspread],
+        [bf(face, inner_all * lanes), bf(face, inner_all * lanes)],
+        flops=0,
+    )
+    outer, zi = call(
+        part(xhalo_kernel, plan, paired),
+        [near(BUF, face, lanes), two(g_all * strip + plan.trows, lanes)],
+        [inner, vx, elo, ehi, from_rlo, from_rhi, ipick, early],
+    )
+    zi = shift_z(zi, paired)
+    acc, order = call(
+        part(outside_kernel, plan),
+        [near(g_all, rows, lanes), near(8, lanes)],
+        [inner, outer, *inside, coef, vai, vdi, acc],
+        [bf(face, BUF * lanes), bf(face, BUF * lanes)],
+        aliases={7: 0},
     )
 
     room = 2 * strip + (corner - 2 * BUF) * cells
@@ -646,9 +681,8 @@
         flops=2 * 10**9,
         far_out=(1,),
     )
-    (blocks,) = call(
-        part(face_kernel, plan, paired), [far(7, width, width)], [diag, mx, my, mz, nx, ny, nz],
-    )
+    (yz,) = call(part(yzface_kernel, plan, paired), [near(4, width, width)], [my, mz, ny, nz])
+    (blocks,) = call(part(xface_kernel, plan), [far(7, width, width)], [diag, yz, mx, nx])
     return basis.reshape(orbitals.shape), blocks[None, None, None]
 
 

time: 47.2 us -> 44.4 us (0.941)
  waiting for transfers between devices: 7.29 us -> 0.6 us
  starting transfers between devices: 17.7 us -> 21 us
    ppermute x13 -> x15, waiting for transfers between devices: 7.29 us -> 0.6 us  [shift(): lax.ppermute(array, axis, [(i, (i + step) % count) for i in range(count)])]
    ppermute x13 -> x15, starting transfers between devices: 17.7 us -> 21 us  [shift(): lax.ppermute(array, axis, [(i, (i + step) % count) for i in range(count)])]
    pallas_call x8 -> x12, Pallas kernels: 21 us -> 21.4 us  [call(): pl.pallas_call(kernel, out_shape=outs, in_specs=[apart if i in far_in els...]
  transfers between devices with their start and end apart: 13 -> 15, of which waited for: 5 -> 2; matrix products, arithmetic and copies ran while one was open for 0% -> 0% of each run, Pallas kernels for 22% -> 26%
where the time goes in v4:
time: 44.4 us; the launch traced here: 44.2 us
  Pallas kernels  21.4 us (48%)
  starting transfers between devices  21 us (47%)
  between operations  0.95 us (2%)
  waiting for transfers between devices  0.6 us (1%)
    pallas_call x12, Pallas kernels, call(): pl.pallas_call(kernel, out_shape=outs, in_specs=[apart if i in far_in els...  21.4 us
    ppermute x15, starting transfers between devices, shift(): lax.ppermute(array, axis, [(i, (i + step) % count) for i in range(count)])  21 us
  transfers between devices with their start and end apart: 15, of which 2 were waited for; matrix products, arithmetic and copies ran while one was open for 0% of the time, Pallas kernels for 26%

profile of v4, /device:TPU:0, one launch (start us, length us, event | category | flops | bytes accessed | tf_op | source)
XLA Modules:
  0.0 44.2 jit_solution(3493861828985554936)
XLA Ops:
  0.6 0.0 copy-start
  0.6 1.7 %shard_map.167 = (f32[152,128]{1,0:T(8,128)S(1)}, f32[152,128]{1,0:T(8,128)S(1)}, f32[240,128]{1,0:T(8,128)S(1)}, f32[240,128]{1,0:T(8,128)S(1)}, f32[16,256]{1,0:T(8,128)S(1)}) custom-call(f32[16,256,64]{2,1,0:T(8,128)} %bitcast.4, f32[256,16]{1,0:T(8,128)} %bitcast.7), custom_call_target="tpu_custom_call" | custom-call | tf_op jit(solution)/shard_map/pallas_call | solution.py:544
  2.4 0.2 copy-done
  2.6 0.4 shard_map.168
  2.9 0.0 copy-start.1
  3.0 0.0 copy-start.2
  3.0 0.0 copy-start.3
  3.0 3.1 %collective-permute-start = (f32[400,128]{1,0:T(8,128)S(1)}, f32[400,128]{1,0:T(8,128)S(1)}, u32[]{:S(2)}, u32[]{:S(2)}) collective-permute-start(f32[400,128]{1,0:T(8,128)S(1)} %get-tuple-element.39), channel_id=1, source_target_pairs={{0,2},{2,4},{4,6},{6,0},{1,3},{3,5},{5,7},{7,1},{8,10},{10,12},{12... | collective-permute-start | bytes 614408 | tf_op jit(solution)/shard_map/ppermute | solution.py:558
  6.1 1.5 %collective-permute-start.2 = (f32[152,128]{1,0:T(8,128)S(1)}, f32[152,128]{1,0:T(8,128)S(1)}, u32[]{:S(2)}, u32[]{:S(2)}) collective-permute-start(f32[152,128]{1,0:T(8,128)S(1)} %get-tuple-element.41), channel_id=1, source_target_pairs={{0,8},{8,16},{16,24},{24,0},{1,9},{9,17},{17,25},{25,1},{2,10},{10... | collective-permute-start | bytes 233480 | tf_op jit(solution)/shard_map/ppermute | solution.py:558
  7.6 1.4 %collective-permute-start.3 = (f32[152,128]{1,0:T(8,128)S(1)}, f32[152,128]{1,0:T(8,128)S(1)}, u32[]{:S(2)}, u32[]{:S(2)}) collective-permute-start(f32[152,128]{1,0:T(8,128)S(1)} %get-tuple-element.42), channel_id=1, source_target_pairs={{0,24},{8,0},{16,8},{24,16},{1,25},{9,1},{17,9},{25,17},{2,26},{10... | collective-permute-start | bytes 233480 | tf_op jit(solution)/shard_map/ppermute | solution.py:558
  9.0 2.1 %collective-permute-start.1 = (f32[400,128]{1,0:T(8,128)S(1)}, f32[400,128]{1,0:T(8,128)S(1)}, u32[]{:S(2)}, u32[]{:S(2)}) collective-permute-start(f32[400,128]{1,0:T(8,128)S(1)} %get-tuple-element.40), channel_id=1, source_target_pairs={{0,6},{2,0},{4,2},{6,4},{1,7},{3,1},{5,3},{7,5},{8,14},{10,8},{12,... | collective-permute-start | bytes 614408 | tf_op jit(solution)/shard_map/ppermute | solution.py:558
  11.1 0.7 %collective-permute-start.6 = (f32[240,128]{1,0:T(8,128)S(1)}, f32[240,128]{1,0:T(8,128)S(1)}, u32[]{:S(2)}, u32[]{:S(2)}) collective-permute-start(f32[240,128]{1,0:T(8,128)S(1)} %get-tuple-element.47), channel_id=1, source_target_pairs={{0,8},{8,16},{16,24},{24,0},{1,9},{9,17},{17,25},{25,1},{2,10},{10... | collective-permute-start | bytes 368648 | tf_op jit(solution)/shard_map/ppermute | solution.py:558
  11.8 0.2 collective-permute-done.2.lo
  12.0 2.0 %collective-permute-start.7 = (f32[240,128]{1,0:T(8,128)S(1)}, f32[240,128]{1,0:T(8,128)S(1)}, u32[]{:S(2)}, u32[]{:S(2)}) collective-permute-start(f32[240,128]{1,0:T(8,128)S(1)} %get-tuple-element.48), channel_id=1, source_target_pairs={{0,24},{8,0},{16,8},{24,16},{1,25},{9,1},{17,9},{25,17},{2,26},{10... | collective-permute-start | bytes 368648 | tf_op jit(solution)/shard_map/ppermute | solution.py:558
  14.0 0.0 collective-permute-done.3.hi
  14.0 0.0 collective-permute-done.ahead.ylo
  14.0 0.1 shard_map.169
  14.1 0.0 copy-start.6
  14.1 1.4 %collective-permute-start.4 = (f32[152,128]{1,0:T(8,128)S(1)}, f32[152,128]{1,0:T(8,128)S(1)}, u32[]{:S(2)}, u32[]{:S(2)}) collective-permute-start(f32[152,128]{1,0:T(8,128)S(1)} %get-tuple-element.43.ehi), channel_id=1, source_target_pairs={{0,2},{2,4},{4,6},{6,0},{1,3},{3,5},{5,7},{7,1},{8,10},{10,12},{12... | collective-permute-start | bytes 233480 | tf_op jit(solution)/shard_map/ppermute | solution.py:558
  15.5 2.5 %collective-permute-start.5 = (f32[152,128]{1,0:T(8,128)S(1)}, f32[152,128]{1,0:T(8,128)S(1)}, u32[]{:S(2)}, u32[]{:S(2)}) collective-permute-start(f32[152,128]{1,0:T(8,128)S(1)} %get-tuple-element.44.elo), channel_id=1, source_target_pairs={{0,6},{2,0},{4,2},{6,4},{1,7},{3,1},{5,3},{7,5},{8,14},{10,8},{12,... | collective-permute-start | bytes 233480 | tf_op jit(solution)/shard_map/ppermute | solution.py:558
  18.0 0.0 copy-done.1
  18.0 0.0 copy-done.2
  18.0 0.0 copy-done.3
  18.0 1.4 %shard_map.170 = (f32[11,496,128]{2,1,0:T(8,128)S(1)}, f32[11,256,128]{2,1,0:T(8,128)S(1)}, f32[11,256,128]{2,1,0:T(8,128)S(1)}, f32[8,128]{1,0:T(8,128)S(1)}) custom-call(f32[8,256,128]{2,1,0:T(8,128)S(1)} %get-tuple-element.45.inner, f32[24,256]{1,0:T(8,128)S(1)} %get-tuple-element.46.vx, bf16[496,256]{1,0:T(8,128)(2,1)S(1)} %copy-done.3, ...), custom_call_target="tpu_custom_call" | custom-call | tf_op jit(solution)/shard_map/pallas_call | solution.py:544
  19.5 0.0 collective-permute-done.6.lo
  19.5 0.0 collective-permute-done.7.hi
  19.5 0.0 copy-done.7
  19.5 0.4 shard_map.171
  19.9 0.1 collective-permute-start.9
  20.0 0.0 copy-done.6
  20.0 0.0 copy-start.13
  20.0 1.5 %shard_map.172 = (f32[11,496,128]{2,1,0:T(8,128)S(1)}, f32[8,128]{1,0:T(8,128)S(1)}) custom-call(f32[8,256,128]{2,1,0:T(8,128)S(1)} %get-tuple-element.45.inner, f32[3,256,128]{2,1,0:T(8,128)S(1)} %get-tuple-element.50.outer, bf16[496,256]{1,0:T(8,128)(2,1)S(1)} %copy-done.3, bf16[496,256]{1,0:T(8,128)(2,1)S(1)} %copy-done.2, ...), custom_call_target="tpu_custom_call", output_to_operand_aliasing={{0}: (7, {})} | custom-call | tf_op jit(solution)/shard_map/pallas_call | solution.py:544
  21.6 0.0 collective-permute-done.1.yhi
  21.6 0.0 collective-permute-done.4.elo
  21.6 0.0 collective-permute-done.5.ehi
  21.6 0.0 copy-done.13
  21.6 0.4 shard_map.173
  22.0 0.5 %collective-permute-start.8 = (f32[2,288,128]{2,1,0:T(8,128)S(1)}, f32[2,288,128]{2,1,0:T(8,128)S(1)}, u32[]{:S(2)}, u32[]{:S(2)}) collective-permute-start(f32[2,288,128]{2,1,0:T(8,128)S(1)} %get-tuple-element.55), channel_id=1, source_target_pairs={{0,1},{1,0},{2,3},{3,2},{4,5},{5,4},{6,7},{7,6},{8,9},{9,8},{10,11... | collective-permute-start | bytes 884744 | tf_op jit(solution)/shard_map/ppermute | solution.py:558
  22.5 0.0 collective-permute-done.9.zi
  22.5 0.0 copy-start.9
  22.5 0.0 copy-start.10
  22.5 1.6 %shard_map.174 = (f32[11,496,128]{2,1,0:T(8,128)S(1)}, f32[11,192,128]{2,1,0:T(8,128)S(1)}, f32[11,192,128]{2,1,0:T(8,128)S(1)}, f32[11,192,128]{2,1,0:T(8,128)S...) custom-call(f32[11,128,128]{2,1,0:T(8,128)S(1)} %get-tuple-element.56.yh, ...), custom_call_target="tpu_custom_call", output_to_operand_aliasing={{0}: (5, {})} | custom-call | tf_op jit(solution)/shard_map/pallas_call | solution.py:544
  24.1 0.0 collective-permute-done.8.zc
  24.1 0.0 copy-done.4
  24.2 0.0 copy-done.5
  24.2 0.0 copy-done.8
  24.2 0.0 copy-done.9
  24.2 0.0 copy-start.11
  24.2 0.0 copy-start.12
  24.2 0.0 copy-start.14
  24.2 7.0 %shard_map.175 = (f32[11,448,128]{2,1,0:T(8,128)S(1)}, f32[256,128]{1,0:T(8,128)S(1)}, f32[256,128]{1,0:T(8,128)S(1)}, f32[256,128]{1,0:T(8,128)S(1)}, f32[256,1...) custom-call(f32[2,288,128]{2,1,0:T(8,128)S(1)} %collective-permute-done.8.zc, f32[8,256,128]{2,1,0:T(8,128)S(1)} %get-tuple-element.45.inner, ...), custom_call_target="tpu_custom_call" | custom-call | tf_op jit(solution)/shard_map/pallas_call | solution.py:544
  31.2 0.1 collective-permute-start.12
  31.3 2.6 %collective-permute-start.11 = (f32[256,128]{1,0:T(8,128)S(1)}, f32[256,128]{1,0:T(8,128)S(1)}, u32[]{:S(2)}, u32[]{:S(2)}) collective-permute-start(f32[256,128]{1,0:T(8,128)S(1)} %get-tuple-element.69.oy_0_), channel_id=1, source_target_pairs={{0,6},{2,0},{4,2},{6,4},{1,7},{3,1},{5,3},{7,5},{8,14},{10,8},{12,... | collective-permute-start | bytes 393224 | tf_op jit(solution)/shard_map/ppermute | solution.py:558
  33.9 0.0 collective-permute-start.10
  33.9 3.0 %collective-permute-start.14 = (f32[256,128]{1,0:T(8,128)S(1)}, f32[256,128]{1,0:T(8,128)S(1)}, u32[]{:S(2)}, u32[]{:S(2)}) collective-permute-start(f32[256,128]{1,0:T(8,128)S(1)} %get-tuple-element.72.ox_0_), channel_id=1, source_target_pairs={{0,24},{8,0},{16,8},{24,16},{1,25},{9,1},{17,9},{25,17},{2,26},{10... | collective-permute-start | bytes 393224 | tf_op jit(solution)/shard_map/ppermute | solution.py:558
  37.0 0.0 collective-permute-start.13
  37.0 5.4 %shard_map.176 = (f32[64,64]{1,0:T(8,128)S(1)}, f32[16,256,64]{2,1,0:T(8,128)}) custom-call(f32[11,448,128]{2,1,0:T(8,128)S(1)} %get-tuple-element.66.f, f32[11,256,128]{2,1,0:T(8,128)S(1)} %get-tuple-element.51.va.vai, f32[11,256,128]{2,1,0:T(8,128)S(1)} %get-tuple-element.52.vd.vdi, bf16[448,448]{1,0:T(8,128)(2,1)S(1)} %copy-done.12, ...), custom_call_target="tpu_custom_call" | custom-call | flops 2000000000 | tf_op jit(solution)/shard_map/pallas_call | solution.py:544
  42.4 0.0 collective-permute-done.11.ny_1_
  42.4 0.0 collective-permute-done.10.ny_0_
  42.4 0.0 collective-permute-done.12.nz
  42.4 0.4 shard_map.177.yz
  42.8 0.0 collective-permute-done.14.nx_1_
  42.9 0.4 collective-permute-done.13.nx_0_
  43.2 1.0 %shard_map.178 = f32[7,64,64]{2,1,0:T(8,128)} custom-call(f32[64,64]{1,0:T(8,128)S(1)} %get-tuple-element.68.diag, f32[4,64,64]{2,1,0:T(8,128)S(1)} %shard_map.177.yz, f32[256,128]{1,0:T(8,128)S(1)} %get-tuple-element.72.ox_0_, f32[256,128]{1,0:T(8,128)S(1)} %get-tuple-element.73.ox_1_, f32[256,128]{1,0:T(8,128)S(1)} %collective-permute-done.13.nx_0_, ...), custom_call_target="tpu_custom_call" | custom-call | tf_op jit(solution)/shard_map/pallas_call | solution.py:544
  (8 shorter events, 0.0 us)
Async XLA Ops:
  0.6 2.0 %copy-start = (f32[16,16,16,64]{3,2,1,0:T(8,128)S(1)}, f32[16,16,16,64]{3,2,1,0:T(8,128)}, u32[]{:S(2)}) copy-start(f32[16,16,16,64]{3,2,1,0:T(8,128)} %param.16) | copy-start | bytes 3145732
  2.9 15.1 %copy-start.1 = (bf16[72,2816]{1,0:T(8,128)(2,1)S(1)}, bf16[72,2816]{1,0:T(8,128)(2,1)}, u32[]{:S(2)}) copy-start(bf16[72,2816]{1,0:T(8,128)(2,1)} %constant.30.clone.vspread) | copy-start | bytes 1216516
  3.0 15.1 %copy-start.2 = (bf16[496,256]{1,0:T(8,128)(2,1)S(1)}, bf16[496,256]{1,0:T(8,128)(2,1)}, u32[]{:S(2)}) copy-start(bf16[496,256]{1,0:T(8,128)(2,1)} %constant.29.clone.wl) | copy-start | bytes 761860
  3.0 15.1 %copy-start.3 = (bf16[496,256]{1,0:T(8,128)(2,1)S(1)}, bf16[496,256]{1,0:T(8,128)(2,1)}, u32[]{:S(2)}) copy-start(bf16[496,256]{1,0:T(8,128)(2,1)} %constant.28.clone.wh) | copy-start | bytes 761860
  3.0 11.0 %collective-permute-start = (f32[400,128]{1,0:T(8,128)S(1)}, f32[400,128]{1,0:T(8,128)S(1)}, u32[]{:S(2)}, u32[]{:S(2)}) collective-permute-start(f32[400,128]{1,0:T(8,128)S(1)} %get-tuple-element.39), channel_id=1, source_target_pairs={{0,2},{2,4},{4,6},{6,0},{1,3},{3,5},{5,7},{7,1},{8,10},{10,12},{12... | collective-permute-start | bytes 614408 | tf_op jit(solution)/shard_map/ppermute | solution.py:558
  6.1 6.0 %collective-permute-start.2 = (f32[152,128]{1,0:T(8,128)S(1)}, f32[152,128]{1,0:T(8,128)S(1)}, u32[]{:S(2)}, u32[]{:S(2)}) collective-permute-start(f32[152,128]{1,0:T(8,128)S(1)} %get-tuple-element.41), channel_id=1, source_target_pairs={{0,8},{8,16},{16,24},{24,0},{1,9},{9,17},{17,25},{25,1},{2,10},{10... | collective-permute-start | bytes 233480 | tf_op jit(solution)/shard_map/ppermute | solution.py:558
  7.6 6.5 %collective-permute-start.3 = (f32[152,128]{1,0:T(8,128)S(1)}, f32[152,128]{1,0:T(8,128)S(1)}, u32[]{:S(2)}, u32[]{:S(2)}) collective-permute-start(f32[152,128]{1,0:T(8,128)S(1)} %get-tuple-element.42), channel_id=1, source_target_pairs={{0,24},{8,0},{16,8},{24,16},{1,25},{9,1},{17,9},{25,17},{2,26},{10... | collective-permute-start | bytes 233480 | tf_op jit(solution)/shard_map/ppermute | solution.py:558
  9.0 12.6 %collective-permute-start.1 = (f32[400,128]{1,0:T(8,128)S(1)}, f32[400,128]{1,0:T(8,128)S(1)}, u32[]{:S(2)}, u32[]{:S(2)}) collective-permute-start(f32[400,128]{1,0:T(8,128)S(1)} %get-tuple-element.40), channel_id=1, source_target_pairs={{0,6},{2,0},{4,2},{6,4},{1,7},{3,1},{5,3},{7,5},{8,14},{10,8},{12,... | collective-permute-start | bytes 614408 | tf_op jit(solution)/shard_map/ppermute | solution.py:558
  11.1 8.4 %collective-permute-start.6 = (f32[240,128]{1,0:T(8,128)S(1)}, f32[240,128]{1,0:T(8,128)S(1)}, u32[]{:S(2)}, u32[]{:S(2)}) collective-permute-start(f32[240,128]{1,0:T(8,128)S(1)} %get-tuple-element.47), channel_id=1, source_target_pairs={{0,8},{8,16},{16,24},{24,0},{1,9},{9,17},{17,25},{25,1},{2,10},{10... | collective-permute-start | bytes 368648 | tf_op jit(solution)/shard_map/ppermute | solution.py:558
  12.0 7.5 %copy-start.7 = (f32[2,256,128]{2,1,0:T(8,128)S(1)}, f32[2,256,128]{2,1,0:T(8,128)}, u32[]{:S(2)}) copy-start(f32[2,256,128]{2,1,0:T(8,128)} %constant.31.clone.zpick) | copy-start | bytes 786436
  12.0 7.5 %collective-permute-start.7 = (f32[240,128]{1,0:T(8,128)S(1)}, f32[240,128]{1,0:T(8,128)S(1)}, u32[]{:S(2)}, u32[]{:S(2)}) collective-permute-start(f32[240,128]{1,0:T(8,128)S(1)} %get-tuple-element.48), channel_id=1, source_target_pairs={{0,24},{8,0},{16,8},{24,16},{1,25},{9,1},{17,9},{25,17},{2,26},{10... | collective-permute-start | bytes 368648 | tf_op jit(solution)/shard_map/ppermute | solution.py:558
  14.1 5.9 %copy-start.6 = (f32[61,128]{1,0:T(8,128)S(1)}, f32[61,128]{1,0:T(8,128)}, u32[]{:S(2)}) copy-start(f32[61,128]{1,0:T(8,128)} %constant.32.clone.coef) | copy-start | bytes 93700
  14.1 7.5 %collective-permute-start.4 = (f32[152,128]{1,0:T(8,128)S(1)}, f32[152,128]{1,0:T(8,128)S(1)}, u32[]{:S(2)}, u32[]{:S(2)}) collective-permute-start(f32[152,128]{1,0:T(8,128)S(1)} %get-tuple-element.43.ehi), channel_id=1, source_target_pairs={{0,2},{2,4},{4,6},{6,0},{1,3},{3,5},{5,7},{7,1},{8,10},{10,12},{12... | collective-permute-start | bytes 233480 | tf_op jit(solution)/shard_map/ppermute | solution.py:558
  15.5 6.1 %collective-permute-start.5 = (f32[152,128]{1,0:T(8,128)S(1)}, f32[152,128]{1,0:T(8,128)S(1)}, u32[]{:S(2)}, u32[]{:S(2)}) collective-permute-start(f32[152,128]{1,0:T(8,128)S(1)} %get-tuple-element.44.elo), channel_id=1, source_target_pairs={{0,6},{2,0},{4,2},{6,4},{1,7},{3,1},{5,3},{7,5},{8,14},{10,8},{12,... | collective-permute-start | bytes 233480 | tf_op jit(solution)/shard_map/ppermute | solution.py:558
  19.9 2.6 %collective-permute-start.9 = (f32[2,552,128]{2,1,0:T(8,128)S(1)}, f32[2,552,128]{2,1,0:T(8,128)S(1)}, u32[]{:S(2)}, u32[]{:S(2)}) collective-permute-start(f32[2,552,128]{2,1,0:T(8,128)S(1)} %get-tuple-element.58), channel_id=1, source_target_pairs={{0,1},{1,0},{2,3},{3,2},{4,5},{5,4},{6,7},{7,6},{8,9},{9,8},{10,11... | collective-permute-start | bytes 1695752 | tf_op jit(solution)/shard_map/ppermute | solution.py:558
  20.0 1.6 %copy-start.13 = (f32[2,128,128]{2,1,0:T(8,128)S(1)}, f32[2,128,128]{2,1,0:T(8,128)}, u32[]{:S(2)}) copy-start(f32[2,128,128]{2,1,0:T(8,128)} %constant.33.clone.zpick) | copy-start | bytes 393220
  22.0 2.1 %collective-permute-start.8 = (f32[2,288,128]{2,1,0:T(8,128)S(1)}, f32[2,288,128]{2,1,0:T(8,128)S(1)}, u32[]{:S(2)}, u32[]{:S(2)}) collective-permute-start(f32[2,288,128]{2,1,0:T(8,128)S(1)} %get-tuple-element.55), channel_id=1, source_target_pairs={{0,1},{1,0},{2,3},{3,2},{4,5},{5,4},{6,7},{7,6},{8,9},{9,8},{10,11... | collective-permute-start | bytes 884744 | tf_op jit(solution)/shard_map/ppermute | solution.py:558
  22.5 1.6 %copy-start.4 = (bf16[448,496]{1,0:T(8,128)(2,1)S(1)}, bf16[448,496]{1,0:T(8,128)(2,1)}, u32[]{:S(2)}) copy-start(bf16[448,496]{1,0:T(8,128)(2,1)} %constant.37.clone.wl) | copy-start | bytes 1333252
  22.5 1.6 %copy-start.5 = (bf16[448,496]{1,0:T(8,128)(2,1)S(1)}, bf16[448,496]{1,0:T(8,128)(2,1)}, u32[]{:S(2)}) copy-start(bf16[448,496]{1,0:T(8,128)(2,1)} %constant.36.clone.wh) | copy-start | bytes 1333252
  22.5 1.7 %copy-start.8 = (bf16[496,240]{1,0:T(8,128)(2,1)S(1)}, bf16[496,240]{1,0:T(8,128)(2,1)}, u32[]{:S(2)}) copy-start(bf16[496,240]{1,0:T(8,128)(2,1)} %constant.35.clone.wrl) | copy-start | bytes 714244
  22.5 1.7 %copy-start.9 = (bf16[496,240]{1,0:T(8,128)(2,1)S(1)}, bf16[496,240]{1,0:T(8,128)(2,1)}, u32[]{:S(2)}) copy-start(bf16[496,240]{1,0:T(8,128)(2,1)} %constant.34.clone.wrh) | copy-start | bytes 714244
  22.5 1.7 %copy-start.10 = (f32[11,128]{1,0:T(8,128)S(1)}, f32[11,128]{1,0:T(8,128)}, u32[]{:S(2)}) copy-start(f32[11,128]{1,0:T(8,128)} %constant.38.clone.dcoef) | copy-start | bytes 16900
  24.2 12.8 %copy-start.11 = (bf16[448,448]{1,0:T(8,128)(2,1)S(1)}, bf16[448,448]{1,0:T(8,128)(2,1)}, u32[]{:S(2)}) copy-start(bf16[448,448]{1,0:T(8,128)(2,1)} %constant.40.clone.bl) | copy-start | bytes 1204228
  24.2 12.7 %copy-start.12 = (bf16[448,448]{1,0:T(8,128)(2,1)S(1)}, bf16[448,448]{1,0:T(8,128)(2,1)}, u32[]{:S(2)}) copy-start(bf16[448,448]{1,0:T(8,128)(2,1)} %constant.39.clone.bh) | copy-start | bytes 1204228
  24.2 12.7 %copy-start.14 = (f32[121,128]{1,0:T(8,128)S(1)}, f32[121,128]{1,0:T(8,128)}, u32[]{:S(2)}) copy-start(f32[121,128]{1,0:T(8,128)} %constant.41.clone.coef) | copy-start | bytes 185860
  31.2 11.2 %collective-permute-start.12 = (f32[2,256,128]{2,1,0:T(8,128)S(1)}, f32[2,256,128]{2,1,0:T(8,128)S(1)}, u32[]{:S(2)}, u32[]{:S(2)}) collective-permute-start(f32[2,256,128]{2,1,0:T(8,128)S(1)} %get-tuple-element.71.oz), channel_id=1, source_target_pairs={{0,1},{1,0},{2,3},{3,2},{4,5},{5,4},{6,7},{7,6},{8,9},{9,8},{10,11... | collective-permute-start | bytes 786440 | tf_op jit(solution)/shard_map/ppermute | solution.py:558
  31.3 11.1 %collective-permute-start.11 = (f32[256,128]{1,0:T(8,128)S(1)}, f32[256,128]{1,0:T(8,128)S(1)}, u32[]{:S(2)}, u32[]{:S(2)}) collective-permute-start(f32[256,128]{1,0:T(8,128)S(1)} %get-tuple-element.69.oy_0_), channel_id=1, source_target_pairs={{0,6},{2,0},{4,2},{6,4},{1,7},{3,1},{5,3},{7,5},{8,14},{10,8},{12,... | collective-permute-start | bytes 393224 | tf_op jit(solution)/shard_map/ppermute | solution.py:558
  33.9 8.5 %collective-permute-start.10 = (f32[256,128]{1,0:T(8,128)S(1)}, f32[256,128]{1,0:T(8,128)S(1)}, u32[]{:S(2)}, u32[]{:S(2)}) collective-permute-start(f32[256,128]{1,0:T(8,128)S(1)} %get-tuple-element.70.oy_1_), channel_id=1, source_target_pairs={{0,2},{2,4},{4,6},{6,0},{1,3},{3,5},{5,7},{7,1},{8,10},{10,12},{12... | collective-permute-start | bytes 393224 | tf_op jit(solution)/shard_map/ppermute | solution.py:558
  33.9 8.9 %collective-permute-start.14 = (f32[256,128]{1,0:T(8,128)S(1)}, f32[256,128]{1,0:T(8,128)S(1)}, u32[]{:S(2)}, u32[]{:S(2)}) collective-permute-start(f32[256,128]{1,0:T(8,128)S(1)} %get-tuple-element.72.ox_0_), channel_id=1, source_target_pairs={{0,24},{8,0},{16,8},{24,16},{1,25},{9,1},{17,9},{25,17},{2,26},{10... | collective-permute-start | bytes 393224 | tf_op jit(solution)/shard_map/ppermute | solution.py:558
  37.0 6.3 %collective-permute-start.13 = (f32[256,128]{1,0:T(8,128)S(1)}, f32[256,128]{1,0:T(8,128)S(1)}, u32[]{:S(2)}, u32[]{:S(2)}) collective-permute-start(f32[256,128]{1,0:T(8,128)S(1)} %get-tuple-element.73.ox_1_), channel_id=1, source_target_pairs={{0,8},{8,16},{16,24},{24,0},{1,9},{9,17},{17,25},{25,1},{2,10},{10... | collective-permute-start | bytes 393224 | tf_op jit(solution)/shard_map/ppermute | solution.py:558

commit v5 on v4

--- a/solution.py
+++ b/solution.py
@@ -175,19 +175,22 @@
     return out
 
 
-def spread_potential(plan, piece, count, vspread, va, vd, at):
-    high = piece.astype(BF).astype(F32)
-    rest = piece - high
-    mid = rest.astype(BF).astype(F32)
-    stacked = jnp.concatenate([high, mid, rest - mid], axis=0)
-    turned = jnp.transpose(stacked)[:count, :].astype(BF)
+def spread_potential(plan, pieces, vspread, va, vd):
+    turned = []
+    for piece, count in pieces:
+        high = piece.astype(BF).astype(F32)
+        rest = piece - high
+        mid = rest.astype(BF).astype(F32)
+        stacked = jnp.concatenate([high, mid, rest - mid], axis=0)
+        turned.append(jnp.transpose(stacked)[:count, :])
+    turned = jnp.concatenate(turned, axis=0).astype(BF)
     g_all, lanes = plan.groups, plan.lanes
     for g0, g1 in pairs(g_all):
         for k, dst, less in ((0, va, CENTER), (1, vd, 0.0)):
             cols = slice((k * g_all + g0) * lanes, (k * g_all + g1) * lanes)
             both = dot(turned, vspread[:, cols]) - less
             for g in range(g0, g1):
-                dst[g, at : at + count, :] = both[:, (g - g0) * lanes : (g - g0 + 1) * lanes]
+                dst[g] = both[:, (g - g0) * lanes : (g - g0 + 1) * lanes]
 
 
 def local_terms(coef, get, count, va, vd, v0):
@@ -198,12 +201,13 @@
     return out
 
 
-def packx_kernel(plan, orb_far, pot_far, slo, shi, rlo, rhi, vt, orb, pot, sem):
-    c, lanes, face, strip = plan.cells, plan.lanes, plan.face, plan.strip
-    half, rest = face // 2, face // 2 - plan.strip
-    slabs = list(range(BUF)) + list(range(c - BUF, c))
-    copies = [pltpu.make_async_copy(pot_far, pot, sem.at[2 * BUF])]
-    copies += [pltpu.make_async_copy(orb_far.at[x], orb.at[k], sem.at[k]) for k, x in enumerate(slabs)]
+def strip_kernel(plan, orb_far, pot_far, slo, shi, ylo, yhi, vt, low, high, pot, sem):
+    c, lanes, face, strip, w = plan.cells, plan.lanes, plan.face, plan.strip, plan.width
+    copies = [
+        pltpu.make_async_copy(pot_far, pot, sem.at[0]),
+        pltpu.make_async_copy(orb_far.at[:, :strip], low, sem.at[1]),
+        pltpu.make_async_copy(orb_far.at[:, face - strip :], high, sem.at[2]),
+    ]
     for copy in copies:
         copy.start()
     copies[0].wait()
@@ -214,25 +218,31 @@
         out[base:, :] = jnp.zeros((8, lanes), F32)
         for part in range(2):
             out[base + part * BUF : base + (part + 1) * BUF, :] = v[first : first + BUF, part * lanes : (part + 1) * lanes]
-    for k in range(2 * BUF):
-        copies[1 + k].wait()
-        at = k % BUF
-        near_out, rest_out = (slo, rlo) if k < BUF else (shi, rhi)
-        near_out[at * strip : (at + 1) * strip, :] = jnp.concatenate([orb[k, :strip], orb[k, face - strip :]], axis=1)
-        rest_out[at * rest : (at + 1) * rest, :] = jnp.concatenate([orb[k, strip:half], orb[k, half : face - strip]], axis=1)
-
-
-def packy_kernel(plan, orb, vt, ylo, yhi, inner):
+    ybase = plan.inner * strip
+    ylo[ybase:, :] = v[:, :lanes]
+    yhi[ybase:, :] = v[:, face - lanes :]
+    copies[1].wait()
+    copies[2].wait()
+    for out, part in ((ylo, low), (yhi, high)):
+        for j in range(plan.inner):
+            a, b = part[j], part[c - 1 - j]
+            out[j * strip : (j + 1) * strip, :] = jnp.concatenate([a + b, a - b], axis=1)
+    for k in range(BUF):
+        rows = slice(k * strip, (k + 1) * strip)
+        slo[rows, :] = jnp.concatenate([low[k], high[k]], axis=1)
+        shi[rows, :] = jnp.concatenate([low[c - BUF + k], high[c - BUF + k]], axis=1)
+
+
+def pack_kernel(plan, orb, rlo, rhi, inner):
     c, strip, face = plan.cells, plan.strip, plan.face
-    ybase = plan.inner * strip
-    ylo[ybase:, :] = vt[:, : plan.lanes]
-    yhi[ybase:, :] = vt[:, face - plan.lanes :]
+    half, rest = face // 2, face // 2 - plan.strip
+    for k in range(BUF):
+        rows = slice(k * rest, (k + 1) * rest)
+        for out, x in ((rlo, k), (rhi, c - BUF + k)):
+            out[rows, :] = jnp.concatenate([orb[x, strip:half], orb[x, half : face - strip]], axis=1)
     for j in range(plan.inner):
         a, b = orb[j], orb[c - 1 - j]
-        e = jnp.concatenate([a + b, a - b], axis=1)
-        inner[j] = e
-        ylo[j * strip : (j + 1) * strip, :] = e[:strip]
-        yhi[j * strip : (j + 1) * strip, :] = e[face - strip :]
+        inner[j] = jnp.concatenate([a + b, a - b], axis=1)
 
 
 def mirror(a, b):
@@ -296,7 +306,7 @@
 
 def inside_kernel(plan, inner, vx, wh, wl, vspread, acc, va, vd, order, xh, xl):
     order[...] = jnp.zeros(order.shape, F32)
-    spread_potential(plan, vx[...], plan.face, vspread, va, vd, 0)
+    spread_potential(plan, [(vx[...], plan.face)], vspread, va, vd)
     row_products(plan, lambda g: inner[g - BUF], BUF, plan.groups, wh, wl, xh, xl, acc)
 
 
@@ -341,10 +351,10 @@
 def halo_kernel(plan, paired, yh, vy, zi, coef, vspread, given, acc, xr, va, vd, xh, xl):
     g_all, lanes, strip, face = plan.groups, plan.lanes, plan.strip, plan.face
     zlo, zhi = sides(zi, paired)[::-1] if paired else zi
-    spread_potential(plan, vy[...], 2 * strip, vspread, va, vd, 0)
+    pots = [(vy[...], 2 * strip)] + [(piece[g_all * strip :, :], strip) for piece in (zlo, zhi)]
+    spread_potential(plan, pots, vspread, va, vd)
     for k, piece in enumerate((zlo, zhi)):
         at = (2 + k) * strip
-        spread_potential(plan, piece[g_all * strip :, :], strip, vspread, va, vd, at)
         for g in range(g_all):
             xr[g, at : at + strip, :] = piece[g * strip : (g + 1) * strip, :]
     for g in range(g_all):
@@ -368,8 +378,8 @@
     rest = 4 * strip
     xh[:rest, :] = xrh[...]
     xl[:rest, :] = xrl[...]
+    spread_potential(plan, [(piece[g_all * span :, :], span) for piece in (zlo, zhi)], vspread, va, vd)
     for k, piece in enumerate((zlo, zhi)):
-        spread_potential(plan, piece[g_all * span :, :], span, vspread, va, vd, k * span)
         for g in range(g_all):
             xc[g, k * span : (k + 1) * span, :] = piece[g * span : (g + 1) * span, :]
     for g in range(g_all):
@@ -520,11 +530,19 @@
         blocks[k] = face_block(plan, own, other, -1.0 if k % 2 == 0 else 1.0, 0.5)
 
 
-def xface_kernel(plan, diag, yz, ox, nx, blocks):
-    blocks[0] = diag[...]
+def xface_kernel(plan, diag, yz, ox, nx, blocks, local, sem):
+    copies = [
+        pltpu.make_async_copy(diag, blocks.at[0], sem.at[0]),
+        pltpu.make_async_copy(yz, blocks.at[3:7], sem.at[1]),
+        pltpu.make_async_copy(local, blocks.at[1:3], sem.at[2]),
+    ]
+    copies[0].start()
+    copies[1].start()
     for k in range(2):
-        blocks[1 + k] = face_block(plan, ox[k], nx[k], -1.0 if k == 0 else 1.0, 1.0)
-    blocks[3:] = yz[...]
+        local[k] = face_block(plan, ox[k], nx[k], -1.0 if k == 0 else 1.0, 1.0)
+    copies[2].start()
+    for copy in copies:
+        copy.wait()
 
 
 def near(*shape):
@@ -579,18 +597,18 @@
 
     srows, rrows, yrows = BUF * strip + 8, BUF * (face // 2 - strip), inner_all * strip + cells
     orb = orbitals.reshape(cells, face, width)
-    slo, shi, rlo, rhi, vt = call(
-        part(packx_kernel, plan),
-        [near(srows, lanes), near(srows, lanes), near(rrows, lanes), near(rrows, lanes), near(cells, face)],
+    slo, shi, ylo, yhi, vt = call(
+        part(strip_kernel, plan),
+        [near(srows, lanes), near(srows, lanes), near(yrows, lanes), near(yrows, lanes), near(cells, face)],
         [orb, potential.reshape(face, cells)],
-        [pltpu.VMEM((2 * BUF, face, width), F32), pltpu.VMEM((face, cells), F32), pltpu.SemaphoreType.DMA((2 * BUF + 1,))],
+        [near(cells, strip, width), near(cells, strip, width), near(face, cells), pltpu.SemaphoreType.DMA((3,))],
         far_in=(0, 1),
     )
+    from_ylo, from_yhi = shift(yhi, "gy", 1), shift(ylo, "gy", -1)
     from_slo, from_shi = shift(shi, "gx", 1), shift(slo, "gx", -1)
-    ylo, yhi, inner = call(
-        part(packy_kernel, plan), [near(yrows, lanes), near(yrows, lanes), near(inner_all, face, lanes)], [orb, vt],
-    )
-    from_ylo, from_yhi = shift(yhi, "gy", 1), shift(ylo, "gy", -1)
+    rlo, rhi, inner = call(
+        part(pack_kernel, plan), [near(rrows, lanes), near(rrows, lanes), near(inner_all, face, lanes)], [orb],
+    )
     from_rlo, from_rhi = shift(rhi, "gx", 1), shift(rlo, "gx", -1)
 
     ipick = np.zeros((2, face, lanes), np.float32)
@@ -604,7 +622,7 @@
                 cpick[side, y * cells + z, k * corner + y] = 1.0
     elo, ehi, vx = call(
         part(edge_kernel, plan), [near(srows, lanes), near(srows, lanes), near(plan.trows, face)], [vt, from_slo, from_shi, from_ylo],
-        flops=10**9,
+        flops=2*10**9,
     )
     from_elo, from_ehi = shift(ehi, "gy", 1), shift(elo, "gy", -1)
 
@@ -682,7 +700,10 @@
         far_out=(1,),
     )
     (yz,) = call(part(yzface_kernel, plan, paired), [near(4, width, width)], [my, mz, ny, nz])
-    (blocks,) = call(part(xface_kernel, plan), [far(7, width, width)], [diag, yz, mx, nx])
+    (blocks,) = call(
+        part(xface_kernel, plan), [far(7, width, width)], [diag, yz, mx, nx],
+        [near(2, width, width), pltpu.SemaphoreType.DMA((3,))], far_out=(0,),
+    )
     return basis.reshape(orbitals.shape), blocks[None, None, None]
 
 

time: 44.4 us -> 43.9 us (0.989)
  transfers between devices with their start and end apart: 15 -> 15, of which waited for: 2 -> 1; matrix products, arithmetic and copies ran while one was open for 0% -> 0% of each run, Pallas kernels for 26% -> 27%
where the time goes in v5:
time: 43.9 us; the launch traced here: 43.7 us
  Pallas kernels  21.1 us (48%)
  starting transfers between devices  20.8 us (47%)
  between operations  1.11 us (3%)
  waiting for transfers between devices  0.65 us (1%)
    pallas_call x12, Pallas kernels, call(): pl.pallas_call(kernel, out_shape=outs, in_specs=[apart if i in far_in els...  21.1 us
    ppermute x15, starting transfers between devices, shift(): lax.ppermute(array, axis, [(i, (i + step) % count) for i in range(count)])  20.8 us
  transfers between devices with their start and end apart: 15, of which 1 were waited for; matrix products, arithmetic and copies ran while one was open for 0% of the time, Pallas kernels for 27%

profile of v5, /device:TPU:0, one launch (start us, length us, event | category | flops | bytes accessed | tf_op | source)
XLA Modules:
  0.0 43.7 jit_solution(195531862745971957)
XLA Ops:
  0.6 0.0 copy-start
  0.6 1.6 %shard_map.167 = (f32[152,128]{1,0:T(8,128)S(1)}, f32[152,128]{1,0:T(8,128)S(1)}, f32[400,128]{1,0:T(8,128)S(1)}, f32[400,128]{1,0:T(8,128)S(1)}, f32[16,256]{1,0:T(8,128)S(1)}) custom-call(f32[16,256,64]{2,1,0:T(8,128)} %bitcast.4, f32[256,16]{1,0:T(8,128)} %bitcast.7), custom_call_target="tpu_custom_call" | custom-call | tf_op jit(solution)/shard_map/pallas_call | solution.py:562
  2.2 3.1 %collective-permute-start = (f32[400,128]{1,0:T(8,128)S(1)}, f32[400,128]{1,0:T(8,128)S(1)}, u32[]{:S(2)}, u32[]{:S(2)}) collective-permute-start(f32[400,128]{1,0:T(8,128)S(1)} %get-tuple-element.38), channel_id=1, source_target_pairs={{0,2},{2,4},{4,6},{6,0},{1,3},{3,5},{5,7},{7,1},{8,10},{10,12},{12... | collective-permute-start | bytes 614408 | tf_op jit(solution)/shard_map/ppermute | solution.py:576
  5.3 1.5 %collective-permute-start.2 = (f32[152,128]{1,0:T(8,128)S(1)}, f32[152,128]{1,0:T(8,128)S(1)}, u32[]{:S(2)}, u32[]{:S(2)}) collective-permute-start(f32[152,128]{1,0:T(8,128)S(1)} %get-tuple-element.41), channel_id=1, source_target_pairs={{0,8},{8,16},{16,24},{24,0},{1,9},{9,17},{17,25},{25,1},{2,10},{10... | collective-permute-start | bytes 233480 | tf_op jit(solution)/shard_map/ppermute | solution.py:576
  6.8 1.4 %collective-permute-start.3 = (f32[152,128]{1,0:T(8,128)S(1)}, f32[152,128]{1,0:T(8,128)S(1)}, u32[]{:S(2)}, u32[]{:S(2)}) collective-permute-start(f32[152,128]{1,0:T(8,128)S(1)} %get-tuple-element.42), channel_id=1, source_target_pairs={{0,24},{8,0},{16,8},{24,16},{1,25},{9,1},{17,9},{25,17},{2,26},{10... | collective-permute-start | bytes 233480 | tf_op jit(solution)/shard_map/ppermute | solution.py:576
  8.2 2.1 %collective-permute-start.1 = (f32[400,128]{1,0:T(8,128)S(1)}, f32[400,128]{1,0:T(8,128)S(1)}, u32[]{:S(2)}, u32[]{:S(2)}) collective-permute-start(f32[400,128]{1,0:T(8,128)S(1)} %get-tuple-element.39), channel_id=1, source_target_pairs={{0,6},{2,0},{4,2},{6,4},{1,7},{3,1},{5,3},{7,5},{8,14},{10,8},{12,... | collective-permute-start | bytes 614408 | tf_op jit(solution)/shard_map/ppermute | solution.py:576
  10.3 0.0 copy-done
  10.3 0.4 shard_map.169
  10.7 0.8 %collective-permute-start.6 = (f32[240,128]{1,0:T(8,128)S(1)}, f32[240,128]{1,0:T(8,128)S(1)}, u32[]{:S(2)}, u32[]{:S(2)}) collective-permute-start(f32[240,128]{1,0:T(8,128)S(1)} %get-tuple-element.47), channel_id=1, source_target_pairs={{0,8},{8,16},{16,24},{24,0},{1,9},{9,17},{17,25},{25,1},{2,10},{10... | collective-permute-start | bytes 368648 | tf_op jit(solution)/shard_map/ppermute | solution.py:576
  11.5 0.0 collective-permute-done.2.lo
  11.5 2.2 %collective-permute-start.7 = (f32[240,128]{1,0:T(8,128)S(1)}, f32[240,128]{1,0:T(8,128)S(1)}, u32[]{:S(2)}, u32[]{:S(2)}) collective-permute-start(f32[240,128]{1,0:T(8,128)S(1)} %get-tuple-element.48), channel_id=1, source_target_pairs={{0,24},{8,0},{16,8},{24,16},{1,25},{9,1},{17,9},{25,17},{2,26},{10... | collective-permute-start | bytes 368648 | tf_op jit(solution)/shard_map/ppermute | solution.py:576
  13.7 0.0 collective-permute-done.3.hi
  13.7 0.0 collective-permute-done.ahead.ylo
  13.7 0.0 copy-start.2
  13.7 0.0 copy-start.3
  13.7 0.1 shard_map.168
  13.8 0.0 copy-start.7
  13.9 0.0 copy-start.6
  13.9 0.9 %collective-permute-start.4 = (f32[152,128]{1,0:T(8,128)S(1)}, f32[152,128]{1,0:T(8,128)S(1)}, u32[]{:S(2)}, u32[]{:S(2)}) collective-permute-start(f32[152,128]{1,0:T(8,128)S(1)} %get-tuple-element.43.ehi), channel_id=1, source_target_pairs={{0,2},{2,4},{4,6},{6,0},{1,3},{3,5},{5,7},{7,1},{8,10},{10,12},{12... | collective-permute-start | bytes 233480 | tf_op jit(solution)/shard_map/ppermute | solution.py:576
  14.8 3.0 %collective-permute-start.5 = (f32[152,128]{1,0:T(8,128)S(1)}, f32[152,128]{1,0:T(8,128)S(1)}, u32[]{:S(2)}, u32[]{:S(2)}) collective-permute-start(f32[152,128]{1,0:T(8,128)S(1)} %get-tuple-element.44.elo), channel_id=1, source_target_pairs={{0,6},{2,0},{4,2},{6,4},{1,7},{3,1},{5,3},{7,5},{8,14},{10,8},{12,... | collective-permute-start | bytes 233480 | tf_op jit(solution)/shard_map/ppermute | solution.py:576
  17.7 0.0 copy-done.1
  17.7 0.0 copy-done.3
  17.8 1.4 %shard_map.170 = (f32[11,496,128]{2,1,0:T(8,128)S(1)}, f32[11,256,128]{2,1,0:T(8,128)S(1)}, f32[11,256,128]{2,1,0:T(8,128)S(1)}, f32[8,128]{1,0:T(8,128)S(1)}) custom-call(f32[8,256,128]{2,1,0:T(8,128)S(1)} %get-tuple-element.45.inner, f32[24,256]{1,0:T(8,128)S(1)} %get-tuple-element.46.vx, bf16[496,256]{1,0:T(8,128)(2,1)S(1)} %copy-done.3, ...), custom_call_target="tpu_custom_call" | custom-call | tf_op jit(solution)/shard_map/pallas_call | solution.py:562
  19.2 0.0 collective-permute-done.6.lo
  19.2 0.0 collective-permute-done.7.hi
  19.2 0.4 shard_map.171
  19.6 0.1 collective-permute-start.9
  19.7 0.0 copy-done.6
  19.7 0.0 copy-start.13
  19.7 1.5 %shard_map.172 = (f32[11,496,128]{2,1,0:T(8,128)S(1)}, f32[8,128]{1,0:T(8,128)S(1)}) custom-call(f32[8,256,128]{2,1,0:T(8,128)S(1)} %get-tuple-element.45.inner, f32[3,256,128]{2,1,0:T(8,128)S(1)} %get-tuple-element.50.outer, bf16[496,256]{1,0:T(8,128)(2,1)S(1)} %copy-done.3, bf16[496,256]{1,0:T(8,128)(2,1)S(1)} %copy-done.2, ...), custom_call_target="tpu_custom_call", output_to_operand_aliasing={{0}: (7, {})} | custom-call | tf_op jit(solution)/shard_map/pallas_call | solution.py:562
  21.3 0.0 collective-permute-done.1.yhi
  21.3 0.0 collective-permute-done.4.elo
  21.3 0.0 collective-permute-done.5.ehi
  21.3 0.0 copy-done.13
  21.3 0.4 shard_map.173
  21.7 0.5 %collective-permute-start.8 = (f32[2,288,128]{2,1,0:T(8,128)S(1)}, f32[2,288,128]{2,1,0:T(8,128)S(1)}, u32[]{:S(2)}, u32[]{:S(2)}) collective-permute-start(f32[2,288,128]{2,1,0:T(8,128)S(1)} %get-tuple-element.55), channel_id=1, source_target_pairs={{0,1},{1,0},{2,3},{3,2},{4,5},{5,4},{6,7},{7,6},{8,9},{9,8},{10,11... | collective-permute-start | bytes 884744 | tf_op jit(solution)/shard_map/ppermute | solution.py:576
  22.2 0.0 collective-permute-done.9.zi
  22.2 0.0 copy-start.9
  22.2 0.0 copy-start.10
  22.3 1.5 %shard_map.174 = (f32[11,496,128]{2,1,0:T(8,128)S(1)}, f32[11,192,128]{2,1,0:T(8,128)S(1)}, f32[11,192,128]{2,1,0:T(8,128)S(1)}, f32[11,192,128]{2,1,0:T(8,128)S...) custom-call(f32[11,128,128]{2,1,0:T(8,128)S(1)} %get-tuple-element.56.yh, ...), custom_call_target="tpu_custom_call", output_to_operand_aliasing={{0}: (5, {})} | custom-call | tf_op jit(solution)/shard_map/pallas_call | solution.py:562
  23.7 0.0 collective-permute-done.8.zc
  23.7 0.0 copy-done.4
  23.7 0.0 copy-done.5
  23.8 0.0 copy-done.8
  23.8 0.0 copy-done.9
  23.8 0.0 copy-done.10
  23.8 0.0 copy-start.11
  23.8 0.0 copy-start.12
  23.8 0.0 copy-start.14
  23.8 6.9 %shard_map.175 = (f32[11,448,128]{2,1,0:T(8,128)S(1)}, f32[256,128]{1,0:T(8,128)S(1)}, f32[256,128]{1,0:T(8,128)S(1)}, f32[256,128]{1,0:T(8,128)S(1)}, f32[256,1...) custom-call(f32[2,288,128]{2,1,0:T(8,128)S(1)} %collective-permute-done.8.zc, f32[8,256,128]{2,1,0:T(8,128)S(1)} %get-tuple-element.45.inner, ...), custom_call_target="tpu_custom_call" | custom-call | tf_op jit(solution)/shard_map/pallas_call | solution.py:562
  30.8 0.1 collective-permute-start.12
  30.9 2.6 %collective-permute-start.11 = (f32[256,128]{1,0:T(8,128)S(1)}, f32[256,128]{1,0:T(8,128)S(1)}, u32[]{:S(2)}, u32[]{:S(2)}) collective-permute-start(f32[256,128]{1,0:T(8,128)S(1)} %get-tuple-element.69.oy_0_), channel_id=1, source_target_pairs={{0,6},{2,0},{4,2},{6,4},{1,7},{3,1},{5,3},{7,5},{8,14},{10,8},{12,... | collective-permute-start | bytes 393224 | tf_op jit(solution)/shard_map/ppermute | solution.py:576
  33.5 0.0 collective-permute-start.10
  33.5 2.6 %collective-permute-start.14 = (f32[256,128]{1,0:T(8,128)S(1)}, f32[256,128]{1,0:T(8,128)S(1)}, u32[]{:S(2)}, u32[]{:S(2)}) collective-permute-start(f32[256,128]{1,0:T(8,128)S(1)} %get-tuple-element.72.ox_0_), channel_id=1, source_target_pairs={{0,24},{8,0},{16,8},{24,16},{1,25},{9,1},{17,9},{25,17},{2,26},{10... | collective-permute-start | bytes 393224 | tf_op jit(solution)/shard_map/ppermute | solution.py:576
  36.1 0.0 collective-permute-start.13
  36.1 0.0 copy-done.12
  36.1 5.4 %shard_map.176 = (f32[64,64]{1,0:T(8,128)S(1)}, f32[16,256,64]{2,1,0:T(8,128)}) custom-call(f32[11,448,128]{2,1,0:T(8,128)S(1)} %get-tuple-element.66.f, f32[11,256,128]{2,1,0:T(8,128)S(1)} %get-tuple-element.51.va.vai, f32[11,256,128]{2,1,0:T(8,128)S(1)} %get-tuple-element.52.vd.vdi, bf16[448,448]{1,0:T(8,128)(2,1)S(1)} %copy-done.12, ...), custom_call_target="tpu_custom_call" | custom-call | flops 2000000000 | tf_op jit(solution)/shard_map/pallas_call | solution.py:562
  41.5 0.0 collective-permute-done.11.ny_1_
  41.5 0.0 collective-permute-done.10.ny_0_
  41.5 0.0 collective-permute-done.12.nz
  41.5 0.4 shard_map.177.yz
  42.0 0.0 collective-permute-done.14.nx_1_
  42.0 0.6 %collective-permute-done.13.nx_0_ = f32[256,128]{1,0:T(8,128)S(1)} collective-permute-done((f32[256,128]{1,0:T(8,128)S(1)}, f32[256,128]{1,0:T(8,128)S(1)}, u32[]{:S(2)}, u32[]{:S(2)}) %collective-permute-start.13) | collective-permute-done | bytes 131104 | tf_op jit(solution)/shard_map/ppermute | solution.py:576
  42.6 1.0 %shard_map.178 = f32[7,64,64]{2,1,0:T(8,128)} custom-call(f32[64,64]{1,0:T(8,128)S(1)} %get-tuple-element.68.diag, f32[4,64,64]{2,1,0:T(8,128)S(1)} %shard_map.177.yz, f32[256,128]{1,0:T(8,128)S(1)} %get-tuple-element.72.ox_0_, f32[256,128]{1,0:T(8,128)S(1)} %get-tuple-element.73.ox_1_, f32[256,128]{1,0:T(8,128)S(1)} %collective-permute-done.13.nx_0_, ...), custom_call_target="tpu_custom_call" | custom-call | tf_op jit(solution)/shard_map/pallas_call | solution.py:562
  (8 shorter events, 0.0 us)
Async XLA Ops:
  0.6 9.7 %copy-start = (f32[16,16,16,64]{3,2,1,0:T(8,128)S(1)}, f32[16,16,16,64]{3,2,1,0:T(8,128)}, u32[]{:S(2)}) copy-start(f32[16,16,16,64]{3,2,1,0:T(8,128)} %param.16) | copy-start | bytes 3145732
  2.2 11.5 %collective-permute-start = (f32[400,128]{1,0:T(8,128)S(1)}, f32[400,128]{1,0:T(8,128)S(1)}, u32[]{:S(2)}, u32[]{:S(2)}) collective-permute-start(f32[400,128]{1,0:T(8,128)S(1)} %get-tuple-element.38), channel_id=1, source_target_pairs={{0,2},{2,4},{4,6},{6,0},{1,3},{3,5},{5,7},{7,1},{8,10},{10,12},{12... | collective-permute-start | bytes 614408 | tf_op jit(solution)/shard_map/ppermute | solution.py:576
  5.3 6.2 %collective-permute-start.2 = (f32[152,128]{1,0:T(8,128)S(1)}, f32[152,128]{1,0:T(8,128)S(1)}, u32[]{:S(2)}, u32[]{:S(2)}) collective-permute-start(f32[152,128]{1,0:T(8,128)S(1)} %get-tuple-element.41), channel_id=1, source_target_pairs={{0,8},{8,16},{16,24},{24,0},{1,9},{9,17},{17,25},{25,1},{2,10},{10... | collective-permute-start | bytes 233480 | tf_op jit(solution)/shard_map/ppermute | solution.py:576
  6.8 6.9 %collective-permute-start.3 = (f32[152,128]{1,0:T(8,128)S(1)}, f32[152,128]{1,0:T(8,128)S(1)}, u32[]{:S(2)}, u32[]{:S(2)}) collective-permute-start(f32[152,128]{1,0:T(8,128)S(1)} %get-tuple-element.42), channel_id=1, source_target_pairs={{0,24},{8,0},{16,8},{24,16},{1,25},{9,1},{17,9},{25,17},{2,26},{10... | collective-permute-start | bytes 233480 | tf_op jit(solution)/shard_map/ppermute | solution.py:576
  8.2 13.1 %collective-permute-start.1 = (f32[400,128]{1,0:T(8,128)S(1)}, f32[400,128]{1,0:T(8,128)S(1)}, u32[]{:S(2)}, u32[]{:S(2)}) collective-permute-start(f32[400,128]{1,0:T(8,128)S(1)} %get-tuple-element.39), channel_id=1, source_target_pairs={{0,6},{2,0},{4,2},{6,4},{1,7},{3,1},{5,3},{7,5},{8,14},{10,8},{12,... | collective-permute-start | bytes 614408 | tf_op jit(solution)/shard_map/ppermute | solution.py:576
  10.7 8.5 %collective-permute-start.6 = (f32[240,128]{1,0:T(8,128)S(1)}, f32[240,128]{1,0:T(8,128)S(1)}, u32[]{:S(2)}, u32[]{:S(2)}) collective-permute-start(f32[240,128]{1,0:T(8,128)S(1)} %get-tuple-element.47), channel_id=1, source_target_pairs={{0,8},{8,16},{16,24},{24,0},{1,9},{9,17},{17,25},{25,1},{2,10},{10... | collective-permute-start | bytes 368648 | tf_op jit(solution)/shard_map/ppermute | solution.py:576
  11.5 7.7 %collective-permute-start.7 = (f32[240,128]{1,0:T(8,128)S(1)}, f32[240,128]{1,0:T(8,128)S(1)}, u32[]{:S(2)}, u32[]{:S(2)}) collective-permute-start(f32[240,128]{1,0:T(8,128)S(1)} %get-tuple-element.48), channel_id=1, source_target_pairs={{0,24},{8,0},{16,8},{24,16},{1,25},{9,1},{17,9},{25,17},{2,26},{10... | collective-permute-start | bytes 368648 | tf_op jit(solution)/shard_map/ppermute | solution.py:576
  13.7 4.1 %copy-start.1 = (bf16[72,2816]{1,0:T(8,128)(2,1)S(1)}, bf16[72,2816]{1,0:T(8,128)(2,1)}, u32[]{:S(2)}) copy-start(bf16[72,2816]{1,0:T(8,128)(2,1)} %constant.30.clone.vspread) | copy-start | bytes 1216516
  13.7 4.0 %copy-start.2 = (bf16[496,256]{1,0:T(8,128)(2,1)S(1)}, bf16[496,256]{1,0:T(8,128)(2,1)}, u32[]{:S(2)}) copy-start(bf16[496,256]{1,0:T(8,128)(2,1)} %constant.29.clone.wl) | copy-start | bytes 761860
  13.7 4.0 %copy-start.3 = (bf16[496,256]{1,0:T(8,128)(2,1)S(1)}, bf16[496,256]{1,0:T(8,128)(2,1)}, u32[]{:S(2)}) copy-start(bf16[496,256]{1,0:T(8,128)(2,1)} %constant.28.clone.wh) | copy-start | bytes 761860
  13.8 5.4 %copy-start.7 = (f32[2,256,128]{2,1,0:T(8,128)S(1)}, f32[2,256,128]{2,1,0:T(8,128)}, u32[]{:S(2)}) copy-start(f32[2,256,128]{2,1,0:T(8,128)} %constant.31.clone.zpick) | copy-start | bytes 786436
  13.9 5.9 %copy-start.6 = (f32[61,128]{1,0:T(8,128)S(1)}, f32[61,128]{1,0:T(8,128)}, u32[]{:S(2)}) copy-start(f32[61,128]{1,0:T(8,128)} %constant.32.clone.coef) | copy-start | bytes 93700
  13.9 7.4 %collective-permute-start.4 = (f32[152,128]{1,0:T(8,128)S(1)}, f32[152,128]{1,0:T(8,128)S(1)}, u32[]{:S(2)}, u32[]{:S(2)}) collective-permute-start(f32[152,128]{1,0:T(8,128)S(1)} %get-tuple-element.43.ehi), channel_id=1, source_target_pairs={{0,2},{2,4},{4,6},{6,0},{1,3},{3,5},{5,7},{7,1},{8,10},{10,12},{12... | collective-permute-start | bytes 233480 | tf_op jit(solution)/shard_map/ppermute | solution.py:576
  14.8 6.5 %collective-permute-start.5 = (f32[152,128]{1,0:T(8,128)S(1)}, f32[152,128]{1,0:T(8,128)S(1)}, u32[]{:S(2)}, u32[]{:S(2)}) collective-permute-start(f32[152,128]{1,0:T(8,128)S(1)} %get-tuple-element.44.elo), channel_id=1, source_target_pairs={{0,6},{2,0},{4,2},{6,4},{1,7},{3,1},{5,3},{7,5},{8,14},{10,8},{12,... | collective-permute-start | bytes 233480 | tf_op jit(solution)/shard_map/ppermute | solution.py:576
  19.6 2.6 %collective-permute-start.9 = (f32[2,552,128]{2,1,0:T(8,128)S(1)}, f32[2,552,128]{2,1,0:T(8,128)S(1)}, u32[]{:S(2)}, u32[]{:S(2)}) collective-permute-start(f32[2,552,128]{2,1,0:T(8,128)S(1)} %get-tuple-element.58), channel_id=1, source_target_pairs={{0,1},{1,0},{2,3},{3,2},{4,5},{5,4},{6,7},{7,6},{8,9},{9,8},{10,11... | collective-permute-start | bytes 1695752 | tf_op jit(solution)/shard_map/ppermute | solution.py:576
  19.7 1.6 %copy-start.13 = (f32[2,128,128]{2,1,0:T(8,128)S(1)}, f32[2,128,128]{2,1,0:T(8,128)}, u32[]{:S(2)}) copy-start(f32[2,128,128]{2,1,0:T(8,128)} %constant.33.clone.zpick) | copy-start | bytes 393220
  21.7 2.0 %collective-permute-start.8 = (f32[2,288,128]{2,1,0:T(8,128)S(1)}, f32[2,288,128]{2,1,0:T(8,128)S(1)}, u32[]{:S(2)}, u32[]{:S(2)}) collective-permute-start(f32[2,288,128]{2,1,0:T(8,128)S(1)} %get-tuple-element.55), channel_id=1, source_target_pairs={{0,1},{1,0},{2,3},{3,2},{4,5},{5,4},{6,7},{7,6},{8,9},{9,8},{10,11... | collective-permute-start | bytes 884744 | tf_op jit(solution)/shard_map/ppermute | solution.py:576
  22.2 1.5 %copy-start.4 = (bf16[448,496]{1,0:T(8,128)(2,1)S(1)}, bf16[448,496]{1,0:T(8,128)(2,1)}, u32[]{:S(2)}) copy-start(bf16[448,496]{1,0:T(8,128)(2,1)} %constant.37.clone.wl) | copy-start | bytes 1333252
  22.2 1.5 %copy-start.5 = (bf16[448,496]{1,0:T(8,128)(2,1)S(1)}, bf16[448,496]{1,0:T(8,128)(2,1)}, u32[]{:S(2)}) copy-start(bf16[448,496]{1,0:T(8,128)(2,1)} %constant.36.clone.wh) | copy-start | bytes 1333252
  22.2 1.5 %copy-start.8 = (bf16[496,240]{1,0:T(8,128)(2,1)S(1)}, bf16[496,240]{1,0:T(8,128)(2,1)}, u32[]{:S(2)}) copy-start(bf16[496,240]{1,0:T(8,128)(2,1)} %constant.35.clone.wrl) | copy-start | bytes 714244
  22.2 1.5 %copy-start.9 = (bf16[496,240]{1,0:T(8,128)(2,1)S(1)}, bf16[496,240]{1,0:T(8,128)(2,1)}, u32[]{:S(2)}) copy-start(bf16[496,240]{1,0:T(8,128)(2,1)} %constant.34.clone.wrh) | copy-start | bytes 714244
  22.2 1.5 %copy-start.10 = (f32[11,128]{1,0:T(8,128)S(1)}, f32[11,128]{1,0:T(8,128)}, u32[]{:S(2)}) copy-start(f32[11,128]{1,0:T(8,128)} %constant.38.clone.dcoef) | copy-start | bytes 16900
  23.8 12.3 %copy-start.11 = (bf16[448,448]{1,0:T(8,128)(2,1)S(1)}, bf16[448,448]{1,0:T(8,128)(2,1)}, u32[]{:S(2)}) copy-start(bf16[448,448]{1,0:T(8,128)(2,1)} %constant.40.clone.bl) | copy-start | bytes 1204228
  23.8 12.3 %copy-start.12 = (bf16[448,448]{1,0:T(8,128)(2,1)S(1)}, bf16[448,448]{1,0:T(8,128)(2,1)}, u32[]{:S(2)}) copy-start(bf16[448,448]{1,0:T(8,128)(2,1)} %constant.39.clone.bh) | copy-start | bytes 1204228
  23.8 12.3 %copy-start.14 = (f32[121,128]{1,0:T(8,128)S(1)}, f32[121,128]{1,0:T(8,128)}, u32[]{:S(2)}) copy-start(f32[121,128]{1,0:T(8,128)} %constant.41.clone.coef) | copy-start | bytes 185860
  30.8 10.8 %collective-permute-start.12 = (f32[2,256,128]{2,1,0:T(8,128)S(1)}, f32[2,256,128]{2,1,0:T(8,128)S(1)}, u32[]{:S(2)}, u32[]{:S(2)}) collective-permute-start(f32[2,256,128]{2,1,0:T(8,128)S(1)} %get-tuple-element.71.oz), channel_id=1, source_target_pairs={{0,1},{1,0},{2,3},{3,2},{4,5},{5,4},{6,7},{7,6},{8,9},{9,8},{10,11... | collective-permute-start | bytes 786440 | tf_op jit(solution)/shard_map/ppermute | solution.py:576
  30.9 10.6 %collective-permute-start.11 = (f32[256,128]{1,0:T(8,128)S(1)}, f32[256,128]{1,0:T(8,128)S(1)}, u32[]{:S(2)}, u32[]{:S(2)}) collective-permute-start(f32[256,128]{1,0:T(8,128)S(1)} %get-tuple-element.69.oy_0_), channel_id=1, source_target_pairs={{0,6},{2,0},{4,2},{6,4},{1,7},{3,1},{5,3},{7,5},{8,14},{10,8},{12,... | collective-permute-start | bytes 393224 | tf_op jit(solution)/shard_map/ppermute | solution.py:576
  33.5 8.0 %collective-permute-start.10 = (f32[256,128]{1,0:T(8,128)S(1)}, f32[256,128]{1,0:T(8,128)S(1)}, u32[]{:S(2)}, u32[]{:S(2)}) collective-permute-start(f32[256,128]{1,0:T(8,128)S(1)} %get-tuple-element.70.oy_1_), channel_id=1, source_target_pairs={{0,2},{2,4},{4,6},{6,0},{1,3},{3,5},{5,7},{7,1},{8,10},{10,12},{12... | collective-permute-start | bytes 393224 | tf_op jit(solution)/shard_map/ppermute | solution.py:576
  33.5 8.5 %collective-permute-start.14 = (f32[256,128]{1,0:T(8,128)S(1)}, f32[256,128]{1,0:T(8,128)S(1)}, u32[]{:S(2)}, u32[]{:S(2)}) collective-permute-start(f32[256,128]{1,0:T(8,128)S(1)} %get-tuple-element.72.ox_0_), channel_id=1, source_target_pairs={{0,24},{8,0},{16,8},{24,16},{1,25},{9,1},{17,9},{25,17},{2,26},{10... | collective-permute-start | bytes 393224 | tf_op jit(solution)/shard_map/ppermute | solution.py:576
  36.1 6.5 %collective-permute-start.13 = (f32[256,128]{1,0:T(8,128)S(1)}, f32[256,128]{1,0:T(8,128)S(1)}, u32[]{:S(2)}, u32[]{:S(2)}) collective-permute-start(f32[256,128]{1,0:T(8,128)S(1)} %get-tuple-element.73.ox_1_), channel_id=1, source_target_pairs={{0,8},{8,16},{16,24},{24,0},{1,9},{9,17},{17,25},{25,1},{2,10},{10... | collective-permute-start | bytes 393224 | tf_op jit(solution)/shard_map/ppermute | solution.py:576

commit v6 on v5

--- a/solution.py
+++ b/solution.py
@@ -36,8 +36,12 @@
         outside = list(range(BUF)) + list(range(BUF + cells, self.ext))
         points = [(y, z) for y in inside for z in inside] + [(y, z) for y in outside for z in inside]
         points += [(y, z) for z in outside for y in inside]
+        gap = self.corner - 2 * BUF
         for z in outside:
-            points += [(y, z) for y in outside] + [None] * (self.corner - 2 * BUF)
+            points += [(y, z) for y in outside[:BUF]] + [None] * gap + [(y, z) for y in outside[BUF:]]
+        self.fold = self.rows // 2
+        self.flat = self.cross // 2
+        self.lot = -(-self.fold // 16) * 16
         self.points = points
         self.first, self.second = spectral(self.ext)
         self.inside = np.isin(np.arange(self.ext), inside)
@@ -66,6 +70,28 @@
     return (by_y + by_z) * real[:, None] * real[None, :]
 
 
+def mirror_basis(plan):
+    c, face, strip = plan.cells, plan.face, plan.strip
+    kept = [(y * c + z, (c - 1 - y) * c + z) for y in range(c // 2) for z in range(c)]
+    kept += [(face + k * c + z, face + (2 * BUF - 1 - k) * c + z) for k in range(BUF) for z in range(c)]
+    kept += [(plan.yext + k * c + y, plan.yext + k * c + c - 1 - y) for k in range(2 * BUF) for y in range(c // 2)]
+    for m in range(BUF):
+        for r in range(plan.corner):
+            at = plan.cross + (2 * m + (r >= plan.corner // 2)) * plan.corner
+            kept.append((at + r, at + plan.corner - 1 - r))
+    out = np.zeros((2, plan.lot, plan.rows))
+    for i, (a, b) in enumerate(kept):
+        out[:, i, a] += 1.0
+        out[0, i, b] += 1.0
+        out[1, i, b] -= 1.0
+    return out
+
+
+def folded_rows(plan, matrix):
+    basis = mirror_basis(plan)
+    return 0.25 * np.einsum("pia,ab,pjb->pij", basis, matrix, basis, optimize=True)
+
+
 def mirrored(plan, along):
     g = plan.groups
     plus = along[:g, :g] + along[:g, ::-1][:, :g]
@@ -125,6 +151,89 @@
 
 def three(wh, wl, sh, sl):
     return dot(wh, sh) + dot(wl, sh) + dot(wh, sl)
+
+
+def flip(x):
+    row = lax.broadcasted_iota(jnp.int32, x.shape, 0)
+    x = pltpu.roll(x, 4, 0)
+    x = jnp.where(lax.rem(row, 4) < 2, pltpu.roll(x, 6, 0), pltpu.roll(x, 2, 0))
+    return jnp.where(lax.rem(row, 2) < 1, pltpu.roll(x, 7, 0), pltpu.roll(x, 1, 0))
+
+
+def put_folded(sh, sl, lot, at, cols, plus, minus):
+    for p, value in enumerate((plus, minus)):
+        h, l = split(value)
+        sh[p * lot + at : p * lot + at + value.shape[0], cols] = h
+        sl[p * lot + at : p * lot + at + value.shape[0], cols] = l
+
+
+def fold_blocks(blocks, put, at):
+    a, b = blocks
+    put(at, a + b, a - b)
+
+
+def fold_planes(blocks, put, at):
+    firsts, lasts = [p[:8] for p in blocks], [flip(p[8:]) for p in blocks]
+    put(at, jnp.concatenate([a + b for a, b in zip(firsts, lasts)], axis=0),
+        jnp.concatenate([a - b for a, b in zip(firsts, lasts)], axis=0))
+
+
+def fold_corners(blocks, put, at):
+    plus, minus = [], []
+    for block in blocks:
+        a, b = block[:8], block[8:]
+        fa, fb = flip(a), flip(b)
+        first = lax.broadcasted_iota(jnp.int32, a.shape, 0) < 4
+        plus.append(jnp.where(first, a + fa, b + fb))
+        minus.append(jnp.where(first, a - fa, b - fb))
+    zero = jnp.zeros_like(plus[0])
+    put(at, jnp.concatenate(plus + [zero], axis=0), jnp.concatenate(minus + [zero], axis=0))
+
+
+def fold_inside(plan, get, put):
+    c = plan.cells
+    for y in range(c // 2):
+        fold_blocks([get(y * c, c), get((c - 1 - y) * c, c)], put, y * c)
+
+
+def fold_halo(plan, get, put):
+    c = plan.cells
+    for k in range(BUF):
+        fold_blocks([get(k * c, c), get((2 * BUF - 1 - k) * c, c)], put, plan.face // 2 + k * c)
+    at = 2 * plan.strip
+    for k in range(0, 2 * BUF, 2):
+        fold_planes([get(at + k * c, c), get(at + (k + 1) * c, c)], put, plan.yext // 2 + k * 8)
+
+
+def unfold(plan, v0, v1, corners):
+    c = plan.cells
+
+    def both(at, n):
+        a, b = v0(at, n), v1(at, n)
+        return a + b, a - b
+
+    for y in range(c // 2):
+        a, b = both(y * c, c)
+        yield fold_blocks, y * c, [(y * c, a), ((c - 1 - y) * c, b)]
+    at = plan.face // 2
+    for k in range(BUF):
+        a, b = both(at + k * c, c)
+        yield fold_blocks, at + k * c, [(plan.face + k * c, a), (plan.face + (2 * BUF - 1 - k) * c, b)]
+    at = plan.yext // 2
+    for k in range(0, 2 * BUF, 2):
+        made = []
+        for m in (k, k + 1):
+            a, b = both(at + m * 8, 8)
+            made.append((plan.yext + m * c, jnp.concatenate([a, flip(b)], axis=0)))
+        yield fold_planes, at + k * 8, made
+    if corners:
+        at, made = plan.cross // 2, []
+        for m in range(BUF):
+            a, b = both(at + m * 8, 8)
+            first = lax.broadcasted_iota(jnp.int32, a.shape, 0) < 4
+            b = flip(b)
+            made.append((plan.cross + m * 16, jnp.concatenate([jnp.where(first, a, b), jnp.where(first, b, a)], axis=0)))
+        yield fold_corners, at, made
 
 
 def low_lanes(shape):
@@ -177,12 +286,12 @@
 
 def spread_potential(plan, pieces, vspread, va, vd):
     turned = []
-    for piece, count in pieces:
+    for piece, start, stop in pieces:
         high = piece.astype(BF).astype(F32)
         rest = piece - high
         mid = rest.astype(BF).astype(F32)
         stacked = jnp.concatenate([high, mid, rest - mid], axis=0)
-        turned.append(jnp.transpose(stacked)[:count, :])
+        turned.append(jnp.transpose(stacked)[start:stop, :])
     turned = jnp.concatenate(turned, axis=0).astype(BF)
     g_all, lanes = plan.groups, plan.lanes
     for g0, g1 in pairs(g_all):
@@ -291,50 +400,40 @@
         dst[plan.groups * strip :, :] = exact(vx[...], zpick[side])
 
 
-def row_products(plan, get, first, stop, wh, wl, xh, xl, acc):
+def inside_kernel(plan, vx, vspread, va, vd, order):
+    order[...] = jnp.zeros(order.shape, F32)
+    spread_potential(plan, [(vx[...], 0, plan.face)], vspread, va, vd)
+
+
+def outside_kernel(plan, inner, outer, coef, va, vd, acc, order, sh, sl):
+    order[...] = jnp.zeros(order.shape, F32)
     lanes = plan.lanes
-    for g in range(first, stop):
-        h, l = split(get(g))
-        xh[:, (g - first) * lanes : (g - first + 1) * lanes] = h
-        xl[:, (g - first) * lanes : (g - first + 1) * lanes] = l
-    for g0, g1 in pairs(stop, first):
-        cols = slice((g0 - first) * lanes, (g1 - first) * lanes)
-        total = three(wh[...], wl[...], xh[:, cols], xl[:, cols])
-        for g in range(g0, g1):
-            acc[g] = total[:, (g - g0) * lanes : (g - g0 + 1) * lanes]
-
-
-def inside_kernel(plan, inner, vx, wh, wl, vspread, acc, va, vd, order, xh, xl):
-    order[...] = jnp.zeros(order.shape, F32)
-    spread_potential(plan, [(vx[...], plan.face)], vspread, va, vd)
-    row_products(plan, lambda g: inner[g - BUF], BUF, plan.groups, wh, wl, xh, xl, acc)
-
-
-def outside_kernel(plan, inner, outer, wh, wl, coef, va, vd, given, acc, order, xh, xl):
-    order[...] = jnp.zeros(order.shape, F32)
-    row_products(plan, lambda g: outer[g], 0, BUF, wh, wl, xh, xl, acc)
 
     def get(g, r0, r1):
         return outer[g, r0:r1, :] if g < BUF else inner[g - BUF, r0:r1, :]
 
+    for g in range(plan.groups):
+        put = functools.partial(put_folded, sh, sl, plan.lot)
+        cols = slice(g * lanes, (g + 1) * lanes)
+        fold_inside(plan, lambda r, n: get(g, r, r + n), lambda at, a, b: put(at, cols, a, b))
     for r0, r1 in chunks(plan.face):
         local = local_terms(coef, lambda g: get(g, r0, r1), r1 - r0, va, vd, r0)
         for g in range(plan.groups):
-            before = acc if g < BUF else given
-            acc[g, r0:r1, :] = before[g, r0:r1, :] + local[g]
+            acc[g, r0:r1, :] = local[g]
 
 
 def ypack_kernel(plan, paired, ylo, yhi, elo, ehi, zpick, order, yh, vy, zc):
     c, lanes, strip, corner = plan.cells, plan.lanes, plan.strip, plan.corner
+    last = yh.shape[1] - strip
     for g in range(plan.groups):
         lo, hi, at = (elo, ehi, g * strip) if g < BUF else (ylo, yhi, (g - BUF) * strip)
         yh[g, :strip] = lo[at : at + strip, :]
-        yh[g, strip : 2 * strip] = hi[at : at + strip, :]
-    yh[:, 2 * strip :] = jnp.zeros((plan.groups, yh.shape[1] - 2 * strip, lanes), F32)
+        yh[g, last:] = hi[at : at + strip, :]
+    yh[:, strip:last] = jnp.zeros((plan.groups, last - strip, lanes), F32)
     ebase, ybase = BUF * strip, plan.inner * strip
     shift_in = lanes - strip
     vy[...] = jnp.zeros(vy.shape, F32)
-    for e, y, cut, at in ((elo, ylo, shift_in, 0), (ehi, yhi, 0, strip)):
+    for e, y, cut, at in ((elo, ylo, shift_in, 0), (ehi, yhi, 0, last)):
         cols = slice(at, at + strip)
         vy[:BUF, cols] = e[ebase : ebase + BUF, :][:, cut : cut + strip]
         vy[BUF + c : plan.ext, cols] = e[ebase + BUF : ebase + 2 * BUF, :][:, cut : cut + strip]
@@ -348,67 +447,63 @@
         dst[plan.groups * BUF * corner :, :] = exact(vy[...], zpick[side])
 
 
-def halo_kernel(plan, paired, yh, vy, zi, coef, vspread, given, acc, xr, va, vd, xh, xl):
+def halo_kernel(plan, paired, yh, vy, zi, coef, vspread, given, sh_in, sl_in, acc, sh, sl, xr, va, vd):
     g_all, lanes, strip, face = plan.groups, plan.lanes, plan.strip, plan.face
+    last = yh.shape[1] - strip
     zlo, zhi = sides(zi, paired)[::-1] if paired else zi
-    pots = [(vy[...], 2 * strip)] + [(piece[g_all * strip :, :], strip) for piece in (zlo, zhi)]
-    spread_potential(plan, pots, vspread, va, vd)
-    for k, piece in enumerate((zlo, zhi)):
-        at = (2 + k) * strip
-        for g in range(g_all):
-            xr[g, at : at + strip, :] = piece[g * strip : (g + 1) * strip, :]
+    pots = [(vy[...], 0, strip), (vy[...], last, last + strip)]
+    spread_potential(plan, pots + [(piece[g_all * strip :, :], 0, strip) for piece in (zlo, zhi)], vspread, va, vd)
     for g in range(g_all):
-        xr[g, : 2 * strip, :] = yh[g, : 2 * strip, :]
-        h, l = split(xr[g])
-        xh[:, g * lanes : (g + 1) * lanes] = h
-        xl[:, g * lanes : (g + 1) * lanes] = l
+        xr[g, :strip, :] = yh[g, :strip, :]
+        xr[g, strip : 2 * strip, :] = yh[g, last:, :]
+        for k, piece in enumerate((zlo, zhi)):
+            xr[g, (2 + k) * strip : (3 + k) * strip, :] = piece[g * strip : (g + 1) * strip, :]
+    for g in range(g_all):
+        cols = slice(g * lanes, (g + 1) * lanes)
+        put = lambda at, a, b: put_folded(sh, sl, plan.lot, at, cols, a, b)
+        fold_halo(plan, lambda r, n: xr[g, r : r + n, :], put)
     for r0, r1 in chunks(4 * strip):
         local = local_terms(coef, lambda g: xr[g, r0:r1, :], r1 - r0, va, vd, r0)
         for g in range(g_all):
-            acc[g, face + r0 : face + r1, :] = given[g, face + r0 : face + r1, :] + local[g]
-
-
-def filter_kernel(plan, paired, zc, inner, outer, xr, xrh, xrl, vai, vdi, vah, vdh, given, wrh, wrl, wh, wl, coef, dcoef,
-                  vspread, out, mx, my, mz, xh, xl, xc, y, yh, yl, va, vd, acc):
+            acc[g, face + r0 : face + r1, :] = local[g]
+
+
+def filter_kernel(plan, paired, zc, inner, outer, xr, vai, vdi, vah, vdh, given, sh_in, sl_in, w1h, w1l, w2h, w2l, coef, dcoef,
+                  vspread, out, mx, my, mz, sh, sl, xc, y, th, tl, va, vd, acc):
     g_all, lanes, rows, face, cross, c = plan.groups, plan.lanes, plan.rows, plan.face, plan.cross, plan.cells
-    strip = plan.strip
-    span = BUF * plan.corner
+    strip, lot, corner = plan.strip, plan.lot, plan.corner
+    span = BUF * corner
     mz = sides(mz, paired)
     zlo, zhi = sides(zc, paired)[::-1] if paired else zc
-    rest = 4 * strip
-    xh[:rest, :] = xrh[...]
-    xl[:rest, :] = xrl[...]
-    spread_potential(plan, [(piece[g_all * span :, :], span) for piece in (zlo, zhi)], vspread, va, vd)
-    for k, piece in enumerate((zlo, zhi)):
+    spread_potential(plan, [(piece[g_all * span :, :], 0, span) for piece in (zlo, zhi)], vspread, va, vd)
+    for g in range(g_all):
+        cols = slice(g * lanes, (g + 1) * lanes)
+        for k, piece in enumerate((zlo, zhi)):
+            xc[g, k * span : (k + 1) * span, :] = piece[g * span : (g + 1) * span, :]
+        put = lambda at, a, b: put_folded(sh, sl, lot, at, cols, a, b)
+        fold_corners([xc[g, k * 2 * corner : (k + 1) * 2 * corner, :] for k in range(BUF)], put, cross // 2)
+
+    for r0, r1 in chunks(2 * span):
+        local = local_terms(coef, lambda g: xc[g, r0:r1, :], r1 - r0, va, vd, r0)
         for g in range(g_all):
-            xc[g, k * span : (k + 1) * span, :] = piece[g * span : (g + 1) * span, :]
-    for g in range(g_all):
-        h, l = split(xc[g])
-        xh[rest:, g * lanes : (g + 1) * lanes] = h
-        xl[rest:, g * lanes : (g + 1) * lanes] = l
-
-    def put(g, r0, r1, value):
-        y[g, r0:r1, :] = value
-        h, l = split(value)
-        yh[r0:r1, g * lanes : (g + 1) * lanes] = h
-        yl[r0:r1, g * lanes : (g + 1) * lanes] = l
-
-    corners = {}
-    for r0, r1 in chunks(2 * span):
-        corners[r0] = local_terms(coef, lambda g: xc[g, r0:r1, :], r1 - r0, va, vd, r0)
-        for g in range(g_all):
-            y[g, cross + r0 : cross + r1, :] = corners[r0][g]
+            y[g, cross + r0 : cross + r1, :] = local[g]
     for n, (g0, g1) in enumerate(pairs(g_all)):
-        slot = n % 2
         cols = slice(g0 * lanes, g1 * lanes)
-        acc[slot, :, : (g1 - g0) * lanes] = three(wrh[...], wrl[...], xh[:, cols], xl[:, cols])
+        for p in range(2):
+            own = slice(p * lot, (p + 1) * lot)
+            acc[n % 2, own, : (g1 - g0) * lanes] = three(w1h[p], w1l[p], sh[own, cols], sl[own, cols])
         for g in range(g0, g1):
             mine = slice((g - g0) * lanes, (g - g0 + 1) * lanes)
-            for r0, r1 in chunks(rows):
-                value = given[g, r0:r1, :] + acc[slot, r0:r1, mine]
-                if r0 >= cross:
-                    value = value + y[g, r0:r1, :]
-                put(g, r0, r1, value * (S0 / HALF_WIDTH))
+            to = slice(g * lanes, (g + 1) * lanes)
+            put = lambda at, a, b: put_folded(th, tl, lot, at, to, a, b)
+            product = unfold(plan, lambda at, k: acc[n % 2, at : at + k, mine], lambda at, k: acc[n % 2, lot + at : lot + at + k, mine], True)
+            for again, at, blocks in product:
+                values = []
+                for r0, block in blocks:
+                    local = given[g, r0 : r0 + 16, :] if r0 < cross else y[g, r0 : r0 + 16, :]
+                    values.append((local + block) * (S0 / HALF_WIDTH))
+                    y[g, r0 : r0 + 16, :] = values[-1]
+                again(values, put, at)
 
     for r0, r1 in chunks(cross):
         v, d, at = (vai, vdi, r0) if r0 < face else (vah, vdh, r0 - face)
@@ -420,15 +515,19 @@
                 else:
                     x = outer[g, r0:r1, :] if g < BUF else inner[g - BUF, r0:r1, :]
                 out[g, r0:r1, :] = local[g] * (2.0 * S1 / HALF_WIDTH) - (S0 * S1) * x
+    flat = plan.flat
     for n, (g0, g1) in enumerate(pairs(g_all)):
-        slot = n % 2
-        top = face if g1 <= BUF else cross
         cols = slice(g0 * lanes, g1 * lanes)
-        acc[slot, :top, : (g1 - g0) * lanes] = three(wh[:top], wl[:top], yh[:, cols], yl[:, cols])
+        for p in range(2):
+            own = slice(p * lot, (p + 1) * lot)
+            acc[n % 2, p * lot : p * lot + flat, : (g1 - g0) * lanes] = three(w2h[p], w2l[p], th[own, cols], tl[own, cols])
         for g in range(g0, g1):
             mine = slice((g - g0) * lanes, (g - g0 + 1) * lanes)
-            for r0, r1 in chunks(face if g < BUF else cross):
-                out[g, r0:r1, :] = out[g, r0:r1, :] + acc[slot, r0:r1, mine] * (2.0 * S1 / HALF_WIDTH)
+            product = unfold(plan, lambda at, k: acc[n % 2, at : at + k, mine], lambda at, k: acc[n % 2, lot + at : lot + at + k, mine], False)
+            for _, _, blocks in product:
+                for r0, block in blocks:
+                    if r0 < face or g >= BUF:
+                        out[g, r0 : r0 + 16, :] = out[g, r0 : r0 + 16, :] + block
 
     for r0, r1 in chunks(face):
         mask = low_lanes((r1 - r0, lanes))
@@ -476,12 +575,12 @@
             value = f[g, r0:r1, :]
             high = value.astype(BF)
             fhi[g, r0:r1, :] = high
-            twice = 2.0 * value - high.astype(F32)
-            f2[g, r0:r1, :] = twice
-            if g >= BUF:
-                h, l = split(twice)
-                f2h[r0:r1, (g - BUF) * lanes : (g - BUF + 1) * lanes] = h
-                f2l[r0:r1, (g - BUF) * lanes : (g - BUF + 1) * lanes] = l
+            f2[g, r0:r1, :] = 2.0 * value - high.astype(F32)
+        if g >= BUF:
+            to = slice((g - BUF) * lanes, (g - BUF + 1) * lanes)
+            put = lambda at, a, b: put_folded(f2h, f2l, plan.flat, at, to, a, b)
+            fold_inside(plan, lambda r, n: f2[g, r : r + n, :], put)
+            fold_halo(plan, lambda r, n: f2[g, face + r : face + r + n, :], put)
     total = jnp.zeros((lanes, 2 * lanes), F32)
 
     def fold(total, g, top, value):
@@ -496,16 +595,21 @@
     for n, (j0, j1) in enumerate(pairs(plan.inner)):
         slot = n % 2
         cols = slice(j0 * lanes, j1 * lanes)
-        acc[slot] = three(bh[...], bl[...], f2h[:, cols], f2l[:, cols])
+        for p in range(2):
+            half = slice(p * plan.flat, (p + 1) * plan.flat)
+            acc[slot, half] = three(bh[p], bl[p], f2h[half, cols], f2l[half, cols])
         for j in range(j0, j1):
             g = BUF + j
             mine = slice((j - j0) * lanes, (j - j0 + 1) * lanes)
+            flat = plan.flat
+            product = unfold(plan, lambda at, k: acc[slot, at : at + k, mine], lambda at, k: acc[slot, flat + at : flat + at + k, mine], False)
+            product = {r0: block for _, _, blocks in product for r0, block in blocks}
             parts = []
             for r0, r1 in chunks(face):
                 own = f2[g, r0:r1, :]
-                value = acc[slot, r0:r1, mine] + mixed(g, r0, r1)
+                value = product[r0] + mixed(g, r0, r1)
                 parts.append(value + (va[g, r0:r1, :] + CENTER) * own + vd[g, r0:r1, :] * swap(own))
-            parts.append(acc[slot, face:, mine])
+            parts += [product[r0] for r0 in range(face, cross, 16)]
             total = fold(total, g, cross, jnp.concatenate(parts, axis=0))
     both = total[:, :lanes] + total[:, lanes:]
     w = plan.width
@@ -618,7 +722,7 @@
             z = side * (cells - BUF) + k
             for y in range(cells):
                 ipick[side, y * cells + z, k * cells + y] = 1.0
-            for y in range(2 * BUF):
+            for y in range(corner):
                 cpick[side, y * cells + z, k * corner + y] = 1.0
     elo, ehi, vx = call(
         part(edge_kernel, plan), [near(srows, lanes), near(srows, lanes), near(plan.trows, face)], [vt, from_slo, from_shi, from_ylo],
@@ -634,13 +738,8 @@
         vspread[plan.ext - 1 - g, 0, g, :] = 0.5
         vspread[plan.ext - 1 - g, 1, g, :] = -0.5
     vspread = np.tile(vspread.reshape(plan.trows, -1), (3, 1)).astype(ml_dtypes.bfloat16)
-    inside = halves(matrix[:, :face])
-    acc, vai, vdi, early = call(
-        part(inside_kernel, plan),
-        [near(g_all, rows, lanes), near(g_all, face, lanes), near(g_all, face, lanes), near(8, lanes)],
-        [inner, vx, *inside, vspread],
-        [bf(face, inner_all * lanes), bf(face, inner_all * lanes)],
-        flops=0,
+    vai, vdi, early = call(
+        part(inside_kernel, plan), [near(g_all, face, lanes), near(g_all, face, lanes), near(8, lanes)], [vx, vspread],
     )
     outer, zi = call(
         part(xhalo_kernel, plan, paired),
@@ -648,12 +747,9 @@
         [inner, vx, elo, ehi, from_rlo, from_rhi, ipick, early],
     )
     zi = shift_z(zi, paired)
-    acc, order = call(
-        part(outside_kernel, plan),
-        [near(g_all, rows, lanes), near(8, lanes)],
-        [inner, outer, *inside, coef, vai, vdi, acc],
-        [bf(face, BUF * lanes), bf(face, BUF * lanes)],
-        aliases={7: 0},
+    both = pltpu.VMEM((2 * plan.lot, wide), BF)
+    acc, order, sh, sl = call(
+        part(outside_kernel, plan), [near(g_all, cross, lanes), near(8, lanes), both, both], [inner, outer, coef, vai, vdi],
     )
 
     room = 2 * strip + (corner - 2 * BUF) * cells
@@ -665,11 +761,12 @@
     )
     zc = shift_z(zc, paired)
     rest = 4 * strip
-    acc, xr, vah, vdh, xrh, xrl = call(
+    base = 5 if paired else 6
+    acc, sh, sl, xr, vah, vdh = call(
         part(halo_kernel, plan, paired),
-        [near(g_all, rows, lanes), near(g_all, rest, lanes), near(g_all, rest, lanes), near(g_all, rest, lanes), bf(rest, wide), bf(rest, wide)],
-        [yh, vy, zi, coef, vspread, acc],
-        aliases={5 if paired else 6: 0},
+        [near(g_all, cross, lanes), both, both, near(g_all, rest, lanes), near(g_all, rest, lanes), near(g_all, rest, lanes)],
+        [yh, vy, zi, coef, vspread, acc, sh, sl],
+        aliases={base: 0, base + 1: 1, base + 2: 2},
     )
 
     p = plan.first[BUF, :g_all] + plan.first[BUF, ::-1][:g_all]
@@ -677,13 +774,16 @@
     dcoef = np.concatenate([np.repeat(p[:, None], width, 1), np.repeat(q[:, None], width, 1)], 1).astype(np.float32)
     msg = near(face, lanes)
     corners = 2 * BUF * corner
-    filtered, mx, my, mz = call(
+    product = folded_rows(plan, matrix)
+    second = 2.0 * S1 / HALF_WIDTH * product[:, : plan.flat]
+    base = 9 if paired else 10
+    filtered, mx, my, mz, _, _ = call(
         part(filter_kernel, plan, paired),
-        [near(g_all, cross, lanes), [msg, msg], [msg, msg], two(face, lanes)],
-        [zc, inner, outer, xr, xrh, xrl, vai, vdi, vah, vdh, acc, *halves(matrix[:, face:]), *halves(matrix[:cross]), coef, dcoef, vspread],
-        [bf(rest + corners, wide), bf(rest + corners, wide), near(g_all, corners, lanes),
-         near(g_all, rows, lanes), bf(rows, wide), bf(rows, wide),
-         near(g_all, corners, lanes), near(g_all, corners, lanes), near(2, rows, 2 * lanes)],
+        [near(g_all, cross, lanes), [msg, msg], [msg, msg], two(face, lanes), both, both],
+        [zc, inner, outer, xr, vai, vdi, vah, vdh, acc, sh, sl, *halves(product), *halves(second), coef, dcoef, vspread],
+        [near(g_all, corners, lanes), near(g_all, rows, lanes), both, both,
+         near(g_all, corners, lanes), near(g_all, corners, lanes), near(2, 2 * plan.lot, 2 * lanes)],
+        aliases={base: 6 if paired else 7, base + 1: 7 if paired else 8},
     )
     ny = [shift(my[1], "gy", 1), shift(my[0], "gy", -1)]
     nx = [shift(mx[1], "gx", 1), shift(mx[0], "gx", -1)]
@@ -693,7 +793,7 @@
     bcoef = mirrored(plan, along).reshape(-1, lanes).astype(np.float32)
     diag, basis = call(
         part(own_kernel, plan), [near(width, width), far(cells, face, width)],
-        [filtered, vai, vdi, *halves(row_matrix(plan, along, True)[:cross, :cross]), bcoef],
+        [filtered, vai, vdi, *halves(folded_rows(plan, row_matrix(plan, along, True))[:, : plan.flat, : plan.flat]), bcoef],
         [near(cells, face, width), near(g_all, cross, lanes), bf(cross, inner_all * lanes), bf(cross, inner_all * lanes), bf(g_all, cross, lanes),
          near(2, cross, 2 * lanes), pltpu.SemaphoreType.DMA((cells,))],
         flops=2 * 10**9,

time: 43.9 us -> 43.5 us (level)
  Pallas kernels: 21.1 us -> 18.9 us
  waiting for transfers between devices: 0.65 us -> 1.65 us
  starting transfers between devices: 20.8 us -> 21.7 us
    pallas_call x12, Pallas kernels: 21.1 us -> 18.9 us  [call(): pl.pallas_call(kernel, out_shape=outs, in_specs=[apart if i in far_in els...]
    ppermute x15, waiting for transfers between devices: 0.65 us -> 1.65 us  [shift(): lax.ppermute(array, axis, [(i, (i + step) % count) for i in range(count)])]
    ppermute x15, starting transfers between devices: 20.8 us -> 21.7 us  [shift(): lax.ppermute(array, axis, [(i, (i + step) % count) for i in range(count)])]
  transfers between devices with their start and end apart: 15 -> 15, of which waited for: 1 -> 2; matrix products, arithmetic and copies ran while one was open for 0% -> 0% of each run, Pallas kernels for 27% -> 22%
where the time goes in v6:
time: 43.5 us; the launch traced here: 43.3 us
  starting transfers between devices  21.7 us (50%)
  Pallas kernels  18.9 us (43%)
  waiting for transfers between devices  1.65 us (4%)
  between operations  1.08 us (2%)
    ppermute x15, starting transfers between devices, shift(): lax.ppermute(array, axis, [(i, (i + step) % count) for i in range(count)])  21.7 us
    pallas_call x12, Pallas kernels, call(): pl.pallas_call(kernel, out_shape=outs, in_specs=[apart if i in far_in els...  18.9 us
    ppermute x15, waiting for transfers between devices, shift(): lax.ppermute(array, axis, [(i, (i + step) % count) for i in range(count)])  1.65 us
  transfers between devices with their start and end apart: 15, of which 2 were waited for; matrix products, arithmetic and copies ran while one was open for 0% of the time, Pallas kernels for 22%

profile of v6, /device:TPU:0, one launch (start us, length us, event | category | flops | bytes accessed | tf_op | source)
XLA Modules:
  0.0 43.3 jit_solution(17225999667047522915)
XLA Ops:
  0.6 0.0 copy-start
  0.6 1.6 %shard_map.149 = (f32[152,128]{1,0:T(8,128)S(1)}, f32[152,128]{1,0:T(8,128)S(1)}, f32[400,128]{1,0:T(8,128)S(1)}, f32[400,128]{1,0:T(8,128)S(1)}, f32[16,256]{1,0:T(8,128)S(1)}) custom-call(f32[16,256,64]{2,1,0:T(8,128)} %bitcast.4, f32[256,16]{1,0:T(8,128)} %bitcast.7), custom_call_target="tpu_custom_call" | custom-call | tf_op jit(solution)/shard_map/pallas_call | solution.py:666
  2.2 3.1 %collective-permute-start = (f32[400,128]{1,0:T(8,128)S(1)}, f32[400,128]{1,0:T(8,128)S(1)}, u32[]{:S(2)}, u32[]{:S(2)}) collective-permute-start(f32[400,128]{1,0:T(8,128)S(1)} %get-tuple-element.39), channel_id=1, source_target_pairs={{0,2},{2,4},{4,6},{6,0},{1,3},{3,5},{5,7},{7,1},{8,10},{10,12},{12... | collective-permute-start | bytes 614408 | tf_op jit(solution)/shard_map/ppermute | solution.py:680
  5.3 1.5 %collective-permute-start.2 = (f32[152,128]{1,0:T(8,128)S(1)}, f32[152,128]{1,0:T(8,128)S(1)}, u32[]{:S(2)}, u32[]{:S(2)}) collective-permute-start(f32[152,128]{1,0:T(8,128)S(1)} %get-tuple-element.42), channel_id=1, source_target_pairs={{0,8},{8,16},{16,24},{24,0},{1,9},{9,17},{17,25},{25,1},{2,10},{10... | collective-permute-start | bytes 233480 | tf_op jit(solution)/shard_map/ppermute | solution.py:680
  6.8 1.4 %collective-permute-start.3 = (f32[152,128]{1,0:T(8,128)S(1)}, f32[152,128]{1,0:T(8,128)S(1)}, u32[]{:S(2)}, u32[]{:S(2)}) collective-permute-start(f32[152,128]{1,0:T(8,128)S(1)} %get-tuple-element.43), channel_id=1, source_target_pairs={{0,24},{8,0},{16,8},{24,16},{1,25},{9,1},{17,9},{25,17},{2,26},{10... | collective-permute-start | bytes 233480 | tf_op jit(solution)/shard_map/ppermute | solution.py:680
  8.2 2.1 %collective-permute-start.1 = (f32[400,128]{1,0:T(8,128)S(1)}, f32[400,128]{1,0:T(8,128)S(1)}, u32[]{:S(2)}, u32[]{:S(2)}) collective-permute-start(f32[400,128]{1,0:T(8,128)S(1)} %get-tuple-element.40), channel_id=1, source_target_pairs={{0,6},{2,0},{4,2},{6,4},{1,7},{3,1},{5,3},{7,5},{8,14},{10,8},{12,... | collective-permute-start | bytes 614408 | tf_op jit(solution)/shard_map/ppermute | solution.py:680
  10.3 0.0 copy-done
  10.3 0.4 shard_map.151
  10.7 0.8 %collective-permute-start.6 = (f32[240,128]{1,0:T(8,128)S(1)}, f32[240,128]{1,0:T(8,128)S(1)}, u32[]{:S(2)}, u32[]{:S(2)}) collective-permute-start(f32[240,128]{1,0:T(8,128)S(1)} %get-tuple-element.48), channel_id=1, source_target_pairs={{0,8},{8,16},{16,24},{24,0},{1,9},{9,17},{17,25},{25,1},{2,10},{10... | collective-permute-start | bytes 368648 | tf_op jit(solution)/shard_map/ppermute | solution.py:680
  11.5 0.0 collective-permute-done.2.lo
  11.5 2.2 %collective-permute-start.7 = (f32[240,128]{1,0:T(8,128)S(1)}, f32[240,128]{1,0:T(8,128)S(1)}, u32[]{:S(2)}, u32[]{:S(2)}) collective-permute-start(f32[240,128]{1,0:T(8,128)S(1)} %get-tuple-element.49), channel_id=1, source_target_pairs={{0,24},{8,0},{16,8},{24,16},{1,25},{9,1},{17,9},{25,17},{2,26},{10... | collective-permute-start | bytes 368648 | tf_op jit(solution)/shard_map/ppermute | solution.py:680
  13.7 0.0 collective-permute-done.3.hi
  13.7 0.0 collective-permute-done.ahead.ylo
  13.7 0.0 copy-start.5
  13.7 0.1 shard_map.150
  13.8 0.0 copy-start.2
  13.8 0.9 %collective-permute-start.4 = (f32[152,128]{1,0:T(8,128)S(1)}, f32[152,128]{1,0:T(8,128)S(1)}, u32[]{:S(2)}, u32[]{:S(2)}) collective-permute-start(f32[152,128]{1,0:T(8,128)S(1)} %get-tuple-element.44.ehi), channel_id=1, source_target_pairs={{0,2},{2,4},{4,6},{6,0},{1,3},{3,5},{5,7},{7,1},{8,10},{10,12},{12... | collective-permute-start | bytes 233480 | tf_op jit(solution)/shard_map/ppermute | solution.py:680
  14.7 3.0 %collective-permute-start.5 = (f32[152,128]{1,0:T(8,128)S(1)}, f32[152,128]{1,0:T(8,128)S(1)}, u32[]{:S(2)}, u32[]{:S(2)}) collective-permute-start(f32[152,128]{1,0:T(8,128)S(1)} %get-tuple-element.45.elo), channel_id=1, source_target_pairs={{0,6},{2,0},{4,2},{6,4},{1,7},{3,1},{5,3},{7,5},{8,14},{10,8},{12,... | collective-permute-start | bytes 233480 | tf_op jit(solution)/shard_map/ppermute | solution.py:680
  17.7 0.0 copy-done.1
  17.7 0.6 %shard_map.152 = (f32[11,256,128]{2,1,0:T(8,128)S(1)}, f32[11,256,128]{2,1,0:T(8,128)S(1)}, f32[8,128]{1,0:T(8,128)S(1)}) custom-call(f32[24,256]{1,0:T(8,128)S(1)} %get-tuple-element.47.vx, bf16[72,2816]{1,0:T(8,128)(2,1)S(1)} %copy-done.1), custom_call_target="tpu_custom_call" | custom-call | tf_op jit(solution)/shard_map/pallas_call | solution.py:666
  18.3 0.0 collective-permute-done.6.lo
  18.3 0.3 collective-permute-done.7.hi
  18.6 0.0 copy-done.5
  18.6 0.4 shard_map.153
  19.0 0.1 collective-permute-start.9
  19.1 0.0 copy-done.2
  19.1 0.0 copy-start.11
  19.1 1.3 %shard_map.154 = (f32[11,448,128]{2,1,0:T(8,128)S(1)}, f32[8,128]{1,0:T(8,128)S(1)}, bf16[512,1408]{1,0:T(8,128)(2,1)S(1)}, bf16[512,1408]{1,0:T(8,128)(2,1)S(1)}) custom-call(f32[8,256,128]{2,1,0:T(8,128)S(1)} %get-tuple-element.46.inner, f32[3,256,128]{2,1,0:T(8,128)S(1)} %get-tuple-element.51.outer, f32[61,128]{1,0:T(8,128)S(1)} %copy-done.2, ...), custom_call_target="tpu_custom_call" | custom-call | tf_op jit(solution)/shard_map/pallas_call | solution.py:666
  20.4 0.0 collective-permute-done.1.yhi
  20.4 0.0 collective-permute-done.4.elo
  20.4 0.0 collective-permute-done.5.ehi
  20.4 0.0 copy-done.11
  20.4 0.4 shard_map.155
  20.8 0.5 %collective-permute-start.8 = (f32[2,288,128]{2,1,0:T(8,128)S(1)}, f32[2,288,128]{2,1,0:T(8,128)S(1)}, u32[]{:S(2)}, u32[]{:S(2)}) collective-permute-start(f32[2,288,128]{2,1,0:T(8,128)S(1)} %get-tuple-element.55), channel_id=1, source_target_pairs={{0,1},{1,0},{2,3},{3,2},{4,5},{5,4},{6,7},{7,6},{8,9},{9,8},{10,11... | collective-permute-start | bytes 884744 | tf_op jit(solution)/shard_map/ppermute | solution.py:680
  21.3 0.0 collective-permute-done.9.zi
  21.3 0.0 copy-start.7
  21.3 0.0 copy-start.8
  21.3 1.4 %shard_map.156 = (f32[11,448,128]{2,1,0:T(8,128)S(1)}, bf16[512,1408]{1,0:T(8,128)(2,1)S(1)}, bf16[512,1408]{1,0:T(8,128)(2,1)S(1)}, f32[11,192,128]{2,1,0:T(8,1...) custom-call(f32[11,128,128]{2,1,0:T(8,128)S(1)} %get-tuple-element.5, ...), custom_call_target="tpu_custom_call", output_to_operand_aliasing={{0}: (5, {}), {1}: (6, {}), {2}: (7, {})} | custom-call | tf_op jit(solution)/shard_map/pallas_call | solution.py:666
  22.7 0.0 collective-permute-done.8.zc
  22.7 0.0 copy-done.3
  22.7 0.0 copy-done.4
  22.8 0.0 copy-done.6
  22.8 0.0 copy-done.7
  22.8 0.0 copy-done.8
  22.8 0.0 copy-start.9
  22.8 0.0 copy-start.10
  22.8 0.0 copy-start.12
  22.8 6.6 %shard_map.157 = (f32[11,448,128]{2,1,0:T(8,128)S(1)}, f32[256,128]{1,0:T(8,128)S(1)}, f32[256,128]{1,0:T(8,128)S(1)}, f32[256,128]{1,0:T(8,128)S(1)}, f32[256,1...) custom-call(f32[2,288,128]{2,1,0:T(8,128)S(1)} %collective-permute-d, ...), custom_call_target="tpu_custom_call", output_to_operand_aliasing={{6}: (9, {}), {7}: (10, {})} | custom-call | tf_op jit(solution)/shard_map/pallas_call | solution.py:666
  29.4 0.2 collective-permute-start.12
  29.6 3.4 %collective-permute-start.11 = (f32[256,128]{1,0:T(8,128)S(1)}, f32[256,128]{1,0:T(8,128)S(1)}, u32[]{:S(2)}, u32[]{:S(2)}) collective-permute-start(f32[256,128]{1,0:T(8,128)S(1)} %get-tuple-element.71.oy_0_), channel_id=1, source_target_pairs={{0,6},{2,0},{4,2},{6,4},{1,7},{3,1},{5,3},{7,5},{8,14},{10,8},{12,... | collective-permute-start | bytes 393224 | tf_op jit(solution)/shard_map/ppermute | solution.py:680
  33.0 0.0 collective-permute-start.10
  33.0 2.6 %collective-permute-start.14 = (f32[256,128]{1,0:T(8,128)S(1)}, f32[256,128]{1,0:T(8,128)S(1)}, u32[]{:S(2)}, u32[]{:S(2)}) collective-permute-start(f32[256,128]{1,0:T(8,128)S(1)} %get-tuple-element.74.ox_0_), channel_id=1, source_target_pairs={{0,24},{8,0},{16,8},{24,16},{1,25},{9,1},{17,9},{25,17},{2,26},{10... | collective-permute-start | bytes 393224 | tf_op jit(solution)/shard_map/ppermute | solution.py:680
  35.6 0.0 collective-permute-start.13
  35.6 0.0 copy-done.9
  35.6 0.0 copy-done.10
  35.6 0.0 copy-done.12
  35.6 4.7 %shard_map.158 = (f32[64,64]{1,0:T(8,128)S(1)}, f32[16,256,64]{2,1,0:T(8,128)}) custom-call(f32[11,448,128]{2,1,0:T(8,128)S(1)} %get-tuple-element.68.f, f32[11,256,128]{2,1,0:T(8,128)S(1)} %get-tuple-element.52.va.vai, f32[11,256,128]{2,1,0:T(8,128)S(1)} %get-tuple-element.53.vd.vdi, bf16[2,224,224]{2,1,0:T(8,128)(2,1)S(1)} %copy-done.10, ...), custom_call_target="tpu_custom_call" | custom-call | flops 2000000000 | tf_op jit(solution)/shard_map/pallas_call | solution.py:666
  40.4 0.0 collective-permute-done.11.ny_1_
  40.4 0.0 collective-permute-done.10.ny_0_
  40.4 0.0 collective-permute-done.12.nz
  40.4 0.4 shard_map.159.yz
  40.8 0.0 collective-permute-done.14.nx_1_
  40.8 1.4 %collective-permute-done.13.nx_0_ = f32[256,128]{1,0:T(8,128)S(1)} collective-permute-done((f32[256,128]{1,0:T(8,128)S(1)}, f32[256,128]{1,0:T(8,128)S(1)}, u32[]{:S(2)}, u32[]{:S(2)}) %collective-permute-start.13) | collective-permute-done | bytes 131104 | tf_op jit(solution)/shard_map/ppermute | solution.py:680
  42.2 1.0 %shard_map.160 = f32[7,64,64]{2,1,0:T(8,128)} custom-call(f32[64,64]{1,0:T(8,128)S(1)} %get-tuple-element.70.diag, f32[4,64,64]{2,1,0:T(8,128)S(1)} %shard_map.159.yz, f32[256,128]{1,0:T(8,128)S(1)} %get-tuple-element.74.ox_0_, f32[256,128]{1,0:T(8,128)S(1)} %get-tuple-element.75.ox_1_, f32[256,128]{1,0:T(8,128)S(1)} %collective-permute-done.13.nx_0_, ...), custom_call_target="tpu_custom_call" | custom-call | tf_op jit(solution)/shard_map/pallas_call | solution.py:666
  (4 shorter events, 0.0 us)
Async XLA Ops:
  0.6 9.7 %copy-start = (f32[16,16,16,64]{3,2,1,0:T(8,128)S(1)}, f32[16,16,16,64]{3,2,1,0:T(8,128)}, u32[]{:S(2)}) copy-start(f32[16,16,16,64]{3,2,1,0:T(8,128)} %param.14) | copy-start | bytes 3145732
  2.2 11.5 %collective-permute-start = (f32[400,128]{1,0:T(8,128)S(1)}, f32[400,128]{1,0:T(8,128)S(1)}, u32[]{:S(2)}, u32[]{:S(2)}) collective-permute-start(f32[400,128]{1,0:T(8,128)S(1)} %get-tuple-element.39), channel_id=1, source_target_pairs={{0,2},{2,4},{4,6},{6,0},{1,3},{3,5},{5,7},{7,1},{8,10},{10,12},{12... | collective-permute-start | bytes 614408 | tf_op jit(solution)/shard_map/ppermute | solution.py:680
  5.3 6.2 %collective-permute-start.2 = (f32[152,128]{1,0:T(8,128)S(1)}, f32[152,128]{1,0:T(8,128)S(1)}, u32[]{:S(2)}, u32[]{:S(2)}) collective-permute-start(f32[152,128]{1,0:T(8,128)S(1)} %get-tuple-element.42), channel_id=1, source_target_pairs={{0,8},{8,16},{16,24},{24,0},{1,9},{9,17},{17,25},{25,1},{2,10},{10... | collective-permute-start | bytes 233480 | tf_op jit(solution)/shard_map/ppermute | solution.py:680
  6.8 6.9 %collective-permute-start.3 = (f32[152,128]{1,0:T(8,128)S(1)}, f32[152,128]{1,0:T(8,128)S(1)}, u32[]{:S(2)}, u32[]{:S(2)}) collective-permute-start(f32[152,128]{1,0:T(8,128)S(1)} %get-tuple-element.43), channel_id=1, source_target_pairs={{0,24},{8,0},{16,8},{24,16},{1,25},{9,1},{17,9},{25,17},{2,26},{10... | collective-permute-start | bytes 233480 | tf_op jit(solution)/shard_map/ppermute | solution.py:680
  8.2 12.2 %collective-permute-start.1 = (f32[400,128]{1,0:T(8,128)S(1)}, f32[400,128]{1,0:T(8,128)S(1)}, u32[]{:S(2)}, u32[]{:S(2)}) collective-permute-start(f32[400,128]{1,0:T(8,128)S(1)} %get-tuple-element.40), channel_id=1, source_target_pairs={{0,6},{2,0},{4,2},{6,4},{1,7},{3,1},{5,3},{7,5},{8,14},{10,8},{12,... | collective-permute-start | bytes 614408 | tf_op jit(solution)/shard_map/ppermute | solution.py:680
  10.7 7.6 %collective-permute-start.6 = (f32[240,128]{1,0:T(8,128)S(1)}, f32[240,128]{1,0:T(8,128)S(1)}, u32[]{:S(2)}, u32[]{:S(2)}) collective-permute-start(f32[240,128]{1,0:T(8,128)S(1)} %get-tuple-element.48), channel_id=1, source_target_pairs={{0,8},{8,16},{16,24},{24,0},{1,9},{9,17},{17,25},{25,1},{2,10},{10... | collective-permute-start | bytes 368648 | tf_op jit(solution)/shard_map/ppermute | solution.py:680
  11.5 7.1 %collective-permute-start.7 = (f32[240,128]{1,0:T(8,128)S(1)}, f32[240,128]{1,0:T(8,128)S(1)}, u32[]{:S(2)}, u32[]{:S(2)}) collective-permute-start(f32[240,128]{1,0:T(8,128)S(1)} %get-tuple-element.49), channel_id=1, source_target_pairs={{0,24},{8,0},{16,8},{24,16},{1,25},{9,1},{17,9},{25,17},{2,26},{10... | collective-permute-start | bytes 368648 | tf_op jit(solution)/shard_map/ppermute | solution.py:680
  13.7 4.0 %copy-start.1 = (bf16[72,2816]{1,0:T(8,128)(2,1)S(1)}, bf16[72,2816]{1,0:T(8,128)(2,1)}, u32[]{:S(2)}) copy-start(bf16[72,2816]{1,0:T(8,128)(2,1)} %constant.24.clone.vspread) | copy-start | bytes 1216516
  13.7 4.9 %copy-start.5 = (f32[2,256,128]{2,1,0:T(8,128)S(1)}, f32[2,256,128]{2,1,0:T(8,128)}, u32[]{:S(2)}) copy-start(f32[2,256,128]{2,1,0:T(8,128)} %constant.25.clone.zpick) | copy-start | bytes 786436
  13.8 5.2 %copy-start.2 = (f32[61,128]{1,0:T(8,128)S(1)}, f32[61,128]{1,0:T(8,128)}, u32[]{:S(2)}) copy-start(f32[61,128]{1,0:T(8,128)} %constant.26.clone.coef) | copy-start | bytes 93700
  13.8 6.5 %collective-permute-start.4 = (f32[152,128]{1,0:T(8,128)S(1)}, f32[152,128]{1,0:T(8,128)S(1)}, u32[]{:S(2)}, u32[]{:S(2)}) collective-permute-start(f32[152,128]{1,0:T(8,128)S(1)} %get-tuple-element.44.ehi), channel_id=1, source_target_pairs={{0,2},{2,4},{4,6},{6,0},{1,3},{3,5},{5,7},{7,1},{8,10},{10,12},{12... | collective-permute-start | bytes 233480 | tf_op jit(solution)/shard_map/ppermute | solution.py:680
  14.7 5.7 %collective-permute-start.5 = (f32[152,128]{1,0:T(8,128)S(1)}, f32[152,128]{1,0:T(8,128)S(1)}, u32[]{:S(2)}, u32[]{:S(2)}) collective-permute-start(f32[152,128]{1,0:T(8,128)S(1)} %get-tuple-element.45.elo), channel_id=1, source_target_pairs={{0,6},{2,0},{4,2},{6,4},{1,7},{3,1},{5,3},{7,5},{8,14},{10,8},{12,... | collective-permute-start | bytes 233480 | tf_op jit(solution)/shard_map/ppermute | solution.py:680
  19.0 2.3 %collective-permute-start.9 = (f32[2,552,128]{2,1,0:T(8,128)S(1)}, f32[2,552,128]{2,1,0:T(8,128)S(1)}, u32[]{:S(2)}, u32[]{:S(2)}) collective-permute-start(f32[2,552,128]{2,1,0:T(8,128)S(1)} %get-tuple-element.58), channel_id=1, source_target_pairs={{0,1},{1,0},{2,3},{3,2},{4,5},{5,4},{6,7},{7,6},{8,9},{9,8},{10,11... | collective-permute-start | bytes 1695752 | tf_op jit(solution)/shard_map/ppermute | solution.py:680
  19.1 1.3 %copy-start.11 = (f32[2,128,128]{2,1,0:T(8,128)S(1)}, f32[2,128,128]{2,1,0:T(8,128)}, u32[]{:S(2)}) copy-start(f32[2,128,128]{2,1,0:T(8,128)} %constant.27.clone.zpick) | copy-start | bytes 393220
  20.8 1.9 %collective-permute-start.8 = (f32[2,288,128]{2,1,0:T(8,128)S(1)}, f32[2,288,128]{2,1,0:T(8,128)S(1)}, u32[]{:S(2)}, u32[]{:S(2)}) collective-permute-start(f32[2,288,128]{2,1,0:T(8,128)S(1)} %get-tuple-element.55), channel_id=1, source_target_pairs={{0,1},{1,0},{2,3},{3,2},{4,5},{5,4},{6,7},{7,6},{8,9},{9,8},{10,11... | collective-permute-start | bytes 884744 | tf_op jit(solution)/shard_map/ppermute | solution.py:680
  21.3 1.4 %copy-start.3 = (bf16[2,256,256]{2,1,0:T(8,128)(2,1)S(1)}, bf16[2,256,256]{2,1,0:T(8,128)(2,1)}, u32[]{:S(2)}) copy-start(bf16[2,256,256]{2,1,0:T(8,128)(2,1)} %constant.29.clone.w1l) | copy-start | bytes 786436
  21.3 1.4 %copy-start.4 = (bf16[2,256,256]{2,1,0:T(8,128)(2,1)S(1)}, bf16[2,256,256]{2,1,0:T(8,128)(2,1)}, u32[]{:S(2)}) copy-start(bf16[2,256,256]{2,1,0:T(8,128)(2,1)} %constant.28.clone.w1h) | copy-start | bytes 786436
  21.3 1.4 %copy-start.6 = (bf16[2,224,256]{2,1,0:T(8,128)(2,1)S(1)}, bf16[2,224,256]{2,1,0:T(8,128)(2,1)}, u32[]{:S(2)}) copy-start(bf16[2,224,256]{2,1,0:T(8,128)(2,1)} %constant.31.clone.w2l) | copy-start | bytes 688132
  21.3 1.5 %copy-start.7 = (bf16[2,224,256]{2,1,0:T(8,128)(2,1)S(1)}, bf16[2,224,256]{2,1,0:T(8,128)(2,1)}, u32[]{:S(2)}) copy-start(bf16[2,224,256]{2,1,0:T(8,128)(2,1)} %constant.30.clone.w2h) | copy-start | bytes 688132
  21.3 1.4 %copy-start.8 = (f32[11,128]{1,0:T(8,128)S(1)}, f32[11,128]{1,0:T(8,128)}, u32[]{:S(2)}) copy-start(f32[11,128]{1,0:T(8,128)} %constant.32.clone.dcoef) | copy-start | bytes 16900
  22.8 12.8 %copy-start.9 = (bf16[2,224,224]{2,1,0:T(8,128)(2,1)S(1)}, bf16[2,224,224]{2,1,0:T(8,128)(2,1)}, u32[]{:S(2)}) copy-start(bf16[2,224,224]{2,1,0:T(8,128)(2,1)} %constant.34.clone.bl) | copy-start | bytes 602116
  22.8 12.8 %copy-start.10 = (bf16[2,224,224]{2,1,0:T(8,128)(2,1)S(1)}, bf16[2,224,224]{2,1,0:T(8,128)(2,1)}, u32[]{:S(2)}) copy-start(bf16[2,224,224]{2,1,0:T(8,128)(2,1)} %constant.33.clone.bh) | copy-start | bytes 602116
  22.8 12.8 %copy-start.12 = (f32[121,128]{1,0:T(8,128)S(1)}, f32[121,128]{1,0:T(8,128)}, u32[]{:S(2)}) copy-start(f32[121,128]{1,0:T(8,128)} %constant.35.clone.coef) | copy-start | bytes 185860
  29.4 11.0 %collective-permute-start.12 = (f32[2,256,128]{2,1,0:T(8,128)S(1)}, f32[2,256,128]{2,1,0:T(8,128)S(1)}, u32[]{:S(2)}, u32[]{:S(2)}) collective-permute-start(f32[2,256,128]{2,1,0:T(8,128)S(1)} %get-tuple-element.73.oz), channel_id=1, source_target_pairs={{0,1},{1,0},{2,3},{3,2},{4,5},{5,4},{6,7},{7,6},{8,9},{9,8},{10,11... | collective-permute-start | bytes 786440 | tf_op jit(solution)/shard_map/ppermute | solution.py:680
  29.6 10.8 %collective-permute-start.11 = (f32[256,128]{1,0:T(8,128)S(1)}, f32[256,128]{1,0:T(8,128)S(1)}, u32[]{:S(2)}, u32[]{:S(2)}) collective-permute-start(f32[256,128]{1,0:T(8,128)S(1)} %get-tuple-element.71.oy_0_), channel_id=1, source_target_pairs={{0,6},{2,0},{4,2},{6,4},{1,7},{3,1},{5,3},{7,5},{8,14},{10,8},{12,... | collective-permute-start | bytes 393224 | tf_op jit(solution)/shard_map/ppermute | solution.py:680
  33.0 7.4 %collective-permute-start.10 = (f32[256,128]{1,0:T(8,128)S(1)}, f32[256,128]{1,0:T(8,128)S(1)}, u32[]{:S(2)}, u32[]{:S(2)}) collective-permute-start(f32[256,128]{1,0:T(8,128)S(1)} %get-tuple-element.72.oy_1_), channel_id=1, source_target_pairs={{0,2},{2,4},{4,6},{6,0},{1,3},{3,5},{5,7},{7,1},{8,10},{10,12},{12... | collective-permute-start | bytes 393224 | tf_op jit(solution)/shard_map/ppermute | solution.py:680
  33.0 7.8 %collective-permute-start.14 = (f32[256,128]{1,0:T(8,128)S(1)}, f32[256,128]{1,0:T(8,128)S(1)}, u32[]{:S(2)}, u32[]{:S(2)}) collective-permute-start(f32[256,128]{1,0:T(8,128)S(1)} %get-tuple-element.74.ox_0_), channel_id=1, source_target_pairs={{0,24},{8,0},{16,8},{24,16},{1,25},{9,1},{17,9},{25,17},{2,26},{10... | collective-permute-start | bytes 393224 | tf_op jit(solution)/shard_map/ppermute | solution.py:680
  35.6 6.6 %collective-permute-start.13 = (f32[256,128]{1,0:T(8,128)S(1)}, f32[256,128]{1,0:T(8,128)S(1)}, u32[]{:S(2)}, u32[]{:S(2)}) collective-permute-start(f32[256,128]{1,0:T(8,128)S(1)} %get-tuple-element.75.ox_1_), channel_id=1, source_target_pairs={{0,8},{8,16},{16,24},{24,0},{1,9},{9,17},{17,25},{25,1},{2,10},{10... | collective-permute-start | bytes 393224 | tf_op jit(solution)/shard_map/ppermute | solution.py:680

commit v7 on v6

--- a/solution.py
+++ b/solution.py
@@ -628,23 +628,25 @@
     return scale * (0.25 * sign * (m[w:, :w] - m[:w, w:]) - 0.5 * PENALTY * m[:w, :w])
 
 
-def yzface_kernel(plan, paired, oy, oz, ny, nz, blocks):
+def early_faces_kernel(plan, paired, ox, oy, oz, nx, ny, nz, blocks):
     oz, nz = sides(oz, paired), sides(nz, paired)[::-1] if paired else nz
-    for k, (own, other) in enumerate(((oy[0], ny[0]), (oy[1], ny[1]), (oz[0], nz[0]), (oz[1], nz[1]))):
-        blocks[k] = face_block(plan, own, other, -1.0 if k % 2 == 0 else 1.0, 0.5)
-
-
-def xface_kernel(plan, diag, yz, ox, nx, blocks, local, sem):
+    blocks[0] = face_block(plan, ox, nx, -1.0, 1.0)
+    for k, (own, other, sign) in enumerate(((oy, ny, 1.0), (oz[0], nz[0], -1.0), (oz[1], nz[1], 1.0))):
+        blocks[1 + k] = face_block(plan, own, other, sign, 0.5)
+
+
+def late_faces_kernel(plan, diag, early, ox, oy, nx, ny, blocks, local, sem):
     copies = [
         pltpu.make_async_copy(diag, blocks.at[0], sem.at[0]),
-        pltpu.make_async_copy(yz, blocks.at[3:7], sem.at[1]),
-        pltpu.make_async_copy(local, blocks.at[1:3], sem.at[2]),
+        pltpu.make_async_copy(early.at[0], blocks.at[1], sem.at[1]),
+        pltpu.make_async_copy(early.at[1:4], blocks.at[4:7], sem.at[2]),
+        pltpu.make_async_copy(local, blocks.at[2:4], sem.at[3]),
     ]
-    copies[0].start()
-    copies[1].start()
-    for k in range(2):
-        local[k] = face_block(plan, ox[k], nx[k], -1.0 if k == 0 else 1.0, 1.0)
-    copies[2].start()
+    for copy in copies[:3]:
+        copy.start()
+    local[0] = face_block(plan, ox, nx, 1.0, 1.0)
+    local[1] = face_block(plan, oy, ny, -1.0, 0.5)
+    copies[3].start()
     for copy in copies:
         copy.wait()
 
@@ -799,10 +801,12 @@
         flops=2 * 10**9,
         far_out=(1,),
     )
-    (yz,) = call(part(yzface_kernel, plan, paired), [near(4, width, width)], [my, mz, ny, nz])
+    (first_faces,) = call(
+        part(early_faces_kernel, plan, paired), [near(4, width, width)], [mx[0], my[1], mz, nx[0], ny[1], nz],
+    )
     (blocks,) = call(
-        part(xface_kernel, plan), [far(7, width, width)], [diag, yz, mx, nx],
-        [near(2, width, width), pltpu.SemaphoreType.DMA((3,))], far_out=(0,),
+        part(late_faces_kernel, plan), [far(7, width, width)], [diag, first_faces, mx[1], my[0], nx[1], ny[0]],
+        [near(2, width, width), pltpu.SemaphoreType.DMA((4,))], far_out=(0,),
     )
     return basis.reshape(orbitals.shape), blocks[None, None, None]
 

time: 43.5 us -> 42.7 us (0.982)
  waiting for transfers between devices: 1.65 us -> 0.67 us
    ppermute x15, waiting for transfers between devices: 1.65 us -> 0.67 us  [shift(): lax.ppermute(array, axis, [(i, (i + step) % count) for i in range(count)])]
  transfers between devices with their start and end apart: 15 -> 15, of which waited for: 2 -> 2; matrix products, arithmetic and copies ran while one was open for 0% -> 0% of each run, Pallas kernels for 22% -> 23%
where the time goes in v7:
time: 42.7 us; the launch traced here: 42.6 us
  starting transfers between devices  21.9 us (51%)
  Pallas kernels  18.9 us (44%)
  between operations  1.06 us (2%)
  waiting for transfers between devices  0.67 us (2%)
    ppermute x15, starting transfers between devices, shift(): lax.ppermute(array, axis, [(i, (i + step) % count) for i in range(count)])  21.9 us
    pallas_call x12, Pallas kernels, call(): pl.pallas_call(kernel, out_shape=outs, in_specs=[apart if i in far_in els...  18.9 us
  transfers between devices with their start and end apart: 15, of which 2 were waited for; matrix products, arithmetic and copies ran while one was open for 0% of the time, Pallas kernels for 23%

profile of v7, /device:TPU:0, one launch (start us, length us, event | category | flops | bytes accessed | tf_op | source)
XLA Modules:
  0.0 42.6 jit_solution(17404318708630580032)
XLA Ops:
  0.6 0.0 copy-start
  0.6 1.6 %shard_map.149 = (f32[152,128]{1,0:T(8,128)S(1)}, f32[152,128]{1,0:T(8,128)S(1)}, f32[400,128]{1,0:T(8,128)S(1)}, f32[400,128]{1,0:T(8,128)S(1)}, f32[16,256]{1,0:T(8,128)S(1)}) custom-call(f32[16,256,64]{2,1,0:T(8,128)} %bitcast.4, f32[256,16]{1,0:T(8,128)} %bitcast.7), custom_call_target="tpu_custom_call" | custom-call | tf_op jit(solution)/shard_map/pallas_call | solution.py:668
  2.2 3.1 %collective-permute-start = (f32[400,128]{1,0:T(8,128)S(1)}, f32[400,128]{1,0:T(8,128)S(1)}, u32[]{:S(2)}, u32[]{:S(2)}) collective-permute-start(f32[400,128]{1,0:T(8,128)S(1)} %get-tuple-element.39), channel_id=1, source_target_pairs={{0,2},{2,4},{4,6},{6,0},{1,3},{3,5},{5,7},{7,1},{8,10},{10,12},{12... | collective-permute-start | bytes 614408 | tf_op jit(solution)/shard_map/ppermute | solution.py:682
  5.3 1.5 %collective-permute-start.2 = (f32[152,128]{1,0:T(8,128)S(1)}, f32[152,128]{1,0:T(8,128)S(1)}, u32[]{:S(2)}, u32[]{:S(2)}) collective-permute-start(f32[152,128]{1,0:T(8,128)S(1)} %get-tuple-element.42), channel_id=1, source_target_pairs={{0,8},{8,16},{16,24},{24,0},{1,9},{9,17},{17,25},{25,1},{2,10},{10... | collective-permute-start | bytes 233480 | tf_op jit(solution)/shard_map/ppermute | solution.py:682
  6.8 1.4 %collective-permute-start.3 = (f32[152,128]{1,0:T(8,128)S(1)}, f32[152,128]{1,0:T(8,128)S(1)}, u32[]{:S(2)}, u32[]{:S(2)}) collective-permute-start(f32[152,128]{1,0:T(8,128)S(1)} %get-tuple-element.43), channel_id=1, source_target_pairs={{0,24},{8,0},{16,8},{24,16},{1,25},{9,1},{17,9},{25,17},{2,26},{10... | collective-permute-start | bytes 233480 | tf_op jit(solution)/shard_map/ppermute | solution.py:682
  8.2 2.1 %collective-permute-start.1 = (f32[400,128]{1,0:T(8,128)S(1)}, f32[400,128]{1,0:T(8,128)S(1)}, u32[]{:S(2)}, u32[]{:S(2)}) collective-permute-start(f32[400,128]{1,0:T(8,128)S(1)} %get-tuple-element.40), channel_id=1, source_target_pairs={{0,6},{2,0},{4,2},{6,4},{1,7},{3,1},{5,3},{7,5},{8,14},{10,8},{12,... | collective-permute-start | bytes 614408 | tf_op jit(solution)/shard_map/ppermute | solution.py:682
  10.3 0.0 copy-done
  10.3 0.4 shard_map.151
  10.7 0.8 %collective-permute-start.6 = (f32[240,128]{1,0:T(8,128)S(1)}, f32[240,128]{1,0:T(8,128)S(1)}, u32[]{:S(2)}, u32[]{:S(2)}) collective-permute-start(f32[240,128]{1,0:T(8,128)S(1)} %get-tuple-element.48), channel_id=1, source_target_pairs={{0,8},{8,16},{16,24},{24,0},{1,9},{9,17},{17,25},{25,1},{2,10},{10... | collective-permute-start | bytes 368648 | tf_op jit(solution)/shard_map/ppermute | solution.py:682
  11.5 0.0 collective-permute-done.2.lo
  11.5 2.2 %collective-permute-start.7 = (f32[240,128]{1,0:T(8,128)S(1)}, f32[240,128]{1,0:T(8,128)S(1)}, u32[]{:S(2)}, u32[]{:S(2)}) collective-permute-start(f32[240,128]{1,0:T(8,128)S(1)} %get-tuple-element.49), channel_id=1, source_target_pairs={{0,24},{8,0},{16,8},{24,16},{1,25},{9,1},{17,9},{25,17},{2,26},{10... | collective-permute-start | bytes 368648 | tf_op jit(solution)/shard_map/ppermute | solution.py:682
  13.7 0.0 collective-permute-done.3.hi
  13.7 0.0 collective-permute-done.ahead.ylo
  13.7 0.0 copy-start.5
  13.7 0.1 shard_map.150
  13.8 0.0 copy-start.2
  13.8 0.9 %collective-permute-start.4 = (f32[152,128]{1,0:T(8,128)S(1)}, f32[152,128]{1,0:T(8,128)S(1)}, u32[]{:S(2)}, u32[]{:S(2)}) collective-permute-start(f32[152,128]{1,0:T(8,128)S(1)} %get-tuple-element.44.ehi), channel_id=1, source_target_pairs={{0,2},{2,4},{4,6},{6,0},{1,3},{3,5},{5,7},{7,1},{8,10},{10,12},{12... | collective-permute-start | bytes 233480 | tf_op jit(solution)/shard_map/ppermute | solution.py:682
  14.7 3.0 %collective-permute-start.5 = (f32[152,128]{1,0:T(8,128)S(1)}, f32[152,128]{1,0:T(8,128)S(1)}, u32[]{:S(2)}, u32[]{:S(2)}) collective-permute-start(f32[152,128]{1,0:T(8,128)S(1)} %get-tuple-element.45.elo), channel_id=1, source_target_pairs={{0,6},{2,0},{4,2},{6,4},{1,7},{3,1},{5,3},{7,5},{8,14},{10,8},{12,... | collective-permute-start | bytes 233480 | tf_op jit(solution)/shard_map/ppermute | solution.py:682
  17.7 0.0 copy-done.1
  17.7 0.6 %shard_map.152 = (f32[11,256,128]{2,1,0:T(8,128)S(1)}, f32[11,256,128]{2,1,0:T(8,128)S(1)}, f32[8,128]{1,0:T(8,128)S(1)}) custom-call(f32[24,256]{1,0:T(8,128)S(1)} %get-tuple-element.47.vx, bf16[72,2816]{1,0:T(8,128)(2,1)S(1)} %copy-done.1), custom_call_target="tpu_custom_call" | custom-call | tf_op jit(solution)/shard_map/pallas_call | solution.py:668
  18.3 0.0 collective-permute-done.6.lo
  18.3 0.3 collective-permute-done.7.hi
  18.6 0.0 copy-done.5
  18.6 0.4 shard_map.153
  19.0 0.1 collective-permute-start.9
  19.1 0.0 copy-done.2
  19.1 0.0 copy-start.11
  19.1 1.3 %shard_map.154 = (f32[11,448,128]{2,1,0:T(8,128)S(1)}, f32[8,128]{1,0:T(8,128)S(1)}, bf16[512,1408]{1,0:T(8,128)(2,1)S(1)}, bf16[512,1408]{1,0:T(8,128)(2,1)S(1)}) custom-call(f32[8,256,128]{2,1,0:T(8,128)S(1)} %get-tuple-element.46.inner, f32[3,256,128]{2,1,0:T(8,128)S(1)} %get-tuple-element.51.outer, f32[61,128]{1,0:T(8,128)S(1)} %copy-done.2, ...), custom_call_target="tpu_custom_call" | custom-call | tf_op jit(solution)/shard_map/pallas_call | solution.py:668
  20.4 0.0 collective-permute-done.1.yhi
  20.4 0.0 collective-permute-done.4.elo
  20.4 0.0 collective-permute-done.5.ehi
  20.4 0.0 copy-done.11
  20.4 0.4 shard_map.155
  20.8 0.5 %collective-permute-start.8 = (f32[2,288,128]{2,1,0:T(8,128)S(1)}, f32[2,288,128]{2,1,0:T(8,128)S(1)}, u32[]{:S(2)}, u32[]{:S(2)}) collective-permute-start(f32[2,288,128]{2,1,0:T(8,128)S(1)} %get-tuple-element.55), channel_id=1, source_target_pairs={{0,1},{1,0},{2,3},{3,2},{4,5},{5,4},{6,7},{7,6},{8,9},{9,8},{10,11... | collective-permute-start | bytes 884744 | tf_op jit(solution)/shard_map/ppermute | solution.py:682
  21.3 0.0 collective-permute-done.9.zi
  21.3 0.0 copy-start.7
  21.3 0.0 copy-start.8
  21.3 1.4 %shard_map.156 = (f32[11,448,128]{2,1,0:T(8,128)S(1)}, bf16[512,1408]{1,0:T(8,128)(2,1)S(1)}, bf16[512,1408]{1,0:T(8,128)(2,1)S(1)}, f32[11,192,128]{2,1,0:T(8,1...) custom-call(f32[11,128,128]{2,1,0:T(8,128)S(1)} %get-tuple-element.5, ...), custom_call_target="tpu_custom_call", output_to_operand_aliasing={{0}: (5, {}), {1}: (6, {}), {2}: (7, {})} | custom-call | tf_op jit(solution)/shard_map/pallas_call | solution.py:668
  22.7 0.0 collective-permute-done.8.zc
  22.7 0.0 copy-done.3
  22.7 0.0 copy-done.4
  22.8 0.0 copy-done.6
  22.8 0.0 copy-done.7
  22.8 0.0 copy-done.8
  22.8 0.0 copy-start.9
  22.8 0.0 copy-start.10
  22.8 0.0 copy-start.12
  22.8 6.6 %shard_map.157 = (f32[11,448,128]{2,1,0:T(8,128)S(1)}, f32[256,128]{1,0:T(8,128)S(1)}, f32[256,128]{1,0:T(8,128)S(1)}, f32[256,128]{1,0:T(8,128)S(1)}, f32[256,1...) custom-call(f32[2,288,128]{2,1,0:T(8,128)S(1)} %collective-permute-d, ...), custom_call_target="tpu_custom_call", output_to_operand_aliasing={{6}: (9, {}), {7}: (10, {})} | custom-call | tf_op jit(solution)/shard_map/pallas_call | solution.py:668
  29.4 0.2 collective-permute-start.12
  29.6 2.4 %collective-permute-start.13 = (f32[256,128]{1,0:T(8,128)S(1)}, f32[256,128]{1,0:T(8,128)S(1)}, u32[]{:S(2)}, u32[]{:S(2)}) collective-permute-start(f32[256,128]{1,0:T(8,128)S(1)} %get-tuple-element.71.ox), channel_id=1, source_target_pairs={{0,24},{8,0},{16,8},{24,16},{1,25},{9,1},{17,9},{25,17},{2,26},{10... | collective-permute-start | bytes 393224 | tf_op jit(solution)/shard_map/ppermute | solution.py:682
  32.0 1.2 %collective-permute-start.14 = (f32[256,128]{1,0:T(8,128)S(1)}, f32[256,128]{1,0:T(8,128)S(1)}, u32[]{:S(2)}, u32[]{:S(2)}) collective-permute-start(f32[256,128]{1,0:T(8,128)S(1)} %get-tuple-element.72.oy), channel_id=1, source_target_pairs={{0,2},{2,4},{4,6},{6,0},{1,3},{3,5},{5,7},{7,1},{8,10},{10,12},{12... | collective-permute-start | bytes 393224 | tf_op jit(solution)/shard_map/ppermute | solution.py:682
  33.2 0.0 collective-permute-start.10
  33.2 2.6 %collective-permute-start.11 = (f32[256,128]{1,0:T(8,128)S(1)}, f32[256,128]{1,0:T(8,128)S(1)}, u32[]{:S(2)}, u32[]{:S(2)}) collective-permute-start(f32[256,128]{1,0:T(8,128)S(1)} %get-tuple-element.75.oy), channel_id=1, source_target_pairs={{0,6},{2,0},{4,2},{6,4},{1,7},{3,1},{5,3},{7,5},{8,14},{10,8},{12,... | collective-permute-start | bytes 393224 | tf_op jit(solution)/shard_map/ppermute | solution.py:682
  35.8 0.0 copy-done.9
  35.8 0.0 copy-done.10
  35.8 0.0 copy-done.12
  35.8 4.7 %shard_map.158 = (f32[64,64]{1,0:T(8,128)S(1)}, f32[16,256,64]{2,1,0:T(8,128)}) custom-call(f32[11,448,128]{2,1,0:T(8,128)S(1)} %get-tuple-element.68.f, f32[11,256,128]{2,1,0:T(8,128)S(1)} %get-tuple-element.52.va.vai, f32[11,256,128]{2,1,0:T(8,128)S(1)} %get-tuple-element.53.vd.vdi, bf16[2,224,224]{2,1,0:T(8,128)(2,1)S(1)} %copy-done.10, ...), custom_call_target="tpu_custom_call" | custom-call | flops 2000000000 | tf_op jit(solution)/shard_map/pallas_call | solution.py:668
  40.6 0.0 collective-permute-done.10.nx
  40.6 0.4 collective-permute-done.11.ny
  40.9 0.0 collective-permute-done.12.nz
  40.9 0.4 shard_map.159.early
  41.4 0.0 collective-permute-done.13.nx
  41.4 0.0 collective-permute-done.14.ny
  41.4 1.0 %shard_map.160 = f32[7,64,64]{2,1,0:T(8,128)} custom-call(f32[64,64]{1,0:T(8,128)S(1)} %get-tuple-element.70.diag, f32[4,64,64]{2,1,0:T(8,128)S(1)} %shard_map.159.early, f32[256,128]{1,0:T(8,128)S(1)} %get-tuple-element.74.ox, f32[256,128]{1,0:T(8,128)S(1)} %get-tuple-element.75.oy, f32[256,128]{1,0:T(8,128)S(1)} %collective-permute-done.13.nx, ...), custom_call_target="tpu_custom_call" | custom-call | tf_op jit(solution)/shard_map/pallas_call | solution.py:668
  (4 shorter events, 0.0 us)
Async XLA Ops:
  0.6 9.7 %copy-start = (f32[16,16,16,64]{3,2,1,0:T(8,128)S(1)}, f32[16,16,16,64]{3,2,1,0:T(8,128)}, u32[]{:S(2)}) copy-start(f32[16,16,16,64]{3,2,1,0:T(8,128)} %param.14) | copy-start | bytes 3145732
  2.2 11.5 %collective-permute-start = (f32[400,128]{1,0:T(8,128)S(1)}, f32[400,128]{1,0:T(8,128)S(1)}, u32[]{:S(2)}, u32[]{:S(2)}) collective-permute-start(f32[400,128]{1,0:T(8,128)S(1)} %get-tuple-element.39), channel_id=1, source_target_pairs={{0,2},{2,4},{4,6},{6,0},{1,3},{3,5},{5,7},{7,1},{8,10},{10,12},{12... | collective-permute-start | bytes 614408 | tf_op jit(solution)/shard_map/ppermute | solution.py:682
  5.3 6.2 %collective-permute-start.2 = (f32[152,128]{1,0:T(8,128)S(1)}, f32[152,128]{1,0:T(8,128)S(1)}, u32[]{:S(2)}, u32[]{:S(2)}) collective-permute-start(f32[152,128]{1,0:T(8,128)S(1)} %get-tuple-element.42), channel_id=1, source_target_pairs={{0,8},{8,16},{16,24},{24,0},{1,9},{9,17},{17,25},{25,1},{2,10},{10... | collective-permute-start | bytes 233480 | tf_op jit(solution)/shard_map/ppermute | solution.py:682
  6.8 6.9 %collective-permute-start.3 = (f32[152,128]{1,0:T(8,128)S(1)}, f32[152,128]{1,0:T(8,128)S(1)}, u32[]{:S(2)}, u32[]{:S(2)}) collective-permute-start(f32[152,128]{1,0:T(8,128)S(1)} %get-tuple-element.43), channel_id=1, source_target_pairs={{0,24},{8,0},{16,8},{24,16},{1,25},{9,1},{17,9},{25,17},{2,26},{10... | collective-permute-start | bytes 233480 | tf_op jit(solution)/shard_map/ppermute | solution.py:682
  8.2 12.2 %collective-permute-start.1 = (f32[400,128]{1,0:T(8,128)S(1)}, f32[400,128]{1,0:T(8,128)S(1)}, u32[]{:S(2)}, u32[]{:S(2)}) collective-permute-start(f32[400,128]{1,0:T(8,128)S(1)} %get-tuple-element.40), channel_id=1, source_target_pairs={{0,6},{2,0},{4,2},{6,4},{1,7},{3,1},{5,3},{7,5},{8,14},{10,8},{12,... | collective-permute-start | bytes 614408 | tf_op jit(solution)/shard_map/ppermute | solution.py:682
  10.7 7.6 %collective-permute-start.6 = (f32[240,128]{1,0:T(8,128)S(1)}, f32[240,128]{1,0:T(8,128)S(1)}, u32[]{:S(2)}, u32[]{:S(2)}) collective-permute-start(f32[240,128]{1,0:T(8,128)S(1)} %get-tuple-element.48), channel_id=1, source_target_pairs={{0,8},{8,16},{16,24},{24,0},{1,9},{9,17},{17,25},{25,1},{2,10},{10... | collective-permute-start | bytes 368648 | tf_op jit(solution)/shard_map/ppermute | solution.py:682
  11.5 7.1 %collective-permute-start.7 = (f32[240,128]{1,0:T(8,128)S(1)}, f32[240,128]{1,0:T(8,128)S(1)}, u32[]{:S(2)}, u32[]{:S(2)}) collective-permute-start(f32[240,128]{1,0:T(8,128)S(1)} %get-tuple-element.49), channel_id=1, source_target_pairs={{0,24},{8,0},{16,8},{24,16},{1,25},{9,1},{17,9},{25,17},{2,26},{10... | collective-permute-start | bytes 368648 | tf_op jit(solution)/shard_map/ppermute | solution.py:682
  13.7 4.0 %copy-start.1 = (bf16[72,2816]{1,0:T(8,128)(2,1)S(1)}, bf16[72,2816]{1,0:T(8,128)(2,1)}, u32[]{:S(2)}) copy-start(bf16[72,2816]{1,0:T(8,128)(2,1)} %constant.24.clone.vspread) | copy-start | bytes 1216516
  13.7 4.9 %copy-start.5 = (f32[2,256,128]{2,1,0:T(8,128)S(1)}, f32[2,256,128]{2,1,0:T(8,128)}, u32[]{:S(2)}) copy-start(f32[2,256,128]{2,1,0:T(8,128)} %constant.25.clone.zpick) | copy-start | bytes 786436
  13.8 5.2 %copy-start.2 = (f32[61,128]{1,0:T(8,128)S(1)}, f32[61,128]{1,0:T(8,128)}, u32[]{:S(2)}) copy-start(f32[61,128]{1,0:T(8,128)} %constant.26.clone.coef) | copy-start | bytes 93700
  13.8 6.5 %collective-permute-start.4 = (f32[152,128]{1,0:T(8,128)S(1)}, f32[152,128]{1,0:T(8,128)S(1)}, u32[]{:S(2)}, u32[]{:S(2)}) collective-permute-start(f32[152,128]{1,0:T(8,128)S(1)} %get-tuple-element.44.ehi), channel_id=1, source_target_pairs={{0,2},{2,4},{4,6},{6,0},{1,3},{3,5},{5,7},{7,1},{8,10},{10,12},{12... | collective-permute-start | bytes 233480 | tf_op jit(solution)/shard_map/ppermute | solution.py:682
  14.7 5.7 %collective-permute-start.5 = (f32[152,128]{1,0:T(8,128)S(1)}, f32[152,128]{1,0:T(8,128)S(1)}, u32[]{:S(2)}, u32[]{:S(2)}) collective-permute-start(f32[152,128]{1,0:T(8,128)S(1)} %get-tuple-element.45.elo), channel_id=1, source_target_pairs={{0,6},{2,0},{4,2},{6,4},{1,7},{3,1},{5,3},{7,5},{8,14},{10,8},{12,... | collective-permute-start | bytes 233480 | tf_op jit(solution)/shard_map/ppermute | solution.py:682
  19.0 2.3 %collective-permute-start.9 = (f32[2,552,128]{2,1,0:T(8,128)S(1)}, f32[2,552,128]{2,1,0:T(8,128)S(1)}, u32[]{:S(2)}, u32[]{:S(2)}) collective-permute-start(f32[2,552,128]{2,1,0:T(8,128)S(1)} %get-tuple-element.58), channel_id=1, source_target_pairs={{0,1},{1,0},{2,3},{3,2},{4,5},{5,4},{6,7},{7,6},{8,9},{9,8},{10,11... | collective-permute-start | bytes 1695752 | tf_op jit(solution)/shard_map/ppermute | solution.py:682
  19.1 1.3 %copy-start.11 = (f32[2,128,128]{2,1,0:T(8,128)S(1)}, f32[2,128,128]{2,1,0:T(8,128)}, u32[]{:S(2)}) copy-start(f32[2,128,128]{2,1,0:T(8,128)} %constant.27.clone.zpick) | copy-start | bytes 393220
  20.8 1.9 %collective-permute-start.8 = (f32[2,288,128]{2,1,0:T(8,128)S(1)}, f32[2,288,128]{2,1,0:T(8,128)S(1)}, u32[]{:S(2)}, u32[]{:S(2)}) collective-permute-start(f32[2,288,128]{2,1,0:T(8,128)S(1)} %get-tuple-element.55), channel_id=1, source_target_pairs={{0,1},{1,0},{2,3},{3,2},{4,5},{5,4},{6,7},{7,6},{8,9},{9,8},{10,11... | collective-permute-start | bytes 884744 | tf_op jit(solution)/shard_map/ppermute | solution.py:682
  21.3 1.4 %copy-start.3 = (bf16[2,256,256]{2,1,0:T(8,128)(2,1)S(1)}, bf16[2,256,256]{2,1,0:T(8,128)(2,1)}, u32[]{:S(2)}) copy-start(bf16[2,256,256]{2,1,0:T(8,128)(2,1)} %constant.29.clone.w1l) | copy-start | bytes 786436
  21.3 1.4 %copy-start.4 = (bf16[2,256,256]{2,1,0:T(8,128)(2,1)S(1)}, bf16[2,256,256]{2,1,0:T(8,128)(2,1)}, u32[]{:S(2)}) copy-start(bf16[2,256,256]{2,1,0:T(8,128)(2,1)} %constant.28.clone.w1h) | copy-start | bytes 786436
  21.3 1.4 %copy-start.6 = (bf16[2,224,256]{2,1,0:T(8,128)(2,1)S(1)}, bf16[2,224,256]{2,1,0:T(8,128)(2,1)}, u32[]{:S(2)}) copy-start(bf16[2,224,256]{2,1,0:T(8,128)(2,1)} %constant.31.clone.w2l) | copy-start | bytes 688132
  21.3 1.5 %copy-start.7 = (bf16[2,224,256]{2,1,0:T(8,128)(2,1)S(1)}, bf16[2,224,256]{2,1,0:T(8,128)(2,1)}, u32[]{:S(2)}) copy-start(bf16[2,224,256]{2,1,0:T(8,128)(2,1)} %constant.30.clone.w2h) | copy-start | bytes 688132
  21.3 1.4 %copy-start.8 = (f32[11,128]{1,0:T(8,128)S(1)}, f32[11,128]{1,0:T(8,128)}, u32[]{:S(2)}) copy-start(f32[11,128]{1,0:T(8,128)} %constant.32.clone.dcoef) | copy-start | bytes 16900
  22.8 13.0 %copy-start.9 = (bf16[2,224,224]{2,1,0:T(8,128)(2,1)S(1)}, bf16[2,224,224]{2,1,0:T(8,128)(2,1)}, u32[]{:S(2)}) copy-start(bf16[2,224,224]{2,1,0:T(8,128)(2,1)} %constant.34.clone.bl) | copy-start | bytes 602116
  22.8 13.0 %copy-start.10 = (bf16[2,224,224]{2,1,0:T(8,128)(2,1)S(1)}, bf16[2,224,224]{2,1,0:T(8,128)(2,1)}, u32[]{:S(2)}) copy-start(bf16[2,224,224]{2,1,0:T(8,128)(2,1)} %constant.33.clone.bh) | copy-start | bytes 602116
  22.8 13.0 %copy-start.12 = (f32[121,128]{1,0:T(8,128)S(1)}, f32[121,128]{1,0:T(8,128)}, u32[]{:S(2)}) copy-start(f32[121,128]{1,0:T(8,128)} %constant.35.clone.coef) | copy-start | bytes 185860
  29.4 11.5 %collective-permute-start.12 = (f32[2,256,128]{2,1,0:T(8,128)S(1)}, f32[2,256,128]{2,1,0:T(8,128)S(1)}, u32[]{:S(2)}, u32[]{:S(2)}) collective-permute-start(f32[2,256,128]{2,1,0:T(8,128)S(1)} %get-tuple-element.73.oz), channel_id=1, source_target_pairs={{0,1},{1,0},{2,3},{3,2},{4,5},{5,4},{6,7},{7,6},{8,9},{9,8},{10,11... | collective-permute-start | bytes 786440 | tf_op jit(solution)/shard_map/ppermute | solution.py:682
  29.6 11.8 %collective-permute-start.13 = (f32[256,128]{1,0:T(8,128)S(1)}, f32[256,128]{1,0:T(8,128)S(1)}, u32[]{:S(2)}, u32[]{:S(2)}) collective-permute-start(f32[256,128]{1,0:T(8,128)S(1)} %get-tuple-element.71.ox), channel_id=1, source_target_pairs={{0,24},{8,0},{16,8},{24,16},{1,25},{9,1},{17,9},{25,17},{2,26},{10... | collective-permute-start | bytes 393224 | tf_op jit(solution)/shard_map/ppermute | solution.py:682
  32.0 9.4 %collective-permute-start.14 = (f32[256,128]{1,0:T(8,128)S(1)}, f32[256,128]{1,0:T(8,128)S(1)}, u32[]{:S(2)}, u32[]{:S(2)}) collective-permute-start(f32[256,128]{1,0:T(8,128)S(1)} %get-tuple-element.72.oy), channel_id=1, source_target_pairs={{0,2},{2,4},{4,6},{6,0},{1,3},{3,5},{5,7},{7,1},{8,10},{10,12},{12... | collective-permute-start | bytes 393224 | tf_op jit(solution)/shard_map/ppermute | solution.py:682
  33.2 7.4 %collective-permute-start.10 = (f32[256,128]{1,0:T(8,128)S(1)}, f32[256,128]{1,0:T(8,128)S(1)}, u32[]{:S(2)}, u32[]{:S(2)}) collective-permute-start(f32[256,128]{1,0:T(8,128)S(1)} %get-tuple-element.74.ox), channel_id=1, source_target_pairs={{0,8},{8,16},{16,24},{24,0},{1,9},{9,17},{17,25},{25,1},{2,10},{10... | collective-permute-start | bytes 393224 | tf_op jit(solution)/shard_map/ppermute | solution.py:682
  33.2 7.8 %collective-permute-start.11 = (f32[256,128]{1,0:T(8,128)S(1)}, f32[256,128]{1,0:T(8,128)S(1)}, u32[]{:S(2)}, u32[]{:S(2)}) collective-permute-start(f32[256,128]{1,0:T(8,128)S(1)} %get-tuple-element.75.oy), channel_id=1, source_target_pairs={{0,6},{2,0},{4,2},{6,4},{1,7},{3,1},{5,3},{7,5},{8,14},{10,8},{12,... | collective-permute-start | bytes 393224 | tf_op jit(solution)/shard_map/ppermute | solution.py:682

commit v8 on v7

--- a/solution.py
+++ b/solution.py
@@ -256,6 +256,7 @@
 HALF_WIDTH = (HIGH_BOUND - CUTOFF) / 2.0
 S0 = HALF_WIDTH / (LOW_BOUND - CENTER)
 S1 = 1.0 / (2.0 / S0 - S0)
+SECOND = (2.0 * S1 / HALF_WIDTH) * (S0 / HALF_WIDTH)
 
 
 def mix(coef, table, items):
@@ -501,7 +502,7 @@
                 values = []
                 for r0, block in blocks:
                     local = given[g, r0 : r0 + 16, :] if r0 < cross else y[g, r0 : r0 + 16, :]
-                    values.append((local + block) * (S0 / HALF_WIDTH))
+                    values.append(local + block)
                     y[g, r0 : r0 + 16, :] = values[-1]
                 again(values, put, at)
 
@@ -514,7 +515,7 @@
                     x = xr[g, r0 - face : r1 - face, :]
                 else:
                     x = outer[g, r0:r1, :] if g < BUF else inner[g - BUF, r0:r1, :]
-                out[g, r0:r1, :] = local[g] * (2.0 * S1 / HALF_WIDTH) - (S0 * S1) * x
+                out[g, r0:r1, :] = local[g] * SECOND - (S0 * S1) * x
     flat = plan.flat
     for n, (g0, g1) in enumerate(pairs(g_all)):
         cols = slice(g0 * lanes, g1 * lanes)
@@ -777,7 +778,7 @@
     msg = near(face, lanes)
     corners = 2 * BUF * corner
     product = folded_rows(plan, matrix)
-    second = 2.0 * S1 / HALF_WIDTH * product[:, : plan.flat]
+    second = SECOND * product[:, : plan.flat]
     base = 9 if paired else 10
     filtered, mx, my, mz, _, _ = call(
         part(filter_kernel, plan, paired),

time: 42.7 us -> 42.3 us (level)
  Pallas kernels: 18.9 us -> 18.4 us
where the time goes in v8:
time: 42.3 us; the launch traced here: 42.1 us
  starting transfers between devices  21.9 us (52%)
  Pallas kernels  18.4 us (43%)
  between operations  1.06 us (3%)
  waiting for transfers between devices  0.66 us (2%)
    ppermute x15, starting transfers between devices, shift(): lax.ppermute(array, axis, [(i, (i + step) % count) for i in range(count)])  21.9 us
    pallas_call x12, Pallas kernels, call(): pl.pallas_call(kernel, out_shape=outs, in_specs=[apart if i in far_in els...  18.4 us
  transfers between devices with their start and end apart: 15, of which 2 were waited for; matrix products, arithmetic and copies ran while one was open for 0% of the time, Pallas kernels for 23%

profile of v8, /device:TPU:0, one launch (start us, length us, event | category | flops | bytes accessed | tf_op | source)
XLA Modules:
  0.0 42.1 jit_solution(7540361707449825439)
XLA Ops:
  0.6 0.0 copy-start
  0.6 1.6 %shard_map.149 = (f32[152,128]{1,0:T(8,128)S(1)}, f32[152,128]{1,0:T(8,128)S(1)}, f32[400,128]{1,0:T(8,128)S(1)}, f32[400,128]{1,0:T(8,128)S(1)}, f32[16,256]{1,0:T(8,128)S(1)}) custom-call(f32[16,256,64]{2,1,0:T(8,128)} %bitcast.4, f32[256,16]{1,0:T(8,128)} %bitcast.7), custom_call_target="tpu_custom_call" | custom-call | tf_op jit(solution)/shard_map/pallas_call | solution.py:669
  2.2 3.1 %collective-permute-start = (f32[400,128]{1,0:T(8,128)S(1)}, f32[400,128]{1,0:T(8,128)S(1)}, u32[]{:S(2)}, u32[]{:S(2)}) collective-permute-start(f32[400,128]{1,0:T(8,128)S(1)} %get-tuple-element.39), channel_id=1, source_target_pairs={{0,2},{2,4},{4,6},{6,0},{1,3},{3,5},{5,7},{7,1},{8,10},{10,12},{12... | collective-permute-start | bytes 614408 | tf_op jit(solution)/shard_map/ppermute | solution.py:683
  5.3 1.5 %collective-permute-start.2 = (f32[152,128]{1,0:T(8,128)S(1)}, f32[152,128]{1,0:T(8,128)S(1)}, u32[]{:S(2)}, u32[]{:S(2)}) collective-permute-start(f32[152,128]{1,0:T(8,128)S(1)} %get-tuple-element.42), channel_id=1, source_target_pairs={{0,8},{8,16},{16,24},{24,0},{1,9},{9,17},{17,25},{25,1},{2,10},{10... | collective-permute-start | bytes 233480 | tf_op jit(solution)/shard_map/ppermute | solution.py:683
  6.8 1.4 %collective-permute-start.3 = (f32[152,128]{1,0:T(8,128)S(1)}, f32[152,128]{1,0:T(8,128)S(1)}, u32[]{:S(2)}, u32[]{:S(2)}) collective-permute-start(f32[152,128]{1,0:T(8,128)S(1)} %get-tuple-element.43), channel_id=1, source_target_pairs={{0,24},{8,0},{16,8},{24,16},{1,25},{9,1},{17,9},{25,17},{2,26},{10... | collective-permute-start | bytes 233480 | tf_op jit(solution)/shard_map/ppermute | solution.py:683
  8.2 2.1 %collective-permute-start.1 = (f32[400,128]{1,0:T(8,128)S(1)}, f32[400,128]{1,0:T(8,128)S(1)}, u32[]{:S(2)}, u32[]{:S(2)}) collective-permute-start(f32[400,128]{1,0:T(8,128)S(1)} %get-tuple-element.40), channel_id=1, source_target_pairs={{0,6},{2,0},{4,2},{6,4},{1,7},{3,1},{5,3},{7,5},{8,14},{10,8},{12,... | collective-permute-start | bytes 614408 | tf_op jit(solution)/shard_map/ppermute | solution.py:683
  10.3 0.0 copy-done
  10.3 0.4 shard_map.151
  10.7 0.8 %collective-permute-start.6 = (f32[240,128]{1,0:T(8,128)S(1)}, f32[240,128]{1,0:T(8,128)S(1)}, u32[]{:S(2)}, u32[]{:S(2)}) collective-permute-start(f32[240,128]{1,0:T(8,128)S(1)} %get-tuple-element.48), channel_id=1, source_target_pairs={{0,8},{8,16},{16,24},{24,0},{1,9},{9,17},{17,25},{25,1},{2,10},{10... | collective-permute-start | bytes 368648 | tf_op jit(solution)/shard_map/ppermute | solution.py:683
  11.5 0.0 collective-permute-done.2.lo
  11.5 2.2 %collective-permute-start.7 = (f32[240,128]{1,0:T(8,128)S(1)}, f32[240,128]{1,0:T(8,128)S(1)}, u32[]{:S(2)}, u32[]{:S(2)}) collective-permute-start(f32[240,128]{1,0:T(8,128)S(1)} %get-tuple-element.49), channel_id=1, source_target_pairs={{0,24},{8,0},{16,8},{24,16},{1,25},{9,1},{17,9},{25,17},{2,26},{10... | collective-permute-start | bytes 368648 | tf_op jit(solution)/shard_map/ppermute | solution.py:683
  13.7 0.0 collective-permute-done.3.hi
  13.7 0.0 collective-permute-done.ahead.ylo
  13.7 0.0 copy-start.5
  13.7 0.1 shard_map.150
  13.8 0.0 copy-start.2
  13.8 0.9 %collective-permute-start.4 = (f32[152,128]{1,0:T(8,128)S(1)}, f32[152,128]{1,0:T(8,128)S(1)}, u32[]{:S(2)}, u32[]{:S(2)}) collective-permute-start(f32[152,128]{1,0:T(8,128)S(1)} %get-tuple-element.44.ehi), channel_id=1, source_target_pairs={{0,2},{2,4},{4,6},{6,0},{1,3},{3,5},{5,7},{7,1},{8,10},{10,12},{12... | collective-permute-start | bytes 233480 | tf_op jit(solution)/shard_map/ppermute | solution.py:683
  14.7 3.0 %collective-permute-start.5 = (f32[152,128]{1,0:T(8,128)S(1)}, f32[152,128]{1,0:T(8,128)S(1)}, u32[]{:S(2)}, u32[]{:S(2)}) collective-permute-start(f32[152,128]{1,0:T(8,128)S(1)} %get-tuple-element.45.elo), channel_id=1, source_target_pairs={{0,6},{2,0},{4,2},{6,4},{1,7},{3,1},{5,3},{7,5},{8,14},{10,8},{12,... | collective-permute-start | bytes 233480 | tf_op jit(solution)/shard_map/ppermute | solution.py:683
  17.7 0.0 copy-done.1
  17.7 0.6 %shard_map.152 = (f32[11,256,128]{2,1,0:T(8,128)S(1)}, f32[11,256,128]{2,1,0:T(8,128)S(1)}, f32[8,128]{1,0:T(8,128)S(1)}) custom-call(f32[24,256]{1,0:T(8,128)S(1)} %get-tuple-element.47.vx, bf16[72,2816]{1,0:T(8,128)(2,1)S(1)} %copy-done.1), custom_call_target="tpu_custom_call" | custom-call | tf_op jit(solution)/shard_map/pallas_call | solution.py:669
  18.3 0.0 collective-permute-done.6.lo
  18.3 0.3 collective-permute-done.7.hi
  18.6 0.0 copy-done.5
  18.6 0.4 shard_map.153
  19.0 0.1 collective-permute-start.9
  19.1 0.0 copy-done.2
  19.1 0.0 copy-start.11
  19.1 1.3 %shard_map.154 = (f32[11,448,128]{2,1,0:T(8,128)S(1)}, f32[8,128]{1,0:T(8,128)S(1)}, bf16[512,1408]{1,0:T(8,128)(2,1)S(1)}, bf16[512,1408]{1,0:T(8,128)(2,1)S(1)}) custom-call(f32[8,256,128]{2,1,0:T(8,128)S(1)} %get-tuple-element.46.inner, f32[3,256,128]{2,1,0:T(8,128)S(1)} %get-tuple-element.51.outer, f32[61,128]{1,0:T(8,128)S(1)} %copy-done.2, ...), custom_call_target="tpu_custom_call" | custom-call | tf_op jit(solution)/shard_map/pallas_call | solution.py:669
  20.4 0.0 collective-permute-done.1.yhi
  20.4 0.0 collective-permute-done.4.elo
  20.4 0.0 collective-permute-done.5.ehi
  20.4 0.0 copy-done.11
  20.4 0.4 shard_map.155
  20.8 0.5 %collective-permute-start.8 = (f32[2,288,128]{2,1,0:T(8,128)S(1)}, f32[2,288,128]{2,1,0:T(8,128)S(1)}, u32[]{:S(2)}, u32[]{:S(2)}) collective-permute-start(f32[2,288,128]{2,1,0:T(8,128)S(1)} %get-tuple-element.55), channel_id=1, source_target_pairs={{0,1},{1,0},{2,3},{3,2},{4,5},{5,4},{6,7},{7,6},{8,9},{9,8},{10,11... | collective-permute-start | bytes 884744 | tf_op jit(solution)/shard_map/ppermute | solution.py:683
  21.3 0.0 collective-permute-done.9.zi
  21.3 0.0 copy-start.7
  21.3 0.0 copy-start.8
  21.3 1.4 %shard_map.156 = (f32[11,448,128]{2,1,0:T(8,128)S(1)}, bf16[512,1408]{1,0:T(8,128)(2,1)S(1)}, bf16[512,1408]{1,0:T(8,128)(2,1)S(1)}, f32[11,192,128]{2,1,0:T(8,1...) custom-call(f32[11,128,128]{2,1,0:T(8,128)S(1)} %get-tuple-element.5, ...), custom_call_target="tpu_custom_call", output_to_operand_aliasing={{0}: (5, {}), {1}: (6, {}), {2}: (7, {})} | custom-call | tf_op jit(solution)/shard_map/pallas_call | solution.py:669
  22.7 0.0 collective-permute-done.8.zc
  22.7 0.0 copy-done.3
  22.7 0.0 copy-done.4
  22.8 0.0 copy-done.6
  22.8 0.0 copy-done.7
  22.8 0.0 copy-done.8
  22.8 0.0 copy-start.9
  22.8 0.0 copy-start.10
  22.8 0.0 copy-start.12
  22.8 6.2 %shard_map.157 = (f32[11,448,128]{2,1,0:T(8,128)S(1)}, f32[256,128]{1,0:T(8,128)S(1)}, f32[256,128]{1,0:T(8,128)S(1)}, f32[256,128]{1,0:T(8,128)S(1)}, f32[256,1...) custom-call(f32[2,288,128]{2,1,0:T(8,128)S(1)} %collective-permute-d, ...), custom_call_target="tpu_custom_call", output_to_operand_aliasing={{6}: (9, {}), {7}: (10, {})} | custom-call | tf_op jit(solution)/shard_map/pallas_call | solution.py:669
  29.0 0.2 collective-permute-start.12
  29.2 2.4 %collective-permute-start.13 = (f32[256,128]{1,0:T(8,128)S(1)}, f32[256,128]{1,0:T(8,128)S(1)}, u32[]{:S(2)}, u32[]{:S(2)}) collective-permute-start(f32[256,128]{1,0:T(8,128)S(1)} %get-tuple-element.71.ox), channel_id=1, source_target_pairs={{0,24},{8,0},{16,8},{24,16},{1,25},{9,1},{17,9},{25,17},{2,26},{10... | collective-permute-start | bytes 393224 | tf_op jit(solution)/shard_map/ppermute | solution.py:683
  31.6 1.2 %collective-permute-start.14 = (f32[256,128]{1,0:T(8,128)S(1)}, f32[256,128]{1,0:T(8,128)S(1)}, u32[]{:S(2)}, u32[]{:S(2)}) collective-permute-start(f32[256,128]{1,0:T(8,128)S(1)} %get-tuple-element.72.oy), channel_id=1, source_target_pairs={{0,2},{2,4},{4,6},{6,0},{1,3},{3,5},{5,7},{7,1},{8,10},{10,12},{12... | collective-permute-start | bytes 393224 | tf_op jit(solution)/shard_map/ppermute | solution.py:683
  32.7 0.0 collective-permute-start.10
  32.7 2.7 %collective-permute-start.11 = (f32[256,128]{1,0:T(8,128)S(1)}, f32[256,128]{1,0:T(8,128)S(1)}, u32[]{:S(2)}, u32[]{:S(2)}) collective-permute-start(f32[256,128]{1,0:T(8,128)S(1)} %get-tuple-element.75.oy), channel_id=1, source_target_pairs={{0,6},{2,0},{4,2},{6,4},{1,7},{3,1},{5,3},{7,5},{8,14},{10,8},{12,... | collective-permute-start | bytes 393224 | tf_op jit(solution)/shard_map/ppermute | solution.py:683
  35.4 0.0 copy-done.9
  35.4 0.0 copy-done.10
  35.4 0.0 copy-done.12
  35.4 4.7 %shard_map.158 = (f32[64,64]{1,0:T(8,128)S(1)}, f32[16,256,64]{2,1,0:T(8,128)}) custom-call(f32[11,448,128]{2,1,0:T(8,128)S(1)} %get-tuple-element.68.f, f32[11,256,128]{2,1,0:T(8,128)S(1)} %get-tuple-element.52.va.vai, f32[11,256,128]{2,1,0:T(8,128)S(1)} %get-tuple-element.53.vd.vdi, bf16[2,224,224]{2,1,0:T(8,128)(2,1)S(1)} %copy-done.10, ...), custom_call_target="tpu_custom_call" | custom-call | flops 2000000000 | tf_op jit(solution)/shard_map/pallas_call | solution.py:669
  40.1 0.0 collective-permute-done.10.nx
  40.1 0.4 collective-permute-done.11.ny
  40.5 0.0 collective-permute-done.12.nz
  40.5 0.4 shard_map.159.early
  40.9 0.0 collective-permute-done.13.nx
  40.9 0.0 collective-permute-done.14.ny
  41.0 1.0 %shard_map.160 = f32[7,64,64]{2,1,0:T(8,128)} custom-call(f32[64,64]{1,0:T(8,128)S(1)} %get-tuple-element.70.diag, f32[4,64,64]{2,1,0:T(8,128)S(1)} %shard_map.159.early, f32[256,128]{1,0:T(8,128)S(1)} %get-tuple-element.74.ox, f32[256,128]{1,0:T(8,128)S(1)} %get-tuple-element.75.oy, f32[256,128]{1,0:T(8,128)S(1)} %collective-permute-done.13.nx, ...), custom_call_target="tpu_custom_call" | custom-call | tf_op jit(solution)/shard_map/pallas_call | solution.py:669
  (4 shorter events, 0.0 us)
Async XLA Ops:
  0.6 9.7 %copy-start = (f32[16,16,16,64]{3,2,1,0:T(8,128)S(1)}, f32[16,16,16,64]{3,2,1,0:T(8,128)}, u32[]{:S(2)}) copy-start(f32[16,16,16,64]{3,2,1,0:T(8,128)} %param.14) | copy-start | bytes 3145732
  2.2 11.5 %collective-permute-start = (f32[400,128]{1,0:T(8,128)S(1)}, f32[400,128]{1,0:T(8,128)S(1)}, u32[]{:S(2)}, u32[]{:S(2)}) collective-permute-start(f32[400,128]{1,0:T(8,128)S(1)} %get-tuple-element.39), channel_id=1, source_target_pairs={{0,2},{2,4},{4,6},{6,0},{1,3},{3,5},{5,7},{7,1},{8,10},{10,12},{12... | collective-permute-start | bytes 614408 | tf_op jit(solution)/shard_map/ppermute | solution.py:683
  5.3 6.2 %collective-permute-start.2 = (f32[152,128]{1,0:T(8,128)S(1)}, f32[152,128]{1,0:T(8,128)S(1)}, u32[]{:S(2)}, u32[]{:S(2)}) collective-permute-start(f32[152,128]{1,0:T(8,128)S(1)} %get-tuple-element.42), channel_id=1, source_target_pairs={{0,8},{8,16},{16,24},{24,0},{1,9},{9,17},{17,25},{25,1},{2,10},{10... | collective-permute-start | bytes 233480 | tf_op jit(solution)/shard_map/ppermute | solution.py:683
  6.8 6.9 %collective-permute-start.3 = (f32[152,128]{1,0:T(8,128)S(1)}, f32[152,128]{1,0:T(8,128)S(1)}, u32[]{:S(2)}, u32[]{:S(2)}) collective-permute-start(f32[152,128]{1,0:T(8,128)S(1)} %get-tuple-element.43), channel_id=1, source_target_pairs={{0,24},{8,0},{16,8},{24,16},{1,25},{9,1},{17,9},{25,17},{2,26},{10... | collective-permute-start | bytes 233480 | tf_op jit(solution)/shard_map/ppermute | solution.py:683
  8.2 12.2 %collective-permute-start.1 = (f32[400,128]{1,0:T(8,128)S(1)}, f32[400,128]{1,0:T(8,128)S(1)}, u32[]{:S(2)}, u32[]{:S(2)}) collective-permute-start(f32[400,128]{1,0:T(8,128)S(1)} %get-tuple-element.40), channel_id=1, source_target_pairs={{0,6},{2,0},{4,2},{6,4},{1,7},{3,1},{5,3},{7,5},{8,14},{10,8},{12,... | collective-permute-start | bytes 614408 | tf_op jit(solution)/shard_map/ppermute | solution.py:683
  10.7 7.6 %collective-permute-start.6 = (f32[240,128]{1,0:T(8,128)S(1)}, f32[240,128]{1,0:T(8,128)S(1)}, u32[]{:S(2)}, u32[]{:S(2)}) collective-permute-start(f32[240,128]{1,0:T(8,128)S(1)} %get-tuple-element.48), channel_id=1, source_target_pairs={{0,8},{8,16},{16,24},{24,0},{1,9},{9,17},{17,25},{25,1},{2,10},{10... | collective-permute-start | bytes 368648 | tf_op jit(solution)/shard_map/ppermute | solution.py:683
  11.5 7.1 %collective-permute-start.7 = (f32[240,128]{1,0:T(8,128)S(1)}, f32[240,128]{1,0:T(8,128)S(1)}, u32[]{:S(2)}, u32[]{:S(2)}) collective-permute-start(f32[240,128]{1,0:T(8,128)S(1)} %get-tuple-element.49), channel_id=1, source_target_pairs={{0,24},{8,0},{16,8},{24,16},{1,25},{9,1},{17,9},{25,17},{2,26},{10... | collective-permute-start | bytes 368648 | tf_op jit(solution)/shard_map/ppermute | solution.py:683
  13.7 4.0 %copy-start.1 = (bf16[72,2816]{1,0:T(8,128)(2,1)S(1)}, bf16[72,2816]{1,0:T(8,128)(2,1)}, u32[]{:S(2)}) copy-start(bf16[72,2816]{1,0:T(8,128)(2,1)} %constant.24.clone.vspread) | copy-start | bytes 1216516
  13.7 4.9 %copy-start.5 = (f32[2,256,128]{2,1,0:T(8,128)S(1)}, f32[2,256,128]{2,1,0:T(8,128)}, u32[]{:S(2)}) copy-start(f32[2,256,128]{2,1,0:T(8,128)} %constant.25.clone.zpick) | copy-start | bytes 786436
  13.8 5.2 %copy-start.2 = (f32[61,128]{1,0:T(8,128)S(1)}, f32[61,128]{1,0:T(8,128)}, u32[]{:S(2)}) copy-start(f32[61,128]{1,0:T(8,128)} %constant.26.clone.coef) | copy-start | bytes 93700
  13.8 6.5 %collective-permute-start.4 = (f32[152,128]{1,0:T(8,128)S(1)}, f32[152,128]{1,0:T(8,128)S(1)}, u32[]{:S(2)}, u32[]{:S(2)}) collective-permute-start(f32[152,128]{1,0:T(8,128)S(1)} %get-tuple-element.44.ehi), channel_id=1, source_target_pairs={{0,2},{2,4},{4,6},{6,0},{1,3},{3,5},{5,7},{7,1},{8,10},{10,12},{12... | collective-permute-start | bytes 233480 | tf_op jit(solution)/shard_map/ppermute | solution.py:683
  14.7 5.7 %collective-permute-start.5 = (f32[152,128]{1,0:T(8,128)S(1)}, f32[152,128]{1,0:T(8,128)S(1)}, u32[]{:S(2)}, u32[]{:S(2)}) collective-permute-start(f32[152,128]{1,0:T(8,128)S(1)} %get-tuple-element.45.elo), channel_id=1, source_target_pairs={{0,6},{2,0},{4,2},{6,4},{1,7},{3,1},{5,3},{7,5},{8,14},{10,8},{12,... | collective-permute-start | bytes 233480 | tf_op jit(solution)/shard_map/ppermute | solution.py:683
  19.0 2.3 %collective-permute-start.9 = (f32[2,552,128]{2,1,0:T(8,128)S(1)}, f32[2,552,128]{2,1,0:T(8,128)S(1)}, u32[]{:S(2)}, u32[]{:S(2)}) collective-permute-start(f32[2,552,128]{2,1,0:T(8,128)S(1)} %get-tuple-element.58), channel_id=1, source_target_pairs={{0,1},{1,0},{2,3},{3,2},{4,5},{5,4},{6,7},{7,6},{8,9},{9,8},{10,11... | collective-permute-start | bytes 1695752 | tf_op jit(solution)/shard_map/ppermute | solution.py:683
  19.1 1.3 %copy-start.11 = (f32[2,128,128]{2,1,0:T(8,128)S(1)}, f32[2,128,128]{2,1,0:T(8,128)}, u32[]{:S(2)}) copy-start(f32[2,128,128]{2,1,0:T(8,128)} %constant.27.clone.zpick) | copy-start | bytes 393220
  20.8 1.9 %collective-permute-start.8 = (f32[2,288,128]{2,1,0:T(8,128)S(1)}, f32[2,288,128]{2,1,0:T(8,128)S(1)}, u32[]{:S(2)}, u32[]{:S(2)}) collective-permute-start(f32[2,288,128]{2,1,0:T(8,128)S(1)} %get-tuple-element.55), channel_id=1, source_target_pairs={{0,1},{1,0},{2,3},{3,2},{4,5},{5,4},{6,7},{7,6},{8,9},{9,8},{10,11... | collective-permute-start | bytes 884744 | tf_op jit(solution)/shard_map/ppermute | solution.py:683
  21.3 1.4 %copy-start.3 = (bf16[2,256,256]{2,1,0:T(8,128)(2,1)S(1)}, bf16[2,256,256]{2,1,0:T(8,128)(2,1)}, u32[]{:S(2)}) copy-start(bf16[2,256,256]{2,1,0:T(8,128)(2,1)} %constant.29.clone.w1l) | copy-start | bytes 786436
  21.3 1.4 %copy-start.4 = (bf16[2,256,256]{2,1,0:T(8,128)(2,1)S(1)}, bf16[2,256,256]{2,1,0:T(8,128)(2,1)}, u32[]{:S(2)}) copy-start(bf16[2,256,256]{2,1,0:T(8,128)(2,1)} %constant.28.clone.w1h) | copy-start | bytes 786436
  21.3 1.4 %copy-start.6 = (bf16[2,224,256]{2,1,0:T(8,128)(2,1)S(1)}, bf16[2,224,256]{2,1,0:T(8,128)(2,1)}, u32[]{:S(2)}) copy-start(bf16[2,224,256]{2,1,0:T(8,128)(2,1)} %constant.31.clone.w2l) | copy-start | bytes 688132
  21.3 1.5 %copy-start.7 = (bf16[2,224,256]{2,1,0:T(8,128)(2,1)S(1)}, bf16[2,224,256]{2,1,0:T(8,128)(2,1)}, u32[]{:S(2)}) copy-start(bf16[2,224,256]{2,1,0:T(8,128)(2,1)} %constant.30.clone.w2h) | copy-start | bytes 688132
  21.3 1.4 %copy-start.8 = (f32[11,128]{1,0:T(8,128)S(1)}, f32[11,128]{1,0:T(8,128)}, u32[]{:S(2)}) copy-start(f32[11,128]{1,0:T(8,128)} %constant.32.clone.dcoef) | copy-start | bytes 16900
  22.8 12.6 %copy-start.9 = (bf16[2,224,224]{2,1,0:T(8,128)(2,1)S(1)}, bf16[2,224,224]{2,1,0:T(8,128)(2,1)}, u32[]{:S(2)}) copy-start(bf16[2,224,224]{2,1,0:T(8,128)(2,1)} %constant.34.clone.bl) | copy-start | bytes 602116
  22.8 12.6 %copy-start.10 = (bf16[2,224,224]{2,1,0:T(8,128)(2,1)S(1)}, bf16[2,224,224]{2,1,0:T(8,128)(2,1)}, u32[]{:S(2)}) copy-start(bf16[2,224,224]{2,1,0:T(8,128)(2,1)} %constant.33.clone.bh) | copy-start | bytes 602116
  22.8 12.6 %copy-start.12 = (f32[121,128]{1,0:T(8,128)S(1)}, f32[121,128]{1,0:T(8,128)}, u32[]{:S(2)}) copy-start(f32[121,128]{1,0:T(8,128)} %constant.35.clone.coef) | copy-start | bytes 185860
  29.0 11.5 %collective-permute-start.12 = (f32[2,256,128]{2,1,0:T(8,128)S(1)}, f32[2,256,128]{2,1,0:T(8,128)S(1)}, u32[]{:S(2)}, u32[]{:S(2)}) collective-permute-start(f32[2,256,128]{2,1,0:T(8,128)S(1)} %get-tuple-element.73.oz), channel_id=1, source_target_pairs={{0,1},{1,0},{2,3},{3,2},{4,5},{5,4},{6,7},{7,6},{8,9},{9,8},{10,11... | collective-permute-start | bytes 786440 | tf_op jit(solution)/shard_map/ppermute | solution.py:683
  29.2 11.8 %collective-permute-start.13 = (f32[256,128]{1,0:T(8,128)S(1)}, f32[256,128]{1,0:T(8,128)S(1)}, u32[]{:S(2)}, u32[]{:S(2)}) collective-permute-start(f32[256,128]{1,0:T(8,128)S(1)} %get-tuple-element.71.ox), channel_id=1, source_target_pairs={{0,24},{8,0},{16,8},{24,16},{1,25},{9,1},{17,9},{25,17},{2,26},{10... | collective-permute-start | bytes 393224 | tf_op jit(solution)/shard_map/ppermute | solution.py:683
  31.6 9.4 %collective-permute-start.14 = (f32[256,128]{1,0:T(8,128)S(1)}, f32[256,128]{1,0:T(8,128)S(1)}, u32[]{:S(2)}, u32[]{:S(2)}) collective-permute-start(f32[256,128]{1,0:T(8,128)S(1)} %get-tuple-element.72.oy), channel_id=1, source_target_pairs={{0,2},{2,4},{4,6},{6,0},{1,3},{3,5},{5,7},{7,1},{8,10},{10,12},{12... | collective-permute-start | bytes 393224 | tf_op jit(solution)/shard_map/ppermute | solution.py:683
  32.7 7.4 %collective-permute-start.10 = (f32[256,128]{1,0:T(8,128)S(1)}, f32[256,128]{1,0:T(8,128)S(1)}, u32[]{:S(2)}, u32[]{:S(2)}) collective-permute-start(f32[256,128]{1,0:T(8,128)S(1)} %get-tuple-element.74.ox), channel_id=1, source_target_pairs={{0,8},{8,16},{16,24},{24,0},{1,9},{9,17},{17,25},{25,1},{2,10},{10... | collective-permute-start | bytes 393224 | tf_op jit(solution)/shard_map/ppermute | solution.py:683
  32.7 7.8 %collective-permute-start.11 = (f32[256,128]{1,0:T(8,128)S(1)}, f32[256,128]{1,0:T(8,128)S(1)}, u32[]{:S(2)}, u32[]{:S(2)}) collective-permute-start(f32[256,128]{1,0:T(8,128)S(1)} %get-tuple-element.75.oy), channel_id=1, source_target_pairs={{0,6},{2,0},{4,2},{6,4},{1,7},{3,1},{5,3},{7,5},{8,14},{10,8},{12,... | collective-permute-start | bytes 393224 | tf_op jit(solution)/shard_map/ppermute | solution.py:683
